TPU v7x, 32 devices: a whole 2x2x4 slice. The times are simulated.
32 devices in a mesh: owner: 4 (over x, core), fsdp: 8 (over z, y).
Axes of the slice: x: 2, y: 2, z: 4, core: 2. Of those that a mesh axis runs over, the one named last changes fastest.
Arguments:
- gradients: bfloat16 [8, 16384, 512], P(None, ('fsdp', 'owner')), may hold values from -120 to 120
- momentum: float32 [8, 16384, 512], P('owner', 'fsdp'), may hold values from -120 to 120
- slot_table: int32 [8], replicated, may hold values from 0 to 7, each once
Outputs:
- updates: bfloat16 [8, 16384, 512], P(None, ('fsdp', 'owner'))
- new_momentum: float32 [8, 16384, 512], P('owner', 'fsdp')
Inputs may be any that keep to these rules, and one draw needn't show every extreme that they name: `slot_table`: each matrix has its own slot.
All inputs are finite; a program needn't handle non-finite values.
Results may differ from a plain program's by a relative error of at most 0.04.
Values may be sent and summed in bfloat16 or wider, within the bound.
No kernel may reach another device: no remote copies, remote signals or barrier semaphores. Data moves between devices by JAX's collectives and lax.ppermute only.
A program may use at most 128 MiB of HBM per device.

v0:
```python
import math

import jax
import jax.numpy as jnp
from jax import lax
from jax.sharding import PartitionSpec as P

LONG = 16384
RANK = 512
ITERS = 5


quintic = (3.4445, -4.775, 2.0315)
momentum_decay = 0.95
epsilon = 1e-07


def slot_inverse(slot_table, matrix_count):
    slots = jnp.arange(matrix_count, dtype=jnp.int32)
    matches = slot_table[None, :] == slots[:, None]
    return jnp.sum(jnp.where(matches, slots[None, :], 0), axis=1)


def on_device(gradients, momentum, slot_table):
    matrix_count = gradients.shape[0]
    inverse = slot_inverse(slot_table, matrix_count)
    ordered = jnp.take(gradients, inverse, axis=0)
    arrived = lax.all_to_all(ordered, "owner", split_axis=0, concat_axis=1, tiled=True)
    gradient = arrived.astype(jnp.float32)
    renewed = momentum_decay * momentum + gradient
    blended = gradient + momentum_decay * renewed
    squares = lax.psum(jnp.sum(blended * blended, axis=(1, 2)), "fsdp")
    panels = (blended / (jnp.sqrt(squares) + epsilon)[:, None, None]).astype(jnp.bfloat16)
    for iteration in range(ITERS):
        partial_value = jnp.einsum(
            "snq,snp->qsp", panels, panels, preferred_element_type=jnp.float32
        )
        gram_matrix = lax.psum(partial_value.astype(jnp.bfloat16), "fsdp")
        squared = jnp.einsum(
            "qsr,rsp->qsp", gram_matrix, gram_matrix, preferred_element_type=jnp.float32
        )
        polynomial = (quintic[1] * gram_matrix.astype(jnp.float32) + quintic[2] * squared).astype(
            jnp.bfloat16
        )
        product = jnp.einsum("snq,qsp->snp", panels, polynomial, preferred_element_type=jnp.float32)
        panels = (quintic[0] * panels.astype(jnp.float32) + product).astype(jnp.bfloat16)
    scaled = (math.sqrt(max(LONG, RANK)) * panels.astype(jnp.float32)).astype(jnp.bfloat16)
    returned = lax.all_to_all(scaled, "owner", split_axis=1, concat_axis=0, tiled=True)
    updates = jnp.take(returned, slot_table, axis=0)
    return (updates, renewed)


def solution(mesh):
    return jax.shard_map(
        on_device,
        mesh=mesh,
        in_specs=(P(None, ("fsdp", "owner"), None), P("owner", "fsdp", None), P()),
        out_specs=(P(None, ("fsdp", "owner"), None), P("owner", "fsdp", None)),
        check_vma=False,
    )
```

profile of v0, /device:TPU:0, one launch (start us, length us, event | category | flops | bytes accessed | tf_op | source)
XLA Modules:
  0.0 655.2 jit_solution(961407926287617743)
XLA Ops:
  7.2 0.0 all-reduce.6.cloned.1.call-start
  7.2 0.8 select_reduce_fusion
  8.0 5.0 gather_fusion
  13.0 2.7 broadcast_select_fusion.1
  15.7 0.0 slice-start
  15.7 52.4 %all_to_all.27 = bf16[8,512,512]{2,1,0:T(8,128)(2,1)S(1)} all-to-all(bf16[8,512,512]{2,1,0:T(8,128)(2,1)S(1)} %broadcast_select_fusion.1), channel_id=1, replica_groups=mesh['owner'=4,'fsdp'=8] {'owner'}, dimensions={0} | all-to-all | bytes 8388608 | tf_op jit(solution)/shard_map/all_to_all | solution.py:28
  68.1 0.0 slice-start.1
  68.1 1.2 copy.64
  69.3 0.0 slice-done
  69.3 1.0 slice-done.1
  70.3 0.0 copy-start
  70.3 5.4 multiply_reduce_fusion
  75.7 0.3 copy-done
  76.1 21.7 %psum.42 = f32[2]{0:T(128)S(1)} all-reduce(f32[2]{0:T(128)S(1)} %get-tuple-element.3), channel_id=1, replica_groups=mesh['owner'=4,'fsdp'=8] {'fsdp'}, use_global_device_ids=true, to_apply=%region_2.4 | all-reduce | flops 2 | bytes 16 | tf_op jit(solution)/shard_map/psum | solution.py:32
  97.7 7.2 %divide_convert_fusion = bf16[2,2048,512]{2,1,0:T(8,128)(2,1)S(1)} fusion(f32[2]{0:T(128)S(1)} %sqrt_add_fusion, f32[2,2048,512]{2,1,0:T(8,128)} %get-tuple-element.4, f32[4,2,512,512]{3,2,0,1:T(8,128)} %copy-done), kind=kLoop, calls=%fused_computation.10 | loop fusion | flops 8388608 | bytes 20971528 | tf_op jit(solution)/shard_map/convert_element_type | solution.py:33
  104.9 0.0 copy-start.1
  104.9 2.0 copy-done.1
  106.9 3.4 fusion.5
  110.3 0.0 all-reduce.6.cloned.1.call-update
  110.3 0.0 all-reduce.8.cloned.1.call-start
  110.3 74.4 %all-reduce.6.cloned.1.call-done = bf16[512,2,512]{0,2,1:T(8,128)(2,1)} async-done(((bf16[512,2,512]{0,2,1:T(8,128)(2,1)}), bf16[512,2,512]{0,2,1:T(8,128)(2,1)}) %all-reduce.6.cloned.1.call-update) | async-done | bytes 1048592 | tf_op jit(solution)/shard_map/psum | solution.py:38
  184.7 9.5 %add_convert_fusion.4 = bf16[2,2048,512]{2,1,0:T(8,128)(2,1)} fusion(bf16[2,2048,512]{2,1,0:T(8,128)(2,1)} %copy-done.1, bf16[512,2,512]{0,2,1:T(8,128)(2,1)} %all-reduce.6.cloned.1.call-done), kind=kOutput, calls=%fused_computation.9 | convolution fusion | flops 2695364608 | bytes 9437184 | tf_op jit(solution)/shard_map/snq,qsp->snp/dot_general | solution.py:45
  194.2 6.8 %fusion.6 = bf16[512,2,512]{0,2,1:T(8,128)(2,1)} fusion(bf16[2,2048,512]{2,1,0:T(8,128)(2,1)} %add_convert_fusion.4), kind=kOutput, calls=%fused_computation.30 | convolution fusion | flops 2148007936 | bytes 5242880 | tf_op jit(solution)/shard_map/snq,snp->qsp/dot_general | solution.py:35
  201.0 0.0 all-reduce.8.cloned.1.call-update
  201.0 0.2 all-reduce.10.cloned.1.call-start
  201.3 77.5 %all-reduce.8.cloned.1.call-done = bf16[512,2,512]{0,2,1:T(8,128)(2,1)} async-done(((bf16[512,2,512]{0,2,1:T(8,128)(2,1)}), bf16[512,2,512]{0,2,1:T(8,128)(2,1)}) %all-reduce.8.cloned.1.call-update) | async-done | bytes 1048592 | tf_op jit(solution)/shard_map/psum | solution.py:38
  278.8 9.4 %add_convert_fusion.3 = bf16[2,2048,512]{2,1,0:T(8,128)(2,1)} fusion(bf16[2,2048,512]{2,1,0:T(8,128)(2,1)} %add_convert_fusion.4, bf16[512,2,512]{0,2,1:T(8,128)(2,1)} %all-reduce.8.cloned.1.call-done), kind=kOutput, calls=%fused_computation.8 | convolution fusion | flops 2695364608 | bytes 9437184 | tf_op jit(solution)/shard_map/snq,qsp->snp/dot_general | solution.py:45
  288.2 6.8 %fusion.7 = bf16[512,2,512]{0,2,1:T(8,128)(2,1)} fusion(bf16[2,2048,512]{2,1,0:T(8,128)(2,1)} %add_convert_fusion.3), kind=kOutput, calls=%fused_computation.31 | convolution fusion | flops 2148007936 | bytes 5242880 | tf_op jit(solution)/shard_map/snq,snp->qsp/dot_general | solution.py:35
  295.0 0.0 all-reduce.10.cloned.1.call-update
  295.0 0.0 all-reduce.12.cloned.1.call-start
  295.1 77.7 %all-reduce.10.cloned.1.call-done = bf16[512,2,512]{0,2,1:T(8,128)(2,1)} async-done(((bf16[512,2,512]{0,2,1:T(8,128)(2,1)}), bf16[512,2,512]{0,2,1:T(8,128)(2,1)}) %all-reduce.10.cloned.1.call-update) | async-done | bytes 1048592 | tf_op jit(solution)/shard_map/psum | solution.py:38
  372.7 9.5 %add_convert_fusion.2 = bf16[2,2048,512]{2,1,0:T(8,128)(2,1)} fusion(bf16[2,2048,512]{2,1,0:T(8,128)(2,1)} %add_convert_fusion.3, bf16[512,2,512]{0,2,1:T(8,128)(2,1)} %all-reduce.10.cloned.1.call-done), kind=kOutput, calls=%fused_computation.7 | convolution fusion | flops 2695364608 | bytes 9437184 | tf_op jit(solution)/shard_map/snq,qsp->snp/dot_general | solution.py:45
  382.2 6.8 %fusion.8 = bf16[512,2,512]{0,2,1:T(8,128)(2,1)} fusion(bf16[2,2048,512]{2,1,0:T(8,128)(2,1)} %add_convert_fusion.2), kind=kOutput, calls=%fused_computation.32 | convolution fusion | flops 2148007936 | bytes 5242880 | tf_op jit(solution)/shard_map/snq,snp->qsp/dot_general | solution.py:35
  389.0 0.0 all-reduce.12.cloned.1.call-update
  389.0 0.3 all-reduce.14.cloned.1.call-start
  389.3 77.4 %all-reduce.12.cloned.1.call-done = bf16[512,2,512]{0,2,1:T(8,128)(2,1)} async-done(((bf16[512,2,512]{0,2,1:T(8,128)(2,1)}), bf16[512,2,512]{0,2,1:T(8,128)(2,1)}) %all-reduce.12.cloned.1.call-update) | async-done | bytes 1048592 | tf_op jit(solution)/shard_map/psum | solution.py:38
  466.7 9.4 %add_convert_fusion.1 = bf16[2,2048,512]{2,1,0:T(8,128)(2,1)} fusion(bf16[2,2048,512]{2,1,0:T(8,128)(2,1)} %add_convert_fusion.2, bf16[512,2,512]{0,2,1:T(8,128)(2,1)} %all-reduce.12.cloned.1.call-done), kind=kOutput, calls=%fused_computation.6 | convolution fusion | flops 2695364608 | bytes 9437184 | tf_op jit(solution)/shard_map/snq,qsp->snp/dot_general | solution.py:45
  476.1 6.8 %fusion.9 = bf16[512,2,512]{0,2,1:T(8,128)(2,1)} fusion(bf16[2,2048,512]{2,1,0:T(8,128)(2,1)} %add_convert_fusion.1), kind=kOutput, calls=%fused_computation.33 | convolution fusion | flops 2148007936 | bytes 5242880 | tf_op jit(solution)/shard_map/snq,snp->qsp/dot_general | solution.py:35
  482.9 0.0 all-reduce.14.cloned.1.call-update
  482.9 77.9 %all-reduce.14.cloned.1.call-done = bf16[512,2,512]{0,2,1:T(8,128)(2,1)} async-done(((bf16[512,2,512]{0,2,1:T(8,128)(2,1)}), bf16[512,2,512]{0,2,1:T(8,128)(2,1)}) %all-reduce.14.cloned.1.call-update) | async-done | bytes 1048592 | tf_op jit(solution)/shard_map/psum | solution.py:38
  560.8 9.6 %multiply_convert_fusion = bf16[2,2048,512]{2,1,0:T(8,128)(2,1)} fusion(bf16[2,2048,512]{2,1,0:T(8,128)(2,1)} %add_convert_fusion.1, bf16[512,2,512]{0,2,1:T(8,128)(2,1)} %all-reduce.14.cloned.1.call-done), kind=kOutput, calls=%fused_computation.4 | convolution fusion | flops 2701656064 | bytes 9437184 | tf_op jit(solution)/shard_map/snq,qsp->snp/dot_general | solution.py:45
  570.4 10.1 %copy.80 = bf16[2,2048,512]{2,0,1:T(2,128)(2,1)} copy(bf16[2,2048,512]{2,1,0:T(8,128)(2,1)} %multiply_convert_fusion) | data formatting | bytes 8388608 | tf_op jit(solution)/shard_map/convert_element_type | solution.py:47
  580.5 0.0 copy-start.2
  580.5 5.0 all-to-all-start.1
  585.5 0.0 copy-done.2
  585.5 48.2 %all-to-all-done.1 = bf16[2,2048,512]{2,0,1:T(2,128)(2,1)} async-done(((bf16[2,2048,512]{2,0,1:T(2,128)(2,1)}), bf16[2,2048,512]{2,0,1:T(2,128)(2,1)}, u32[]{:S(2)}, u32[]{:S(2)}) %all-to-all-start.1) | async-done | bytes 4194336 | tf_op jit(solution)/shard_map/all_to_all | solution.py:48
  633.7 2.9 copy.81
  636.5 2.5 copy.82
  639.0 4.9 gather_fusion.1
  644.0 4.7 broadcast_select_fusion
  (8 shorter events, 0.0 us)
Async XLA Ops:
  7.2 177.6 %all-reduce.6.cloned.1.call-start = ((), (), s32[]{:S(2)}) async-start(), calls=%async_computation.2 | async-start | bytes 2097152 | tf_op jit(solution)/shard_map/psum | solution.py:38
  15.7 53.6 %slice-start = ((s8[8388608]{0:T(1024)(128)(4,1)}), s8[4194304]{0:T(1024)(128)(4,1)S(1)}, s32[]{:S(2)}) async-start(s8[8388608]{0:T(1024)(128)(4,1)} %bitcast.84), calls=%async_computation.7 | async-start | bytes 8388608
  68.1 2.2 slice-start.1
  70.3 5.7 copy-start
  104.9 2.0 copy-start.1
  110.3 168.5 %all-reduce.8.cloned.1.call-start = ((), (), s32[]{:S(2)}) async-start(), calls=%async_computation.3 | async-start | bytes 2097152 | tf_op jit(solution)/shard_map/psum | solution.py:38
  201.0 171.7 %all-reduce.10.cloned.1.call-start = ((), (), s32[]{:S(2)}) async-start(), calls=%async_computation.4 | async-start | bytes 2097152 | tf_op jit(solution)/shard_map/psum | solution.py:38
  295.0 171.7 %all-reduce.12.cloned.1.call-start = ((), (), s32[]{:S(2)}) async-start(), calls=%async_computation.5 | async-start | bytes 2097152 | tf_op jit(solution)/shard_map/psum | solution.py:38
  389.0 171.8 %all-reduce.14.cloned.1.call-start = ((), (), s32[]{:S(2)}) async-start(), calls=%async_computation.6 | async-start | bytes 2097152 | tf_op jit(solution)/shard_map/psum | solution.py:38
  580.5 5.0 copy-start.2
  580.5 53.2 %all-to-all-start.1 = ((bf16[2,2048,512]{2,0,1:T(2,128)(2,1)}), bf16[2,2048,512]{2,0,1:T(2,128)(2,1)}, u32[]{:S(2)}, u32[]{:S(2)}) async-start(bf16[2,2048,512]{2,0,1:T(2,128)(2,1)} %copy.80), calls=%async_computation.1 | async-start | bytes 8388608 | tf_op jit(solution)/shard_map/all_to_all | solution.py:48
Sparse Core Ops, SparseCore 0:
  110.4 74.2 all-reduce.5
  201.2 77.5 all-reduce.7
  295.1 77.5 all-reduce.9
  389.1 77.5 all-reduce.11
  483.0 77.6 all-reduce.13
where the time goes:
time: 656 us; the launch traced here: 655 us
  waiting for transfers between devices  433 us (66%)
  matrix products  77.9 us (12%)
  blocking collectives  74.1 us (11%)
  local copies, waits for them, and re-layouts  29.9 us (5%)
  other arithmetic  20.7 us (3%)
  between operations  13.9 us (2%)
    psum x5, waiting for transfers between devices, on_device(): gram_matrix = lax.psum(partial_value.astype(jnp.bfloat16), 'fsdp')  385 us
    all_to_all x1, blocking collectives, on_device(): lax.all_to_all(ordered, 'owner', split_axis=0, concat_axis=1, tiled=True)  52.4 us
    all_to_all x1, waiting for transfers between devices, on_device(): lax.all_to_all(scaled, 'owner', split_axis=1, concat_axis=0, tiled=True)  48.2 us
    dot_general x5, matrix products, on_device(): jnp.einsum('snq,qsp->snp', panels, polynomial, preferred_element_type=jnp...  47.3 us
    dot_general x5, matrix products, on_device(): jnp.einsum('snq,snp->qsp', panels, panels, preferred_element_type=jnp.flo...  30.6 us
    psum x1, blocking collectives, on_device(): squares = lax.psum(jnp.sum(blended * blended, axis=(1, 2)), 'fsdp')  21.7 us
  transfers between devices with their start and end apart: 6, of which 6 were waited for; matrix products, arithmetic and copies ran while one was open for 0% of the time, Pallas kernels for 0%

commit v1 on v0

v1 whole, which is shorter than its diff:
```python
import functools
import math

import jax
import jax.numpy as jnp
from jax import lax
from jax.experimental import pallas as pl
from jax.experimental.pallas import tpu as pltpu
from jax.sharding import PartitionSpec as P

LONG = 16384
RANK = 512
ITERS = 5
TILE = 128

quintic = (3.4445, -4.775, 2.0315)
momentum_decay = 0.95
epsilon = 1e-07

BLOCKS = [(i, j) for i in range(RANK // TILE) for j in range(i, RANK // TILE)]
PACKED = len(BLOCKS) * TILE

f32, bf16 = jnp.float32, jnp.bfloat16


def slot_inverse(slot_table, matrix_count):
    slots = jnp.arange(matrix_count, dtype=jnp.int32)
    matches = slot_table[None, :] == slots[:, None]
    return jnp.sum(jnp.where(matches, slots[None, :], 0), axis=1)


def partners(size, step):
    return [(i, i ^ step) for i in range(size)]


def blend_kernel(shares, has_buffer, has_sum, *refs):
    refs = list(refs)
    place = refs.pop(0)
    gradient, momentum = refs.pop(0), refs.pop(0)
    if has_buffer:
        refs.pop(0)
    before = refs.pop(0) if has_sum else None
    renewed, rows, total, held = refs
    step = pl.program_id(0)

    @pl.when(step == 0)
    def _():
        held[...] = before[...] if has_sum else jnp.zeros_like(held)

    g = gradient[...].astype(f32)
    m = momentum_decay * momentum[...] + g
    renewed[...] = m
    x = (g + momentum_decay * m).astype(bf16)
    rows[...] = x
    half = RANK // 2
    dims = (((0,), (0,)), ((), ()))
    upper = lax.dot_general(x[:, :half], x, dims, preferred_element_type=f32)
    lower = lax.dot_general(x[:, half:], x[:, half:], dims, preferred_element_type=f32)
    for n, (i, j) in enumerate(BLOCKS):
        part, i0, j0 = (upper, i, j) if i < half // TILE else (lower, i - half // TILE, j - half // TILE)
        held[n * TILE : (n + 1) * TILE, :] += part[
            i0 * TILE : (i0 + 1) * TILE, j0 * TILE : (j0 + 1) * TILE
        ]

    @pl.when(step == pl.num_programs(0) - 1)
    def _():
        if shares is None:
            total[...] = held[...]
        else:
            near, far = shares
            count = PACKED // (near * far)
            for e1 in range(near):
                for e2 in range(far):
                    who = jnp.bitwise_xor(place[2], e2 * near + e1)
                    start = pl.multiple_of(who * count, 8)
                    total[e1, e2] = held[pl.ds(start, count), :]


def blend(place, gradient, local, momentum, slot, piece_rows, buffer, before, shares):
    tile = min(256, piece_rows)
    steps = piece_rows // tile
    if local:
        gradient_spec = pl.BlockSpec((None, tile, RANK), lambda i, p: (p[1], i, 0))
    else:
        gradient_spec = pl.BlockSpec((tile, RANK), lambda i, p: (i, 0))
    momentum_spec = pl.BlockSpec((None, tile, RANK), lambda i, p: (slot, p[0] * steps + i, 0))
    in_specs, operands = [gradient_spec, momentum_spec], [gradient, momentum]
    aliases = {}
    if buffer is not None:
        aliases = {1 + len(operands): 0}
        in_specs.append(pl.BlockSpec(memory_space=pl.ANY))
        operands.append(buffer)
    if before is not None:
        in_specs.append(pl.BlockSpec((PACKED, TILE), lambda i, p: (0, 0)))
        operands.append(before)
    if shares is None:
        total = (PACKED, TILE)
    else:
        total = (*shares, PACKED // (shares[0] * shares[1]), TILE)
    return pl.pallas_call(
        functools.partial(blend_kernel, shares, buffer is not None, before is not None),
        grid_spec=pltpu.PrefetchScalarGridSpec(
            num_scalar_prefetch=1,
            grid=(steps,),
            in_specs=in_specs,
            out_specs=[
                momentum_spec,
                pl.BlockSpec((tile, RANK), lambda i, p: (i, 0)),
                pl.BlockSpec(total, lambda i, p: (0,) * len(total)),
            ],
            scratch_shapes=[pltpu.VMEM((PACKED, TILE), f32)],
        ),
        out_shape=[
            jax.ShapeDtypeStruct(momentum.shape, f32),
            jax.ShapeDtypeStruct((piece_rows, RANK), bf16),
            jax.ShapeDtypeStruct(total, f32),
        ],
        input_output_aliases=aliases,
        compiler_params=pltpu.CompilerParams(vmem_limit_bytes=24 * 2**20),
        cost_estimate=pl.CostEstimate(
            flops=2 * piece_rows * RANK * RANK, bytes_accessed=piece_rows * RANK * 12, transcendentals=0
        ),
        name="blend",
    )(place, *operands)


def two(x):
    high = x.astype(bf16)
    return high, (x - high.astype(f32)).astype(bf16)


def dot(a, b):
    return jnp.dot(a, b, preferred_element_type=f32)


def product(a, b):
    (ah, al), (bh, bl) = a, b
    return dot(ah, bh) + (dot(ah, bl) + dot(al, bh))


def polynomial_kernel(near, far, count, place, *refs):
    refs = list(refs)
    packed = refs.pop()
    result = refs.pop()
    for e2 in range(far):
        who = jnp.bitwise_xor(place[2], e2 * near)
        packed[pl.ds(pl.multiple_of(who * count, 8), count), :] = refs.pop(0)[...]
    for e1 in range(1, near):
        other = refs.pop(0)
        for e2 in range(far):
            who = jnp.bitwise_xor(place[2], e2 * near + e1)
            packed[pl.ds(pl.multiple_of(who * count, 8), count), :] = other[e2]
    sides = RANK // TILE
    parts = {}
    trace = jnp.zeros((), f32)
    rows_id = lax.broadcasted_iota(jnp.int32, (TILE, TILE), 0)
    cols_id = lax.broadcasted_iota(jnp.int32, (TILE, TILE), 1)
    for n, (i, j) in enumerate(BLOCKS):
        block = packed[n * TILE : (n + 1) * TILE, :]
        parts[i, j] = block
        if i == j:
            trace = trace + jnp.sum(jnp.where(rows_id == cols_id, block, 0.0))
        else:
            parts[j, i] = block.T
    gram = jnp.concatenate(
        [jnp.concatenate([parts[i, j] for j in range(sides)], axis=1) for i in range(sides)], axis=0
    )
    scale = 1.0 / (jnp.sqrt(jnp.full((1, 1), trace, f32)) + epsilon)
    gram = (gram * scale) * scale
    a, b, c = quintic
    r_id = lax.broadcasted_iota(jnp.int32, (RANK, RANK), 0)
    c_id = lax.broadcasted_iota(jnp.int32, (RANK, RANK), 1)
    poly = None
    for iteration in range(ITERS):
        g = two(gram)
        rest = b * gram + c * product(g, g)
        r = two(rest)
        if poly is None:
            poly = rest + jnp.where(r_id == c_id, a, 0.0)
        else:
            poly = a * poly + product(two(poly), r)
        if iteration < ITERS - 1:
            middle = a * gram + product(g, r)
            gram = a * middle + product(two(middle), r)
    high, low = two(poly * (scale * math.sqrt(max(LONG, RANK))))
    result[:RANK, :] = high
    result[RANK:, :] = low


def polynomial(place, shares, own, others):
    near, far = shares
    count = PACKED // (near * far)
    operands = [*own, *others]
    return pl.pallas_call(
        functools.partial(polynomial_kernel, near, far, count),
        grid_spec=pltpu.PrefetchScalarGridSpec(
            num_scalar_prefetch=1,
            grid=(1,),
            in_specs=[pl.BlockSpec(x.shape, lambda i, p, r=x.ndim: (0,) * r) for x in operands],
            out_specs=pl.BlockSpec((2 * RANK, RANK), lambda i, p: (0, 0)),
            scratch_shapes=[pltpu.VMEM((PACKED, TILE), f32)],
        ),
        out_shape=jax.ShapeDtypeStruct((2 * RANK, RANK), bf16),
        compiler_params=pltpu.CompilerParams(vmem_limit_bytes=40 * 2**20),
        cost_estimate=pl.CostEstimate(flops=51 * 2 * RANK**3, bytes_accessed=2 * 2**20, transcendentals=0),
        name="polynomial",
    )(place, *operands)


def apply_kernel(rows, poly, out):
    x = rows[...]
    out[...] = (dot(x, poly[:RANK, :]) + dot(x, poly[RANK:, :])).astype(bf16)


def apply_polynomial(rows, poly):
    return pl.pallas_call(
        apply_kernel,
        out_shape=jax.ShapeDtypeStruct(rows.shape, bf16),
        compiler_params=pltpu.CompilerParams(vmem_limit_bytes=16 * 2**20),
        cost_estimate=pl.CostEstimate(
            flops=4 * rows.shape[0] * RANK * RANK, bytes_accessed=2 * 2**20, transcendentals=0
        ),
        name="apply",
    )(rows, poly)


def on_device(gradients, momentum, slot_table, *, owners, group):
    matrix_count, piece_rows, _ = gradients.shape
    held_slots = momentum.shape[0]
    inverse = slot_inverse(slot_table, matrix_count)
    me_owner, me_group = lax.axis_index("owner"), lax.axis_index("fsdp")
    near = 1 << ((group.bit_length() - 1) // 2)
    shares = (near, group // near)

    def matrix_of(slot, d):
        return inverse[held_slots * jnp.bitwise_xor(me_owner, d) + slot]

    far_steps, near_steps = list(range(2, owners)), list(range(1, min(2, owners)))
    arrived = {}
    for slot in range(held_slots):
        for d in far_steps + near_steps:
            piece = lax.dynamic_index_in_dim(gradients, matrix_of(slot, d), 0, keepdims=False)
            arrived[slot, d] = lax.ppermute(piece, "owner", partners(owners, d))

    order = [(slot, d) for slot in range(held_slots) for d in [0] + near_steps]
    order += [(slot, d) for slot in range(held_slots) for d in far_steps]
    renewed, rows, sums = None, {}, {}
    for slot, d in order:
        place = jnp.stack([jnp.bitwise_xor(me_owner, d), matrix_of(slot, d), me_group]).astype(jnp.int32)
        last = d == owners - 1
        renewed, rows[slot, d], sums[slot] = blend(
            place,
            gradients if d == 0 else arrived[slot, d],
            d == 0,
            momentum,
            slot,
            piece_rows,
            renewed,
            sums.get(slot),
            shares if last else None,
        )

    place = jnp.stack([me_owner, me_owner, me_group]).astype(jnp.int32)
    updates = jnp.zeros(gradients.shape, bf16)
    for slot in range(held_slots):
        share = sums[slot]
        line = share[0]
        for e1 in range(1, shares[0]):
            line = line + lax.ppermute(share[e1], "fsdp", partners(group, e1))
        mine = line[0]
        for e2 in range(1, shares[1]):
            mine = mine + lax.ppermute(line[e2], "fsdp", partners(group, e2 * near))
        own = [mine]
        for e2 in range(1, shares[1]):
            own.append(lax.ppermute(mine, "fsdp", partners(group, e2 * near)))
        stacked = jnp.stack(own)
        others = [lax.ppermute(stacked, "fsdp", partners(group, e1)) for e1 in range(1, shares[0])]
        poly = polynomial(place, shares, own, others)
        for d in far_steps + near_steps + [0]:
            out = apply_polynomial(rows[slot, d], poly)
            if d:
                out = lax.ppermute(out, "owner", partners(owners, d))
            updates = lax.dynamic_update_index_in_dim(updates, out, matrix_of(slot, d), 0)
    return (updates, renewed)


def solution(mesh):
    return jax.shard_map(
        functools.partial(on_device, owners=mesh.shape["owner"], group=mesh.shape["fsdp"]),
        mesh=mesh,
        in_specs=(P(None, ("fsdp", "owner"), None), P("owner", "fsdp", None), P()),
        out_specs=(P(None, ("fsdp", "owner"), None), P("owner", "fsdp", None)),
        check_vma=False,
    )
```

time: 656 us -> 179 us (0.27)
  waiting for transfers between devices: 433 us -> 43.7 us
  matrix products: 77.9 us -> 0 us
  blocking collectives: 74.1 us -> 0 us
  Pallas kernels: 0 us -> 56 us
  starting transfers between devices: 5.59 us -> 30 us
  other arithmetic: 20.7 us -> 8.95 us
  local copies, waits for them, and re-layouts: 29.9 us -> 23.2 us
    psum x5 -> x0, waiting for transfers between devices: 385 us -> none  [on_device(): gram_matrix = lax.psum(partial_value.astype(jnp.bfloat16), 'fsdp')]
    dot_general x10 -> x0, matrix products: 77.9 us -> none  [the longest x5 47.3 us: on_device(): jnp.einsum('snq,qsp->snp', panels, polynomial, preferred_element_type=jnp...]
    pallas_call x0 -> x16, Pallas kernels: none -> 56 us  [the longest x2 31.6 us: polynomial(): pl.pallas_call(functools.partial(polynomial_kernel, near, far, count), gr...]
    all_to_all x1 -> x0, blocking collectives: 52.4 us -> none  [on_device(): lax.all_to_all(ordered, 'owner', split_axis=0, concat_axis=1, tiled=True)]
    all_to_all x1 -> x0, waiting for transfers between devices: 48.2 us -> none  [on_device(): lax.all_to_all(scaled, 'owner', split_axis=1, concat_axis=0, tiled=True)]
    ppermute x0 -> x28, waiting for transfers between devices: none -> 43.7 us  [the longest x6 23.6 us: on_device(): out = lax.ppermute(out, 'owner', partners(owners, d))]
    ppermute x0 -> x28, starting transfers between devices: none -> 30 us  [the longest x6 8.9 us: on_device(): mine = mine + lax.ppermute(line[e2], 'fsdp', partners(group, e2 * near))]
    psum x1 -> x0, blocking collectives: 21.7 us -> none  [on_device(): squares = lax.psum(jnp.sum(blended * blended, axis=(1, 2)), 'fsdp')]
  transfers between devices with their start and end apart: 6 -> 28, of which waited for: 6 -> 8; matrix products, arithmetic and copies ran while one was open for 0% -> 5% of each run, Pallas kernels for 0% -> 31%
where the time goes in v1:
time: 179 us; the launch traced here: 178 us
  Pallas kernels  56 us (31%)
  waiting for transfers between devices  43.7 us (24%)
  starting transfers between devices  30 us (17%)
  local copies, waits for them, and re-layouts  23.2 us (13%)
  between operations  16.2 us (9%)
  other arithmetic  8.95 us (5%)
    pallas_call x2, Pallas kernels, polynomial(): pl.pallas_call(functools.partial(polynomial_kernel, near, far, count), gr...  31.6 us
    ppermute x6, waiting for transfers between devices, on_device(): out = lax.ppermute(out, 'owner', partners(owners, d))  23.6 us
    pallas_call x8, Pallas kernels, blend(): pl.pallas_call(functools.partial(blend_kernel, shares, buffer is not None...  20 us
    unnamed x26, local copies, waits for them, and re-layouts  17.9 us
    ppermute x6, starting transfers between devices, on_device(): mine = mine + lax.ppermute(line[e2], 'fsdp', partners(group, e2 * near))  8.9 us
    ppermute x6, starting transfers between devices, on_device(): own.append(lax.ppermute(mine, 'fsdp', partners(group, e2 * near)))  8.9 us
    ppermute x6, waiting for transfers between devices, on_device(): mine = mine + lax.ppermute(line[e2], 'fsdp', partners(group, e2 * near))  8.75 us
    ppermute x6, waiting for transfers between devices, on_device(): own.append(lax.ppermute(mine, 'fsdp', partners(group, e2 * near)))  7.86 us
  transfers between devices with their start and end apart: 28, of which 8 were waited for; matrix products, arithmetic and copies ran while one was open for 5% of the time, Pallas kernels for 31%

profile of v1, /device:TPU:0, one launch (start us, length us, event | category | flops | bytes accessed | tf_op | source)
XLA Modules:
  0.0 178.0 jit_solution(15320620016227245611)
XLA Ops:
  0.7 0.8 select_reduce_fusion
  1.5 0.7 fusion.6
  13.6 3.3 %dynamic-slice_bitcast_fusion = (bf16[512,512]{1,0:T(8,128)(2,1)}, bf16[512,512]{1,0:T(8,128)(2,1)}, bf16[512,512]{1,0:T(8,128)(2,1)S(1)}, bf16[512,512]{1,0:T(8...) fusion(bf16[8,512,512]{2,1,0:T(8,128)(2,1)} %refs_1_.3, s32[]{:T(128)S(6)} %select_n.89, ...), kind=kLoop, calls=%fused_computation.8 | loop fusion | bytes 6291480 | tf_op jit(solution)/shard_map/jit(dynamic_index_in_dim)/squeeze | solution.py:242
  17.4 2.9 %collective-permute-start = (bf16[512,512]{1,0:T(8,128)(2,1)}, bf16[512,512]{1,0:T(8,128)(2,1)}, u32[]{:S(2)}, u32[]{:S(2)}) collective-permute-start(bf16[512,512]{1,0:T(8,128)(2,1)} %get-tuple-element.54), channel_id=1, source_target_pairs={{0,16},{8,24},{16,0},{24,8},{1,17},{9,25},{17,1},{25,9},{2,18},{10... | collective-permute-start | bytes 1572872 | tf_op jit(solution)/shard_map/ppermute | solution.py:243
  20.3 1.4 collective-permute-start.15
  21.7 0.8 add_add_fusion.refs_0_
  22.5 0.7 add_add_fusion.7.refs_0_
  23.1 0.7 add_add_fusion.1.refs_0_
  24.5 1.4 add_add_fusion.2
  26.9 3.4 %copy-done = f32[2,2048,512]{2,1,0:T(8,128)S(1)} copy-done((f32[2,2048,512]{2,1,0:T(8,128)S(1)}, f32[2,2048,512]{2,1,0:T(8,128)}, u32[]{:S(2)}) %copy-start) | copy-done | bytes 8388632
  30.3 2.2 %copy-done.3 = bf16[8,512,512]{2,1,0:T(8,128)(2,1)S(1)} copy-done((bf16[8,512,512]{2,1,0:T(8,128)(2,1)S(1)}, bf16[8,512,512]{2,1,0:T(8,128)(2,1)}, u32[]{:S(2)}) %copy-start.3) | copy-done | bytes 4194328
  32.5 2.1 %blend.8 = (f32[2,2048,512]{2,1,0:T(8,128)}, bf16[512,512]{1,0:T(8,128)(2,1)S(1)}, f32[1280,128]{1,0:T(8,128)S(1)}) custom-call(s32[3]{0:T(128)S(1)} %add_add_fusion.4.refs_0_, bf16[8,512,512]{2,1,0:T(8,128)(2,1)S(1)} %copy-done.3, f32[2,2048,512]{2,1,0:T(8,128)S(1)} %copy-done), custom_call_target="tpu_custom_call" | custom-call | flops 268435456 | bytes 3145728 | tf_op jit(solution)/shard_map/blend/pallas_call | solution.py:100
  34.6 1.6 copy-done.1
  36.2 2.1 %blend.9 = (f32[2,2048,512]{2,1,0:T(8,128)}, bf16[512,512]{1,0:T(8,128)(2,1)S(1)}, f32[1280,128]{1,0:T(8,128)S(1)}) custom-call(s32[3]{0:T(128)S(1)} %get-tuple-element.71.refs_0_, bf16[512,512]{1,0:T(8,128)(2,1)S(1)} %collective-permute-done.2.refs_1_, f32[2,2048,512]{2,1,0:T(8,128)S(1)} %copy-done.1, ...), custom_call_target="tpu_custom_call", output_to_operand_aliasing={{0}: (3, {})} | custom-call | flops 268435456 | bytes 3145728 | tf_op jit(solution)/shard_map/blend/pallas_call | solution.py:100
  38.4 2.1 %blend.10 = (f32[2,2048,512]{2,1,0:T(8,128)}, bf16[512,512]{1,0:T(8,128)(2,1)S(1)}, f32[1280,128]{1,0:T(8,128)S(1)}) custom-call(s32[3]{0:T(128)S(1)} %get-tuple-element.70.refs_0_, bf16[8,512,512]{2,1,0:T(8,128)(2,1)S(1)} %copy-done.3, f32[2,2048,512]{2,1,0:T(8,128)S(1)} %copy-done.1, ...), custom_call_target="tpu_custom_call", output_to_operand_aliasing={{0}: (3, {})} | custom-call | flops 268435456 | bytes 3145728 | tf_op jit(solution)/shard_map/blend/pallas_call | solution.py:100
  40.5 0.8 copy-done.10
  41.3 1.0 copy-done.11
  42.4 2.1 %blend.11 = (f32[2,2048,512]{2,1,0:T(8,128)}, bf16[512,512]{1,0:T(8,128)(2,1)S(1)}, f32[1280,128]{1,0:T(8,128)S(1)}) custom-call(s32[3]{0:T(128)S(1)} %add_add_fusion.1.refs_0_, bf16[512,512]{1,0:T(8,128)(2,1)S(1)} %copy-done.11, f32[2,2048,512]{2,1,0:T(8,128)S(1)} %copy-done.1, ...), custom_call_target="tpu_custom_call", output_to_operand_aliasing={{0}: (3, {})} | custom-call | flops 268435456 | bytes 3145728 | tf_op jit(solution)/shard_map/blend/pallas_call | solution.py:100
  44.5 3.1 %blend.12 = (f32[2,2048,512]{2,1,0:T(8,128)}, bf16[512,512]{1,0:T(8,128)(2,1)S(1)}, f32[1280,128]{1,0:T(8,128)S(1)}) custom-call(s32[3]{0:T(128)S(1)} %add_add_fusion.refs_0_, bf16[512,512]{1,0:T(8,128)(2,1)} %collective-permute-done.refs_1_, f32[2,2048,512]{2,1,0:T(8,128)S(1)} %copy-done.1, ...), custom_call_target="tpu_custom_call", output_to_operand_aliasing={{0}: (3, {})} | custom-call | flops 268435456 | bytes 3145728 | tf_op jit(solution)/shard_map/blend/pallas_call | solution.py:100
  47.6 0.8 copy-done.4
  48.4 0.8 copy-done.8
  49.2 1.0 copy-done.9
  50.3 2.1 %blend.13 = (f32[2,2048,512]{2,1,0:T(8,128)}, bf16[512,512]{1,0:T(8,128)(2,1)S(1)}, f32[2,4,160,128]{3,2,1,0:T(8,128)S(1)}) custom-call(s32[3]{0:T(128)S(1)} %add_add_fusion.6.refs_0_, bf16[512,512]{1,0:T(8,128)(2,1)S(1)} %copy-done.9, f32[2,2048,512]{2,1,0:T(8,128)S(1)} %copy-done.1, ...), custom_call_target="tpu_custom_call", output_to_operand_aliasing={{0}: (3, {})} | custom-call | flops 268435456 | bytes 3145728 | tf_op jit(solution)/shard_map/blend/pallas_call | solution.py:100
  52.4 0.8 copy-done.6
  53.2 0.7 slice_bitcast_fusion.1
  53.9 1.8 collective-permute-start.4
  55.7 0.8 add_add_fusion.8.refs_0_
  60.2 3.4 %copy-done.2 = f32[2,2048,512]{2,1,0:T(8,128)S(1)} copy-done((f32[2,2048,512]{2,1,0:T(8,128)S(1)}, f32[2,2048,512]{2,1,0:T(8,128)}, u32[]{:S(2)}) %copy-start.2) | copy-done | bytes 8388632
  63.6 3.1 %blend.14 = (f32[2,2048,512]{2,1,0:T(8,128)}, bf16[512,512]{1,0:T(8,128)(2,1)S(1)}, f32[1280,128]{1,0:T(8,128)S(1)}) custom-call(s32[3]{0:T(128)S(1)} %add_add_fusion.7.refs_0_, bf16[512,512]{1,0:T(8,128)(2,1)} %collective-permute-done.15.refs_1_, f32[2,2048,512]{2,1,0:T(8,128)S(1)} %copy-done.2, ...), custom_call_target="tpu_custom_call", output_to_operand_aliasing={{0}: (3, {})} | custom-call | flops 268435456 | bytes 3145728 | tf_op jit(solution)/shard_map/blend/pallas_call | solution.py:100
  66.7 3.1 %blend.15 = (f32[2,2048,512]{2,1,0:T(8,128)}, bf16[512,512]{1,0:T(8,128)(2,1)S(1)}, f32[2,4,160,128]{3,2,1,0:T(8,128)S(1)}) custom-call(s32[3]{0:T(128)S(1)} %add_add_fusion.8.refs_0_, bf16[512,512]{1,0:T(8,128)(2,1)} %collective-permute-done.16.refs_1_, f32[2,2048,512]{2,1,0:T(8,128)S(1)} %copy-done.2, ...), custom_call_target="tpu_custom_call", output_to_operand_aliasing={{0}: (3, {})} | custom-call | flops 268435456 | bytes 3145728 | tf_op jit(solution)/shard_map/blend/pallas_call | solution.py:100
  69.8 0.6 collective-permute-start.17
  70.4 1.0 bitcast_add_fusion.1
  71.5 1.6 collective-permute-start.5
  73.1 2.6 %collective-permute-start.6 = (f32[160,128]{1,0:T(8,128)S(1)}, f32[160,128]{1,0:T(8,128)S(1)}, u32[]{:S(2)}, u32[]{:S(2)}) collective-permute-start(f32[160,128]{1,0:T(8,128)S(1)} %get-tuple-element.61), channel_id=1, source_target_pairs={{0,4},{1,5},{2,6},{3,7},{4,0},{5,1},{6,2},{7,3},{8,12},{9,13},{10,... | collective-permute-start | bytes 245768 | tf_op jit(solution)/shard_map/ppermute | solution.py:272
  75.9 3.4 %collective-permute-done.17 = f32[4,160,128]{2,1,0:T(8,128)S(1)} collective-permute-done((f32[4,160,128]{2,1,0:T(8,128)S(1)}, f32[4,160,128]{2,1,0:T(8,128)S(1)}, u32[]{:S(2)}, u32[]{:S(2)}) %collective-permute-start.17) | collective-permute-done | bytes 327712 | tf_op jit(solution)/shard_map/ppermute | solution.py:269
  79.4 3.3 %collective-permute-done.6 = f32[160,128]{1,0:T(8,128)S(1)} collective-permute-done((f32[160,128]{1,0:T(8,128)S(1)}, f32[160,128]{1,0:T(8,128)S(1)}, u32[]{:S(2)}, u32[]{:S(2)}) %collective-permute-start.6) | collective-permute-done | bytes 81952 | tf_op jit(solution)/shard_map/ppermute | solution.py:272
  82.7 1.8 %collective-permute-start.8 = (f32[160,128]{1,0:T(8,128)S(1)}, f32[160,128]{1,0:T(8,128)S(1)}, u32[]{:S(2)}, u32[]{:S(2)}) collective-permute-start(f32[160,128]{1,0:T(8,128)S(1)} %fusion.5.refs_0_), channel_id=1, source_target_pairs={{0,2},{1,3},{2,0},{3,1},{4,6},{5,7},{6,4},{7,5},{8,10},{9,11},{10,... | collective-permute-start | bytes 245768 | tf_op jit(solution)/shard_map/ppermute | solution.py:275
  84.5 1.5 collective-permute-start.9
  86.0 1.2 collective-permute-start.10
  87.2 0.9 collective-permute-start.18
  88.1 2.4 %collective-permute-start.19 = (f32[160,128]{1,0:T(8,128)S(1)}, f32[160,128]{1,0:T(8,128)S(1)}, u32[]{:S(2)}, u32[]{:S(2)}) collective-permute-start(f32[160,128]{1,0:T(8,128)S(1)} %get-tuple-element.58), channel_id=1, source_target_pairs={{0,4},{1,5},{2,6},{3,7},{4,0},{5,1},{6,2},{7,3},{8,12},{9,13},{10,... | collective-permute-start | bytes 245768 | tf_op jit(solution)/shard_map/ppermute | solution.py:272
  90.5 1.2 collective-permute-start.20
  91.6 2.6 %collective-permute-done.9.refs_2_ = f32[160,128]{1,0:T(8,128)S(1)} collective-permute-done((f32[160,128]{1,0:T(8,128)S(1)}, f32[160,128]{1,0:T(8,128)S(1)}, u32[]{:S(2)}, u32[]{:S(2)}) %collective-permute-start.9) | collective-permute-done | bytes 81952 | tf_op jit(solution)/shard_map/ppermute | solution.py:275
  94.3 0.7 collective-permute-start.11
  95.0 5.5 %collective-permute-done.19 = f32[160,128]{1,0:T(8,128)S(1)} collective-permute-done((f32[160,128]{1,0:T(8,128)S(1)}, f32[160,128]{1,0:T(8,128)S(1)}, u32[]{:S(2)}, u32[]{:S(2)}) %collective-permute-start.19) | collective-permute-done | bytes 81952 | tf_op jit(solution)/shard_map/ppermute | solution.py:272
  100.5 1.5 collective-permute-start.21
  102.0 1.3 collective-permute-start.22
  103.3 1.6 collective-permute-start.23
  105.5 4.8 %collective-permute-done.22.refs_2_ = f32[160,128]{1,0:T(8,128)S(1)} collective-permute-done((f32[160,128]{1,0:T(8,128)S(1)}, f32[160,128]{1,0:T(8,128)S(1)}, u32[]{:S(2)}, u32[]{:S(2)}) %collective-permute-start.22) | collective-permute-done | bytes 81952 | tf_op jit(solution)/shard_map/ppermute | solution.py:275
  110.4 15.8 %polynomial.2.poly = bf16[1024,512]{1,0:T(8,128)(2,1)S(1)} custom-call(s32[3]{0:T(128)S(1)} %add_add_fusion.5.place, f32[160,128]{1,0:T(8,128)S(1)} %fusion.5.refs_0_, f32[160,128]{1,0:T(8,128)S(1)} %collective-permute-done.8.refs_1_, f32[160,128]{1,0:T(8,128)S(1)} %collective-permute-done.9.refs_2_, f32[160,128]{1,0:T(8,128)S(1)} %collective-permute-done.10.refs_3_, ...), custom_call_target="tpu_custom_call" | custom-call | flops 13690208256 | bytes 2097152 | tf_op jit(solution)/shard_map/polynomial/pallas_call | solution.py:194
  126.2 0.9 apply.9
  127.2 0.7 apply.8
  127.9 1.6 collective-permute-start.12
  129.5 15.8 %polynomial.3.poly = bf16[1024,512]{1,0:T(8,128)(2,1)S(1)} custom-call(s32[3]{0:T(128)S(1)} %add_add_fusion.5.place, f32[160,128]{1,0:T(8,128)S(1)} %fusion.2.refs_0_, f32[160,128]{1,0:T(8,128)S(1)} %collective-permute-done.21.refs_1_, f32[160,128]{1,0:T(8,128)S(1)} %collective-permute-done.22.refs_2_, f32[160,128]{1,0:T(8,128)S(1)} %collective-permute-done.23.refs_3_, ...), custom_call_target="tpu_custom_call" | custom-call | flops 13690208256 | bytes 2097152 | tf_op jit(solution)/shard_map/polynomial/pallas_call | solution.py:194
  145.3 0.7 apply.13
  146.4 0.7 apply.12
  147.1 1.2 collective-permute-start.26
  148.3 0.7 apply.10
  149.5 0.7 apply.11
  150.3 2.4 %collective-permute-done.12 = bf16[512,512]{1,0:T(8,128)(2,1)S(1)} collective-permute-done((bf16[512,512]{1,0:T(8,128)(2,1)S(1)}, bf16[512,512]{1,0:T(8,128)(2,1)S(1)}, u32[]{:S(2)}, u32[]{:S(2)}) %collective-permute-start.12) | collective-permute-done | bytes 524320 | tf_op jit(solution)/shard_map/ppermute | solution.py:282
  153.2 0.7 apply.15
  153.9 21.2 %collective-permute-done.25 = bf16[512,512]{1,0:T(8,128)(2,1)S(1)} collective-permute-done((bf16[512,512]{1,0:T(8,128)(2,1)S(1)}, bf16[512,512]{1,0:T(8,128)(2,1)S(1)}, u32[]{:S(2)}, u32[]{:S(2)}) %collective-permute-start.25) | collective-permute-done | bytes 524320 | tf_op jit(solution)/shard_map/ppermute | solution.py:282
  175.3 0.7 apply.14
  176.0 2.0 %copy-done.12 = bf16[8,512,512]{2,1,0:T(8,128)(2,1)} copy-done((bf16[8,512,512]{2,1,0:T(8,128)(2,1)}, bf16[8,512,512]{2,1,0:T(8,128)(2,1)S(1)}, u32[]{:S(2)}) %copy-start.12) | copy-done | bytes 4194328
  (64 shorter events, 4.9 us)
Async XLA Ops:
  16.9 9.6 %collective-permute-start.2 = (bf16[512,512]{1,0:T(8,128)(2,1)S(1)}, bf16[512,512]{1,0:T(8,128)(2,1)S(1)}, u32[]{:S(2)}, u32[]{:S(2)}) collective-permute-start(bf16[512,512]{1,0:T(8,128)(2,1)S(1)} %get-tuple-element.52), channel_id=1, source_target_pairs={{0,8},{8,0},{16,24},{24,16},{1,9},{9,1},{17,25},{25,17},{2,10},{10... | collective-permute-start | bytes 1572872 | tf_op jit(solution)/shard_map/ppermute | solution.py:243
  17.3 23.2 %collective-permute-start.1 = (bf16[512,512]{1,0:T(8,128)(2,1)S(1)}, bf16[512,512]{1,0:T(8,128)(2,1)S(1)}, u32[]{:S(2)}, u32[]{:S(2)}) collective-permute-start(bf16[512,512]{1,0:T(8,128)(2,1)S(1)} %get-tuple-element.53), channel_id=1, source_target_pairs={{0,8},{8,0},{16,24},{24,16},{1,9},{9,1},{17,25},{25,17},{2,10},{10... | collective-permute-start | bytes 1572872 | tf_op jit(solution)/shard_map/ppermute | solution.py:243
  17.4 27.1 %collective-permute-start = (bf16[512,512]{1,0:T(8,128)(2,1)}, bf16[512,512]{1,0:T(8,128)(2,1)}, u32[]{:S(2)}, u32[]{:S(2)}) collective-permute-start(bf16[512,512]{1,0:T(8,128)(2,1)} %get-tuple-element.54), channel_id=1, source_target_pairs={{0,16},{8,24},{16,0},{24,8},{1,17},{9,25},{17,1},{25,9},{2,18},{10... | collective-permute-start | bytes 1572872 | tf_op jit(solution)/shard_map/ppermute | solution.py:243
  20.3 28.1 %collective-permute-start.3 = (bf16[512,512]{1,0:T(8,128)(2,1)}, bf16[512,512]{1,0:T(8,128)(2,1)S(1)}, u32[]{:S(2)}, u32[]{:S(2)}) collective-permute-start(bf16[512,512]{1,0:T(8,128)(2,1)} %get-tuple-element.51), channel_id=1, source_target_pairs={{0,24},{8,16},{16,8},{24,0},{1,25},{9,17},{17,9},{25,1},{2,26},{10... | collective-permute-start | bytes 1572872 | tf_op jit(solution)/shard_map/ppermute | solution.py:243
  20.3 39.9 %collective-permute-start.15 = (bf16[512,512]{1,0:T(8,128)(2,1)}, bf16[512,512]{1,0:T(8,128)(2,1)}, u32[]{:S(2)}, u32[]{:S(2)}) collective-permute-start(bf16[512,512]{1,0:T(8,128)(2,1)} %get-tuple-element.55), channel_id=1, source_target_pairs={{0,16},{8,24},{16,0},{24,8},{1,17},{9,25},{17,1},{25,9},{2,18},{10... | collective-permute-start | bytes 1572872 | tf_op jit(solution)/shard_map/ppermute | solution.py:243
  26.5 40.2 %collective-permute-start.16 = (bf16[512,512]{1,0:T(8,128)(2,1)}, bf16[512,512]{1,0:T(8,128)(2,1)}, u32[]{:S(2)}, u32[]{:S(2)}) collective-permute-start(bf16[512,512]{1,0:T(8,128)(2,1)} %get-tuple-element.50), channel_id=1, source_target_pairs={{0,24},{8,16},{16,8},{24,0},{1,25},{9,17},{17,9},{25,1},{2,26},{10... | collective-permute-start | bytes 1572872 | tf_op jit(solution)/shard_map/ppermute | solution.py:243
  26.9 3.4 %copy-start = (f32[2,2048,512]{2,1,0:T(8,128)S(1)}, f32[2,2048,512]{2,1,0:T(8,128)}, u32[]{:S(2)}) copy-start(f32[2,2048,512]{2,1,0:T(8,128)} %refs_2_.15) | copy-start | bytes 25165828
  30.3 2.2 %copy-start.3 = (bf16[8,512,512]{2,1,0:T(8,128)(2,1)S(1)}, bf16[8,512,512]{2,1,0:T(8,128)(2,1)}, u32[]{:S(2)}) copy-start(bf16[8,512,512]{2,1,0:T(8,128)(2,1)} %refs_1_.3) | copy-start | bytes 12582916
  32.5 3.8 %copy-start.1 = (f32[2,2048,512]{2,1,0:T(8,128)S(1)}, f32[2,2048,512]{2,1,0:T(8,128)}, u32[]{:S(2)}) copy-start(f32[2,2048,512]{2,1,0:T(8,128)} %refs_2_.15) | copy-start | bytes 25165828
  40.5 0.8 copy-start.10
  41.3 1.0 copy-start.11
  47.6 0.8 copy-start.4
  48.4 0.8 copy-start.8
  49.2 1.0 copy-start.9
  52.4 0.8 copy-start.6
  53.9 16.5 %collective-permute-start.4 = (f32[4,160,128]{2,1,0:T(8,128)}, f32[4,160,128]{2,1,0:T(8,128)}, u32[]{:S(2)}, u32[]{:S(2)}) collective-permute-start(f32[4,160,128]{2,1,0:T(8,128)} %slice_bitcast_fusion.1), channel_id=1, source_target_pairs={{0,1},{1,0},{2,3},{3,2},{4,5},{5,4},{6,7},{7,6},{8,9},{9,8},{10,11... | collective-permute-start | bytes 983048 | tf_op jit(solution)/shard_map/ppermute | solution.py:269
  60.2 3.4 %copy-start.2 = (f32[2,2048,512]{2,1,0:T(8,128)S(1)}, f32[2,2048,512]{2,1,0:T(8,128)}, u32[]{:S(2)}) copy-start(f32[2,2048,512]{2,1,0:T(8,128)} %refs_2_.15) | copy-start | bytes 25165828
  69.8 9.6 %collective-permute-start.17 = (f32[4,160,128]{2,1,0:T(8,128)S(1)}, f32[4,160,128]{2,1,0:T(8,128)S(1)}, u32[]{:S(2)}, u32[]{:S(2)}) collective-permute-start(f32[4,160,128]{2,1,0:T(8,128)S(1)} %slice_bitcast_fusion), channel_id=1, source_target_pairs={{0,1},{1,0},{2,3},{3,2},{4,5},{5,4},{6,7},{7,6},{8,9},{9,8},{10,11... | collective-permute-start | bytes 983048 | tf_op jit(solution)/shard_map/ppermute | solution.py:269
  71.5 7.9 %collective-permute-start.5 = (f32[160,128]{1,0:T(8,128)S(1)}, f32[160,128]{1,0:T(8,128)S(1)}, u32[]{:S(2)}, u32[]{:S(2)}) collective-permute-start(f32[160,128]{1,0:T(8,128)S(1)} %get-tuple-element.59), channel_id=1, source_target_pairs={{0,2},{1,3},{2,0},{3,1},{4,6},{5,7},{6,4},{7,5},{8,10},{9,11},{10,... | collective-permute-start | bytes 245768 | tf_op jit(solution)/shard_map/ppermute | solution.py:272
  73.1 9.6 %collective-permute-start.6 = (f32[160,128]{1,0:T(8,128)S(1)}, f32[160,128]{1,0:T(8,128)S(1)}, u32[]{:S(2)}, u32[]{:S(2)}) collective-permute-start(f32[160,128]{1,0:T(8,128)S(1)} %get-tuple-element.61), channel_id=1, source_target_pairs={{0,4},{1,5},{2,6},{3,7},{4,0},{5,1},{6,2},{7,3},{8,12},{9,13},{10,... | collective-permute-start | bytes 245768 | tf_op jit(solution)/shard_map/ppermute | solution.py:272
  75.7 7.0 %collective-permute-start.7 = (f32[160,128]{1,0:T(8,128)S(1)}, f32[160,128]{1,0:T(8,128)S(1)}, u32[]{:S(2)}, u32[]{:S(2)}) collective-permute-start(f32[160,128]{1,0:T(8,128)S(1)} %get-tuple-element.60), channel_id=1, source_target_pairs={{0,6},{1,7},{2,4},{3,5},{4,2},{5,3},{6,0},{7,1},{8,14},{9,15},{10,... | collective-permute-start | bytes 245768 | tf_op jit(solution)/shard_map/ppermute | solution.py:272
  82.7 7.8 %collective-permute-start.8 = (f32[160,128]{1,0:T(8,128)S(1)}, f32[160,128]{1,0:T(8,128)S(1)}, u32[]{:S(2)}, u32[]{:S(2)}) collective-permute-start(f32[160,128]{1,0:T(8,128)S(1)} %fusion.5.refs_0_), channel_id=1, source_target_pairs={{0,2},{1,3},{2,0},{3,1},{4,6},{5,7},{6,4},{7,5},{8,10},{9,11},{10,... | collective-permute-start | bytes 245768 | tf_op jit(solution)/shard_map/ppermute | solution.py:275
  84.5 9.7 %collective-permute-start.9 = (f32[160,128]{1,0:T(8,128)S(1)}, f32[160,128]{1,0:T(8,128)S(1)}, u32[]{:S(2)}, u32[]{:S(2)}) collective-permute-start(f32[160,128]{1,0:T(8,128)S(1)} %fusion.5.refs_0_), channel_id=1, source_target_pairs={{0,4},{1,5},{2,6},{3,7},{4,0},{5,1},{6,2},{7,3},{8,12},{9,13},{10,... | collective-permute-start | bytes 245768 | tf_op jit(solution)/shard_map/ppermute | solution.py:275
  86.0 8.3 %collective-permute-start.10 = (f32[160,128]{1,0:T(8,128)S(1)}, f32[160,128]{1,0:T(8,128)S(1)}, u32[]{:S(2)}, u32[]{:S(2)}) collective-permute-start(f32[160,128]{1,0:T(8,128)S(1)} %fusion.5.refs_0_), channel_id=1, source_target_pairs={{0,6},{1,7},{2,4},{3,5},{4,2},{5,3},{6,0},{7,1},{8,14},{9,15},{10,... | collective-permute-start | bytes 245768 | tf_op jit(solution)/shard_map/ppermute | solution.py:275
  87.2 7.8 %collective-permute-start.18 = (f32[160,128]{1,0:T(8,128)S(1)}, f32[160,128]{1,0:T(8,128)S(1)}, u32[]{:S(2)}, u32[]{:S(2)}) collective-permute-start(f32[160,128]{1,0:T(8,128)S(1)} %get-tuple-element.56), channel_id=1, source_target_pairs={{0,2},{1,3},{2,0},{3,1},{4,6},{5,7},{6,4},{7,5},{8,10},{9,11},{10,... | collective-permute-start | bytes 245768 | tf_op jit(solution)/shard_map/ppermute | solution.py:272
  88.1 12.3 %collective-permute-start.19 = (f32[160,128]{1,0:T(8,128)S(1)}, f32[160,128]{1,0:T(8,128)S(1)}, u32[]{:S(2)}, u32[]{:S(2)}) collective-permute-start(f32[160,128]{1,0:T(8,128)S(1)} %get-tuple-element.58), channel_id=1, source_target_pairs={{0,4},{1,5},{2,6},{3,7},{4,0},{5,1},{6,2},{7,3},{8,12},{9,13},{10,... | collective-permute-start | bytes 245768 | tf_op jit(solution)/shard_map/ppermute | solution.py:272
  90.5 10.0 %collective-permute-start.20 = (f32[160,128]{1,0:T(8,128)S(1)}, f32[160,128]{1,0:T(8,128)S(1)}, u32[]{:S(2)}, u32[]{:S(2)}) collective-permute-start(f32[160,128]{1,0:T(8,128)S(1)} %get-tuple-element.57), channel_id=1, source_target_pairs={{0,6},{1,7},{2,4},{3,5},{4,2},{5,3},{6,0},{7,1},{8,14},{9,15},{10,... | collective-permute-start | bytes 245768 | tf_op jit(solution)/shard_map/ppermute | solution.py:272
  94.3 16.1 %collective-permute-start.11 = (f32[4,160,128]{2,1,0:T(8,128)S(1)}, f32[4,160,128]{2,1,0:T(8,128)S(1)}, u32[]{:S(2)}, u32[]{:S(2)}) collective-permute-start(f32[4,160,128]{2,1,0:T(8,128)S(1)} %pad_maximum_fusion), channel_id=1, source_target_pairs={{0,1},{1,0},{2,3},{3,2},{4,5},{5,4},{6,7},{7,6},{8,9},{9,8},{10,11... | collective-permute-start | bytes 983048 | tf_op jit(solution)/shard_map/ppermute | solution.py:277
  100.5 5.0 %collective-permute-start.21 = (f32[160,128]{1,0:T(8,128)S(1)}, f32[160,128]{1,0:T(8,128)S(1)}, u32[]{:S(2)}, u32[]{:S(2)}) collective-permute-start(f32[160,128]{1,0:T(8,128)S(1)} %fusion.2.refs_0_), channel_id=1, source_target_pairs={{0,2},{1,3},{2,0},{3,1},{4,6},{5,7},{6,4},{7,5},{8,10},{9,11},{10,... | collective-permute-start | bytes 245768 | tf_op jit(solution)/shard_map/ppermute | solution.py:275
  102.0 8.3 %collective-permute-start.22 = (f32[160,128]{1,0:T(8,128)S(1)}, f32[160,128]{1,0:T(8,128)S(1)}, u32[]{:S(2)}, u32[]{:S(2)}) collective-permute-start(f32[160,128]{1,0:T(8,128)S(1)} %fusion.2.refs_0_), channel_id=1, source_target_pairs={{0,4},{1,5},{2,6},{3,7},{4,0},{5,1},{6,2},{7,3},{8,12},{9,13},{10,... | collective-permute-start | bytes 245768 | tf_op jit(solution)/shard_map/ppermute | solution.py:275
  103.3 7.0 %collective-permute-start.23 = (f32[160,128]{1,0:T(8,128)S(1)}, f32[160,128]{1,0:T(8,128)S(1)}, u32[]{:S(2)}, u32[]{:S(2)}) collective-permute-start(f32[160,128]{1,0:T(8,128)S(1)} %fusion.2.refs_0_), channel_id=1, source_target_pairs={{0,6},{1,7},{2,4},{3,5},{4,2},{5,3},{6,0},{7,1},{8,14},{9,15},{10,... | collective-permute-start | bytes 245768 | tf_op jit(solution)/shard_map/ppermute | solution.py:275
  110.3 15.9 %copy-start.7 = (bf16[512,512]{1,0:T(8,128)(2,1)S(1)}, bf16[512,512]{1,0:T(8,128)(2,1)}, u32[]{:S(2)}) copy-start(bf16[512,512]{1,0:T(8,128)(2,1)} %copy-done.6) | copy-start | bytes 1572868
  110.3 16.9 %copy-start.5 = (bf16[512,512]{1,0:T(8,128)(2,1)S(1)}, bf16[512,512]{1,0:T(8,128)(2,1)}, u32[]{:S(2)}) copy-start(bf16[512,512]{1,0:T(8,128)(2,1)} %copy-done.4) | copy-start | bytes 1572868
  110.3 19.2 %collective-permute-start.24 = (f32[4,160,128]{2,1,0:T(8,128)S(1)}, f32[4,160,128]{2,1,0:T(8,128)S(1)}, u32[]{:S(2)}, u32[]{:S(2)}) collective-permute-start(f32[4,160,128]{2,1,0:T(8,128)S(1)} %pad_maximum_fusion.1), channel_id=1, source_target_pairs={{0,1},{1,0},{2,3},{3,2},{4,5},{5,4},{6,7},{7,6},{8,9},{9,8},{10,11... | collective-permute-start | bytes 983048 | tf_op jit(solution)/shard_map/ppermute | solution.py:277
  127.1 26.0 %collective-permute-start.13 = (bf16[512,512]{1,0:T(8,128)(2,1)S(1)}, bf16[512,512]{1,0:T(8,128)(2,1)S(1)}, u32[]{:S(2)}, u32[]{:S(2)}) collective-permute-start(bf16[512,512]{1,0:T(8,128)(2,1)S(1)} %apply.9), channel_id=1, source_target_pairs={{0,24},{8,16},{16,8},{24,0},{1,25},{9,17},{17,9},{25,1},{2,26},{10... | collective-permute-start | bytes 1572872 | tf_op jit(solution)/shard_map/ppermute | solution.py:282
  127.9 24.8 %collective-permute-start.12 = (bf16[512,512]{1,0:T(8,128)(2,1)S(1)}, bf16[512,512]{1,0:T(8,128)(2,1)S(1)}, u32[]{:S(2)}, u32[]{:S(2)}) collective-permute-start(bf16[512,512]{1,0:T(8,128)(2,1)S(1)} %apply.8), channel_id=1, source_target_pairs={{0,16},{8,24},{16,0},{24,8},{1,17},{9,25},{17,1},{25,9},{2,18},{10... | collective-permute-start | bytes 1572872 | tf_op jit(solution)/shard_map/ppermute | solution.py:282
  146.0 29.2 %collective-permute-start.27 = (bf16[512,512]{1,0:T(8,128)(2,1)S(1)}, bf16[512,512]{1,0:T(8,128)(2,1)S(1)}, u32[]{:S(2)}, u32[]{:S(2)}) collective-permute-start(bf16[512,512]{1,0:T(8,128)(2,1)S(1)} %apply.13), channel_id=1, source_target_pairs={{0,8},{8,0},{16,24},{24,16},{1,9},{9,1},{17,25},{25,17},{2,10},{10... | collective-permute-start | bytes 1572872 | tf_op jit(solution)/shard_map/ppermute | solution.py:282
  147.1 28.1 %collective-permute-start.26 = (bf16[512,512]{1,0:T(8,128)(2,1)S(1)}, bf16[512,512]{1,0:T(8,128)(2,1)S(1)}, u32[]{:S(2)}, u32[]{:S(2)}) collective-permute-start(bf16[512,512]{1,0:T(8,128)(2,1)S(1)} %apply.12), channel_id=1, source_target_pairs={{0,24},{8,16},{16,8},{24,0},{1,25},{9,17},{17,9},{25,1},{2,26},{10... | collective-permute-start | bytes 1572872 | tf_op jit(solution)/shard_map/ppermute | solution.py:282
  149.0 4.2 %collective-permute-start.14 = (bf16[512,512]{1,0:T(8,128)(2,1)S(1)}, bf16[512,512]{1,0:T(8,128)(2,1)S(1)}, u32[]{:S(2)}, u32[]{:S(2)}) collective-permute-start(bf16[512,512]{1,0:T(8,128)(2,1)S(1)} %apply.10), channel_id=1, source_target_pairs={{0,8},{8,0},{16,24},{24,16},{1,9},{9,1},{17,25},{25,17},{2,10},{10... | collective-permute-start | bytes 1572872 | tf_op jit(solution)/shard_map/ppermute | solution.py:282
  152.7 22.4 %collective-permute-start.25 = (bf16[512,512]{1,0:T(8,128)(2,1)S(1)}, bf16[512,512]{1,0:T(8,128)(2,1)S(1)}, u32[]{:S(2)}, u32[]{:S(2)}) collective-permute-start(bf16[512,512]{1,0:T(8,128)(2,1)S(1)} %apply.11), channel_id=1, source_target_pairs={{0,16},{8,24},{16,0},{24,8},{1,17},{9,25},{17,1},{25,9},{2,18},{10... | collective-permute-start | bytes 1572872 | tf_op jit(solution)/shard_map/ppermute | solution.py:282
  176.0 2.0 %copy-start.12 = (bf16[8,512,512]{2,1,0:T(8,128)(2,1)}, bf16[8,512,512]{2,1,0:T(8,128)(2,1)S(1)}, u32[]{:S(2)}) copy-start(bf16[8,512,512]{2,1,0:T(8,128)(2,1)S(1)} %apply.14) | copy-start | bytes 12582916

commit v2 on v1

--- a/solution.py
+++ b/solution.py
@@ -23,10 +23,20 @@
 f32, bf16 = jnp.float32, jnp.bfloat16
 
 
-def slot_inverse(slot_table, matrix_count):
-    slots = jnp.arange(matrix_count, dtype=jnp.int32)
-    matches = slot_table[None, :] == slots[:, None]
-    return jnp.sum(jnp.where(matches, slots[None, :], 0), axis=1)
+def in_hbm(x):
+    return pltpu.with_memory_space_constraint(x, pltpu.HBM)
+
+
+def matrix_of(place, count, slots, slot, d):
+    wanted = slots * jnp.bitwise_xor(place[count], d) + slot
+    found = jnp.int32(0)
+    for m in range(1, count):
+        found = found + jnp.where(place[m] == wanted, m, 0)
+    return found
+
+
+def group_index(place):
+    return place[place.shape[0] - 1]
 
 
 def partners(size, step):
@@ -71,25 +81,89 @@
             count = PACKED // (near * far)
             for e1 in range(near):
                 for e2 in range(far):
-                    who = jnp.bitwise_xor(place[2], e2 * near + e1)
+                    who = jnp.bitwise_xor(group_index(place), e2 * near + e1)
                     start = pl.multiple_of(who * count, 8)
                     total[e1, e2] = held[pl.ds(start, count), :]
 
 
-def blend(place, gradient, local, momentum, slot, piece_rows, buffer, before, shares):
+def pick_kernel(place, *refs):
+    half = len(refs) // 2
+    for source, target in zip(refs[:half], refs[half:]):
+        target[...] = source[...]
+
+
+def pick(place, gradients, slots, wanted):
+    count, rows, _ = gradients.shape
+
+    def spec(slot, d):
+        return pl.BlockSpec(
+            (None, rows, RANK), lambda i, p: (matrix_of(p, count, slots, slot, d), 0, 0)
+        )
+
+    return pl.pallas_call(
+        pick_kernel,
+        grid_spec=pltpu.PrefetchScalarGridSpec(
+            num_scalar_prefetch=1,
+            grid=(1,),
+            in_specs=[spec(slot, d) for slot, d in wanted],
+            out_specs=[pl.BlockSpec((rows, RANK), lambda i, p: (0, 0)) for _ in wanted],
+        ),
+        out_shape=[jax.ShapeDtypeStruct((rows, RANK), bf16) for _ in wanted],
+        compiler_params=pltpu.CompilerParams(vmem_limit_bytes=16 * 2**20),
+        cost_estimate=pl.CostEstimate(
+            flops=0, bytes_accessed=4 * len(wanted) * rows * RANK, transcendentals=0
+        ),
+        name="pick",
+    )(place, *[in_hbm(gradients)] * len(wanted))
+
+
+def drop_kernel(place, piece, *refs):
+    refs[-1][...] = piece[...]
+
+
+def drop(place, piece, shape, slots, slot, d, buffer):
+    count, rows, _ = shape
+    operands = [piece] + ([] if buffer is None else [in_hbm(buffer)])
+    return pl.pallas_call(
+        drop_kernel,
+        grid_spec=pltpu.PrefetchScalarGridSpec(
+            num_scalar_prefetch=1,
+            grid=(1,),
+            in_specs=[pl.BlockSpec((rows, RANK), lambda i, p: (0, 0))]
+            + [pl.BlockSpec(memory_space=pltpu.HBM)] * (len(operands) - 1),
+            out_specs=pl.BlockSpec(
+                (None, rows, RANK), lambda i, p: (matrix_of(p, count, slots, slot, d), 0, 0)
+            ),
+        ),
+        out_shape=pltpu.HBM(shape, bf16),
+        input_output_aliases={} if buffer is None else {2: 0},
+        compiler_params=pltpu.CompilerParams(vmem_limit_bytes=16 * 2**20),
+        cost_estimate=pl.CostEstimate(flops=0, bytes_accessed=4 * rows * RANK, transcendentals=0),
+        name="drop",
+    )(place, *operands)
+
+
+def blend(place, gradient, momentum, slot, d, count, buffer, before, shares):
+    slots = momentum.shape[0]
+    piece_rows = gradient.shape[-2]
     tile = min(256, piece_rows)
     steps = piece_rows // tile
-    if local:
-        gradient_spec = pl.BlockSpec((None, tile, RANK), lambda i, p: (p[1], i, 0))
+    if d == 0:
+        gradient_spec = pl.BlockSpec(
+            (None, tile, RANK), lambda i, p: (matrix_of(p, count, slots, slot, 0), i, 0)
+        )
+        gradient = in_hbm(gradient)
     else:
         gradient_spec = pl.BlockSpec((tile, RANK), lambda i, p: (i, 0))
-    momentum_spec = pl.BlockSpec((None, tile, RANK), lambda i, p: (slot, p[0] * steps + i, 0))
-    in_specs, operands = [gradient_spec, momentum_spec], [gradient, momentum]
+    momentum_spec = pl.BlockSpec(
+        (None, tile, RANK), lambda i, p: (slot, jnp.bitwise_xor(p[count], d) * steps + i, 0)
+    )
+    in_specs, operands = [gradient_spec, momentum_spec], [gradient, in_hbm(momentum)]
     aliases = {}
     if buffer is not None:
         aliases = {1 + len(operands): 0}
-        in_specs.append(pl.BlockSpec(memory_space=pl.ANY))
-        operands.append(buffer)
+        in_specs.append(pl.BlockSpec(memory_space=pltpu.HBM))
+        operands.append(in_hbm(buffer))
     if before is not None:
         in_specs.append(pl.BlockSpec((PACKED, TILE), lambda i, p: (0, 0)))
         operands.append(before)
@@ -111,7 +185,7 @@
             scratch_shapes=[pltpu.VMEM((PACKED, TILE), f32)],
         ),
         out_shape=[
-            jax.ShapeDtypeStruct(momentum.shape, f32),
+            pltpu.HBM(momentum.shape, f32),
             jax.ShapeDtypeStruct((piece_rows, RANK), bf16),
             jax.ShapeDtypeStruct(total, f32),
         ],
@@ -143,12 +217,12 @@
     packed = refs.pop()
     result = refs.pop()
     for e2 in range(far):
-        who = jnp.bitwise_xor(place[2], e2 * near)
+        who = jnp.bitwise_xor(group_index(place), e2 * near)
         packed[pl.ds(pl.multiple_of(who * count, 8), count), :] = refs.pop(0)[...]
     for e1 in range(1, near):
         other = refs.pop(0)
         for e2 in range(far):
-            who = jnp.bitwise_xor(place[2], e2 * near + e1)
+            who = jnp.bitwise_xor(group_index(place), e2 * near + e1)
             packed[pl.ds(pl.multiple_of(who * count, 8), count), :] = other[e2]
     sides = RANK // TILE
     parts = {}
@@ -225,43 +299,44 @@
 
 
 def on_device(gradients, momentum, slot_table, *, owners, group):
-    matrix_count, piece_rows, _ = gradients.shape
+    matrix_count = gradients.shape[0]
     held_slots = momentum.shape[0]
-    inverse = slot_inverse(slot_table, matrix_count)
-    me_owner, me_group = lax.axis_index("owner"), lax.axis_index("fsdp")
     near = 1 << ((group.bit_length() - 1) // 2)
     shares = (near, group // near)
-
-    def matrix_of(slot, d):
-        return inverse[held_slots * jnp.bitwise_xor(me_owner, d) + slot]
+    place = jnp.concatenate(
+        [
+            slot_table.astype(jnp.int32),
+            jnp.stack([lax.axis_index("owner"), lax.axis_index("fsdp")]).astype(jnp.int32),
+        ]
+    )
 
     far_steps, near_steps = list(range(2, owners)), list(range(1, min(2, owners)))
     arrived = {}
-    for slot in range(held_slots):
-        for d in far_steps + near_steps:
-            piece = lax.dynamic_index_in_dim(gradients, matrix_of(slot, d), 0, keepdims=False)
+    first = [(0, d) for d in far_steps]
+    later = [(slot, d) for slot in range(1, held_slots) for d in far_steps]
+    beside = [(slot, d) for slot in range(held_slots) for d in near_steps]
+    for wanted in (first, beside, later):
+        pieces = pick(place, gradients, held_slots, wanted)
+        for (slot, d), piece in zip(wanted, pieces):
             arrived[slot, d] = lax.ppermute(piece, "owner", partners(owners, d))
 
     order = [(slot, d) for slot in range(held_slots) for d in [0] + near_steps]
     order += [(slot, d) for slot in range(held_slots) for d in far_steps]
     renewed, rows, sums = None, {}, {}
     for slot, d in order:
-        place = jnp.stack([jnp.bitwise_xor(me_owner, d), matrix_of(slot, d), me_group]).astype(jnp.int32)
-        last = d == owners - 1
         renewed, rows[slot, d], sums[slot] = blend(
             place,
-            gradients if d == 0 else arrived[slot, d],
-            d == 0,
+            arrived[slot, d] if d else gradients,
             momentum,
             slot,
-            piece_rows,
+            d,
+            matrix_count,
             renewed,
             sums.get(slot),
-            shares if last else None,
+            shares if d == owners - 1 else None,
         )
 
-    place = jnp.stack([me_owner, me_owner, me_group]).astype(jnp.int32)
-    updates = jnp.zeros(gradients.shape, bf16)
+    updates = None
     for slot in range(held_slots):
         share = sums[slot]
         line = share[0]
@@ -280,7 +355,7 @@
             out = apply_polynomial(rows[slot, d], poly)
             if d:
                 out = lax.ppermute(out, "owner", partners(owners, d))
-            updates = lax.dynamic_update_index_in_dim(updates, out, matrix_of(slot, d), 0)
+            updates = drop(place, out, gradients.shape, held_slots, slot, d, updates)
     return (updates, renewed)
 
 

time: 179 us -> 168 us (0.939)
  Pallas kernels: 56 us -> 79.5 us
  local copies, waits for them, and re-layouts: 23.2 us -> 0.08 us
  between operations: 16.2 us -> 0.81 us
  waiting for transfers between devices: 43.7 us -> 55.5 us
  other arithmetic: 8.95 us -> 0.88 us
    unnamed x26 -> x0, local copies, waits for them, and re-layouts: 17.9 us -> none
    ppermute x6, waiting for transfers between devices: 0.02 us -> 17.5 us  [on_device(): arrived[slot, d] = lax.ppermute(piece, 'owner', partners(owners, d))]
    pallas_call x0 -> x11, Pallas kernels: none -> 16.4 us  [the longest x8 10.9 us: drop(): pl.pallas_call(drop_kernel, grid_spec=pltpu.PrefetchScalarGridSpec(num_sc...]
    ppermute x6, waiting for transfers between devices: 23.6 us -> 16.6 us  [on_device(): out = lax.ppermute(out, 'owner', partners(owners, d))]
    pallas_call x8, Pallas kernels: 20 us -> 25.7 us  [blend(): pl.pallas_call(functools.partial(blend_kernel, shares, buffer is not None...]
    another operation x8 -> x0, other arithmetic: 5.64 us -> none  [the longest x7 5.57 us: on_device(): jnp.stack([jnp.bitwise_xor(me_owner, d), matrix_of(slot, d), me_group])]
    squeeze x1 -> x0, local copies, waits for them, and re-layouts: 3.25 us -> none  [on_device(): lax.dynamic_index_in_dim(gradients, matrix_of(slot, d), 0, keepdims=False)]
    pallas_call x6 -> x8, Pallas kernels: 4.43 us -> 5.85 us  [apply_polynomial(): pl.pallas_call(apply_kernel, out_shape=jax.ShapeDtypeStruct(rows.shape, b...]
  transfers between devices with their start and end apart: 28 -> 28, of which waited for: 8 -> 16; matrix products, arithmetic and copies ran while one was open for 5% -> 0% of each run, Pallas kernels for 31% -> 45%
where the time goes in v2:
time: 168 us; the launch traced here: 167 us
  Pallas kernels  79.5 us (47%)
  waiting for transfers between devices  55.5 us (33%)
  starting transfers between devices  30.4 us (18%)
    pallas_call x2, Pallas kernels, polynomial(): pl.pallas_call(functools.partial(polynomial_kernel, near, far, count), gr...  31.6 us
    pallas_call x8, Pallas kernels, blend(): pl.pallas_call(functools.partial(blend_kernel, shares, buffer is not None...  25.7 us
    ppermute x6, waiting for transfers between devices, on_device(): arrived[slot, d] = lax.ppermute(piece, 'owner', partners(owners, d))  17.5 us
    ppermute x6, waiting for transfers between devices, on_device(): out = lax.ppermute(out, 'owner', partners(owners, d))  16.6 us
    pallas_call x8, Pallas kernels, drop(): pl.pallas_call(drop_kernel, grid_spec=pltpu.PrefetchScalarGridSpec(num_sc...  10.9 us
    ppermute x6, waiting for transfers between devices, on_device(): mine = mine + lax.ppermute(line[e2], 'fsdp', partners(group, e2 * near))  9.64 us
    ppermute x6, starting transfers between devices, on_device(): own.append(lax.ppermute(mine, 'fsdp', partners(group, e2 * near)))  8.91 us
    ppermute x6, starting transfers between devices, on_device(): mine = mine + lax.ppermute(line[e2], 'fsdp', partners(group, e2 * near))  7.79 us
  transfers between devices with their start and end apart: 28, of which 16 were waited for; matrix products, arithmetic and copies ran while one was open for 0% of the time, Pallas kernels for 45%

profile of v2, /device:TPU:0, one launch (start us, length us, event | category | flops | bytes accessed | tf_op | source)
XLA Modules:
  0.0 167.2 jit_solution(11246914124326203173)
XLA Ops:
  0.6 0.7 pad_add_fusion.place.refs_0_
  1.4 1.8 %pick.3 = (bf16[512,512]{1,0:T(8,128)(2,1)S(1)}, bf16[512,512]{1,0:T(8,128)(2,1)S(1)}) custom-call(s32[10]{0:T(128)S(1)} %pad_add_fusion.place.refs_0_, bf16[8,512,512]{2,1,0:T(8,128)(2,1)} %refs_1_.9, bf16[8,512,512]{2,1,0:T(8,128)(2,1)} %refs_1_.9), custom_call_target="tpu_custom_call" | custom-call | bytes 2097152 | tf_op jit(solution)/shard_map/pick/pallas_call | solution.py:103
  3.2 0.5 collective-permute-start
  3.8 1.8 %pick.5 = (bf16[512,512]{1,0:T(8,128)(2,1)S(1)}, bf16[512,512]{1,0:T(8,128)(2,1)S(1)}) custom-call(s32[10]{0:T(128)S(1)} %pad_add_fusion.place.refs_0_, bf16[8,512,512]{2,1,0:T(8,128)(2,1)} %refs_1_.9, bf16[8,512,512]{2,1,0:T(8,128)(2,1)} %refs_1_.9), custom_call_target="tpu_custom_call" | custom-call | bytes 2097152 | tf_op jit(solution)/shard_map/pick/pallas_call | solution.py:103
  5.6 3.0 %collective-permute-start.4 = (bf16[512,512]{1,0:T(8,128)(2,1)S(1)}, bf16[512,512]{1,0:T(8,128)(2,1)S(1)}, u32[]{:S(2)}, u32[]{:S(2)}) collective-permute-start(bf16[512,512]{1,0:T(8,128)(2,1)S(1)} %get-tuple-element.40), channel_id=1, source_target_pairs={{0,16},{8,24},{16,0},{24,8},{1,17},{9,25},{17,1},{25,9},{2,18},{10... | collective-permute-start | bytes 1572872 | tf_op jit(solution)/shard_map/ppermute | solution.py:321
  8.6 1.8 %pick.4 = (bf16[512,512]{1,0:T(8,128)(2,1)S(1)}, bf16[512,512]{1,0:T(8,128)(2,1)S(1)}) custom-call(s32[10]{0:T(128)S(1)} %pad_add_fusion.place.refs_0_, bf16[8,512,512]{2,1,0:T(8,128)(2,1)} %refs_1_.9, bf16[8,512,512]{2,1,0:T(8,128)(2,1)} %refs_1_.9), custom_call_target="tpu_custom_call" | custom-call | bytes 2097152 | tf_op jit(solution)/shard_map/pick/pallas_call | solution.py:103
  10.4 1.5 collective-permute-start.2
  12.3 3.3 %blend.8 = (f32[2,2048,512]{2,1,0:T(8,128)}, bf16[512,512]{1,0:T(8,128)(2,1)S(1)}, f32[1280,128]{1,0:T(8,128)S(1)}) custom-call(s32[10]{0:T(128)S(1)} %pad_add_fusion.place.refs_0_, bf16[8,512,512]{2,1,0:T(8,128)(2,1)} %refs_1_.9, f32[2,2048,512]{2,1,0:T(8,128)} %refs_2_.15), custom_call_target="tpu_custom_call" | custom-call | flops 268435456 | bytes 3145728 | tf_op jit(solution)/shard_map/blend/pallas_call | solution.py:174
  15.6 3.2 %blend.9 = (f32[2,2048,512]{2,1,0:T(8,128)}, bf16[512,512]{1,0:T(8,128)(2,1)S(1)}, f32[1280,128]{1,0:T(8,128)S(1)}) custom-call(s32[10]{0:T(128)S(1)} %pad_add_fusion.place.refs_0_, bf16[512,512]{1,0:T(8,128)(2,1)S(1)} %collective-permute-done.refs_1_, f32[2,2048,512]{2,1,0:T(8,128)} %refs_2_.15, ...), custom_call_target="tpu_custom_call", output_to_operand_aliasing={{0}: (3, {})} | custom-call | flops 268435456 | bytes 3145728 | tf_op jit(solution)/shard_map/blend/pallas_call | solution.py:174
  18.8 3.3 %blend.10 = (f32[2,2048,512]{2,1,0:T(8,128)}, bf16[512,512]{1,0:T(8,128)(2,1)S(1)}, f32[1280,128]{1,0:T(8,128)S(1)}) custom-call(s32[10]{0:T(128)S(1)} %pad_add_fusion.place.refs_0_, bf16[8,512,512]{2,1,0:T(8,128)(2,1)} %refs_1_.9, f32[2,2048,512]{2,1,0:T(8,128)} %refs_2_.15, f32[2,2048,512]{2,1,0:T(8,128)} %get-tuple-element.35.refs_3_), custom_call_target="tpu_custom_call", output_to_operand_aliasing={{0}: (3, {})} | custom-call | flops 268435456 | bytes 3145728 | tf_op jit(solution)/shard_map/blend/pallas_call | solution.py:174
  22.1 3.2 %blend.11 = (f32[2,2048,512]{2,1,0:T(8,128)}, bf16[512,512]{1,0:T(8,128)(2,1)S(1)}, f32[1280,128]{1,0:T(8,128)S(1)}) custom-call(s32[10]{0:T(128)S(1)} %pad_add_fusion.place.refs_0_, bf16[512,512]{1,0:T(8,128)(2,1)S(1)} %collective-permute-done.5.refs_1_, f32[2,2048,512]{2,1,0:T(8,128)} %refs_2_.15, ...), custom_call_target="tpu_custom_call", output_to_operand_aliasing={{0}: (3, {})} | custom-call | flops 268435456 | bytes 3145728 | tf_op jit(solution)/shard_map/blend/pallas_call | solution.py:174
  25.3 3.2 %blend.12 = (f32[2,2048,512]{2,1,0:T(8,128)}, bf16[512,512]{1,0:T(8,128)(2,1)S(1)}, f32[1280,128]{1,0:T(8,128)S(1)}) custom-call(s32[10]{0:T(128)S(1)} %pad_add_fusion.place.refs_0_, bf16[512,512]{1,0:T(8,128)(2,1)S(1)} %collective-permute-done.4.refs_1_, f32[2,2048,512]{2,1,0:T(8,128)} %refs_2_.15, ...), custom_call_target="tpu_custom_call", output_to_operand_aliasing={{0}: (3, {})} | custom-call | flops 268435456 | bytes 3145728 | tf_op jit(solution)/shard_map/blend/pallas_call | solution.py:174
  28.4 3.7 %collective-permute-done.3.refs_1_ = bf16[512,512]{1,0:T(8,128)(2,1)S(1)} collective-permute-done((bf16[512,512]{1,0:T(8,128)(2,1)S(1)}, bf16[512,512]{1,0:T(8,128)(2,1)S(1)}, u32[]{:S(2)}, u32[]{:S(2)}) %collective-permute-start.3) | collective-permute-done | bytes 524320 | tf_op jit(solution)/shard_map/ppermute | solution.py:321
  32.1 3.2 %blend.13 = (f32[2,2048,512]{2,1,0:T(8,128)}, bf16[512,512]{1,0:T(8,128)(2,1)S(1)}, f32[2,4,160,128]{3,2,1,0:T(8,128)S(1)}) custom-call(s32[10]{0:T(128)S(1)} %pad_add_fusion.place.refs_0_, bf16[512,512]{1,0:T(8,128)(2,1)S(1)} %collective-permute-done.3.refs_1_, f32[2,2048,512]{2,1,0:T(8,128)} %refs_2_.15, ...), custom_call_target="tpu_custom_call", output_to_operand_aliasing={{0}: (3, {})} | custom-call | flops 268435456 | bytes 3145728 | tf_op jit(solution)/shard_map/blend/pallas_call | solution.py:174
  35.3 1.6 collective-permute-start.17
  36.9 6.9 %collective-permute-done.2.refs_1_ = bf16[512,512]{1,0:T(8,128)(2,1)S(1)} collective-permute-done((bf16[512,512]{1,0:T(8,128)(2,1)S(1)}, bf16[512,512]{1,0:T(8,128)(2,1)S(1)}, u32[]{:S(2)}, u32[]{:S(2)}) %collective-permute-start.2) | collective-permute-done | bytes 524320 | tf_op jit(solution)/shard_map/ppermute | solution.py:321
  43.8 3.2 %blend.14 = (f32[2,2048,512]{2,1,0:T(8,128)}, bf16[512,512]{1,0:T(8,128)(2,1)S(1)}, f32[1280,128]{1,0:T(8,128)S(1)}) custom-call(s32[10]{0:T(128)S(1)} %pad_add_fusion.place.refs_0_, bf16[512,512]{1,0:T(8,128)(2,1)S(1)} %collective-permute-done.2.refs_1_, f32[2,2048,512]{2,1,0:T(8,128)} %refs_2_.15, ...), custom_call_target="tpu_custom_call", output_to_operand_aliasing={{0}: (3, {})} | custom-call | flops 268435456 | bytes 3145728 | tf_op jit(solution)/shard_map/blend/pallas_call | solution.py:174
  47.0 6.9 %collective-permute-done.1.refs_1_ = bf16[512,512]{1,0:T(8,128)(2,1)S(1)} collective-permute-done((bf16[512,512]{1,0:T(8,128)(2,1)S(1)}, bf16[512,512]{1,0:T(8,128)(2,1)S(1)}, u32[]{:S(2)}, u32[]{:S(2)}) %collective-permute-start.1) | collective-permute-done | bytes 524320 | tf_op jit(solution)/shard_map/ppermute | solution.py:321
  53.9 3.2 %blend.15 = (f32[2,2048,512]{2,1,0:T(8,128)}, bf16[512,512]{1,0:T(8,128)(2,1)S(1)}, f32[2,4,160,128]{3,2,1,0:T(8,128)S(1)}) custom-call(s32[10]{0:T(128)S(1)} %pad_add_fusion.place.refs_0_, bf16[512,512]{1,0:T(8,128)(2,1)S(1)} %collective-permute-done.1.refs_1_, f32[2,2048,512]{2,1,0:T(8,128)} %refs_2_.15, ...), custom_call_target="tpu_custom_call", output_to_operand_aliasing={{0}: (3, {})} | custom-call | flops 268435456 | bytes 3145728 | tf_op jit(solution)/shard_map/blend/pallas_call | solution.py:174
  57.1 1.5 collective-permute-start.6
  58.7 1.6 collective-permute-start.18
  60.4 2.5 %collective-permute-start.20 = (f32[160,128]{1,0:T(8,128)S(1)}, f32[160,128]{1,0:T(8,128)S(1)}, u32[]{:S(2)}, u32[]{:S(2)}) collective-permute-start(f32[160,128]{1,0:T(8,128)S(1)} %get-tuple-element.63), channel_id=1, source_target_pairs={{0,6},{1,7},{2,4},{3,5},{4,2},{5,3},{6,0},{7,1},{8,14},{9,15},{10,... | collective-permute-start | bytes 245768 | tf_op jit(solution)/shard_map/ppermute | solution.py:347
  63.0 4.3 %collective-permute-done.6 = f32[4,160,128]{2,1,0:T(8,128)S(1)} collective-permute-done((f32[4,160,128]{2,1,0:T(8,128)S(1)}, f32[4,160,128]{2,1,0:T(8,128)S(1)}, u32[]{:S(2)}, u32[]{:S(2)}) %collective-permute-start.6) | collective-permute-done | bytes 327712 | tf_op jit(solution)/shard_map/ppermute | solution.py:344
  67.3 0.6 collective-permute-done.20
  67.9 3.0 %collective-permute-done.19 = f32[160,128]{1,0:T(8,128)S(1)} collective-permute-done((f32[160,128]{1,0:T(8,128)S(1)}, f32[160,128]{1,0:T(8,128)S(1)}, u32[]{:S(2)}, u32[]{:S(2)}) %collective-permute-start.19) | collective-permute-done | bytes 81952 | tf_op jit(solution)/shard_map/ppermute | solution.py:347
  70.9 2.8 %collective-permute-start.23 = (f32[160,128]{1,0:T(8,128)S(1)}, f32[160,128]{1,0:T(8,128)S(1)}, u32[]{:S(2)}, u32[]{:S(2)}) collective-permute-start(f32[160,128]{1,0:T(8,128)S(1)} %fusion.2.refs_0_), channel_id=1, source_target_pairs={{0,6},{1,7},{2,4},{3,5},{4,2},{5,3},{6,0},{7,1},{8,14},{9,15},{10,... | collective-permute-start | bytes 245768 | tf_op jit(solution)/shard_map/ppermute | solution.py:350
  73.7 1.7 %collective-permute-start.21 = (f32[160,128]{1,0:T(8,128)S(1)}, f32[160,128]{1,0:T(8,128)S(1)}, u32[]{:S(2)}, u32[]{:S(2)}) collective-permute-start(f32[160,128]{1,0:T(8,128)S(1)} %fusion.2.refs_0_), channel_id=1, source_target_pairs={{0,2},{1,3},{2,0},{3,1},{4,6},{5,7},{6,4},{7,5},{8,10},{9,11},{10,... | collective-permute-start | bytes 245768 | tf_op jit(solution)/shard_map/ppermute | solution.py:350
  75.4 0.4 collective-permute-start.7
  75.8 2.4 %collective-permute-start.9 = (f32[160,128]{1,0:T(8,128)S(1)}, f32[160,128]{1,0:T(8,128)S(1)}, u32[]{:S(2)}, u32[]{:S(2)}) collective-permute-start(f32[160,128]{1,0:T(8,128)S(1)} %get-tuple-element.66), channel_id=1, source_target_pairs={{0,6},{1,7},{2,4},{3,5},{4,2},{5,3},{6,0},{7,1},{8,14},{9,15},{10,... | collective-permute-start | bytes 245768 | tf_op jit(solution)/shard_map/ppermute | solution.py:347
  78.3 0.7 collective-permute-start.8
  79.0 1.9 %collective-permute-done.22.refs_2_ = f32[160,128]{1,0:T(8,128)S(1)} collective-permute-done((f32[160,128]{1,0:T(8,128)S(1)}, f32[160,128]{1,0:T(8,128)S(1)}, u32[]{:S(2)}, u32[]{:S(2)}) %collective-permute-start.22) | collective-permute-done | bytes 81952 | tf_op jit(solution)/shard_map/ppermute | solution.py:350
  81.2 0.6 collective-permute-start.24
  81.8 1.4 collective-permute-done.7
  83.2 2.0 %collective-permute-done.9 = f32[160,128]{1,0:T(8,128)S(1)} collective-permute-done((f32[160,128]{1,0:T(8,128)S(1)}, f32[160,128]{1,0:T(8,128)S(1)}, u32[]{:S(2)}, u32[]{:S(2)}) %collective-permute-start.9) | collective-permute-done | bytes 81952 | tf_op jit(solution)/shard_map/ppermute | solution.py:347
  85.3 2.5 %collective-permute-done.8 = f32[160,128]{1,0:T(8,128)S(1)} collective-permute-done((f32[160,128]{1,0:T(8,128)S(1)}, f32[160,128]{1,0:T(8,128)S(1)}, u32[]{:S(2)}, u32[]{:S(2)}) %collective-permute-start.8) | collective-permute-done | bytes 81952 | tf_op jit(solution)/shard_map/ppermute | solution.py:347
  87.8 2.0 %collective-permute-start.12 = (f32[160,128]{1,0:T(8,128)S(1)}, f32[160,128]{1,0:T(8,128)S(1)}, u32[]{:S(2)}, u32[]{:S(2)}) collective-permute-start(f32[160,128]{1,0:T(8,128)S(1)} %fusion.5.refs_0_), channel_id=1, source_target_pairs={{0,6},{1,7},{2,4},{3,5},{4,2},{5,3},{6,0},{7,1},{8,14},{9,15},{10,... | collective-permute-start | bytes 245768 | tf_op jit(solution)/shard_map/ppermute | solution.py:350
  89.8 2.5 %collective-permute-start.10 = (f32[160,128]{1,0:T(8,128)S(1)}, f32[160,128]{1,0:T(8,128)S(1)}, u32[]{:S(2)}, u32[]{:S(2)}) collective-permute-start(f32[160,128]{1,0:T(8,128)S(1)} %fusion.5.refs_0_), channel_id=1, source_target_pairs={{0,2},{1,3},{2,0},{3,1},{4,6},{5,7},{6,4},{7,5},{8,10},{9,11},{10,... | collective-permute-start | bytes 245768 | tf_op jit(solution)/shard_map/ppermute | solution.py:350
  92.3 2.8 %collective-permute-done.12.refs_3_ = f32[160,128]{1,0:T(8,128)S(1)} collective-permute-done((f32[160,128]{1,0:T(8,128)S(1)}, f32[160,128]{1,0:T(8,128)S(1)}, u32[]{:S(2)}, u32[]{:S(2)}) %collective-permute-start.12) | collective-permute-done | bytes 81952 | tf_op jit(solution)/shard_map/ppermute | solution.py:350
  95.0 2.5 %collective-permute-done.11.refs_2_ = f32[160,128]{1,0:T(8,128)S(1)} collective-permute-done((f32[160,128]{1,0:T(8,128)S(1)}, f32[160,128]{1,0:T(8,128)S(1)}, u32[]{:S(2)}, u32[]{:S(2)}) %collective-permute-start.11) | collective-permute-done | bytes 81952 | tf_op jit(solution)/shard_map/ppermute | solution.py:350
  97.6 0.6 collective-permute-start.13
  98.2 15.8 %polynomial.3.poly = bf16[1024,512]{1,0:T(8,128)(2,1)S(1)} custom-call(s32[10]{0:T(128)S(1)} %pad_add_fusion.place.refs_0_, f32[160,128]{1,0:T(8,128)S(1)} %fusion.2.refs_0_, f32[160,128]{1,0:T(8,128)S(1)} %collective-permute-done.21.refs_1_, f32[160,128]{1,0:T(8,128)S(1)} %collective-permute-done.22.refs_2_, ...), custom_call_target="tpu_custom_call" | custom-call | flops 13690208256 | bytes 2097152 | tf_op jit(solution)/shard_map/polynomial/pallas_call | solution.py:268
  114.0 0.9 apply.13
  115.0 0.7 apply.14
  115.7 1.7 collective-permute-start.26
  117.4 0.7 apply.15
  118.1 0.6 collective-permute-start.27
  118.7 15.8 %polynomial.2.poly = bf16[1024,512]{1,0:T(8,128)(2,1)S(1)} custom-call(s32[10]{0:T(128)S(1)} %pad_add_fusion.place.refs_0_, f32[160,128]{1,0:T(8,128)S(1)} %fusion.5.refs_0_, f32[160,128]{1,0:T(8,128)S(1)} %collective-permute-done.10.refs_1_, f32[160,128]{1,0:T(8,128)S(1)} %collective-permute-done.11.refs_2_, ...), custom_call_target="tpu_custom_call" | custom-call | flops 13690208256 | bytes 2097152 | tf_op jit(solution)/shard_map/polynomial/pallas_call | solution.py:268
  134.5 0.7 apply.11
  135.2 1.6 collective-permute-start.16
  136.7 0.7 apply.10
  137.4 0.7 apply.9
  138.2 3.6 %collective-permute-done.27.piece = bf16[512,512]{1,0:T(8,128)(2,1)S(1)} collective-permute-done((bf16[512,512]{1,0:T(8,128)(2,1)S(1)}, bf16[512,512]{1,0:T(8,128)(2,1)S(1)}, u32[]{:S(2)}, u32[]{:S(2)}) %collective-permute-start.27) | collective-permute-done | bytes 524320 | tf_op jit(solution)/shard_map/ppermute | solution.py:357
  141.8 0.7 apply.8.piece
  142.6 0.7 apply.12.piece
  143.3 1.4 drop.8.refs_0_
  144.6 1.4 drop.9.refs_0_
  146.0 1.4 drop.10.refs_0_
  147.4 1.4 drop.11.refs_0_
  148.7 4.3 %collective-permute-done.16.piece = bf16[512,512]{1,0:T(8,128)(2,1)S(1)} collective-permute-done((bf16[512,512]{1,0:T(8,128)(2,1)S(1)}, bf16[512,512]{1,0:T(8,128)(2,1)S(1)}, u32[]{:S(2)}, u32[]{:S(2)}) %collective-permute-start.16) | collective-permute-done | bytes 524320 | tf_op jit(solution)/shard_map/ppermute | solution.py:357
  153.1 1.4 drop.12.refs_0_
  154.4 8.6 %collective-permute-done.15.piece = bf16[512,512]{1,0:T(8,128)(2,1)S(1)} collective-permute-done((bf16[512,512]{1,0:T(8,128)(2,1)S(1)}, bf16[512,512]{1,0:T(8,128)(2,1)S(1)}, u32[]{:S(2)}, u32[]{:S(2)}) %collective-permute-start.15) | collective-permute-done | bytes 524320 | tf_op jit(solution)/shard_map/ppermute | solution.py:357
  163.1 1.4 drop.13.refs_0_
  164.4 1.4 drop.14.refs_0_
  165.8 1.4 drop.15
  (32 shorter events, 1.4 us)
Async XLA Ops:
  3.2 8.7 %collective-permute-start = (bf16[512,512]{1,0:T(8,128)(2,1)S(1)}, bf16[512,512]{1,0:T(8,128)(2,1)S(1)}, u32[]{:S(2)}, u32[]{:S(2)}) collective-permute-start(bf16[512,512]{1,0:T(8,128)(2,1)S(1)} %get-tuple-element.32), channel_id=1, source_target_pairs={{0,8},{8,0},{16,24},{24,16},{1,9},{9,1},{17,25},{25,17},{2,10},{10... | collective-permute-start | bytes 1572872 | tf_op jit(solution)/shard_map/ppermute | solution.py:321
  3.7 18.4 %collective-permute-start.5 = (bf16[512,512]{1,0:T(8,128)(2,1)S(1)}, bf16[512,512]{1,0:T(8,128)(2,1)S(1)}, u32[]{:S(2)}, u32[]{:S(2)}) collective-permute-start(bf16[512,512]{1,0:T(8,128)(2,1)S(1)} %get-tuple-element.41), channel_id=1, source_target_pairs={{0,8},{8,0},{16,24},{24,16},{1,9},{9,1},{17,25},{25,17},{2,10},{10... | collective-permute-start | bytes 1572872 | tf_op jit(solution)/shard_map/ppermute | solution.py:321
  5.6 19.6 %collective-permute-start.4 = (bf16[512,512]{1,0:T(8,128)(2,1)S(1)}, bf16[512,512]{1,0:T(8,128)(2,1)S(1)}, u32[]{:S(2)}, u32[]{:S(2)}) collective-permute-start(bf16[512,512]{1,0:T(8,128)(2,1)S(1)} %get-tuple-element.40), channel_id=1, source_target_pairs={{0,16},{8,24},{16,0},{24,8},{1,17},{9,25},{17,1},{25,9},{2,18},{10... | collective-permute-start | bytes 1572872 | tf_op jit(solution)/shard_map/ppermute | solution.py:321
  8.6 23.5 %collective-permute-start.3 = (bf16[512,512]{1,0:T(8,128)(2,1)S(1)}, bf16[512,512]{1,0:T(8,128)(2,1)S(1)}, u32[]{:S(2)}, u32[]{:S(2)}) collective-permute-start(bf16[512,512]{1,0:T(8,128)(2,1)S(1)} %get-tuple-element.39), channel_id=1, source_target_pairs={{0,24},{8,16},{16,8},{24,0},{1,25},{9,17},{17,9},{25,1},{2,26},{10... | collective-permute-start | bytes 1572872 | tf_op jit(solution)/shard_map/ppermute | solution.py:321
  10.4 33.4 %collective-permute-start.2 = (bf16[512,512]{1,0:T(8,128)(2,1)S(1)}, bf16[512,512]{1,0:T(8,128)(2,1)S(1)}, u32[]{:S(2)}, u32[]{:S(2)}) collective-permute-start(bf16[512,512]{1,0:T(8,128)(2,1)S(1)} %get-tuple-element.38), channel_id=1, source_target_pairs={{0,16},{8,24},{16,0},{24,8},{1,17},{9,25},{17,1},{25,9},{2,18},{10... | collective-permute-start | bytes 1572872 | tf_op jit(solution)/shard_map/ppermute | solution.py:321
  11.9 42.0 %collective-permute-start.1 = (bf16[512,512]{1,0:T(8,128)(2,1)S(1)}, bf16[512,512]{1,0:T(8,128)(2,1)S(1)}, u32[]{:S(2)}, u32[]{:S(2)}) collective-permute-start(bf16[512,512]{1,0:T(8,128)(2,1)S(1)} %get-tuple-element.37), channel_id=1, source_target_pairs={{0,24},{8,16},{16,8},{24,0},{1,25},{9,17},{17,9},{25,1},{2,26},{10... | collective-permute-start | bytes 1572872 | tf_op jit(solution)/shard_map/ppermute | solution.py:321
  35.3 23.3 %collective-permute-start.17 = (f32[4,160,128]{2,1,0:T(8,128)S(1)}, f32[4,160,128]{2,1,0:T(8,128)S(1)}, u32[]{:S(2)}, u32[]{:S(2)}) collective-permute-start(f32[4,160,128]{2,1,0:T(8,128)S(1)} %slice_bitcast_fusion), channel_id=1, source_target_pairs={{0,1},{1,0},{2,3},{3,2},{4,5},{5,4},{6,7},{7,6},{8,9},{9,8},{10,11... | collective-permute-start | bytes 983048 | tf_op jit(solution)/shard_map/ppermute | solution.py:344
  57.1 10.1 %collective-permute-start.6 = (f32[4,160,128]{2,1,0:T(8,128)S(1)}, f32[4,160,128]{2,1,0:T(8,128)S(1)}, u32[]{:S(2)}, u32[]{:S(2)}) collective-permute-start(f32[4,160,128]{2,1,0:T(8,128)S(1)} %slice_bitcast_fusion.1), channel_id=1, source_target_pairs={{0,1},{1,0},{2,3},{3,2},{4,5},{5,4},{6,7},{7,6},{8,9},{9,8},{10,11... | collective-permute-start | bytes 983048 | tf_op jit(solution)/shard_map/ppermute | solution.py:344
  58.7 8.5 %collective-permute-start.18 = (f32[160,128]{1,0:T(8,128)S(1)}, f32[160,128]{1,0:T(8,128)S(1)}, u32[]{:S(2)}, u32[]{:S(2)}) collective-permute-start(f32[160,128]{1,0:T(8,128)S(1)} %get-tuple-element.62), channel_id=1, source_target_pairs={{0,2},{1,3},{2,0},{3,1},{4,6},{5,7},{6,4},{7,5},{8,10},{9,11},{10,... | collective-permute-start | bytes 245768 | tf_op jit(solution)/shard_map/ppermute | solution.py:347
  60.4 7.5 %collective-permute-start.20 = (f32[160,128]{1,0:T(8,128)S(1)}, f32[160,128]{1,0:T(8,128)S(1)}, u32[]{:S(2)}, u32[]{:S(2)}) collective-permute-start(f32[160,128]{1,0:T(8,128)S(1)} %get-tuple-element.63), channel_id=1, source_target_pairs={{0,6},{1,7},{2,4},{3,5},{4,2},{5,3},{6,0},{7,1},{8,14},{9,15},{10,... | collective-permute-start | bytes 245768 | tf_op jit(solution)/shard_map/ppermute | solution.py:347
  62.8 8.1 %collective-permute-start.19 = (f32[160,128]{1,0:T(8,128)S(1)}, f32[160,128]{1,0:T(8,128)S(1)}, u32[]{:S(2)}, u32[]{:S(2)}) collective-permute-start(f32[160,128]{1,0:T(8,128)S(1)} %get-tuple-element.64), channel_id=1, source_target_pairs={{0,4},{1,5},{2,6},{3,7},{4,0},{5,1},{6,2},{7,3},{8,12},{9,13},{10,... | collective-permute-start | bytes 245768 | tf_op jit(solution)/shard_map/ppermute | solution.py:347
  70.9 7.3 %collective-permute-start.23 = (f32[160,128]{1,0:T(8,128)S(1)}, f32[160,128]{1,0:T(8,128)S(1)}, u32[]{:S(2)}, u32[]{:S(2)}) collective-permute-start(f32[160,128]{1,0:T(8,128)S(1)} %fusion.2.refs_0_), channel_id=1, source_target_pairs={{0,6},{1,7},{2,4},{3,5},{4,2},{5,3},{6,0},{7,1},{8,14},{9,15},{10,... | collective-permute-start | bytes 245768 | tf_op jit(solution)/shard_map/ppermute | solution.py:350
  73.7 7.2 %collective-permute-start.22 = (f32[160,128]{1,0:T(8,128)S(1)}, f32[160,128]{1,0:T(8,128)S(1)}, u32[]{:S(2)}, u32[]{:S(2)}) collective-permute-start(f32[160,128]{1,0:T(8,128)S(1)} %fusion.2.refs_0_), channel_id=1, source_target_pairs={{0,4},{1,5},{2,6},{3,7},{4,0},{5,1},{6,2},{7,3},{8,12},{9,13},{10,... | collective-permute-start | bytes 245768 | tf_op jit(solution)/shard_map/ppermute | solution.py:350
  73.7 7.5 %collective-permute-start.21 = (f32[160,128]{1,0:T(8,128)S(1)}, f32[160,128]{1,0:T(8,128)S(1)}, u32[]{:S(2)}, u32[]{:S(2)}) collective-permute-start(f32[160,128]{1,0:T(8,128)S(1)} %fusion.2.refs_0_), channel_id=1, source_target_pairs={{0,2},{1,3},{2,0},{3,1},{4,6},{5,7},{6,4},{7,5},{8,10},{9,11},{10,... | collective-permute-start | bytes 245768 | tf_op jit(solution)/shard_map/ppermute | solution.py:350
  75.4 7.8 %collective-permute-start.7 = (f32[160,128]{1,0:T(8,128)S(1)}, f32[160,128]{1,0:T(8,128)S(1)}, u32[]{:S(2)}, u32[]{:S(2)}) collective-permute-start(f32[160,128]{1,0:T(8,128)S(1)} %get-tuple-element.65), channel_id=1, source_target_pairs={{0,2},{1,3},{2,0},{3,1},{4,6},{5,7},{6,4},{7,5},{8,10},{9,11},{10,... | collective-permute-start | bytes 245768 | tf_op jit(solution)/shard_map/ppermute | solution.py:347
  75.8 9.4 %collective-permute-start.9 = (f32[160,128]{1,0:T(8,128)S(1)}, f32[160,128]{1,0:T(8,128)S(1)}, u32[]{:S(2)}, u32[]{:S(2)}) collective-permute-start(f32[160,128]{1,0:T(8,128)S(1)} %get-tuple-element.66), channel_id=1, source_target_pairs={{0,6},{1,7},{2,4},{3,5},{4,2},{5,3},{6,0},{7,1},{8,14},{9,15},{10,... | collective-permute-start | bytes 245768 | tf_op jit(solution)/shard_map/ppermute | solution.py:347
  78.3 9.5 %collective-permute-start.8 = (f32[160,128]{1,0:T(8,128)S(1)}, f32[160,128]{1,0:T(8,128)S(1)}, u32[]{:S(2)}, u32[]{:S(2)}) collective-permute-start(f32[160,128]{1,0:T(8,128)S(1)} %get-tuple-element.67), channel_id=1, source_target_pairs={{0,4},{1,5},{2,6},{3,7},{4,0},{5,1},{6,2},{7,3},{8,12},{9,13},{10,... | collective-permute-start | bytes 245768 | tf_op jit(solution)/shard_map/ppermute | solution.py:347
  81.2 16.9 %collective-permute-start.24 = (f32[4,160,128]{2,1,0:T(8,128)S(1)}, f32[4,160,128]{2,1,0:T(8,128)S(1)}, u32[]{:S(2)}, u32[]{:S(2)}) collective-permute-start(f32[4,160,128]{2,1,0:T(8,128)S(1)} %pad_maximum_fusion.1), channel_id=1, source_target_pairs={{0,1},{1,0},{2,3},{3,2},{4,5},{5,4},{6,7},{7,6},{8,9},{9,8},{10,11... | collective-permute-start | bytes 983048 | tf_op jit(solution)/shard_map/ppermute | solution.py:352
  87.8 7.2 %collective-permute-start.12 = (f32[160,128]{1,0:T(8,128)S(1)}, f32[160,128]{1,0:T(8,128)S(1)}, u32[]{:S(2)}, u32[]{:S(2)}) collective-permute-start(f32[160,128]{1,0:T(8,128)S(1)} %fusion.5.refs_0_), channel_id=1, source_target_pairs={{0,6},{1,7},{2,4},{3,5},{4,2},{5,3},{6,0},{7,1},{8,14},{9,15},{10,... | collective-permute-start | bytes 245768 | tf_op jit(solution)/shard_map/ppermute | solution.py:350
  89.8 7.8 %collective-permute-start.11 = (f32[160,128]{1,0:T(8,128)S(1)}, f32[160,128]{1,0:T(8,128)S(1)}, u32[]{:S(2)}, u32[]{:S(2)}) collective-permute-start(f32[160,128]{1,0:T(8,128)S(1)} %fusion.5.refs_0_), channel_id=1, source_target_pairs={{0,4},{1,5},{2,6},{3,7},{4,0},{5,1},{6,2},{7,3},{8,12},{9,13},{10,... | collective-permute-start | bytes 245768 | tf_op jit(solution)/shard_map/ppermute | solution.py:350
  89.8 7.8 %collective-permute-start.10 = (f32[160,128]{1,0:T(8,128)S(1)}, f32[160,128]{1,0:T(8,128)S(1)}, u32[]{:S(2)}, u32[]{:S(2)}) collective-permute-start(f32[160,128]{1,0:T(8,128)S(1)} %fusion.5.refs_0_), channel_id=1, source_target_pairs={{0,2},{1,3},{2,0},{3,1},{4,6},{5,7},{6,4},{7,5},{8,10},{9,11},{10,... | collective-permute-start | bytes 245768 | tf_op jit(solution)/shard_map/ppermute | solution.py:350
  97.6 21.1 %collective-permute-start.13 = (f32[4,160,128]{2,1,0:T(8,128)S(1)}, f32[4,160,128]{2,1,0:T(8,128)S(1)}, u32[]{:S(2)}, u32[]{:S(2)}) collective-permute-start(f32[4,160,128]{2,1,0:T(8,128)S(1)} %pad_maximum_fusion), channel_id=1, source_target_pairs={{0,1},{1,0},{2,3},{3,2},{4,5},{5,4},{6,7},{7,6},{8,9},{9,8},{10,11... | collective-permute-start | bytes 983048 | tf_op jit(solution)/shard_map/ppermute | solution.py:352
  114.9 31.1 %collective-permute-start.25 = (bf16[512,512]{1,0:T(8,128)(2,1)S(1)}, bf16[512,512]{1,0:T(8,128)(2,1)S(1)}, u32[]{:S(2)}, u32[]{:S(2)}) collective-permute-start(bf16[512,512]{1,0:T(8,128)(2,1)S(1)} %apply.13), channel_id=1, source_target_pairs={{0,8},{8,0},{16,24},{24,16},{1,9},{9,1},{17,25},{25,17},{2,10},{10... | collective-permute-start | bytes 1572872 | tf_op jit(solution)/shard_map/ppermute | solution.py:357
  115.7 28.9 %collective-permute-start.26 = (bf16[512,512]{1,0:T(8,128)(2,1)S(1)}, bf16[512,512]{1,0:T(8,128)(2,1)S(1)}, u32[]{:S(2)}, u32[]{:S(2)}) collective-permute-start(bf16[512,512]{1,0:T(8,128)(2,1)S(1)} %apply.14), channel_id=1, source_target_pairs={{0,24},{8,16},{16,8},{24,0},{1,25},{9,17},{17,9},{25,1},{2,26},{10... | collective-permute-start | bytes 1572872 | tf_op jit(solution)/shard_map/ppermute | solution.py:357
  118.1 23.8 %collective-permute-start.27 = (bf16[512,512]{1,0:T(8,128)(2,1)S(1)}, bf16[512,512]{1,0:T(8,128)(2,1)S(1)}, u32[]{:S(2)}, u32[]{:S(2)}) collective-permute-start(bf16[512,512]{1,0:T(8,128)(2,1)S(1)} %apply.15), channel_id=1, source_target_pairs={{0,16},{8,24},{16,0},{24,8},{1,17},{9,25},{17,1},{25,9},{2,18},{10... | collective-permute-start | bytes 1572872 | tf_op jit(solution)/shard_map/ppermute | solution.py:357
  135.2 17.9 %collective-permute-start.16 = (bf16[512,512]{1,0:T(8,128)(2,1)S(1)}, bf16[512,512]{1,0:T(8,128)(2,1)S(1)}, u32[]{:S(2)}, u32[]{:S(2)}) collective-permute-start(bf16[512,512]{1,0:T(8,128)(2,1)S(1)} %apply.11), channel_id=1, source_target_pairs={{0,16},{8,24},{16,0},{24,8},{1,17},{9,25},{17,1},{25,9},{2,18},{10... | collective-permute-start | bytes 1572872 | tf_op jit(solution)/shard_map/ppermute | solution.py:357
  138.2 24.9 %collective-permute-start.15 = (bf16[512,512]{1,0:T(8,128)(2,1)S(1)}, bf16[512,512]{1,0:T(8,128)(2,1)S(1)}, u32[]{:S(2)}, u32[]{:S(2)}) collective-permute-start(bf16[512,512]{1,0:T(8,128)(2,1)S(1)} %apply.10), channel_id=1, source_target_pairs={{0,24},{8,16},{16,8},{24,0},{1,25},{9,17},{17,9},{25,1},{2,26},{10... | collective-permute-start | bytes 1572872 | tf_op jit(solution)/shard_map/ppermute | solution.py:357
  141.8 22.6 %collective-permute-start.14 = (bf16[512,512]{1,0:T(8,128)(2,1)S(1)}, bf16[512,512]{1,0:T(8,128)(2,1)S(1)}, u32[]{:S(2)}, u32[]{:S(2)}) collective-permute-start(bf16[512,512]{1,0:T(8,128)(2,1)S(1)} %apply.9), channel_id=1, source_target_pairs={{0,8},{8,0},{16,24},{24,16},{1,9},{9,1},{17,25},{25,17},{2,10},{10... | collective-permute-start | bytes 1572872 | tf_op jit(solution)/shard_map/ppermute | solution.py:357

commit v3 on v0

v3 whole, which is shorter than its diff:
```python
import functools
import math

import jax
import jax.numpy as jnp
from jax import lax
from jax.experimental import pallas as pl
from jax.experimental.pallas import tpu as pltpu
from jax.sharding import PartitionSpec as P

LONG = 16384
RANK = 512
ITERS = 5
TILE = 128

quintic = (3.4445, -4.775, 2.0315)
momentum_decay = 0.95
epsilon = 1e-07

BLOCKS = [(i, j) for i in range(RANK // TILE) for j in range(i, RANK // TILE)]
PACKED = len(BLOCKS) * TILE
TAIL = 16

f32, bf16 = jnp.float32, jnp.bfloat16


def in_hbm(x):
    return pltpu.with_memory_space_constraint(x, pltpu.HBM)


def matrix_of(place, count, slots, slot, d):
    wanted = slots * jnp.bitwise_xor(place[count], d) + slot
    found = jnp.int32(0)
    for m in range(1, count):
        found = found + jnp.where(place[m] == wanted, m, 0)
    return found


def group_index(place):
    return place[place.shape[0] - 1]


def partners(size, step):
    return [(i, i ^ step) for i in range(size)]


def blend_kernel(shares, buffers, has_sum, *refs):
    refs = list(refs)
    place = refs.pop(0)
    gradient, momentum = refs.pop(0), refs.pop(0)
    del refs[:buffers]
    before = refs.pop(0) if has_sum else None
    renewed, rows, total, held = refs
    step = pl.program_id(0)

    @pl.when(step == 0)
    def _():
        held[...] = before[...] if has_sum else jnp.zeros_like(held)

    g = gradient[...].astype(f32)
    m = momentum_decay * momentum[...] + g
    renewed[...] = m
    x = (g + momentum_decay * m).astype(bf16)
    rows[...] = x
    half = RANK // 2
    dims = (((0,), (0,)), ((), ()))
    upper = lax.dot_general(x[:, :half], x, dims, preferred_element_type=f32)
    lower = lax.dot_general(x[:, half:], x[:, half:], dims, preferred_element_type=f32)
    for n, (i, j) in enumerate(BLOCKS):
        part, i0, j0 = (upper, i, j) if i < half // TILE else (lower, i - half // TILE, j - half // TILE)
        held[n * TILE : (n + 1) * TILE, :] += part[
            i0 * TILE : (i0 + 1) * TILE, j0 * TILE : (j0 + 1) * TILE
        ]

    @pl.when(step == pl.num_programs(0) - 1)
    def _():
        if shares is None:
            total[...] = held[...]
        else:
            near, far = shares
            count = PACKED // (near * far)
            for e1 in range(near):
                for e2 in range(far):
                    who = jnp.bitwise_xor(group_index(place), e2 * near + e1)
                    start = pl.multiple_of(who * count, 8)
                    total[e1, e2] = held[pl.ds(start, count), :]


class Line:
    def __init__(self, place):
        self.place, self.last, self.due, self.waiting, self.passed = place, None, [], {}, {}

    def run(
        self,
        kernel,
        operands,
        specs,
        out_shape,
        out_specs,
        *,
        name,
        work,
        token=0,
        grid=(1,),
        scratch=(),
        aliases=None,
        vmem=8,
    ):
        before = [] if self.last is None or (token is None and out_shape) else [self.last]
        before += self.due
        keys = list(self.waiting)
        before += [self.waiting[key] for key in keys]
        skip, given, results = len(before), len(before) + len(operands), len(out_shape)
        aliases = {1 + skip + i: o for i, o in (aliases or {}).items()}
        for k in range(len(keys)):
            aliases[1 + skip - len(keys) + k] = results + k

        def body(place, *refs):
            kernel(place, *refs[skip : given + results], *refs[given + results + len(keys) :])

        any_spec = pl.BlockSpec(memory_space=pl.ANY)
        flops, moved = work
        outs = pl.pallas_call(
            body,
            grid_spec=pltpu.PrefetchScalarGridSpec(
                num_scalar_prefetch=1,
                grid=grid,
                in_specs=[any_spec] * skip + specs,
                out_specs=out_specs + [any_spec] * len(keys),
                scratch_shapes=list(scratch),
            ),
            out_shape=out_shape
            + [jax.ShapeDtypeStruct(self.waiting[key].shape, self.waiting[key].dtype) for key in keys],
            input_output_aliases=aliases,
            compiler_params=pltpu.CompilerParams(vmem_limit_bytes=vmem * 2**20),
            cost_estimate=pl.CostEstimate(flops=20 * flops, bytes_accessed=20 * moved, transcendentals=0),
            name=name,
        )(self.place, *before, *operands)
        if token is not None:
            self.last = outs[token]
        elif not out_shape:
            self.last = outs[0]
        self.due, self.waiting = [], {}
        self.passed.update(zip(keys, outs[results:]))
        return outs[:results]


IN_VMEM = pl.BlockSpec(memory_space=pltpu.VMEM)
IN_HBM = pl.BlockSpec(memory_space=pltpu.HBM)


def pick_kernel(slots, count, wanted, place, gradients, *refs):
    targets, sems = refs[:-1], refs[-1]
    copies = []
    for n, (slot, d) in enumerate(wanted):
        source = gradients.at[matrix_of(place, count, slots, slot, d)]
        copies.append(pltpu.make_async_copy(source, targets[n], sems.at[n]))
        copies[-1].start()
    for copy in copies:
        copy.wait()


def pick(line, gradients, slots, wanted):
    count, rows, _ = gradients.shape
    return line.run(
        functools.partial(pick_kernel, slots, count, wanted),
        [in_hbm(gradients)],
        [IN_HBM],
        [jax.ShapeDtypeStruct((rows, RANK), bf16) for _ in wanted],
        [IN_VMEM for _ in wanted],
        name="pick",
        scratch=[pltpu.SemaphoreType.DMA((len(wanted),))],
        work=(0, 4 * len(wanted) * rows * RANK),
    )


def blend(line, gradient, momentum, slot, d, count, buffer, pair, before, shares):
    slots = momentum.shape[0]
    piece_rows = gradient.shape[-2]
    tile = min(256, piece_rows)
    steps = piece_rows // tile
    if d == 0:
        gradient_spec = pl.BlockSpec(
            (None, tile, RANK), lambda i, p: (matrix_of(p, count, slots, slot, 0), i, 0)
        )
        gradient = in_hbm(gradient)
    else:
        gradient_spec = pl.BlockSpec((tile, RANK), lambda i, p: (i, 0))
    momentum_spec = pl.BlockSpec(
        (None, tile, RANK), lambda i, p: (slot, jnp.bitwise_xor(p[count], d) * steps + i, 0)
    )
    in_specs, operands = [gradient_spec, momentum_spec], [gradient, in_hbm(momentum)]
    aliases = {}
    for result, array in enumerate((buffer, pair)):
        if array is not None:
            aliases[len(operands)] = result
            in_specs.append(IN_HBM if result == 0 else pl.BlockSpec(memory_space=pl.ANY))
            operands.append(in_hbm(array) if result == 0 else array)
    if d < 2:
        rows_shape, rows_spec = (piece_rows, RANK), pl.BlockSpec((tile, RANK), lambda i, p: (i, 0))
    else:
        rows_shape = (2, piece_rows, RANK)
        rows_spec = pl.BlockSpec((None, tile, RANK), lambda i, p: (d % 2, i, 0))
    if before is not None:
        in_specs.append(pl.BlockSpec((PACKED, TILE), lambda i, p: (0, 0)))
        operands.append(before)
    if shares is None:
        total = (PACKED, TILE)
    else:
        total = (*shares, PACKED // (shares[0] * shares[1]), TILE)
    return line.run(
        functools.partial(blend_kernel, shares, len(aliases), before is not None),
        operands,
        in_specs,
        [
            pltpu.HBM(momentum.shape, f32),
            jax.ShapeDtypeStruct(rows_shape, bf16),
            jax.ShapeDtypeStruct(total, f32),
        ],
        [
            momentum_spec,
            rows_spec,
            pl.BlockSpec(total, lambda i, p: (0,) * len(total)),
        ],
        name="blend",
        token=2,
        grid=(steps,),
        scratch=[pltpu.VMEM((PACKED, TILE), f32)],
        aliases=aliases,
        vmem=12,
        work=(2 * piece_rows * RANK * RANK, piece_rows * RANK * 12),
    )


def add_near_kernel(place, share, *refs):
    far = share.shape[1]
    received, targets = refs[: len(refs) - far], refs[len(refs) - far :]
    for e2, target in enumerate(targets):
        total = share[0, e2]
        for other in received:
            total = total + other[e2]
        target[...] = total


def add_near(line, share, received):
    _, far, count, _ = share.shape
    return line.run(
        add_near_kernel,
        [share, *received],
        [IN_VMEM] * (1 + len(received)),
        [jax.ShapeDtypeStruct((count, TILE), f32)] * far,
        [IN_VMEM] * far,
        name="add_near",
        work=(0, 12 * far * count * TILE),
    )


def add_far_kernel(place, *refs):
    total = refs[0][...]
    for other in refs[1:-1]:
        total = total + other[...]
    refs[-1][...] = total


def add_far(line, parts):
    return line.run(
        add_far_kernel,
        list(parts),
        [IN_VMEM] * len(parts),
        [jax.ShapeDtypeStruct(parts[0].shape, f32)],
        [IN_VMEM],
        name="add_far",
        work=(0, 4 * (len(parts) + 1) * parts[0].size),
    )[0]


def step(line, array):
    line.waiting["step"] = array
    line.run(lambda place: None, [], [], [], [], name="step", token=None, work=(0, 0))
    return line.passed["step"]


def stack_kernel(place, *refs):
    for e, part in enumerate(refs[:-1]):
        refs[-1][e] = part[...]


def stack(line, parts):
    return line.run(
        stack_kernel,
        list(parts),
        [IN_VMEM] * len(parts),
        [jax.ShapeDtypeStruct((len(parts), *parts[0].shape), f32)],
        [IN_VMEM],
        name="stack",
        work=(0, 8 * len(parts) * parts[0].size),
    )[0]


SHIFTS = (0.0, 0.0, 0.1, 0.6, 0.85)
PASSES = (1, 1, 3, 1, 1)
HALF = RANK // 2


def dot(a, b):
    return jnp.dot(a, b, preferred_element_type=f32)


def whole(x):
    top, corner = x
    return jnp.concatenate([top, jnp.concatenate([top[:, HALF:].T, corner], axis=1)], axis=0)


def operand(x, passes):
    high = tuple(part.astype(bf16) for part in x)
    if passes == 1:
        return (whole(high),)
    low = tuple((part - rounded.astype(f32)).astype(bf16) for part, rounded in zip(x, high))
    return (whole(high), whole(low))


def product(a, b):
    top, corner = dot(a[0][:HALF], b[0]), dot(a[0][HALF:], b[0][:, HALF:])
    if len(a) > 1:
        top += dot(a[0][:HALF], b[1]) + dot(a[1][:HALF], b[0])
        corner += dot(a[0][HALF:], b[1][:, HALF:]) + dot(a[1][HALF:], b[0][:, HALF:])
    return (top, corner)


def combine(*terms):
    return tuple(
        functools.reduce(lambda x, y: x + y, [w * x[part] for w, x in terms]) for part in range(2)
    )


def add_identity(x, value):
    top, corner = x
    row = lax.broadcasted_iota(jnp.int32, (HALF, HALF), 0)
    column = lax.broadcasted_iota(jnp.int32, (HALF, HALF), 1)
    eye = jnp.where(row == column, value, 0.0)
    return (jnp.concatenate([top[:, :HALF] + eye, top[:, HALF:]], axis=1), corner + eye)


def polynomial_kernel(near, far, count, place, *refs):
    *shared, result, packed = refs
    for e1, other in enumerate(shared):
        for e2 in range(far):
            who = jnp.bitwise_xor(group_index(place), e2 * near + e1)
            packed[pl.ds(pl.multiple_of(who * count, 8), count), :] = other[e2]
    parts = {}
    trace = jnp.zeros((), f32)
    row = lax.broadcasted_iota(jnp.int32, (TILE, TILE), 0)
    column = lax.broadcasted_iota(jnp.int32, (TILE, TILE), 1)
    for n, (i, j) in enumerate(BLOCKS):
        block = packed[n * TILE : (n + 1) * TILE, :]
        parts[i, j] = block
        if i == j:
            trace = trace + jnp.sum(jnp.where(row == column, block, 0.0))
    for i, j in ((0, 1), (2, 3)):
        parts[j, i] = parts[i, j].T

    def rows_of(count, first):
        return jnp.concatenate(
            [
                jnp.concatenate([parts[i, j] for j in range(first, RANK // TILE)], axis=1)
                for i in range(first, first + count)
            ],
            axis=0,
        )

    half = HALF // TILE
    scale = 1.0 / (jnp.sqrt(jnp.full((1, 1), trace, f32)) + epsilon)
    rest = tuple((x * scale) * scale for x in (rows_of(half, 0), rows_of(half, half)))
    a, b, c = quintic
    poly = None
    for k in range(ITERS):
        shift = SHIFTS[k]
        gain = a + b * shift + c * shift * shift
        d = operand(rest, PASSES[k])
        step = combine((b + 2 * c * shift, rest), (c, product(d, d)))
        s = operand(step, PASSES[k])
        if poly is None:
            poly = add_identity(step, gain)
        else:
            poly = combine((gain, poly), (1.0, product(operand(poly, PASSES[k]), s)))
        if k < ITERS - 1:
            middle = combine((gain, rest), (shift, step), (1.0, product(d, s)))
            turned = product(operand(middle, PASSES[k]), s)
            rest = combine((gain, middle), (gain * shift, step), (1.0, turned))
            rest = add_identity(rest, gain * gain * shift - SHIFTS[k + 1])
    top, corner = tuple(x * (scale * math.sqrt(max(LONG, RANK))) for x in poly)
    for n, (i, j) in enumerate(BLOCKS):
        part, i0, j0 = (top, i, j) if i < half else (corner, i - half, j - half)
        block = part[i0 * TILE : (i0 + 1) * TILE, j0 * TILE : (j0 + 1) * TILE]
        high = block.astype(bf16)
        result[n * TILE : (n + 1) * TILE, :] = high
        if i == j:
            low = jnp.where(row == column, block - high.astype(f32), 0.0)
            result[PACKED + i * TAIL : PACKED + (i + 1) * TAIL, :] = jnp.broadcast_to(
                jnp.sum(low, axis=0, keepdims=True), (TAIL, TILE)
            ).astype(bf16)


def polynomial(line, shared):
    near, (far, count, _) = len(shared), shared[0].shape
    return line.run(
        functools.partial(polynomial_kernel, near, far, count),
        list(shared),
        [IN_VMEM] * near,
        [jax.ShapeDtypeStruct((PACKED + RANK // TILE * TAIL, TILE), bf16)],
        [IN_VMEM],
        name="polynomial",
        scratch=[pltpu.VMEM((PACKED, TILE), f32)],
        vmem=20,
        work=(20 * 2 * RANK**3, 2 * 2**20),
    )[0]


def finish_kernel(slots, slot, steps, matrices, picks, place, *refs):
    refs = list(refs)
    count = len(steps)
    pieces, polys = refs[:count], refs[count : 2 * count]
    updates, _, held, sems = refs[-4:]
    copies = []
    for n, d in enumerate(steps):
        parts = {}
        for k, (i, j) in enumerate(BLOCKS):
            parts[i, j] = polys[n][k * TILE : (k + 1) * TILE, :]
            if i != j:
                parts[j, i] = parts[i, j].T
        sides = range(RANK // TILE)
        poly = jnp.concatenate(
            [jnp.concatenate([parts[i, j] for j in sides], axis=1) for i in sides], axis=0
        )
        low = jnp.concatenate(
            [polys[n][PACKED + i * TAIL : PACKED + (i + 1) * TAIL, :][:1] for i in sides], axis=1
        )
        x = pieces[n][...] if picks[n] is None else pieces[n][picks[n]]
        held[n] = (dot(x, poly) + x.astype(f32) * low.astype(f32)).astype(bf16)
        target = updates.at[matrix_of(place, matrices, slots, slot, d)]
        copies.append(pltpu.make_async_copy(held.at[n], target, sems.at[n]))
        copies[-1].start()
    for copy in copies:
        copy.wait()


def finish(line, slots, slot, steps, pieces, polys, shape, buffer):
    operands = [piece for piece, _ in pieces] + list(polys)
    specs = [IN_VMEM] * len(operands)
    aliases = {}
    if buffer is not None:
        aliases = {len(operands): 0}
        operands.append(in_hbm(buffer))
        specs.append(IN_HBM)
    return line.run(
        functools.partial(finish_kernel, slots, slot, steps, shape[0], [index for _, index in pieces]),
        operands,
        specs,
        [pltpu.HBM(shape, bf16), jax.ShapeDtypeStruct((8, TILE), f32)],
        [IN_HBM, IN_VMEM],
        name="finish",
        token=1,
        scratch=[pltpu.VMEM((len(steps), shape[1], RANK), bf16), pltpu.SemaphoreType.DMA((len(steps),))],
        aliases=aliases,
        vmem=12,
        work=(2 * len(steps) * shape[1] * RANK * RANK, 4 * len(steps) * shape[1] * RANK),
    )[0]


def on_device(gradients, momentum, slot_table, *, owners, group):
    matrix_count = gradients.shape[0]
    held_slots = momentum.shape[0]
    near = 1 << ((group.bit_length() - 1) // 2)
    shares = (near, group // near)
    place = jnp.concatenate(
        [
            slot_table.astype(jnp.int32),
            jnp.stack([lax.axis_index("owner"), lax.axis_index("fsdp")]).astype(jnp.int32),
        ]
    )

    line = Line(place)
    all_slots = range(held_slots)
    far_steps, near_steps = list(range(2, owners)), list(range(1, min(2, owners)))
    arrived = {}
    wanted = [(0, d) for d in far_steps] + [(slot, d) for slot in all_slots for d in near_steps]
    wanted += [(slot, d) for slot in range(1, held_slots) for d in far_steps]
    picked = {}
    for few in (wanted[:1], wanted[1:]):
        picked.update(zip(few, pick(line, gradients, held_slots, few)))

    def send(pieces):
        for slot, d in pieces:
            arrived[slot, d] = lax.ppermute(picked[slot, d], "owner", partners(owners, d))

    renewed, rows, returned, sums, lines, mine, gathered, polys = None, {}, {}, {}, {}, {}, {}, {}

    def blend_piece(slot, d, then=()):
        nonlocal renewed
        line.waiting.update({piece: picked[piece] for piece in then})
        renewed, rows[slot, d], sums[slot] = blend(
            line,
            arrived[slot, d] if d else gradients,
            momentum,
            slot,
            d,
            matrix_count,
            renewed,
            rows[slot, d - 1] if d > 1 and d % 2 else None,
            sums.get(slot),
            shares if d == owners - 1 else None,
        )
        picked.update({piece: line.passed[piece] for piece in then})
        send(then)

    def send_back(slot, d):
        if d == 0:
            returned[slot, 0] = rows[slot, 0], None
        elif d == 1:
            returned[slot, 1] = lax.ppermute(rows[slot, 1], "owner", partners(owners, 1)), None
        else:
            pair = lax.ppermute(rows[slot, d + 1], "owner", partners(owners, d))
            returned[slot, d] = pair, 0
            returned[slot, d + 1] = lax.ppermute(pair, "owner", partners(owners, 1)), 1

    def across_near(x, e1):
        return lax.ppermute(x, "fsdp", partners(group, e1))

    def across_far(x, e2):
        return lax.ppermute(x, "fsdp", partners(group, e2 * near))

    def first_sum(slot):
        received = [across_near(sums[slot][e1], e1) for e1 in range(1, near)]
        lines[slot] = add_near(line, sums[slot], received)

    def second_sum(slot):
        parts = lines[slot]
        received = [across_far(parts[e2], e2) for e2 in range(1, shares[1])]
        mine[slot] = add_far(line, [parts[0], *received])

    def collect(slot):
        part = mine[slot]
        whole_line = stack(line, [part] + [across_far(part, e2) for e2 in range(1, shares[1])])
        gathered[slot] = [whole_line] + [across_near(whole_line, e1) for e1 in range(1, near)]

    def make_polynomial(slot):
        polys[slot, 0] = polynomial(line, gathered[slot])
        for d in far_steps[::2]:
            polys[slot, d] = lax.ppermute(polys[slot, 0], "owner", partners(owners, d))
        for d in near_steps:
            polys[slot, d] = lax.ppermute(polys[slot, 0], "owner", partners(owners, d))

    def pass_polynomials(slot):
        for d in far_steps[::2]:
            polys[slot, d] = step(line, polys[slot, d])
            polys[slot, d + 1] = lax.ppermute(polys[slot, d], "owner", partners(owners, 1))

    updates = None

    def finish_steps(slot, steps):
        nonlocal updates
        updates = finish(
            line,
            held_slots,
            slot,
            steps,
            [returned[slot, d] for d in steps],
            [polys[slot, d] for d in steps],
            gradients.shape,
            updates,
        )

    def expect(*wanted):
        line.due += [returned[slot, d][0] for slot, d in wanted if d < owners]

    far_pieces = [(slot, d) for slot in all_slots for d in far_steps]
    near_pieces = [(slot, d) for slot in all_slots for d in near_steps]
    send(far_pieces[:2] + near_pieces[:1])
    blend_piece(0, 0, far_pieces[2:] + near_pieces[1:])
    blend_piece(1, 0)
    for slot in all_slots:
        send_back(slot, 0)
    for d in near_steps:
        for slot in all_slots:
            blend_piece(slot, d)
            send_back(slot, d)
    for d in far_steps[:-1]:
        blend_piece(0, d)
    expect((0, 1))
    for d in far_steps[-1:]:
        blend_piece(0, d)
    expect((1, 1))
    for d in far_steps[:-1]:
        blend_piece(1, d)
    for d in far_steps[1::2]:
        line.waiting[d] = rows[0, d]
    first_sum(0)
    for d in far_steps[1::2]:
        rows[0, d] = line.passed[d]
        send_back(0, d - 1)
    for d in far_steps[-1:]:
        blend_piece(1, d)
    line.waiting["sum"] = sums[1]
    second_sum(0)
    sums[1] = line.passed["sum"]
    first_sum(1)
    collect(0)
    expect(*[(0, d) for d in far_steps[::2]])
    for d in far_steps[1::2]:
        rows[1, d] = step(line, rows[1, d])
        send_back(1, d - 1)
    second_sum(1)
    collect(1)
    make_polynomial(0)
    make_polynomial(1)
    finish_steps(0, [0] + near_steps)
    pass_polynomials(0)
    finish_steps(1, [0] + near_steps)
    finish_steps(0, far_steps)
    pass_polynomials(1)
    for d in far_steps:
        finish_steps(1, [d])
    return (updates, renewed)


def solution(mesh):
    return jax.shard_map(
        functools.partial(on_device, owners=mesh.shape["owner"], group=mesh.shape["fsdp"]),
        mesh=mesh,
        in_specs=(P(None, ("fsdp", "owner"), None), P("owner", "fsdp", None), P()),
        out_specs=(P(None, ("fsdp", "owner"), None), P("owner", "fsdp", None)),
        check_vma=False,
    )
```

time: 656 us -> 132 us (0.20)
  waiting for transfers between devices: 433 us -> 32.3 us
  matrix products: 77.9 us -> 0 us
  blocking collectives: 74.1 us -> 0 us
  Pallas kernels: 0 us -> 63.1 us
  local copies, waits for them, and re-layouts: 29.9 us -> 0.11 us
  starting transfers between devices: 5.59 us -> 34.2 us
  other arithmetic: 20.7 us -> 0.73 us
  between operations: 13.9 us -> 1.08 us
    psum x5 -> x0, waiting for transfers between devices: 385 us -> none  [on_device(): gram_matrix = lax.psum(partial_value.astype(jnp.bfloat16), 'fsdp')]
    dot_general x10 -> x0, matrix products: 77.9 us -> none  [the longest x5 47.3 us: on_device(): jnp.einsum('snq,qsp->snp', panels, polynomial, preferred_element_type=jnp...]
    pallas_call x0 -> x26, Pallas kernels: none -> 63.1 us  [run(): pl.pallas_call(body, grid_spec=pltpu.PrefetchScalarGridSpec(num_scalar_pr...]
    all_to_all x1 -> x0, blocking collectives: 52.4 us -> none  [on_device(): lax.all_to_all(ordered, 'owner', split_axis=0, concat_axis=1, tiled=True)]
    all_to_all x1 -> x0, waiting for transfers between devices: 48.2 us -> none  [on_device(): lax.all_to_all(scaled, 'owner', split_axis=1, concat_axis=0, tiled=True)]
    ppermute x0 -> x34, starting transfers between devices: none -> 34.2 us  [the longest x12 18 us: across_far(): return lax.ppermute(x, 'fsdp', partners(group, e2 * near))]
    ppermute x0 -> x34, waiting for transfers between devices: none -> 32.3 us  [the longest x12 12.1 us: across_far(): return lax.ppermute(x, 'fsdp', partners(group, e2 * near))]
    psum x1 -> x0, blocking collectives: 21.7 us -> none  [on_device(): squares = lax.psum(jnp.sum(blended * blended, axis=(1, 2)), 'fsdp')]
  transfers between devices with their start and end apart: 6 -> 34, of which waited for: 6 -> 11; matrix products, arithmetic and copies ran while one was open for 0% -> 0% of each run, Pallas kernels for 0% -> 45%
where the time goes in v3:
time: 132 us
  Pallas kernels  63.1 us (48%)
  starting transfers between devices  34.2 us (26%)
  waiting for transfers between devices  32.3 us (24%)
    pallas_call x26, Pallas kernels, run(): pl.pallas_call(body, grid_spec=pltpu.PrefetchScalarGridSpec(num_scalar_pr...  63.1 us
    ppermute x12, starting transfers between devices, across_far(): return lax.ppermute(x, 'fsdp', partners(group, e2 * near))  18 us
    ppermute x12, waiting for transfers between devices, across_far(): return lax.ppermute(x, 'fsdp', partners(group, e2 * near))  12.1 us
    ppermute x6, waiting for transfers between devices, send(): lax.ppermute(picked[slot, d], 'owner', partners(owners, d))  9.56 us
    ppermute x4, waiting for transfers between devices, make_polynomial(): polys[slot, d] = lax.ppermute(polys[slot, 0], 'owner', partners(owners, d))  6.76 us
    ppermute x6, starting transfers between devices, send(): lax.ppermute(picked[slot, d], 'owner', partners(owners, d))  5.33 us
    ppermute x4, starting transfers between devices, across_near(): return lax.ppermute(x, 'fsdp', partners(group, e1))  5.02 us
    ppermute x4, waiting for transfers between devices, across_near(): return lax.ppermute(x, 'fsdp', partners(group, e1))  3.85 us
  transfers between devices with their start and end apart: 34, of which 11 were waited for; matrix products, arithmetic and copies ran while one was open for 0% of the time, Pallas kernels for 45%

profile of v3, /device:TPU:0, one launch (start us, length us, event | category | flops | bytes accessed | tf_op | source)
XLA Modules:
  0.0 131.6 jit_solution(672771499310014523)
XLA Ops:
  0.6 0.7 pad_add_fusion.place
  1.4 1.6 %pick.2.refs_0_ = bf16[512,512]{1,0:T(8,128)(2,1)S(1)} custom-call(s32[10]{0:T(128)S(1)} %pad_add_fusion.place, bf16[8,512,512]{2,1,0:T(8,128)(2,1)} %refs_1_.3), custom_call_target="tpu_custom_call" | custom-call | bytes 20971520 | tf_op jit(solution)/shard_map/pick/pallas_call | solution.py:123
  3.0 3.0 %collective-permute-start.2 = (bf16[512,512]{1,0:T(8,128)(2,1)S(1)}, bf16[512,512]{1,0:T(8,128)(2,1)S(1)}, u32[]{:S(2)}, u32[]{:S(2)}) collective-permute-start(bf16[512,512]{1,0:T(8,128)(2,1)S(1)} %pick.2.refs_0_), channel_id=1, source_target_pairs={{0,16},{8,24},{16,0},{24,8},{1,17},{9,25},{17,1},{25,9},{2,18},{10... | collective-permute-start | bytes 1572872 | tf_op jit(solution)/shard_map/ppermute | solution.py:494
  6.0 2.3 %pick.3 = (bf16[512,512]{1,0:T(8,128)(2,1)S(1)}, bf16[512,512]{1,0:T(8,128)(2,1)S(1)}, bf16[512,512]{1,0:T(8,128)(2,1)S(1)}, bf16[512,512]{1,0:T(8,128)(2,1)S(1)}, bf16[512,512]{1,0:T(8,128)(2,1)S(1)}) custom-call(s32[10]{0:T(128)S(1)} %pad_add_fusion.place, bf16[512,512]{1,0:T(8,128)(2,1)S(1)} %pick.2.refs_0_, bf16[8,512,512]{2,1,0:T(8,128)(2,1)} %refs_1_.3), custom_call_target="tpu_custom_call" | custom-call | bytes 104857600 | tf_op jit(solution)/shard_map/pick/pallas_call | solution.py:123
  8.3 0.1 collective-permute-start.4
  8.5 3.3 %blend.8 = (f32[2,2048,512]{2,1,0:T(8,128)}, bf16[512,512]{1,0:T(8,128)(2,1)S(1)}, f32[1280,128]{1,0:T(8,128)S(1)}, bf16[512,512]{1,0:T(8,128)(2,1)S(1)}, bf16[5...) custom-call(s32[10]{0:T(128)S(1)} %pad_add_fusion.place, ...), custom_call_target="tpu_custom_call", output_to_operand_aliasing={{3}: (2, {}), {4}: (3, {}), {5}: (4, {})} | custom-call | flops 5368709120 | bytes 62914560 | tf_op jit(solution)/shard_map/blend/pallas_call | solution.py:123
  11.8 0.4 collective-permute-start.1
  12.1 1.7 %collective-permute-start.6 = (bf16[512,512]{1,0:T(8,128)(2,1)S(1)}, bf16[512,512]{1,0:T(8,128)(2,1)S(1)}, u32[]{:S(2)}, u32[]{:S(2)}) collective-permute-start(bf16[512,512]{1,0:T(8,128)(2,1)S(1)} %get-tuple-element.74), channel_id=1, source_target_pairs={{0,16},{8,24},{16,0},{24,8},{1,17},{9,25},{17,1},{25,9},{2,18},{10... | collective-permute-start | bytes 1572872 | tf_op jit(solution)/shard_map/ppermute | solution.py:494
  13.8 3.3 %blend.9 = (f32[2,2048,512]{2,1,0:T(8,128)}, bf16[512,512]{1,0:T(8,128)(2,1)S(1)}, f32[1280,128]{1,0:T(8,128)S(1)}) custom-call(s32[10]{0:T(128)S(1)} %pad_add_fusion.place, f32[1280,128]{1,0:T(8,128)S(1)} %get-tuple-element.58.refs_0_.refs_4_, bf16[8,512,512]{2,1,0:T(8,128)(2,1)} %refs_1_.3, ...), custom_call_target="tpu_custom_call", output_to_operand_aliasing={{0}: (4, {})} | custom-call | flops 5368709120 | bytes 62914560 | tf_op jit(solution)/shard_map/blend/pallas_call | solution.py:123
  17.2 3.2 %blend.10 = (f32[2,2048,512]{2,1,0:T(8,128)}, bf16[512,512]{1,0:T(8,128)(2,1)S(1)}, f32[1280,128]{1,0:T(8,128)S(1)}) custom-call(s32[10]{0:T(128)S(1)} %pad_add_fusion.place, f32[1280,128]{1,0:T(8,128)S(1)} %get-tuple-element.60.refs_0_.refs_4_, bf16[512,512]{1,0:T(8,128)(2,1)S(1)} %collective-permute-done.refs_1_, ...), custom_call_target="tpu_custom_call", output_to_operand_aliasing={{0}: (4, {})} | custom-call | flops 5368709120 | bytes 62914560 | tf_op jit(solution)/shard_map/blend/pallas_call | solution.py:123
  20.4 0.4 collective-permute-start.3
  20.7 3.2 %blend.11 = (f32[2,2048,512]{2,1,0:T(8,128)}, bf16[512,512]{1,0:T(8,128)(2,1)S(1)}, f32[1280,128]{1,0:T(8,128)S(1)}) custom-call(s32[10]{0:T(128)S(1)} %pad_add_fusion.place, f32[1280,128]{1,0:T(8,128)S(1)} %get-tuple-element.63.refs_0_.refs_4_, bf16[512,512]{1,0:T(8,128)(2,1)S(1)} %collective-permute-done.1.refs_1_, ...), custom_call_target="tpu_custom_call", output_to_operand_aliasing={{0}: (4, {})} | custom-call | flops 5368709120 | bytes 62914560 | tf_op jit(solution)/shard_map/blend/pallas_call | solution.py:123
  23.9 0.1 collective-permute-start.5
  24.0 3.2 %blend.12 = (f32[2,2048,512]{2,1,0:T(8,128)}, bf16[2,512,512]{2,1,0:T(8,128)(2,1)S(1)}, f32[1280,128]{1,0:T(8,128)S(1)}) custom-call(s32[10]{0:T(128)S(1)} %pad_add_fusion.place, f32[1280,128]{1,0:T(8,128)S(1)} %get-tuple-element.66.refs_0_.refs_5_, bf16[512,512]{1,0:T(8,128)(2,1)S(1)} %collective-permute-done.2.refs_1_, ...), custom_call_target="tpu_custom_call", output_to_operand_aliasing={{0}: (4, {})} | custom-call | flops 5368709120 | bytes 62914560 | tf_op jit(solution)/shard_map/blend/pallas_call | solution.py:123
  27.2 2.3 %collective-permute-done.4.refs_2_ = bf16[512,512]{1,0:T(8,128)(2,1)S(1)} collective-permute-done((bf16[512,512]{1,0:T(8,128)(2,1)S(1)}, bf16[512,512]{1,0:T(8,128)(2,1)S(1)}, u32[]{:S(2)}, u32[]{:S(2)}) %collective-permute-start.4) | collective-permute-done | bytes 524320 | tf_op jit(solution)/shard_map/ppermute | solution.py:494
  29.5 3.2 %blend.13 = (f32[2,2048,512]{2,1,0:T(8,128)}, bf16[2,512,512]{2,1,0:T(8,128)(2,1)S(1)}, f32[2,4,160,128]{3,2,1,0:T(8,128)S(1)}) custom-call(s32[10]{0:T(128)S(1)} %pad_add_fusion.place, f32[1280,128]{1,0:T(8,128)S(1)} %get-tuple-element.68.refs_0_.refs_6_, ...), custom_call_target="tpu_custom_call", output_to_operand_aliasing={{0}: (5, {}), {1}: (6, {})} | custom-call | flops 5368709120 | bytes 62914560 | tf_op jit(solution)/shard_map/blend/pallas_call | solution.py:123
  32.8 1.6 %collective-permute-start.7 = (f32[4,160,128]{2,1,0:T(8,128)S(1)}, f32[4,160,128]{2,1,0:T(8,128)S(1)}, u32[]{:S(2)}, u32[]{:S(2)}) collective-permute-start(f32[4,160,128]{2,1,0:T(8,128)S(1)} %slice_bitcast_fusion.1), channel_id=1, source_target_pairs={{0,1},{1,0},{2,3},{3,2},{4,5},{5,4},{6,7},{7,6},{8,9},{9,8},{10,11... | collective-permute-start | bytes 983048 | tf_op jit(solution)/shard_map/ppermute | solution.py:527
  34.4 6.8 %collective-permute-done.6.refs_2_ = bf16[512,512]{1,0:T(8,128)(2,1)S(1)} collective-permute-done((bf16[512,512]{1,0:T(8,128)(2,1)S(1)}, bf16[512,512]{1,0:T(8,128)(2,1)S(1)}, u32[]{:S(2)}, u32[]{:S(2)}) %collective-permute-start.6) | collective-permute-done | bytes 524320 | tf_op jit(solution)/shard_map/ppermute | solution.py:494
  41.2 3.3 %blend.14 = (f32[2,2048,512]{2,1,0:T(8,128)}, bf16[2,512,512]{2,1,0:T(8,128)(2,1)}, f32[1280,128]{1,0:T(8,128)S(1)}) custom-call(s32[10]{0:T(128)S(1)} %pad_add_fusion.place, f32[2,4,160,128]{3,2,1,0:T(8,128)S(1)} %get-tuple-element.72.refs_0_.refs_2_, bf16[512,512]{1,0:T(8,128)(2,1)S(1)} %collective-permute-done.5.refs_1_.refs_2_, ...), custom_call_target="tpu_custom_call", output_to_operand_aliasing={{0}: (5, {})} | custom-call | flops 5368709120 | bytes 62914560 | tf_op jit(solution)/shard_map/blend/pallas_call | solution.py:123
  44.5 0.6 add_near.2
  45.1 2.2 %collective-permute-start.9 = (f32[160,128]{1,0:T(8,128)S(1)}, f32[160,128]{1,0:T(8,128)S(1)}, u32[]{:S(2)}, u32[]{:S(2)}) collective-permute-start(f32[160,128]{1,0:T(8,128)S(1)} %get-tuple-element.83), channel_id=1, source_target_pairs={{0,2},{1,3},{2,0},{3,1},{4,6},{5,7},{6,4},{7,5},{8,10},{9,11},{10,... | collective-permute-start | bytes 245768 | tf_op jit(solution)/shard_map/ppermute | solution.py:530
  47.3 2.6 %collective-permute-start.10 = (f32[160,128]{1,0:T(8,128)S(1)}, f32[160,128]{1,0:T(8,128)S(1)}, u32[]{:S(2)}, u32[]{:S(2)}) collective-permute-start(f32[160,128]{1,0:T(8,128)S(1)} %get-tuple-element.84), channel_id=1, source_target_pairs={{0,4},{1,5},{2,6},{3,7},{4,0},{5,1},{6,2},{7,3},{8,12},{9,13},{10,... | collective-permute-start | bytes 245768 | tf_op jit(solution)/shard_map/ppermute | solution.py:530
  49.9 1.7 %collective-permute-start.16 = (bf16[2,512,512]{2,1,0:T(8,128)(2,1)S(1)}, bf16[2,512,512]{2,1,0:T(8,128)(2,1)}, u32[]{:S(2)}, u32[]{:S(2)}) collective-permute-start(bf16[2,512,512]{2,1,0:T(8,128)(2,1)S(1)} %get-tuple-element.89), channel_id=1, source_target_pairs={{0,16},{8,24},{16,0},{24,8},{1,17},{9,25},{17,1},{25,9},{2,18},{10... | collective-permute-start | bytes 3145736 | tf_op jit(solution)/shard_map/ppermute | solution.py:522
  51.6 0.4 collective-permute-done.8.refs_1_
  52.0 3.3 %blend.15 = (f32[2,2048,512]{2,1,0:T(8,128)}, bf16[2,512,512]{2,1,0:T(8,128)(2,1)}, f32[2,4,160,128]{3,2,1,0:T(8,128)S(1)}) custom-call(s32[10]{0:T(128)S(1)} %pad_add_fusion.place, f32[160,128]{1,0:T(8,128)S(1)} %get-tuple-element.78.refs_0_.refs_2_, ...), custom_call_target="tpu_custom_call", output_to_operand_aliasing={{0}: (4, {}), {1}: (5, {})} | custom-call | flops 5368709120 | bytes 62914560 | tf_op jit(solution)/shard_map/blend/pallas_call | solution.py:123
  55.4 0.7 collective-permute-done.11.refs_5_
  56.2 0.6 add_far.2
  56.8 1.6 %collective-permute-start.12 = (f32[4,160,128]{2,1,0:T(8,128)S(1)}, f32[4,160,128]{2,1,0:T(8,128)S(1)}, u32[]{:S(2)}, u32[]{:S(2)}) collective-permute-start(f32[4,160,128]{2,1,0:T(8,128)S(1)} %slice_bitcast_fusion), channel_id=1, source_target_pairs={{0,1},{1,0},{2,3},{3,2},{4,5},{5,4},{6,7},{7,6},{8,9},{9,8},{10,11... | collective-permute-start | bytes 983048 | tf_op jit(solution)/shard_map/ppermute | solution.py:527
  58.4 2.9 %collective-permute-start.15 = (f32[160,128]{1,0:T(8,128)S(1)}, f32[160,128]{1,0:T(8,128)S(1)}, u32[]{:S(2)}, u32[]{:S(2)}) collective-permute-start(f32[160,128]{1,0:T(8,128)S(1)} %get-tuple-element.86.refs_0_.refs_1_), channel_id=1, source_target_pairs={{0,6},{1,7},{2,4},{3,5},{4,2},{5,3},{6,0},{7,1},{8,14},{9,15},{10,... | collective-permute-start | bytes 245768 | tf_op jit(solution)/shard_map/ppermute | solution.py:530
  61.2 1.5 %collective-permute-start.13 = (f32[160,128]{1,0:T(8,128)S(1)}, f32[160,128]{1,0:T(8,128)S(1)}, u32[]{:S(2)}, u32[]{:S(2)}) collective-permute-start(f32[160,128]{1,0:T(8,128)S(1)} %get-tuple-element.86.refs_0_.refs_1_), channel_id=1, source_target_pairs={{0,2},{1,3},{2,0},{3,1},{4,6},{5,7},{6,4},{7,5},{8,10},{9,11},{10,... | collective-permute-start | bytes 245768 | tf_op jit(solution)/shard_map/ppermute | solution.py:530
  62.8 3.8 %collective-permute-done.12.refs_2_ = f32[4,160,128]{2,1,0:T(8,128)S(1)} collective-permute-done((f32[4,160,128]{2,1,0:T(8,128)S(1)}, f32[4,160,128]{2,1,0:T(8,128)S(1)}, u32[]{:S(2)}, u32[]{:S(2)}) %collective-permute-start.12) | collective-permute-done | bytes 327712 | tf_op jit(solution)/shard_map/ppermute | solution.py:527
  66.6 0.6 add_near.3
  67.2 1.8 %collective-permute-done.14.refs_3_ = f32[160,128]{1,0:T(8,128)S(1)} collective-permute-done((f32[160,128]{1,0:T(8,128)S(1)}, f32[160,128]{1,0:T(8,128)S(1)}, u32[]{:S(2)}, u32[]{:S(2)}) %collective-permute-start.14) | collective-permute-done | bytes 81952 | tf_op jit(solution)/shard_map/ppermute | solution.py:530
  69.0 0.6 stack.10.refs_0_.refs_1_
  69.6 0.6 collective-permute-start.23
  70.2 0.9 collective-permute-start.17
  71.1 2.4 %collective-permute-start.18 = (f32[160,128]{1,0:T(8,128)S(1)}, f32[160,128]{1,0:T(8,128)S(1)}, u32[]{:S(2)}, u32[]{:S(2)}) collective-permute-start(f32[160,128]{1,0:T(8,128)S(1)} %get-tuple-element.92), channel_id=1, source_target_pairs={{0,4},{1,5},{2,6},{3,7},{4,0},{5,1},{6,2},{7,3},{8,12},{9,13},{10,... | collective-permute-start | bytes 245768 | tf_op jit(solution)/shard_map/ppermute | solution.py:530
  73.5 1.1 collective-permute-start.19
  74.5 0.5 step.3.refs_0_
  75.1 0.3 collective-permute-done.17.refs_2_
  75.4 4.9 %collective-permute-done.18.refs_3_ = f32[160,128]{1,0:T(8,128)S(1)} collective-permute-done((f32[160,128]{1,0:T(8,128)S(1)}, f32[160,128]{1,0:T(8,128)S(1)}, u32[]{:S(2)}, u32[]{:S(2)}) %collective-permute-start.18) | collective-permute-done | bytes 81952 | tf_op jit(solution)/shard_map/ppermute | solution.py:530
  80.3 0.6 add_far.3.refs_0_.refs_1_
  80.9 2.4 %collective-permute-start.22 = (f32[160,128]{1,0:T(8,128)S(1)}, f32[160,128]{1,0:T(8,128)S(1)}, u32[]{:S(2)}, u32[]{:S(2)}) collective-permute-start(f32[160,128]{1,0:T(8,128)S(1)} %add_far.3.refs_0_.refs_1_), channel_id=1, source_target_pairs={{0,6},{1,7},{2,4},{3,5},{4,2},{5,3},{6,0},{7,1},{8,14},{9,15},{10,... | collective-permute-start | bytes 245768 | tf_op jit(solution)/shard_map/ppermute | solution.py:530
  83.3 0.6 collective-permute-start.21
  83.9 1.5 %collective-permute-start.20 = (f32[160,128]{1,0:T(8,128)S(1)}, f32[160,128]{1,0:T(8,128)S(1)}, u32[]{:S(2)}, u32[]{:S(2)}) collective-permute-start(f32[160,128]{1,0:T(8,128)S(1)} %add_far.3.refs_0_.refs_1_), channel_id=1, source_target_pairs={{0,2},{1,3},{2,0},{3,1},{4,6},{5,7},{6,4},{7,5},{8,10},{9,11},{10,... | collective-permute-start | bytes 245768 | tf_op jit(solution)/shard_map/ppermute | solution.py:530
  85.3 0.5 collective-permute-start.31
  85.8 1.9 %collective-permute-done.22.refs_4_ = f32[160,128]{1,0:T(8,128)S(1)} collective-permute-done((f32[160,128]{1,0:T(8,128)S(1)}, f32[160,128]{1,0:T(8,128)S(1)}, u32[]{:S(2)}, u32[]{:S(2)}) %collective-permute-start.22) | collective-permute-done | bytes 81952 | tf_op jit(solution)/shard_map/ppermute | solution.py:530
  87.7 2.4 %collective-permute-done.21.refs_3_ = f32[160,128]{1,0:T(8,128)S(1)} collective-permute-done((f32[160,128]{1,0:T(8,128)S(1)}, f32[160,128]{1,0:T(8,128)S(1)}, u32[]{:S(2)}, u32[]{:S(2)}) %collective-permute-start.21) | collective-permute-done | bytes 81952 | tf_op jit(solution)/shard_map/ppermute | solution.py:530
  90.1 0.6 stack.11.refs_0_.refs_1_
  90.7 1.3 collective-permute-start.24
  92.0 7.4 %polynomial.2.refs_0_.refs_3_ = bf16[1344,128]{1,0:T(8,128)(2,1)S(1)} custom-call(s32[10]{0:T(128)S(1)} %pad_add_fusion.place, f32[4,160,128]{2,1,0:T(8,128)S(1)} %stack.11.refs_0_.refs_1_, f32[4,160,128]{2,1,0:T(8,128)S(1)} %stack.10.refs_0_.refs_1_, f32[4,160,128]{2,1,0:T(8,128)S(1)} %collective-permute-done.23.refs_2_), custom_call_target="tpu_custom_call" | custom-call | flops 107374182400 | bytes 41943040 | tf_op jit(solution)/shard_map/polynomial/pallas_call | solution.py:123
  99.4 1.2 collective-permute-start.26
  100.6 7.7 %polynomial.3.refs_0_.refs_3_ = bf16[1344,128]{1,0:T(8,128)(2,1)S(1)} custom-call(s32[10]{0:T(128)S(1)} %pad_add_fusion.place, bf16[1344,128]{1,0:T(8,128)(2,1)S(1)} %polynomial.2.refs_0_.refs_3_, f32[4,160,128]{2,1,0:T(8,128)S(1)} %stack.11.refs_0_.refs_1_, f32[4,160,128]{2,1,0:T(8,128)S(1)} %collective-permute-done.24.refs_2_), custom_call_target="tpu_custom_call" | custom-call | flops 107374182400 | bytes 41943040 | tf_op jit(solution)/shard_map/polynomial/pallas_call | solution.py:123
  108.3 1.0 collective-permute-start.30
  109.2 0.2 collective-permute-start.27
  109.5 2.1 %finish.5 = (bf16[8,512,512]{2,1,0:T(8,128)(2,1)}, f32[8,128]{1,0:T(8,128)S(1)}) custom-call(s32[10]{0:T(128)S(1)} %pad_add_fusion.place, bf16[1344,128]{1,0:T(8,128)(2,1)S(1)} %polynomial.3.refs_0_.refs_3_, bf16[512,512]{1,0:T(8,128)(2,1)S(1)} %get-tuple-element.94.refs_1_, bf16[512,512]{1,0:T(8,128)(2,1)S(1)} %copy-done.1, ...), custom_call_target="tpu_custom_call" | custom-call | flops 10737418240 | bytes 41943040 | tf_op jit(solution)/shard_map/finish/pallas_call | solution.py:123
  111.6 6.8 %collective-permute-done.26.refs_1_ = bf16[1344,128]{1,0:T(8,128)(2,1)S(1)} collective-permute-done((bf16[1344,128]{1,0:T(8,128)(2,1)S(1)}, bf16[1344,128]{1,0:T(8,128)(2,1)S(1)}, u32[]{:S(2)}, u32[]{:S(2)}) %collective-permute-start.26) | collective-permute-done | bytes 344096 | tf_op jit(solution)/shard_map/ppermute | solution.py:549
  118.3 0.5 step.4.refs_0_.refs_3_
  119.0 2.1 %finish.6 = (bf16[8,512,512]{2,1,0:T(8,128)(2,1)}, f32[8,128]{1,0:T(8,128)S(1)}) custom-call(s32[10]{0:T(128)S(1)} %pad_add_fusion.place, bf16[1344,128]{1,0:T(8,128)(2,1)S(1)} %step.4.refs_0_.refs_3_, bf16[512,512]{1,0:T(8,128)(2,1)S(1)} %get-tuple-element.96.refs_1_, bf16[512,512]{1,0:T(8,128)(2,1)S(1)} %copy-done.3, ...), custom_call_target="tpu_custom_call", output_to_operand_aliasing={{0}: (6, {})} | custom-call | flops 10737418240 | bytes 41943040 | tf_op jit(solution)/shard_map/finish/pallas_call | solution.py:123
  121.1 0.5 collective-permute-start.32
  121.6 3.6 %finish.7 = (bf16[8,512,512]{2,1,0:T(8,128)(2,1)}, f32[8,128]{1,0:T(8,128)S(1)}) custom-call(s32[10]{0:T(128)S(1)} %pad_add_fusion.place, f32[8,128]{1,0:T(8,128)S(1)} %get-tuple-element.98.refs_0_, bf16[2,512,512]{2,1,0:T(8,128)(2,1)} %collective-permute-done.16.refs_1_, ...), custom_call_target="tpu_custom_call", output_to_operand_aliasing={{0}: (6, {})} | custom-call | flops 10737418240 | bytes 41943040 | tf_op jit(solution)/shard_map/finish/pallas_call | solution.py:123
  125.3 0.5 step.5.refs_0_.refs_2_
  125.9 3.0 %finish.8 = (bf16[8,512,512]{2,1,0:T(8,128)(2,1)}, f32[8,128]{1,0:T(8,128)S(1)}) custom-call(s32[10]{0:T(128)S(1)} %pad_add_fusion.place, bf16[1344,128]{1,0:T(8,128)(2,1)S(1)} %step.5.refs_0_.refs_2_, bf16[2,512,512]{2,1,0:T(8,128)(2,1)} %collective-permute-done.31.refs_1_, ...), custom_call_target="tpu_custom_call", output_to_operand_aliasing={{0}: (4, {})} | custom-call | flops 5368709120 | bytes 20971520 | tf_op jit(solution)/shard_map/finish/pallas_call | solution.py:123
  129.0 2.4 %finish.9 = (bf16[8,512,512]{2,1,0:T(8,128)(2,1)}, f32[8,128]{1,0:T(8,128)}) custom-call(s32[10]{0:T(128)S(1)} %pad_add_fusion.place, f32[8,128]{1,0:T(8,128)S(1)} %get-tuple-element.102.refs_0_, bf16[2,512,512]{2,1,0:T(8,128)(2,1)S(1)} %collective-permute-done.32.refs_1_, ...), custom_call_target="tpu_custom_call", output_to_operand_aliasing={{0}: (4, {})} | custom-call | flops 5368709120 | bytes 20971520 | tf_op jit(solution)/shard_map/finish/pallas_call | solution.py:123
  (42 shorter events, 0.5 us)
Async XLA Ops:
  3.0 20.9 %collective-permute-start.2 = (bf16[512,512]{1,0:T(8,128)(2,1)S(1)}, bf16[512,512]{1,0:T(8,128)(2,1)S(1)}, u32[]{:S(2)}, u32[]{:S(2)}) collective-permute-start(bf16[512,512]{1,0:T(8,128)(2,1)S(1)} %pick.2.refs_0_), channel_id=1, source_target_pairs={{0,16},{8,24},{16,0},{24,8},{1,17},{9,25},{17,1},{25,9},{2,18},{10... | collective-permute-start | bytes 1572872 | tf_op jit(solution)/shard_map/ppermute | solution.py:494
  8.3 8.8 %collective-permute-start = (bf16[512,512]{1,0:T(8,128)(2,1)S(1)}, bf16[512,512]{1,0:T(8,128)(2,1)S(1)}, u32[]{:S(2)}, u32[]{:S(2)}) collective-permute-start(bf16[512,512]{1,0:T(8,128)(2,1)S(1)} %get-tuple-element.61), channel_id=1, source_target_pairs={{0,8},{8,0},{16,24},{24,16},{1,9},{9,1},{17,25},{25,17},{2,10},{10... | collective-permute-start | bytes 1572872 | tf_op jit(solution)/shard_map/ppermute | solution.py:494
  8.3 21.2 %collective-permute-start.4 = (bf16[512,512]{1,0:T(8,128)(2,1)S(1)}, bf16[512,512]{1,0:T(8,128)(2,1)S(1)}, u32[]{:S(2)}, u32[]{:S(2)}) collective-permute-start(bf16[512,512]{1,0:T(8,128)(2,1)S(1)} %get-tuple-element.54.refs_0_), channel_id=1, source_target_pairs={{0,24},{8,16},{16,8},{24,0},{1,25},{9,17},{17,9},{25,1},{2,26},{10... | collective-permute-start | bytes 1572872 | tf_op jit(solution)/shard_map/ppermute | solution.py:494
  11.8 8.6 %collective-permute-start.1 = (bf16[512,512]{1,0:T(8,128)(2,1)S(1)}, bf16[512,512]{1,0:T(8,128)(2,1)S(1)}, u32[]{:S(2)}, u32[]{:S(2)}) collective-permute-start(bf16[512,512]{1,0:T(8,128)(2,1)S(1)} %get-tuple-element.64), channel_id=1, source_target_pairs={{0,8},{8,0},{16,24},{24,16},{1,9},{9,1},{17,25},{25,17},{2,10},{10... | collective-permute-start | bytes 1572872 | tf_op jit(solution)/shard_map/ppermute | solution.py:494
  12.1 29.1 %collective-permute-start.6 = (bf16[512,512]{1,0:T(8,128)(2,1)S(1)}, bf16[512,512]{1,0:T(8,128)(2,1)S(1)}, u32[]{:S(2)}, u32[]{:S(2)}) collective-permute-start(bf16[512,512]{1,0:T(8,128)(2,1)S(1)} %get-tuple-element.74), channel_id=1, source_target_pairs={{0,16},{8,24},{16,0},{24,8},{1,17},{9,25},{17,1},{25,9},{2,18},{10... | collective-permute-start | bytes 1572872 | tf_op jit(solution)/shard_map/ppermute | solution.py:494
  17.1 34.9 %collective-permute-start.8 = (bf16[512,512]{1,0:T(8,128)(2,1)S(1)}, bf16[512,512]{1,0:T(8,128)(2,1)S(1)}, u32[]{:S(2)}, u32[]{:S(2)}) collective-permute-start(bf16[512,512]{1,0:T(8,128)(2,1)S(1)} %get-tuple-element.79), channel_id=1, source_target_pairs={{0,24},{8,16},{16,8},{24,0},{1,25},{9,17},{17,9},{25,1},{2,26},{10... | collective-permute-start | bytes 1572872 | tf_op jit(solution)/shard_map/ppermute | solution.py:494
  20.4 9.2 %collective-permute-start.3 = (bf16[512,512]{1,0:T(8,128)(2,1)S(1)}, bf16[512,512]{1,0:T(8,128)(2,1)S(1)}, u32[]{:S(2)}, u32[]{:S(2)}) collective-permute-start(bf16[512,512]{1,0:T(8,128)(2,1)S(1)} %get-tuple-element.69), channel_id=1, source_target_pairs={{0,8},{8,0},{16,24},{24,16},{1,9},{9,1},{17,25},{25,17},{2,10},{10... | collective-permute-start | bytes 1572872 | tf_op jit(solution)/shard_map/ppermute | solution.py:520
  23.9 17.3 %collective-permute-start.5 = (bf16[512,512]{1,0:T(8,128)(2,1)S(1)}, bf16[512,512]{1,0:T(8,128)(2,1)S(1)}, u32[]{:S(2)}, u32[]{:S(2)}) collective-permute-start(bf16[512,512]{1,0:T(8,128)(2,1)S(1)} %get-tuple-element.73), channel_id=1, source_target_pairs={{0,8},{8,0},{16,24},{24,16},{1,9},{9,1},{17,25},{25,17},{2,10},{10... | collective-permute-start | bytes 1572872 | tf_op jit(solution)/shard_map/ppermute | solution.py:520
  29.5 3.2 %copy-start = (bf16[512,512]{1,0:T(8,128)(2,1)}, bf16[512,512]{1,0:T(8,128)(2,1)S(1)}, u32[]{:S(2)}) copy-start(bf16[512,512]{1,0:T(8,128)(2,1)S(1)} %collective-permute-done.3.refs_1_.refs_2_) | copy-start | bytes 1572868
  32.8 11.7 %collective-permute-start.7 = (f32[4,160,128]{2,1,0:T(8,128)S(1)}, f32[4,160,128]{2,1,0:T(8,128)S(1)}, u32[]{:S(2)}, u32[]{:S(2)}) collective-permute-start(f32[4,160,128]{2,1,0:T(8,128)S(1)} %slice_bitcast_fusion.1), channel_id=1, source_target_pairs={{0,1},{1,0},{2,3},{3,2},{4,5},{5,4},{6,7},{7,6},{8,9},{9,8},{10,11... | collective-permute-start | bytes 983048 | tf_op jit(solution)/shard_map/ppermute | solution.py:527
  41.2 3.3 %copy-start.2 = (bf16[512,512]{1,0:T(8,128)(2,1)}, bf16[512,512]{1,0:T(8,128)(2,1)S(1)}, u32[]{:S(2)}) copy-start(bf16[512,512]{1,0:T(8,128)(2,1)S(1)} %collective-permute-done.5.refs_1_.refs_2_) | copy-start | bytes 1572868
  45.1 10.3 %collective-permute-start.9 = (f32[160,128]{1,0:T(8,128)S(1)}, f32[160,128]{1,0:T(8,128)S(1)}, u32[]{:S(2)}, u32[]{:S(2)}) collective-permute-start(f32[160,128]{1,0:T(8,128)S(1)} %get-tuple-element.83), channel_id=1, source_target_pairs={{0,2},{1,3},{2,0},{3,1},{4,6},{5,7},{6,4},{7,5},{8,10},{9,11},{10,... | collective-permute-start | bytes 245768 | tf_op jit(solution)/shard_map/ppermute | solution.py:530
  47.3 8.1 %collective-permute-start.10 = (f32[160,128]{1,0:T(8,128)S(1)}, f32[160,128]{1,0:T(8,128)S(1)}, u32[]{:S(2)}, u32[]{:S(2)}) collective-permute-start(f32[160,128]{1,0:T(8,128)S(1)} %get-tuple-element.84), channel_id=1, source_target_pairs={{0,4},{1,5},{2,6},{3,7},{4,0},{5,1},{6,2},{7,3},{8,12},{9,13},{10,... | collective-permute-start | bytes 245768 | tf_op jit(solution)/shard_map/ppermute | solution.py:530
  49.9 6.3 %collective-permute-start.11 = (f32[160,128]{1,0:T(8,128)S(1)}, f32[160,128]{1,0:T(8,128)S(1)}, u32[]{:S(2)}, u32[]{:S(2)}) collective-permute-start(f32[160,128]{1,0:T(8,128)S(1)} %get-tuple-element.85), channel_id=1, source_target_pairs={{0,6},{1,7},{2,4},{3,5},{4,2},{5,3},{6,0},{7,1},{8,14},{9,15},{10,... | collective-permute-start | bytes 245768 | tf_op jit(solution)/shard_map/ppermute | solution.py:530
  49.9 24.6 %collective-permute-start.16 = (bf16[2,512,512]{2,1,0:T(8,128)(2,1)S(1)}, bf16[2,512,512]{2,1,0:T(8,128)(2,1)}, u32[]{:S(2)}, u32[]{:S(2)}) collective-permute-start(bf16[2,512,512]{2,1,0:T(8,128)(2,1)S(1)} %get-tuple-element.89), channel_id=1, source_target_pairs={{0,16},{8,24},{16,0},{24,8},{1,17},{9,25},{17,1},{25,9},{2,18},{10... | collective-permute-start | bytes 3145736 | tf_op jit(solution)/shard_map/ppermute | solution.py:522
  56.8 9.8 %collective-permute-start.12 = (f32[4,160,128]{2,1,0:T(8,128)S(1)}, f32[4,160,128]{2,1,0:T(8,128)S(1)}, u32[]{:S(2)}, u32[]{:S(2)}) collective-permute-start(f32[4,160,128]{2,1,0:T(8,128)S(1)} %slice_bitcast_fusion), channel_id=1, source_target_pairs={{0,1},{1,0},{2,3},{3,2},{4,5},{5,4},{6,7},{7,6},{8,9},{9,8},{10,11... | collective-permute-start | bytes 983048 | tf_op jit(solution)/shard_map/ppermute | solution.py:527
  58.4 8.8 %collective-permute-start.15 = (f32[160,128]{1,0:T(8,128)S(1)}, f32[160,128]{1,0:T(8,128)S(1)}, u32[]{:S(2)}, u32[]{:S(2)}) collective-permute-start(f32[160,128]{1,0:T(8,128)S(1)} %get-tuple-element.86.refs_0_.refs_1_), channel_id=1, source_target_pairs={{0,6},{1,7},{2,4},{3,5},{4,2},{5,3},{6,0},{7,1},{8,14},{9,15},{10,... | collective-permute-start | bytes 245768 | tf_op jit(solution)/shard_map/ppermute | solution.py:530
  61.2 7.8 %collective-permute-start.14 = (f32[160,128]{1,0:T(8,128)S(1)}, f32[160,128]{1,0:T(8,128)S(1)}, u32[]{:S(2)}, u32[]{:S(2)}) collective-permute-start(f32[160,128]{1,0:T(8,128)S(1)} %get-tuple-element.86.refs_0_.refs_1_), channel_id=1, source_target_pairs={{0,4},{1,5},{2,6},{3,7},{4,0},{5,1},{6,2},{7,3},{8,12},{9,13},{10,... | collective-permute-start | bytes 245768 | tf_op jit(solution)/shard_map/ppermute | solution.py:530
  61.2 7.8 %collective-permute-start.13 = (f32[160,128]{1,0:T(8,128)S(1)}, f32[160,128]{1,0:T(8,128)S(1)}, u32[]{:S(2)}, u32[]{:S(2)}) collective-permute-start(f32[160,128]{1,0:T(8,128)S(1)} %get-tuple-element.86.refs_0_.refs_1_), channel_id=1, source_target_pairs={{0,2},{1,3},{2,0},{3,1},{4,6},{5,7},{6,4},{7,5},{8,10},{9,11},{10,... | collective-permute-start | bytes 245768 | tf_op jit(solution)/shard_map/ppermute | solution.py:530
  69.6 22.4 %collective-permute-start.23 = (f32[4,160,128]{2,1,0:T(8,128)S(1)}, f32[4,160,128]{2,1,0:T(8,128)S(1)}, u32[]{:S(2)}, u32[]{:S(2)}) collective-permute-start(f32[4,160,128]{2,1,0:T(8,128)S(1)} %stack.10.refs_0_.refs_1_), channel_id=1, source_target_pairs={{0,1},{1,0},{2,3},{3,2},{4,5},{5,4},{6,7},{7,6},{8,9},{9,8},{10,11... | collective-permute-start | bytes 983048 | tf_op jit(solution)/shard_map/ppermute | solution.py:527
  70.2 5.2 %collective-permute-start.17 = (f32[160,128]{1,0:T(8,128)S(1)}, f32[160,128]{1,0:T(8,128)S(1)}, u32[]{:S(2)}, u32[]{:S(2)}) collective-permute-start(f32[160,128]{1,0:T(8,128)S(1)} %get-tuple-element.91), channel_id=1, source_target_pairs={{0,2},{1,3},{2,0},{3,1},{4,6},{5,7},{6,4},{7,5},{8,10},{9,11},{10,... | collective-permute-start | bytes 245768 | tf_op jit(solution)/shard_map/ppermute | solution.py:530
  71.1 9.2 %collective-permute-start.18 = (f32[160,128]{1,0:T(8,128)S(1)}, f32[160,128]{1,0:T(8,128)S(1)}, u32[]{:S(2)}, u32[]{:S(2)}) collective-permute-start(f32[160,128]{1,0:T(8,128)S(1)} %get-tuple-element.92), channel_id=1, source_target_pairs={{0,4},{1,5},{2,6},{3,7},{4,0},{5,1},{6,2},{7,3},{8,12},{9,13},{10,... | collective-permute-start | bytes 245768 | tf_op jit(solution)/shard_map/ppermute | solution.py:530
  73.5 6.8 %collective-permute-start.19 = (f32[160,128]{1,0:T(8,128)S(1)}, f32[160,128]{1,0:T(8,128)S(1)}, u32[]{:S(2)}, u32[]{:S(2)}) collective-permute-start(f32[160,128]{1,0:T(8,128)S(1)} %get-tuple-element.93), channel_id=1, source_target_pairs={{0,6},{1,7},{2,4},{3,5},{4,2},{5,3},{6,0},{7,1},{8,14},{9,15},{10,... | collective-permute-start | bytes 245768 | tf_op jit(solution)/shard_map/ppermute | solution.py:530
  80.9 6.8 %collective-permute-start.22 = (f32[160,128]{1,0:T(8,128)S(1)}, f32[160,128]{1,0:T(8,128)S(1)}, u32[]{:S(2)}, u32[]{:S(2)}) collective-permute-start(f32[160,128]{1,0:T(8,128)S(1)} %add_far.3.refs_0_.refs_1_), channel_id=1, source_target_pairs={{0,6},{1,7},{2,4},{3,5},{4,2},{5,3},{6,0},{7,1},{8,14},{9,15},{10,... | collective-permute-start | bytes 245768 | tf_op jit(solution)/shard_map/ppermute | solution.py:530
  83.3 6.9 %collective-permute-start.21 = (f32[160,128]{1,0:T(8,128)S(1)}, f32[160,128]{1,0:T(8,128)S(1)}, u32[]{:S(2)}, u32[]{:S(2)}) collective-permute-start(f32[160,128]{1,0:T(8,128)S(1)} %add_far.3.refs_0_.refs_1_), channel_id=1, source_target_pairs={{0,4},{1,5},{2,6},{3,7},{4,0},{5,1},{6,2},{7,3},{8,12},{9,13},{10,... | collective-permute-start | bytes 245768 | tf_op jit(solution)/shard_map/ppermute | solution.py:530
  83.9 6.3 %collective-permute-start.20 = (f32[160,128]{1,0:T(8,128)S(1)}, f32[160,128]{1,0:T(8,128)S(1)}, u32[]{:S(2)}, u32[]{:S(2)}) collective-permute-start(f32[160,128]{1,0:T(8,128)S(1)} %add_far.3.refs_0_.refs_1_), channel_id=1, source_target_pairs={{0,2},{1,3},{2,0},{3,1},{4,6},{5,7},{6,4},{7,5},{8,10},{9,11},{10,... | collective-permute-start | bytes 245768 | tf_op jit(solution)/shard_map/ppermute | solution.py:530
  85.3 35.7 %collective-permute-start.31 = (bf16[2,512,512]{2,1,0:T(8,128)(2,1)}, bf16[2,512,512]{2,1,0:T(8,128)(2,1)}, u32[]{:S(2)}, u32[]{:S(2)}) collective-permute-start(bf16[2,512,512]{2,1,0:T(8,128)(2,1)} %step.3.refs_0_), channel_id=1, source_target_pairs={{0,16},{8,24},{16,0},{24,8},{1,17},{9,25},{17,1},{25,9},{2,18},{10... | collective-permute-start | bytes 3145736 | tf_op jit(solution)/shard_map/ppermute | solution.py:522
  87.7 33.9 %collective-permute-start.28 = (bf16[2,512,512]{2,1,0:T(8,128)(2,1)}, bf16[2,512,512]{2,1,0:T(8,128)(2,1)}, u32[]{:S(2)}, u32[]{:S(2)}) collective-permute-start(bf16[2,512,512]{2,1,0:T(8,128)(2,1)} %collective-permute-done.16.refs_1_), channel_id=1, source_target_pairs={{0,8},{8,0},{16,24},{24,16},{1,9},{9,1},{17,25},{25,17},{2,10},{10... | collective-permute-start | bytes 3145736 | tf_op jit(solution)/shard_map/ppermute | solution.py:524
  90.7 9.9 %collective-permute-start.24 = (f32[4,160,128]{2,1,0:T(8,128)S(1)}, f32[4,160,128]{2,1,0:T(8,128)S(1)}, u32[]{:S(2)}, u32[]{:S(2)}) collective-permute-start(f32[4,160,128]{2,1,0:T(8,128)S(1)} %stack.11.refs_0_.refs_1_), channel_id=1, source_target_pairs={{0,1},{1,0},{2,3},{3,2},{4,5},{5,4},{6,7},{7,6},{8,9},{9,8},{10,11... | collective-permute-start | bytes 983048 | tf_op jit(solution)/shard_map/ppermute | solution.py:527
  99.4 10.1 %copy-start.1 = (bf16[512,512]{1,0:T(8,128)(2,1)S(1)}, bf16[512,512]{1,0:T(8,128)(2,1)}, u32[]{:S(2)}) copy-start(bf16[512,512]{1,0:T(8,128)(2,1)} %copy-done) | copy-start | bytes 1572868
  99.4 18.9 %collective-permute-start.26 = (bf16[1344,128]{1,0:T(8,128)(2,1)S(1)}, bf16[1344,128]{1,0:T(8,128)(2,1)S(1)}, u32[]{:S(2)}, u32[]{:S(2)}) collective-permute-start(bf16[1344,128]{1,0:T(8,128)(2,1)S(1)} %polynomial.2.refs_0_.refs_3_), channel_id=1, source_target_pairs={{0,16},{8,24},{16,0},{24,8},{1,17},{9,25},{17,1},{25,9},{2,18},{10... | collective-permute-start | bytes 1032200 | tf_op jit(solution)/shard_map/ppermute | solution.py:549
  100.6 8.6 %collective-permute-start.25 = (bf16[1344,128]{1,0:T(8,128)(2,1)S(1)}, bf16[1344,128]{1,0:T(8,128)(2,1)S(1)}, u32[]{:S(2)}, u32[]{:S(2)}) collective-permute-start(bf16[1344,128]{1,0:T(8,128)(2,1)S(1)} %polynomial.2.refs_0_.refs_3_), channel_id=1, source_target_pairs={{0,8},{8,0},{16,24},{24,16},{1,9},{9,1},{17,25},{25,17},{2,10},{10... | collective-permute-start | bytes 1032200 | tf_op jit(solution)/shard_map/ppermute | solution.py:551
  108.3 17.0 %collective-permute-start.30 = (bf16[1344,128]{1,0:T(8,128)(2,1)S(1)}, bf16[1344,128]{1,0:T(8,128)(2,1)S(1)}, u32[]{:S(2)}, u32[]{:S(2)}) collective-permute-start(bf16[1344,128]{1,0:T(8,128)(2,1)S(1)} %polynomial.3.refs_0_.refs_3_), channel_id=1, source_target_pairs={{0,16},{8,24},{16,0},{24,8},{1,17},{9,25},{17,1},{25,9},{2,18},{10... | collective-permute-start | bytes 1032200 | tf_op jit(solution)/shard_map/ppermute | solution.py:549
  109.2 9.7 %collective-permute-start.27 = (bf16[1344,128]{1,0:T(8,128)(2,1)S(1)}, bf16[1344,128]{1,0:T(8,128)(2,1)S(1)}, u32[]{:S(2)}, u32[]{:S(2)}) collective-permute-start(bf16[1344,128]{1,0:T(8,128)(2,1)S(1)} %polynomial.3.refs_0_.refs_3_), channel_id=1, source_target_pairs={{0,8},{8,0},{16,24},{24,16},{1,9},{9,1},{17,25},{25,17},{2,10},{10... | collective-permute-start | bytes 1032200 | tf_op jit(solution)/shard_map/ppermute | solution.py:551
  109.5 9.5 %copy-start.3 = (bf16[512,512]{1,0:T(8,128)(2,1)S(1)}, bf16[512,512]{1,0:T(8,128)(2,1)}, u32[]{:S(2)}) copy-start(bf16[512,512]{1,0:T(8,128)(2,1)} %copy-done.2) | copy-start | bytes 1572868
  118.9 2.8 %collective-permute-start.29 = (bf16[1344,128]{1,0:T(8,128)(2,1)S(1)}, bf16[1344,128]{1,0:T(8,128)(2,1)S(1)}, u32[]{:S(2)}, u32[]{:S(2)}) collective-permute-start(bf16[1344,128]{1,0:T(8,128)(2,1)S(1)} %step.4.refs_0_.refs_3_), channel_id=1, source_target_pairs={{0,8},{8,0},{16,24},{24,16},{1,9},{9,1},{17,25},{25,17},{2,10},{10... | collective-permute-start | bytes 1032200 | tf_op jit(solution)/shard_map/ppermute | solution.py:556
  121.1 7.9 %collective-permute-start.32 = (bf16[2,512,512]{2,1,0:T(8,128)(2,1)}, bf16[2,512,512]{2,1,0:T(8,128)(2,1)S(1)}, u32[]{:S(2)}, u32[]{:S(2)}) collective-permute-start(bf16[2,512,512]{2,1,0:T(8,128)(2,1)} %collective-permute-done.31.refs_1_), channel_id=1, source_target_pairs={{0,8},{8,0},{16,24},{24,16},{1,9},{9,1},{17,25},{25,17},{2,10},{10... | collective-permute-start | bytes 3145736 | tf_op jit(solution)/shard_map/ppermute | solution.py:524
  125.8 3.1 %collective-permute-start.33 = (bf16[1344,128]{1,0:T(8,128)(2,1)S(1)}, bf16[1344,128]{1,0:T(8,128)(2,1)S(1)}, u32[]{:S(2)}, u32[]{:S(2)}) collective-permute-start(bf16[1344,128]{1,0:T(8,128)(2,1)S(1)} %step.5.refs_0_.refs_2_), channel_id=1, source_target_pairs={{0,8},{8,0},{16,24},{24,16},{1,9},{9,1},{17,25},{25,17},{2,10},{10... | collective-permute-start | bytes 1032200 | tf_op jit(solution)/shard_map/ppermute | solution.py:556

commit v4 on v3

--- a/solution.py
+++ b/solution.py
@@ -412,7 +412,7 @@
         name="polynomial",
         scratch=[pltpu.VMEM((PACKED, TILE), f32)],
         vmem=20,
-        work=(20 * 2 * RANK**3, 2 * 2**20),
+        work=(RANK**3, 2**16),
     )[0]
 
 
@@ -607,11 +607,14 @@
     collect(0)
     expect(*[(0, d) for d in far_steps[::2]])
     for d in far_steps[1::2]:
-        rows[1, d] = step(line, rows[1, d])
+        line.waiting[d] = rows[1, d]
+    second_sum(1)
+    for d in far_steps[1::2]:
+        rows[1, d] = line.passed[d]
         send_back(1, d - 1)
-    second_sum(1)
     collect(1)
     make_polynomial(0)
+    expect(*[(1, d) for d in far_steps[::2]])
     make_polynomial(1)
     finish_steps(0, [0] + near_steps)
     pass_polynomials(0)

time: 132 us -> 125 us (0.947)
  waiting for transfers between devices: 32.3 us -> 27.4 us
  Pallas kernels: 63.1 us -> 59.5 us
    ppermute x4, waiting for transfers between devices: 6.76 us -> 0.01 us  [make_polynomial(): polys[slot, d] = lax.ppermute(polys[slot, 0], 'owner', partners(owners, d))]
    pallas_call x26 -> x25, Pallas kernels: 63.1 us -> 59.5 us  [run(): pl.pallas_call(body, grid_spec=pltpu.PrefetchScalarGridSpec(num_scalar_pr...]
    ppermute x2, waiting for transfers between devices: 0.01 us -> 1.51 us  [send_back(): pair = lax.ppermute(rows[slot, d + 1], 'owner', partners(owners, d))]
  transfers between devices with their start and end apart: 34 -> 34, of which waited for: 11 -> 9; matrix products, arithmetic and copies ran while one was open for 0% -> 0% of each run, Pallas kernels for 45% -> 44%
where the time goes in v4:
time: 125 us; the launch traced here: 124 us
  Pallas kernels  59.5 us (48%)
  starting transfers between devices  35 us (28%)
  waiting for transfers between devices  27.4 us (22%)
    pallas_call x25, Pallas kernels, run(): pl.pallas_call(body, grid_spec=pltpu.PrefetchScalarGridSpec(num_scalar_pr...  59.5 us
    ppermute x12, starting transfers between devices, across_far(): return lax.ppermute(x, 'fsdp', partners(group, e2 * near))  18 us
    ppermute x12, waiting for transfers between devices, across_far(): return lax.ppermute(x, 'fsdp', partners(group, e2 * near))  12.3 us
    ppermute x6, waiting for transfers between devices, send(): lax.ppermute(picked[slot, d], 'owner', partners(owners, d))  9.73 us
    ppermute x6, starting transfers between devices, send(): lax.ppermute(picked[slot, d], 'owner', partners(owners, d))  5.33 us
    ppermute x4, starting transfers between devices, across_near(): return lax.ppermute(x, 'fsdp', partners(group, e1))  5.29 us
    ppermute x4, waiting for transfers between devices, across_near(): return lax.ppermute(x, 'fsdp', partners(group, e1))  3.84 us
  transfers between devices with their start and end apart: 34, of which 9 were waited for; matrix products, arithmetic and copies ran while one was open for 0% of the time, Pallas kernels for 44%

profile of v4, /device:TPU:0, one launch (start us, length us, event | category | flops | bytes accessed | tf_op | source)
XLA Modules:
  0.0 123.9 jit_solution(9927976104429312053)
XLA Ops:
  0.6 0.7 pad_add_fusion.place
  1.4 1.6 %pick.2.refs_0_ = bf16[512,512]{1,0:T(8,128)(2,1)S(1)} custom-call(s32[10]{0:T(128)S(1)} %pad_add_fusion.place, bf16[8,512,512]{2,1,0:T(8,128)(2,1)} %refs_1_.3), custom_call_target="tpu_custom_call" | custom-call | bytes 20971520 | tf_op jit(solution)/shard_map/pick/pallas_call | solution.py:123
  3.0 3.0 %collective-permute-start.2 = (bf16[512,512]{1,0:T(8,128)(2,1)S(1)}, bf16[512,512]{1,0:T(8,128)(2,1)S(1)}, u32[]{:S(2)}, u32[]{:S(2)}) collective-permute-start(bf16[512,512]{1,0:T(8,128)(2,1)S(1)} %pick.2.refs_0_), channel_id=1, source_target_pairs={{0,16},{8,24},{16,0},{24,8},{1,17},{9,25},{17,1},{25,9},{2,18},{10... | collective-permute-start | bytes 1572872 | tf_op jit(solution)/shard_map/ppermute | solution.py:494
  6.0 2.3 %pick.3 = (bf16[512,512]{1,0:T(8,128)(2,1)S(1)}, bf16[512,512]{1,0:T(8,128)(2,1)S(1)}, bf16[512,512]{1,0:T(8,128)(2,1)S(1)}, bf16[512,512]{1,0:T(8,128)(2,1)S(1)}, bf16[512,512]{1,0:T(8,128)(2,1)S(1)}) custom-call(s32[10]{0:T(128)S(1)} %pad_add_fusion.place, bf16[512,512]{1,0:T(8,128)(2,1)S(1)} %pick.2.refs_0_, bf16[8,512,512]{2,1,0:T(8,128)(2,1)} %refs_1_.3), custom_call_target="tpu_custom_call" | custom-call | bytes 104857600 | tf_op jit(solution)/shard_map/pick/pallas_call | solution.py:123
  8.3 0.1 collective-permute-start
  8.3 0.1 collective-permute-start.4
  8.5 3.3 %blend.8 = (f32[2,2048,512]{2,1,0:T(8,128)}, bf16[512,512]{1,0:T(8,128)(2,1)S(1)}, f32[1280,128]{1,0:T(8,128)S(1)}, bf16[512,512]{1,0:T(8,128)(2,1)S(1)}, bf16[5...) custom-call(s32[10]{0:T(128)S(1)} %pad_add_fusion.place, ...), custom_call_target="tpu_custom_call", output_to_operand_aliasing={{3}: (2, {}), {4}: (3, {}), {5}: (4, {})} | custom-call | flops 5368709120 | bytes 62914560 | tf_op jit(solution)/shard_map/blend/pallas_call | solution.py:123
  11.8 0.4 collective-permute-start.1
  12.1 1.7 %collective-permute-start.6 = (bf16[512,512]{1,0:T(8,128)(2,1)S(1)}, bf16[512,512]{1,0:T(8,128)(2,1)S(1)}, u32[]{:S(2)}, u32[]{:S(2)}) collective-permute-start(bf16[512,512]{1,0:T(8,128)(2,1)S(1)} %get-tuple-element.76), channel_id=1, source_target_pairs={{0,16},{8,24},{16,0},{24,8},{1,17},{9,25},{17,1},{25,9},{2,18},{10... | collective-permute-start | bytes 1572872 | tf_op jit(solution)/shard_map/ppermute | solution.py:494
  13.8 3.3 %blend.9 = (f32[2,2048,512]{2,1,0:T(8,128)}, bf16[512,512]{1,0:T(8,128)(2,1)S(1)}, f32[1280,128]{1,0:T(8,128)S(1)}) custom-call(s32[10]{0:T(128)S(1)} %pad_add_fusion.place, f32[1280,128]{1,0:T(8,128)S(1)} %get-tuple-element.60.refs_0_.refs_4_, bf16[8,512,512]{2,1,0:T(8,128)(2,1)} %refs_1_.3, ...), custom_call_target="tpu_custom_call", output_to_operand_aliasing={{0}: (4, {})} | custom-call | flops 5368709120 | bytes 62914560 | tf_op jit(solution)/shard_map/blend/pallas_call | solution.py:123
  17.2 3.2 %blend.10 = (f32[2,2048,512]{2,1,0:T(8,128)}, bf16[512,512]{1,0:T(8,128)(2,1)S(1)}, f32[1280,128]{1,0:T(8,128)S(1)}) custom-call(s32[10]{0:T(128)S(1)} %pad_add_fusion.place, f32[1280,128]{1,0:T(8,128)S(1)} %get-tuple-element.62.refs_0_.refs_4_, bf16[512,512]{1,0:T(8,128)(2,1)S(1)} %collective-permute-done.refs_1_, ...), custom_call_target="tpu_custom_call", output_to_operand_aliasing={{0}: (4, {})} | custom-call | flops 5368709120 | bytes 62914560 | tf_op jit(solution)/shard_map/blend/pallas_call | solution.py:123
  20.3 0.4 collective-permute-start.3
  20.7 3.2 %blend.11 = (f32[2,2048,512]{2,1,0:T(8,128)}, bf16[512,512]{1,0:T(8,128)(2,1)S(1)}, f32[1280,128]{1,0:T(8,128)S(1)}) custom-call(s32[10]{0:T(128)S(1)} %pad_add_fusion.place, f32[1280,128]{1,0:T(8,128)S(1)} %get-tuple-element.65.refs_0_.refs_4_, bf16[512,512]{1,0:T(8,128)(2,1)S(1)} %collective-permute-done.1.refs_1_, ...), custom_call_target="tpu_custom_call", output_to_operand_aliasing={{0}: (4, {})} | custom-call | flops 5368709120 | bytes 62914560 | tf_op jit(solution)/shard_map/blend/pallas_call | solution.py:123
  23.9 0.1 collective-permute-start.5
  24.0 3.2 %blend.12 = (f32[2,2048,512]{2,1,0:T(8,128)}, bf16[2,512,512]{2,1,0:T(8,128)(2,1)S(1)}, f32[1280,128]{1,0:T(8,128)S(1)}) custom-call(s32[10]{0:T(128)S(1)} %pad_add_fusion.place, f32[1280,128]{1,0:T(8,128)S(1)} %get-tuple-element.68.refs_0_.refs_5_, bf16[512,512]{1,0:T(8,128)(2,1)S(1)} %collective-permute-done.2.refs_1_, ...), custom_call_target="tpu_custom_call", output_to_operand_aliasing={{0}: (4, {})} | custom-call | flops 5368709120 | bytes 62914560 | tf_op jit(solution)/shard_map/blend/pallas_call | solution.py:123
  27.2 2.3 %collective-permute-done.4.refs_2_ = bf16[512,512]{1,0:T(8,128)(2,1)S(1)} collective-permute-done((bf16[512,512]{1,0:T(8,128)(2,1)S(1)}, bf16[512,512]{1,0:T(8,128)(2,1)S(1)}, u32[]{:S(2)}, u32[]{:S(2)}) %collective-permute-start.4) | collective-permute-done | bytes 524320 | tf_op jit(solution)/shard_map/ppermute | solution.py:494
  29.5 3.2 %blend.13 = (f32[2,2048,512]{2,1,0:T(8,128)}, bf16[2,512,512]{2,1,0:T(8,128)(2,1)S(1)}, f32[2,4,160,128]{3,2,1,0:T(8,128)S(1)}) custom-call(s32[10]{0:T(128)S(1)} %pad_add_fusion.place, f32[1280,128]{1,0:T(8,128)S(1)} %get-tuple-element.70.refs_0_.refs_6_, ...), custom_call_target="tpu_custom_call", output_to_operand_aliasing={{0}: (5, {}), {1}: (6, {})} | custom-call | flops 5368709120 | bytes 62914560 | tf_op jit(solution)/shard_map/blend/pallas_call | solution.py:123
  32.8 1.6 %collective-permute-start.7 = (f32[4,160,128]{2,1,0:T(8,128)S(1)}, f32[4,160,128]{2,1,0:T(8,128)S(1)}, u32[]{:S(2)}, u32[]{:S(2)}) collective-permute-start(f32[4,160,128]{2,1,0:T(8,128)S(1)} %slice_bitcast_fusion.1), channel_id=1, source_target_pairs={{0,1},{1,0},{2,3},{3,2},{4,5},{5,4},{6,7},{7,6},{8,9},{9,8},{10,11... | collective-permute-start | bytes 983048 | tf_op jit(solution)/shard_map/ppermute | solution.py:527
  34.3 6.9 %collective-permute-done.6.refs_2_ = bf16[512,512]{1,0:T(8,128)(2,1)S(1)} collective-permute-done((bf16[512,512]{1,0:T(8,128)(2,1)S(1)}, bf16[512,512]{1,0:T(8,128)(2,1)S(1)}, u32[]{:S(2)}, u32[]{:S(2)}) %collective-permute-start.6) | collective-permute-done | bytes 524320 | tf_op jit(solution)/shard_map/ppermute | solution.py:494
  41.2 3.2 %blend.14 = (f32[2,2048,512]{2,1,0:T(8,128)}, bf16[2,512,512]{2,1,0:T(8,128)(2,1)S(1)}, f32[1280,128]{1,0:T(8,128)S(1)}) custom-call(s32[10]{0:T(128)S(1)} %pad_add_fusion.place, f32[2,4,160,128]{3,2,1,0:T(8,128)S(1)} %get-tuple-element.74.refs_0_.refs_2_, ...), custom_call_target="tpu_custom_call", output_to_operand_aliasing={{0}: (5, {})} | custom-call | flops 5368709120 | bytes 62914560 | tf_op jit(solution)/shard_map/blend/pallas_call | solution.py:123
  44.4 0.6 add_near.2
  45.0 2.2 %collective-permute-start.9 = (f32[160,128]{1,0:T(8,128)S(1)}, f32[160,128]{1,0:T(8,128)S(1)}, u32[]{:S(2)}, u32[]{:S(2)}) collective-permute-start(f32[160,128]{1,0:T(8,128)S(1)} %get-tuple-element.85), channel_id=1, source_target_pairs={{0,2},{1,3},{2,0},{3,1},{4,6},{5,7},{6,4},{7,5},{8,10},{9,11},{10,... | collective-permute-start | bytes 245768 | tf_op jit(solution)/shard_map/ppermute | solution.py:530
  47.2 2.6 %collective-permute-start.10 = (f32[160,128]{1,0:T(8,128)S(1)}, f32[160,128]{1,0:T(8,128)S(1)}, u32[]{:S(2)}, u32[]{:S(2)}) collective-permute-start(f32[160,128]{1,0:T(8,128)S(1)} %get-tuple-element.86), channel_id=1, source_target_pairs={{0,4},{1,5},{2,6},{3,7},{4,0},{5,1},{6,2},{7,3},{8,12},{9,13},{10,... | collective-permute-start | bytes 245768 | tf_op jit(solution)/shard_map/ppermute | solution.py:530
  49.8 1.7 %collective-permute-start.16 = (bf16[2,512,512]{2,1,0:T(8,128)(2,1)S(1)}, bf16[2,512,512]{2,1,0:T(8,128)(2,1)S(1)}, u32[]{:S(2)}, u32[]{:S(2)}) collective-permute-start(bf16[2,512,512]{2,1,0:T(8,128)(2,1)S(1)} %get-tuple-element.91), channel_id=1, source_target_pairs={{0,16},{8,24},{16,0},{24,8},{1,17},{9,25},{17,1},{25,9},{2,18},{10... | collective-permute-start | bytes 3145736 | tf_op jit(solution)/shard_map/ppermute | solution.py:522
  51.5 0.5 collective-permute-done.8.refs_1_
  52.0 3.2 %blend.15 = (f32[2,2048,512]{2,1,0:T(8,128)}, bf16[2,512,512]{2,1,0:T(8,128)(2,1)S(1)}, f32[2,4,160,128]{3,2,1,0:T(8,128)S(1)}) custom-call(s32[10]{0:T(128)S(1)} %pad_add_fusion.place, f32[160,128]{1,0:T(8,128)S(1)} %get-tuple-element.80.refs_0_.refs_2_, ...), custom_call_target="tpu_custom_call", output_to_operand_aliasing={{0}: (4, {}), {1}: (5, {})} | custom-call | flops 5368709120 | bytes 62914560 | tf_op jit(solution)/shard_map/blend/pallas_call | solution.py:123
  55.3 0.8 collective-permute-done.11.refs_5_
  56.0 0.6 add_far.2
  56.6 1.6 %collective-permute-start.12 = (f32[4,160,128]{2,1,0:T(8,128)S(1)}, f32[4,160,128]{2,1,0:T(8,128)S(1)}, u32[]{:S(2)}, u32[]{:S(2)}) collective-permute-start(f32[4,160,128]{2,1,0:T(8,128)S(1)} %slice_bitcast_fusion), channel_id=1, source_target_pairs={{0,1},{1,0},{2,3},{3,2},{4,5},{5,4},{6,7},{7,6},{8,9},{9,8},{10,11... | collective-permute-start | bytes 983048 | tf_op jit(solution)/shard_map/ppermute | solution.py:527
  58.2 2.8 %collective-permute-start.15 = (f32[160,128]{1,0:T(8,128)S(1)}, f32[160,128]{1,0:T(8,128)S(1)}, u32[]{:S(2)}, u32[]{:S(2)}) collective-permute-start(f32[160,128]{1,0:T(8,128)S(1)} %get-tuple-element.88.refs_0_.refs_1_), channel_id=1, source_target_pairs={{0,6},{1,7},{2,4},{3,5},{4,2},{5,3},{6,0},{7,1},{8,14},{9,15},{10,... | collective-permute-start | bytes 245768 | tf_op jit(solution)/shard_map/ppermute | solution.py:530
  61.1 1.5 %collective-permute-start.13 = (f32[160,128]{1,0:T(8,128)S(1)}, f32[160,128]{1,0:T(8,128)S(1)}, u32[]{:S(2)}, u32[]{:S(2)}) collective-permute-start(f32[160,128]{1,0:T(8,128)S(1)} %get-tuple-element.88.refs_0_.refs_1_), channel_id=1, source_target_pairs={{0,2},{1,3},{2,0},{3,1},{4,6},{5,7},{6,4},{7,5},{8,10},{9,11},{10,... | collective-permute-start | bytes 245768 | tf_op jit(solution)/shard_map/ppermute | solution.py:530
  62.6 3.8 %collective-permute-done.12.refs_2_ = f32[4,160,128]{2,1,0:T(8,128)S(1)} collective-permute-done((f32[4,160,128]{2,1,0:T(8,128)S(1)}, f32[4,160,128]{2,1,0:T(8,128)S(1)}, u32[]{:S(2)}, u32[]{:S(2)}) %collective-permute-start.12) | collective-permute-done | bytes 327712 | tf_op jit(solution)/shard_map/ppermute | solution.py:527
  66.5 0.6 add_near.3
  67.0 1.7 %collective-permute-start.17 = (f32[160,128]{1,0:T(8,128)S(1)}, f32[160,128]{1,0:T(8,128)S(1)}, u32[]{:S(2)}, u32[]{:S(2)}) collective-permute-start(f32[160,128]{1,0:T(8,128)S(1)} %get-tuple-element.93), channel_id=1, source_target_pairs={{0,2},{1,3},{2,0},{3,1},{4,6},{5,7},{6,4},{7,5},{8,10},{9,11},{10,... | collective-permute-start | bytes 245768 | tf_op jit(solution)/shard_map/ppermute | solution.py:530
  68.7 2.5 %collective-permute-start.18 = (f32[160,128]{1,0:T(8,128)S(1)}, f32[160,128]{1,0:T(8,128)S(1)}, u32[]{:S(2)}, u32[]{:S(2)}) collective-permute-start(f32[160,128]{1,0:T(8,128)S(1)} %get-tuple-element.94), channel_id=1, source_target_pairs={{0,4},{1,5},{2,6},{3,7},{4,0},{5,1},{6,2},{7,3},{8,12},{9,13},{10,... | collective-permute-start | bytes 245768 | tf_op jit(solution)/shard_map/ppermute | solution.py:530
  71.2 0.3 collective-permute-start.19
  71.5 0.6 stack.10.refs_0_.refs_1_
  72.1 6.0 %collective-permute-done.18.refs_5_ = f32[160,128]{1,0:T(8,128)S(1)} collective-permute-done((f32[160,128]{1,0:T(8,128)S(1)}, f32[160,128]{1,0:T(8,128)S(1)}, u32[]{:S(2)}, u32[]{:S(2)}) %collective-permute-start.18) | collective-permute-done | bytes 81952 | tf_op jit(solution)/shard_map/ppermute | solution.py:530
  78.1 0.6 add_far.3
  78.7 0.4 collective-permute-start.24
  79.1 1.5 %collective-permute-start.23 = (f32[4,160,128]{2,1,0:T(8,128)S(1)}, f32[4,160,128]{2,1,0:T(8,128)S(1)}, u32[]{:S(2)}, u32[]{:S(2)}) collective-permute-start(f32[4,160,128]{2,1,0:T(8,128)S(1)} %stack.10.refs_0_.refs_1_), channel_id=1, source_target_pairs={{0,1},{1,0},{2,3},{3,2},{4,5},{5,4},{6,7},{7,6},{8,9},{9,8},{10,11... | collective-permute-start | bytes 983048 | tf_op jit(solution)/shard_map/ppermute | solution.py:527
  80.7 2.2 %collective-permute-start.22 = (f32[160,128]{1,0:T(8,128)S(1)}, f32[160,128]{1,0:T(8,128)S(1)}, u32[]{:S(2)}, u32[]{:S(2)}) collective-permute-start(f32[160,128]{1,0:T(8,128)S(1)} %get-tuple-element.96.refs_0_.refs_1_), channel_id=1, source_target_pairs={{0,6},{1,7},{2,4},{3,5},{4,2},{5,3},{6,0},{7,1},{8,14},{9,15},{10,... | collective-permute-start | bytes 245768 | tf_op jit(solution)/shard_map/ppermute | solution.py:530
  82.9 1.0 collective-permute-start.21
  83.9 1.2 collective-permute-start.20
  85.1 2.7 %collective-permute-done.22.refs_4_ = f32[160,128]{1,0:T(8,128)S(1)} collective-permute-done((f32[160,128]{1,0:T(8,128)S(1)}, f32[160,128]{1,0:T(8,128)S(1)}, u32[]{:S(2)}, u32[]{:S(2)}) %collective-permute-start.22) | collective-permute-done | bytes 81952 | tf_op jit(solution)/shard_map/ppermute | solution.py:530
  87.7 2.8 %collective-permute-done.21.refs_3_ = f32[160,128]{1,0:T(8,128)S(1)} collective-permute-done((f32[160,128]{1,0:T(8,128)S(1)}, f32[160,128]{1,0:T(8,128)S(1)}, u32[]{:S(2)}, u32[]{:S(2)}) %collective-permute-start.21) | collective-permute-done | bytes 81952 | tf_op jit(solution)/shard_map/ppermute | solution.py:530
  90.6 0.6 stack.11.refs_0_.refs_2_
  91.2 0.6 collective-permute-start.25
  91.7 7.4 %polynomial.2.refs_0_.refs_3_ = bf16[1344,128]{1,0:T(8,128)(2,1)S(1)} custom-call(s32[10]{0:T(128)S(1)} %pad_add_fusion.place, f32[4,160,128]{2,1,0:T(8,128)S(1)} %stack.11.refs_0_.refs_2_, f32[4,160,128]{2,1,0:T(8,128)S(1)} %stack.10.refs_0_.refs_1_, f32[4,160,128]{2,1,0:T(8,128)S(1)} %collective-permute-done.23.refs_2_), custom_call_target="tpu_custom_call" | custom-call | flops 2684354560 | bytes 1310720 | tf_op jit(solution)/shard_map/polynomial/pallas_call | solution.py:123
  99.2 0.5 collective-permute-start.29
  99.7 0.5 collective-permute-start.27
  100.2 1.5 %collective-permute-done.24.refs_1_ = bf16[2,512,512]{2,1,0:T(8,128)(2,1)S(1)} collective-permute-done((bf16[2,512,512]{2,1,0:T(8,128)(2,1)S(1)}, bf16[2,512,512]{2,1,0:T(8,128)(2,1)S(1)}, u32[]{:S(2)}, u32[]{:S(2)}) %collective-permute-start.24) | collective-permute-done | bytes 1048608 | tf_op jit(solution)/shard_map/ppermute | solution.py:522
  101.8 7.6 %polynomial.3.refs_0_.refs_3_ = bf16[1344,128]{1,0:T(8,128)(2,1)S(1)} custom-call(s32[10]{0:T(128)S(1)} %pad_add_fusion.place, bf16[1344,128]{1,0:T(8,128)(2,1)S(1)} %polynomial.2.refs_0_.refs_3_, bf16[2,512,512]{2,1,0:T(8,128)(2,1)S(1)} %collective-permute-done.24.refs_1_, f32[4,160,128]{2,1,0:T(8,128)S(1)} %stack.11.refs_0_.refs_2_, ...), custom_call_target="tpu_custom_call" | custom-call | flops 2684354560 | bytes 1310720 | tf_op jit(solution)/shard_map/polynomial/pallas_call | solution.py:123
  109.4 1.5 %collective-permute-start.31 = (bf16[1344,128]{1,0:T(8,128)(2,1)S(1)}, bf16[1344,128]{1,0:T(8,128)(2,1)S(1)}, u32[]{:S(2)}, u32[]{:S(2)}) collective-permute-start(bf16[1344,128]{1,0:T(8,128)(2,1)S(1)} %polynomial.3.refs_0_.refs_3_), channel_id=1, source_target_pairs={{0,16},{8,24},{16,0},{24,8},{1,17},{9,25},{17,1},{25,9},{2,18},{10... | collective-permute-start | bytes 1032200 | tf_op jit(solution)/shard_map/ppermute | solution.py:549
  110.9 2.1 %finish.5 = (bf16[8,512,512]{2,1,0:T(8,128)(2,1)}, f32[8,128]{1,0:T(8,128)S(1)}) custom-call(s32[10]{0:T(128)S(1)} %pad_add_fusion.place, bf16[1344,128]{1,0:T(8,128)(2,1)S(1)} %polynomial.3.refs_0_.refs_3_, bf16[512,512]{1,0:T(8,128)(2,1)S(1)} %get-tuple-element.98.refs_1_, bf16[512,512]{1,0:T(8,128)(2,1)S(1)} %collective-permute-done.3.refs_1_.refs_2_, ...), custom_call_target="tpu_custom_call" | custom-call | flops 10737418240 | bytes 41943040 | tf_op jit(solution)/shard_map/finish/pallas_call | solution.py:123
  113.0 0.5 step.2.refs_0_.refs_3_
  113.5 0.6 collective-permute-start.30
  114.1 0.1 collective-permute-start.32
  114.2 2.1 %finish.6 = (bf16[8,512,512]{2,1,0:T(8,128)(2,1)}, f32[8,128]{1,0:T(8,128)S(1)}) custom-call(s32[10]{0:T(128)S(1)} %pad_add_fusion.place, bf16[1344,128]{1,0:T(8,128)(2,1)S(1)} %step.2.refs_0_.refs_3_, bf16[512,512]{1,0:T(8,128)(2,1)S(1)} %get-tuple-element.100.refs_1_, ...), custom_call_target="tpu_custom_call", output_to_operand_aliasing={{0}: (6, {})} | custom-call | flops 10737418240 | bytes 41943040 | tf_op jit(solution)/shard_map/finish/pallas_call | solution.py:123
  116.3 2.1 %finish.7 = (bf16[8,512,512]{2,1,0:T(8,128)(2,1)}, f32[8,128]{1,0:T(8,128)S(1)}) custom-call(s32[10]{0:T(128)S(1)} %pad_add_fusion.place, f32[8,128]{1,0:T(8,128)S(1)} %get-tuple-element.102.refs_0_, bf16[2,512,512]{2,1,0:T(8,128)(2,1)S(1)} %collective-permute-done.16.refs_1_, ...), custom_call_target="tpu_custom_call", output_to_operand_aliasing={{0}: (6, {})} | custom-call | flops 10737418240 | bytes 41943040 | tf_op jit(solution)/shard_map/finish/pallas_call | solution.py:123
  118.4 0.5 step.3.refs_0_.refs_2_
  119.0 0.5 collective-permute-start.33
  119.5 1.8 %finish.8 = (bf16[8,512,512]{2,1,0:T(8,128)(2,1)}, f32[8,128]{1,0:T(8,128)S(1)}) custom-call(s32[10]{0:T(128)S(1)} %pad_add_fusion.place, bf16[1344,128]{1,0:T(8,128)(2,1)S(1)} %step.3.refs_0_.refs_2_, bf16[2,512,512]{2,1,0:T(8,128)(2,1)S(1)} %collective-permute-done.24.refs_1_, ...), custom_call_target="tpu_custom_call", output_to_operand_aliasing={{0}: (4, {})} | custom-call | flops 5368709120 | bytes 20971520 | tf_op jit(solution)/shard_map/finish/pallas_call | solution.py:123
  121.3 2.4 %finish.9 = (bf16[8,512,512]{2,1,0:T(8,128)(2,1)}, f32[8,128]{1,0:T(8,128)}) custom-call(s32[10]{0:T(128)S(1)} %pad_add_fusion.place, f32[8,128]{1,0:T(8,128)S(1)} %get-tuple-element.106.refs_0_, bf16[2,512,512]{2,1,0:T(8,128)(2,1)S(1)} %collective-permute-done.32.refs_1_, ...), custom_call_target="tpu_custom_call", output_to_operand_aliasing={{0}: (4, {})} | custom-call | flops 5368709120 | bytes 20971520 | tf_op jit(solution)/shard_map/finish/pallas_call | solution.py:123
  (33 shorter events, 0.3 us)
Async XLA Ops:
  3.0 20.9 %collective-permute-start.2 = (bf16[512,512]{1,0:T(8,128)(2,1)S(1)}, bf16[512,512]{1,0:T(8,128)(2,1)S(1)}, u32[]{:S(2)}, u32[]{:S(2)}) collective-permute-start(bf16[512,512]{1,0:T(8,128)(2,1)S(1)} %pick.2.refs_0_), channel_id=1, source_target_pairs={{0,16},{8,24},{16,0},{24,8},{1,17},{9,25},{17,1},{25,9},{2,18},{10... | collective-permute-start | bytes 1572872 | tf_op jit(solution)/shard_map/ppermute | solution.py:494
  8.3 8.8 %collective-permute-start = (bf16[512,512]{1,0:T(8,128)(2,1)S(1)}, bf16[512,512]{1,0:T(8,128)(2,1)S(1)}, u32[]{:S(2)}, u32[]{:S(2)}) collective-permute-start(bf16[512,512]{1,0:T(8,128)(2,1)S(1)} %get-tuple-element.63), channel_id=1, source_target_pairs={{0,8},{8,0},{16,24},{24,16},{1,9},{9,1},{17,25},{25,17},{2,10},{10... | collective-permute-start | bytes 1572872 | tf_op jit(solution)/shard_map/ppermute | solution.py:494
  8.3 21.2 %collective-permute-start.4 = (bf16[512,512]{1,0:T(8,128)(2,1)S(1)}, bf16[512,512]{1,0:T(8,128)(2,1)S(1)}, u32[]{:S(2)}, u32[]{:S(2)}) collective-permute-start(bf16[512,512]{1,0:T(8,128)(2,1)S(1)} %get-tuple-element.56.refs_0_), channel_id=1, source_target_pairs={{0,24},{8,16},{16,8},{24,0},{1,25},{9,17},{17,9},{25,1},{2,26},{10... | collective-permute-start | bytes 1572872 | tf_op jit(solution)/shard_map/ppermute | solution.py:494
  11.8 8.6 %collective-permute-start.1 = (bf16[512,512]{1,0:T(8,128)(2,1)S(1)}, bf16[512,512]{1,0:T(8,128)(2,1)S(1)}, u32[]{:S(2)}, u32[]{:S(2)}) collective-permute-start(bf16[512,512]{1,0:T(8,128)(2,1)S(1)} %get-tuple-element.66), channel_id=1, source_target_pairs={{0,8},{8,0},{16,24},{24,16},{1,9},{9,1},{17,25},{25,17},{2,10},{10... | collective-permute-start | bytes 1572872 | tf_op jit(solution)/shard_map/ppermute | solution.py:494
  12.1 29.1 %collective-permute-start.6 = (bf16[512,512]{1,0:T(8,128)(2,1)S(1)}, bf16[512,512]{1,0:T(8,128)(2,1)S(1)}, u32[]{:S(2)}, u32[]{:S(2)}) collective-permute-start(bf16[512,512]{1,0:T(8,128)(2,1)S(1)} %get-tuple-element.76), channel_id=1, source_target_pairs={{0,16},{8,24},{16,0},{24,8},{1,17},{9,25},{17,1},{25,9},{2,18},{10... | collective-permute-start | bytes 1572872 | tf_op jit(solution)/shard_map/ppermute | solution.py:494
  17.1 34.9 %collective-permute-start.8 = (bf16[512,512]{1,0:T(8,128)(2,1)S(1)}, bf16[512,512]{1,0:T(8,128)(2,1)S(1)}, u32[]{:S(2)}, u32[]{:S(2)}) collective-permute-start(bf16[512,512]{1,0:T(8,128)(2,1)S(1)} %get-tuple-element.81), channel_id=1, source_target_pairs={{0,24},{8,16},{16,8},{24,0},{1,25},{9,17},{17,9},{25,1},{2,26},{10... | collective-permute-start | bytes 1572872 | tf_op jit(solution)/shard_map/ppermute | solution.py:494
  20.3 9.2 %collective-permute-start.3 = (bf16[512,512]{1,0:T(8,128)(2,1)S(1)}, bf16[512,512]{1,0:T(8,128)(2,1)S(1)}, u32[]{:S(2)}, u32[]{:S(2)}) collective-permute-start(bf16[512,512]{1,0:T(8,128)(2,1)S(1)} %get-tuple-element.71), channel_id=1, source_target_pairs={{0,8},{8,0},{16,24},{24,16},{1,9},{9,1},{17,25},{25,17},{2,10},{10... | collective-permute-start | bytes 1572872 | tf_op jit(solution)/shard_map/ppermute | solution.py:520
  23.9 17.3 %collective-permute-start.5 = (bf16[512,512]{1,0:T(8,128)(2,1)S(1)}, bf16[512,512]{1,0:T(8,128)(2,1)S(1)}, u32[]{:S(2)}, u32[]{:S(2)}) collective-permute-start(bf16[512,512]{1,0:T(8,128)(2,1)S(1)} %get-tuple-element.75), channel_id=1, source_target_pairs={{0,8},{8,0},{16,24},{24,16},{1,9},{9,1},{17,25},{25,17},{2,10},{10... | collective-permute-start | bytes 1572872 | tf_op jit(solution)/shard_map/ppermute | solution.py:520
  32.8 11.6 %collective-permute-start.7 = (f32[4,160,128]{2,1,0:T(8,128)S(1)}, f32[4,160,128]{2,1,0:T(8,128)S(1)}, u32[]{:S(2)}, u32[]{:S(2)}) collective-permute-start(f32[4,160,128]{2,1,0:T(8,128)S(1)} %slice_bitcast_fusion.1), channel_id=1, source_target_pairs={{0,1},{1,0},{2,3},{3,2},{4,5},{5,4},{6,7},{7,6},{8,9},{9,8},{10,11... | collective-permute-start | bytes 983048 | tf_op jit(solution)/shard_map/ppermute | solution.py:527
  45.0 10.3 %collective-permute-start.9 = (f32[160,128]{1,0:T(8,128)S(1)}, f32[160,128]{1,0:T(8,128)S(1)}, u32[]{:S(2)}, u32[]{:S(2)}) collective-permute-start(f32[160,128]{1,0:T(8,128)S(1)} %get-tuple-element.85), channel_id=1, source_target_pairs={{0,2},{1,3},{2,0},{3,1},{4,6},{5,7},{6,4},{7,5},{8,10},{9,11},{10,... | collective-permute-start | bytes 245768 | tf_op jit(solution)/shard_map/ppermute | solution.py:530
  47.2 8.1 %collective-permute-start.10 = (f32[160,128]{1,0:T(8,128)S(1)}, f32[160,128]{1,0:T(8,128)S(1)}, u32[]{:S(2)}, u32[]{:S(2)}) collective-permute-start(f32[160,128]{1,0:T(8,128)S(1)} %get-tuple-element.86), channel_id=1, source_target_pairs={{0,4},{1,5},{2,6},{3,7},{4,0},{5,1},{6,2},{7,3},{8,12},{9,13},{10,... | collective-permute-start | bytes 245768 | tf_op jit(solution)/shard_map/ppermute | solution.py:530
  49.8 6.3 %collective-permute-start.11 = (f32[160,128]{1,0:T(8,128)S(1)}, f32[160,128]{1,0:T(8,128)S(1)}, u32[]{:S(2)}, u32[]{:S(2)}) collective-permute-start(f32[160,128]{1,0:T(8,128)S(1)} %get-tuple-element.87), channel_id=1, source_target_pairs={{0,6},{1,7},{2,4},{3,5},{4,2},{5,3},{6,0},{7,1},{8,14},{9,15},{10,... | collective-permute-start | bytes 245768 | tf_op jit(solution)/shard_map/ppermute | solution.py:530
  49.8 28.3 %collective-permute-start.16 = (bf16[2,512,512]{2,1,0:T(8,128)(2,1)S(1)}, bf16[2,512,512]{2,1,0:T(8,128)(2,1)S(1)}, u32[]{:S(2)}, u32[]{:S(2)}) collective-permute-start(bf16[2,512,512]{2,1,0:T(8,128)(2,1)S(1)} %get-tuple-element.91), channel_id=1, source_target_pairs={{0,16},{8,24},{16,0},{24,8},{1,17},{9,25},{17,1},{25,9},{2,18},{10... | collective-permute-start | bytes 3145736 | tf_op jit(solution)/shard_map/ppermute | solution.py:522
  56.6 9.8 %collective-permute-start.12 = (f32[4,160,128]{2,1,0:T(8,128)S(1)}, f32[4,160,128]{2,1,0:T(8,128)S(1)}, u32[]{:S(2)}, u32[]{:S(2)}) collective-permute-start(f32[4,160,128]{2,1,0:T(8,128)S(1)} %slice_bitcast_fusion), channel_id=1, source_target_pairs={{0,1},{1,0},{2,3},{3,2},{4,5},{5,4},{6,7},{7,6},{8,9},{9,8},{10,11... | collective-permute-start | bytes 983048 | tf_op jit(solution)/shard_map/ppermute | solution.py:527
  58.2 10.5 %collective-permute-start.15 = (f32[160,128]{1,0:T(8,128)S(1)}, f32[160,128]{1,0:T(8,128)S(1)}, u32[]{:S(2)}, u32[]{:S(2)}) collective-permute-start(f32[160,128]{1,0:T(8,128)S(1)} %get-tuple-element.88.refs_0_.refs_1_), channel_id=1, source_target_pairs={{0,6},{1,7},{2,4},{3,5},{4,2},{5,3},{6,0},{7,1},{8,14},{9,15},{10,... | collective-permute-start | bytes 245768 | tf_op jit(solution)/shard_map/ppermute | solution.py:530
  61.1 10.1 %collective-permute-start.14 = (f32[160,128]{1,0:T(8,128)S(1)}, f32[160,128]{1,0:T(8,128)S(1)}, u32[]{:S(2)}, u32[]{:S(2)}) collective-permute-start(f32[160,128]{1,0:T(8,128)S(1)} %get-tuple-element.88.refs_0_.refs_1_), channel_id=1, source_target_pairs={{0,4},{1,5},{2,6},{3,7},{4,0},{5,1},{6,2},{7,3},{8,12},{9,13},{10,... | collective-permute-start | bytes 245768 | tf_op jit(solution)/shard_map/ppermute | solution.py:530
  61.1 10.4 %collective-permute-start.13 = (f32[160,128]{1,0:T(8,128)S(1)}, f32[160,128]{1,0:T(8,128)S(1)}, u32[]{:S(2)}, u32[]{:S(2)}) collective-permute-start(f32[160,128]{1,0:T(8,128)S(1)} %get-tuple-element.88.refs_0_.refs_1_), channel_id=1, source_target_pairs={{0,2},{1,3},{2,0},{3,1},{4,6},{5,7},{6,4},{7,5},{8,10},{9,11},{10,... | collective-permute-start | bytes 245768 | tf_op jit(solution)/shard_map/ppermute | solution.py:530
  67.0 5.0 %collective-permute-start.17 = (f32[160,128]{1,0:T(8,128)S(1)}, f32[160,128]{1,0:T(8,128)S(1)}, u32[]{:S(2)}, u32[]{:S(2)}) collective-permute-start(f32[160,128]{1,0:T(8,128)S(1)} %get-tuple-element.93), channel_id=1, source_target_pairs={{0,2},{1,3},{2,0},{3,1},{4,6},{5,7},{6,4},{7,5},{8,10},{9,11},{10,... | collective-permute-start | bytes 245768 | tf_op jit(solution)/shard_map/ppermute | solution.py:530
  68.7 9.4 %collective-permute-start.18 = (f32[160,128]{1,0:T(8,128)S(1)}, f32[160,128]{1,0:T(8,128)S(1)}, u32[]{:S(2)}, u32[]{:S(2)}) collective-permute-start(f32[160,128]{1,0:T(8,128)S(1)} %get-tuple-element.94), channel_id=1, source_target_pairs={{0,4},{1,5},{2,6},{3,7},{4,0},{5,1},{6,2},{7,3},{8,12},{9,13},{10,... | collective-permute-start | bytes 245768 | tf_op jit(solution)/shard_map/ppermute | solution.py:530
  71.2 6.9 %collective-permute-start.19 = (f32[160,128]{1,0:T(8,128)S(1)}, f32[160,128]{1,0:T(8,128)S(1)}, u32[]{:S(2)}, u32[]{:S(2)}) collective-permute-start(f32[160,128]{1,0:T(8,128)S(1)} %get-tuple-element.95), channel_id=1, source_target_pairs={{0,6},{1,7},{2,4},{3,5},{4,2},{5,3},{6,0},{7,1},{8,14},{9,15},{10,... | collective-permute-start | bytes 245768 | tf_op jit(solution)/shard_map/ppermute | solution.py:530
  78.7 23.1 %collective-permute-start.24 = (bf16[2,512,512]{2,1,0:T(8,128)(2,1)S(1)}, bf16[2,512,512]{2,1,0:T(8,128)(2,1)S(1)}, u32[]{:S(2)}, u32[]{:S(2)}) collective-permute-start(bf16[2,512,512]{2,1,0:T(8,128)(2,1)S(1)} %get-tuple-element.97), channel_id=1, source_target_pairs={{0,16},{8,24},{16,0},{24,8},{1,17},{9,25},{17,1},{25,9},{2,18},{10... | collective-permute-start | bytes 3145736 | tf_op jit(solution)/shard_map/ppermute | solution.py:522
  79.1 12.6 %collective-permute-start.23 = (f32[4,160,128]{2,1,0:T(8,128)S(1)}, f32[4,160,128]{2,1,0:T(8,128)S(1)}, u32[]{:S(2)}, u32[]{:S(2)}) collective-permute-start(f32[4,160,128]{2,1,0:T(8,128)S(1)} %stack.10.refs_0_.refs_1_), channel_id=1, source_target_pairs={{0,1},{1,0},{2,3},{3,2},{4,5},{5,4},{6,7},{7,6},{8,9},{9,8},{10,11... | collective-permute-start | bytes 983048 | tf_op jit(solution)/shard_map/ppermute | solution.py:527
  80.7 7.1 %collective-permute-start.22 = (f32[160,128]{1,0:T(8,128)S(1)}, f32[160,128]{1,0:T(8,128)S(1)}, u32[]{:S(2)}, u32[]{:S(2)}) collective-permute-start(f32[160,128]{1,0:T(8,128)S(1)} %get-tuple-element.96.refs_0_.refs_1_), channel_id=1, source_target_pairs={{0,6},{1,7},{2,4},{3,5},{4,2},{5,3},{6,0},{7,1},{8,14},{9,15},{10,... | collective-permute-start | bytes 245768 | tf_op jit(solution)/shard_map/ppermute | solution.py:530
  82.9 7.7 %collective-permute-start.21 = (f32[160,128]{1,0:T(8,128)S(1)}, f32[160,128]{1,0:T(8,128)S(1)}, u32[]{:S(2)}, u32[]{:S(2)}) collective-permute-start(f32[160,128]{1,0:T(8,128)S(1)} %get-tuple-element.96.refs_0_.refs_1_), channel_id=1, source_target_pairs={{0,4},{1,5},{2,6},{3,7},{4,0},{5,1},{6,2},{7,3},{8,12},{9,13},{10,... | collective-permute-start | bytes 245768 | tf_op jit(solution)/shard_map/ppermute | solution.py:530
  83.9 6.7 %collective-permute-start.20 = (f32[160,128]{1,0:T(8,128)S(1)}, f32[160,128]{1,0:T(8,128)S(1)}, u32[]{:S(2)}, u32[]{:S(2)}) collective-permute-start(f32[160,128]{1,0:T(8,128)S(1)} %get-tuple-element.96.refs_0_.refs_1_), channel_id=1, source_target_pairs={{0,2},{1,3},{2,0},{3,1},{4,6},{5,7},{6,4},{7,5},{8,10},{9,11},{10,... | collective-permute-start | bytes 245768 | tf_op jit(solution)/shard_map/ppermute | solution.py:530
  91.2 9.1 %collective-permute-start.25 = (f32[4,160,128]{2,1,0:T(8,128)S(1)}, f32[4,160,128]{2,1,0:T(8,128)S(1)}, u32[]{:S(2)}, u32[]{:S(2)}) collective-permute-start(f32[4,160,128]{2,1,0:T(8,128)S(1)} %stack.11.refs_0_.refs_2_), channel_id=1, source_target_pairs={{0,1},{1,0},{2,3},{3,2},{4,5},{5,4},{6,7},{7,6},{8,9},{9,8},{10,11... | collective-permute-start | bytes 983048 | tf_op jit(solution)/shard_map/ppermute | solution.py:527
  99.2 11.7 %collective-permute-start.26 = (bf16[1344,128]{1,0:T(8,128)(2,1)S(1)}, bf16[1344,128]{1,0:T(8,128)(2,1)S(1)}, u32[]{:S(2)}, u32[]{:S(2)}) collective-permute-start(bf16[1344,128]{1,0:T(8,128)(2,1)S(1)} %polynomial.2.refs_0_.refs_3_), channel_id=1, source_target_pairs={{0,8},{8,0},{16,24},{24,16},{1,9},{9,1},{17,25},{25,17},{2,10},{10... | collective-permute-start | bytes 1032200 | tf_op jit(solution)/shard_map/ppermute | solution.py:551
  99.2 17.1 %collective-permute-start.29 = (bf16[2,512,512]{2,1,0:T(8,128)(2,1)S(1)}, bf16[2,512,512]{2,1,0:T(8,128)(2,1)S(1)}, u32[]{:S(2)}, u32[]{:S(2)}) collective-permute-start(bf16[2,512,512]{2,1,0:T(8,128)(2,1)S(1)} %collective-permute-done.16.refs_1_), channel_id=1, source_target_pairs={{0,8},{8,0},{16,24},{24,16},{1,9},{9,1},{17,25},{25,17},{2,10},{10... | collective-permute-start | bytes 3145736 | tf_op jit(solution)/shard_map/ppermute | solution.py:524
  99.7 13.3 %collective-permute-start.27 = (bf16[1344,128]{1,0:T(8,128)(2,1)S(1)}, bf16[1344,128]{1,0:T(8,128)(2,1)S(1)}, u32[]{:S(2)}, u32[]{:S(2)}) collective-permute-start(bf16[1344,128]{1,0:T(8,128)(2,1)S(1)} %polynomial.2.refs_0_.refs_3_), channel_id=1, source_target_pairs={{0,16},{8,24},{16,0},{24,8},{1,17},{9,25},{17,1},{25,9},{2,18},{10... | collective-permute-start | bytes 1032200 | tf_op jit(solution)/shard_map/ppermute | solution.py:549
  109.4 9.0 %collective-permute-start.31 = (bf16[1344,128]{1,0:T(8,128)(2,1)S(1)}, bf16[1344,128]{1,0:T(8,128)(2,1)S(1)}, u32[]{:S(2)}, u32[]{:S(2)}) collective-permute-start(bf16[1344,128]{1,0:T(8,128)(2,1)S(1)} %polynomial.3.refs_0_.refs_3_), channel_id=1, source_target_pairs={{0,16},{8,24},{16,0},{24,8},{1,17},{9,25},{17,1},{25,9},{2,18},{10... | collective-permute-start | bytes 1032200 | tf_op jit(solution)/shard_map/ppermute | solution.py:549
  110.9 3.3 %collective-permute-start.28 = (bf16[1344,128]{1,0:T(8,128)(2,1)S(1)}, bf16[1344,128]{1,0:T(8,128)(2,1)S(1)}, u32[]{:S(2)}, u32[]{:S(2)}) collective-permute-start(bf16[1344,128]{1,0:T(8,128)(2,1)S(1)} %polynomial.3.refs_0_.refs_3_), channel_id=1, source_target_pairs={{0,8},{8,0},{16,24},{24,16},{1,9},{9,1},{17,25},{25,17},{2,10},{10... | collective-permute-start | bytes 1032200 | tf_op jit(solution)/shard_map/ppermute | solution.py:551
  113.5 2.8 %collective-permute-start.30 = (bf16[1344,128]{1,0:T(8,128)(2,1)S(1)}, bf16[1344,128]{1,0:T(8,128)(2,1)S(1)}, u32[]{:S(2)}, u32[]{:S(2)}) collective-permute-start(bf16[1344,128]{1,0:T(8,128)(2,1)S(1)} %step.2.refs_0_.refs_3_), channel_id=1, source_target_pairs={{0,8},{8,0},{16,24},{24,16},{1,9},{9,1},{17,25},{25,17},{2,10},{10... | collective-permute-start | bytes 1032200 | tf_op jit(solution)/shard_map/ppermute | solution.py:556
  114.1 7.2 %collective-permute-start.32 = (bf16[2,512,512]{2,1,0:T(8,128)(2,1)S(1)}, bf16[2,512,512]{2,1,0:T(8,128)(2,1)S(1)}, u32[]{:S(2)}, u32[]{:S(2)}) collective-permute-start(bf16[2,512,512]{2,1,0:T(8,128)(2,1)S(1)} %collective-permute-done.24.refs_1_), channel_id=1, source_target_pairs={{0,8},{8,0},{16,24},{24,16},{1,9},{9,1},{17,25},{25,17},{2,10},{10... | collective-permute-start | bytes 3145736 | tf_op jit(solution)/shard_map/ppermute | solution.py:524
  119.0 2.3 %collective-permute-start.33 = (bf16[1344,128]{1,0:T(8,128)(2,1)S(1)}, bf16[1344,128]{1,0:T(8,128)(2,1)S(1)}, u32[]{:S(2)}, u32[]{:S(2)}) collective-permute-start(bf16[1344,128]{1,0:T(8,128)(2,1)S(1)} %step.3.refs_0_.refs_2_), channel_id=1, source_target_pairs={{0,8},{8,0},{16,24},{24,16},{1,9},{9,1},{17,25},{25,17},{2,10},{10... | collective-permute-start | bytes 1032200 | tf_op jit(solution)/shard_map/ppermute | solution.py:556

commit v5 on v4

--- a/solution.py
+++ b/solution.py
@@ -17,9 +17,11 @@
 momentum_decay = 0.95
 epsilon = 1e-07
 
-BLOCKS = [(i, j) for i in range(RANK // TILE) for j in range(i, RANK // TILE)]
-PACKED = len(BLOCKS) * TILE
-TAIL = 16
+SIDES = RANK // TILE
+ABOVE = [(i, j) for i in range(SIDES) for j in range(i + 1, SIDES)]
+TWOS = [(i, i + 1) for i in range(0, SIDES, 2)]
+DIAGONALS = (len(ABOVE) + len(TWOS)) * TILE
+POLY_ROWS = DIAGONALS + 16
 
 f32, bf16 = jnp.float32, jnp.bfloat16
 
@@ -40,11 +42,44 @@
     return place[place.shape[0] - 1]
 
 
+def packed_rows(group):
+    return -(-(DIAGONALS + 8) // (8 * group)) * (8 * group)
+
+
+def block_ids():
+    return (
+        lax.broadcasted_iota(jnp.int32, (TILE, TILE), 0),
+        lax.broadcasted_iota(jnp.int32, (TILE, TILE), 1),
+    )
+
+
+def diagonal_of(block):
+    row, column = block_ids()
+    return jnp.sum(jnp.where(row == column, block, 0.0), axis=0, keepdims=True)
+
+
+def pack(block):
+    row, column = block_ids()
+    blocks = [block(i, j) for i, j in ABOVE]
+    blocks += [jnp.where(row <= column, block(i, i), block(j, j)) for i, j in TWOS]
+    return blocks, [diagonal_of(block(j, j)) for _, j in TWOS]
+
+
+def unpack(blocks, diagonals):
+    row, column = block_ids()
+    parts = dict(zip(ABOVE, blocks))
+    for (i, j), both, diagonal in zip(TWOS, blocks[len(ABOVE) :], diagonals):
+        turned = both.T
+        parts[i, i] = jnp.where(row <= column, both, turned)
+        parts[j, j] = jnp.where(row > column, both, jnp.where(row < column, turned, diagonal))
+    return parts
+
+
 def partners(size, step):
     return [(i, i ^ step) for i in range(size)]
 
 
-def blend_kernel(shares, buffers, has_sum, *refs):
+def blend_kernel(buffers, has_sum, *refs):
     refs = list(refs)
     place = refs.pop(0)
     gradient, momentum = refs.pop(0), refs.pop(0)
@@ -62,28 +97,99 @@
     renewed[...] = m
     x = (g + momentum_decay * m).astype(bf16)
     rows[...] = x
-    half = RANK // 2
-    dims = (((0,), (0,)), ((), ()))
+    add_gram(held, x)
+
+    @pl.when(step == pl.num_programs(0) - 1)
+    def _():
+        total[...] = held[...]
+
+
+def add_gram(held, x):
+    half, dims = RANK // 2, (((0,), (0,)), ((), ()))
     upper = lax.dot_general(x[:, :half], x, dims, preferred_element_type=f32)
     lower = lax.dot_general(x[:, half:], x[:, half:], dims, preferred_element_type=f32)
-    for n, (i, j) in enumerate(BLOCKS):
-        part, i0, j0 = (upper, i, j) if i < half // TILE else (lower, i - half // TILE, j - half // TILE)
-        held[n * TILE : (n + 1) * TILE, :] += part[
-            i0 * TILE : (i0 + 1) * TILE, j0 * TILE : (j0 + 1) * TILE
-        ]
-
-    @pl.when(step == pl.num_programs(0) - 1)
-    def _():
-        if shares is None:
-            total[...] = held[...]
-        else:
-            near, far = shares
-            count = PACKED // (near * far)
-            for e1 in range(near):
-                for e2 in range(far):
-                    who = jnp.bitwise_xor(group_index(place), e2 * near + e1)
-                    start = pl.multiple_of(who * count, 8)
-                    total[e1, e2] = held[pl.ds(start, count), :]
+
+    def block(i, j):
+        part, i0, j0 = (upper, i, j) if i < SIDES // 2 else (lower, i - SIDES // 2, j - SIDES // 2)
+        return part[i0 * TILE : (i0 + 1) * TILE, j0 * TILE : (j0 + 1) * TILE]
+
+    blocks, diagonals = pack(block)
+    for n, part in enumerate(blocks):
+        held[n * TILE : (n + 1) * TILE, :] += part
+    for n, part in enumerate(diagonals):
+        held[DIAGONALS + n : DIAGONALS + n + 1, :] += part
+
+
+def fetch_kernel(slot, d, count, place, momentum, target, sem):
+    rows = target.shape[0]
+    start = pl.multiple_of(jnp.bitwise_xor(place[count], d) * rows, 8)
+    copy = pltpu.make_async_copy(momentum.at[slot, pl.ds(start, rows)], target, sem)
+    copy.start()
+    copy.wait()
+
+
+def fetch(line, momentum, slot, d, count, piece_rows):
+    return line.run(
+        functools.partial(fetch_kernel, slot, d, count),
+        [in_hbm(momentum)],
+        [IN_HBM],
+        [jax.ShapeDtypeStruct((piece_rows, RANK), f32)],
+        [IN_VMEM],
+        name="fetch",
+        scratch=[pltpu.SemaphoreType.DMA],
+        work=(0, 8 * piece_rows * RANK),
+    )[0]
+
+
+def blend_last_kernel(slot, d, count, place, gradient, momentum, _buffer, _pair, before, renewed, pair, total, held, new, sems):
+    rows = gradient.shape[0]
+    tile = min(256, rows)
+    first = jnp.bitwise_xor(place[count], d) * rows
+    copies = []
+    for n in range(rows // tile):
+        part = pl.ds(n * tile, tile)
+        g = gradient[part].astype(f32)
+        m = momentum_decay * momentum[part] + g
+        new[part] = m
+        target = renewed.at[slot, pl.ds(pl.multiple_of(first + n * tile, 8), tile)]
+        copies.append(pltpu.make_async_copy(new.at[part], target, sems.at[n]))
+        copies[-1].start()
+        pair[1, part] = (g + momentum_decay * m).astype(bf16)
+    held[...] = before[...]
+    add_gram(held, pair[1])
+    near, far, size, _ = total.shape
+    for e1 in range(near):
+        for e2 in range(far):
+            who = jnp.bitwise_xor(group_index(place), e2 * near + e1)
+            total[e1, e2] = held[pl.ds(pl.multiple_of(who * size, 8), size), :]
+    for copy in copies:
+        copy.wait()
+
+
+def blend_last(line, gradient, momentum, slot, d, count, buffer, pair, before, shares):
+    piece_rows = gradient.shape[0]
+    total = (*shares, before.shape[0] // (shares[0] * shares[1]), TILE)
+    return line.run(
+        functools.partial(blend_last_kernel, slot, d, count),
+        [gradient, momentum, in_hbm(buffer), pair, before],
+        [IN_VMEM, IN_VMEM, IN_HBM, IN_VMEM, IN_VMEM],
+        [
+            pltpu.HBM(buffer.shape, f32),
+            jax.ShapeDtypeStruct(pair.shape, bf16),
+            jax.ShapeDtypeStruct(total, f32),
+        ],
+        [IN_HBM, IN_VMEM, IN_VMEM],
+        name="blend_last",
+        token=2,
+        scratch=[
+            pltpu.VMEM(before.shape, f32),
+            pltpu.VMEM((piece_rows, RANK), f32),
+            pltpu.SemaphoreType.DMA((piece_rows // min(256, piece_rows),)),
+        ],
+        aliases={2: 0, 3: 1},
+        vmem=12,
+        work=(2 * piece_rows * RANK * RANK, piece_rows * RANK * 12),
+    )
 
 
 class Line:
@@ -174,7 +280,7 @@
     )
 
 
-def blend(line, gradient, momentum, slot, d, count, buffer, pair, before, shares):
+def blend(line, gradient, momentum, slot, d, count, buffer, pair, before, summed):
     slots = momentum.shape[0]
     piece_rows = gradient.shape[-2]
     tile = min(256, piece_rows)
@@ -201,15 +307,12 @@
     else:
         rows_shape = (2, piece_rows, RANK)
         rows_spec = pl.BlockSpec((None, tile, RANK), lambda i, p: (d % 2, i, 0))
+    total = (summed, TILE)
     if before is not None:
-        in_specs.append(pl.BlockSpec((PACKED, TILE), lambda i, p: (0, 0)))
+        in_specs.append(pl.BlockSpec(total, lambda i, p: (0, 0)))
         operands.append(before)
-    if shares is None:
-        total = (PACKED, TILE)
-    else:
-        total = (*shares, PACKED // (shares[0] * shares[1]), TILE)
-    return line.run(
-        functools.partial(blend_kernel, shares, len(aliases), before is not None),
+    return line.run(
+        functools.partial(blend_kernel, len(aliases), before is not None),
         operands,
         in_specs,
         [
@@ -220,12 +323,12 @@
         [
             momentum_spec,
             rows_spec,
-            pl.BlockSpec(total, lambda i, p: (0,) * len(total)),
+            pl.BlockSpec(total, lambda i, p: (0, 0)),
         ],
         name="blend",
         token=2,
         grid=(steps,),
-        scratch=[pltpu.VMEM((PACKED, TILE), f32)],
+        scratch=[pltpu.VMEM(total, f32)],
         aliases=aliases,
         vmem=12,
         work=(2 * piece_rows * RANK * RANK, piece_rows * RANK * 12),
@@ -298,7 +401,7 @@
 
 
 SHIFTS = (0.0, 0.0, 0.1, 0.6, 0.85)
-PASSES = (1, 1, 3, 1, 1)
+FINE_TURN, FINE_POLY = 2, 3
 HALF = RANK // 2
 
 
@@ -347,22 +450,17 @@
         for e2 in range(far):
             who = jnp.bitwise_xor(group_index(place), e2 * near + e1)
             packed[pl.ds(pl.multiple_of(who * count, 8), count), :] = other[e2]
-    parts = {}
-    trace = jnp.zeros((), f32)
-    row = lax.broadcasted_iota(jnp.int32, (TILE, TILE), 0)
-    column = lax.broadcasted_iota(jnp.int32, (TILE, TILE), 1)
-    for n, (i, j) in enumerate(BLOCKS):
-        block = packed[n * TILE : (n + 1) * TILE, :]
-        parts[i, j] = block
-        if i == j:
-            trace = trace + jnp.sum(jnp.where(row == column, block, 0.0))
+    blocks = [packed[n * TILE : (n + 1) * TILE, :] for n in range(len(ABOVE) + len(TWOS))]
+    diagonals = [packed[DIAGONALS + n : DIAGONALS + n + 1, :] for n in range(len(TWOS))]
+    parts = unpack(blocks, diagonals)
+    trace = jnp.sum(sum(diagonals) + sum(diagonal_of(both) for both in blocks[len(ABOVE) :]))
     for i, j in ((0, 1), (2, 3)):
         parts[j, i] = parts[i, j].T
 
     def rows_of(count, first):
         return jnp.concatenate(
             [
-                jnp.concatenate([parts[i, j] for j in range(first, RANK // TILE)], axis=1)
+                jnp.concatenate([parts[i, j] for j in range(first, SIDES)], axis=1)
                 for i in range(first, first + count)
             ],
             axis=0,
@@ -376,29 +474,35 @@
     for k in range(ITERS):
         shift = SHIFTS[k]
         gain = a + b * shift + c * shift * shift
-        d = operand(rest, PASSES[k])
-        step = combine((b + 2 * c * shift, rest), (c, product(d, d)))
-        s = operand(step, PASSES[k])
+        d = operand(rest, 3 if k == FINE_TURN else 1)
+        step = combine((b + 2 * c * shift, rest), (c, product(d[:1], d[:1])))
+        s = operand(step, 3 if k in (FINE_TURN, FINE_POLY) else 1)
         if poly is None:
             poly = add_identity(step, gain)
         else:
-            poly = combine((gain, poly), (1.0, product(operand(poly, PASSES[k]), s)))
+            p = operand(poly, 3 if k == FINE_POLY else 1)
+            poly = combine((gain, poly), (1.0, product(p, s)))
         if k < ITERS - 1:
             middle = combine((gain, rest), (shift, step), (1.0, product(d, s)))
-            turned = product(operand(middle, PASSES[k]), s)
+            turned = product(operand(middle, 1), s)
             rest = combine((gain, middle), (gain * shift, step), (1.0, turned))
             rest = add_identity(rest, gain * gain * shift - SHIFTS[k + 1])
     top, corner = tuple(x * (scale * math.sqrt(max(LONG, RANK))) for x in poly)
-    for n, (i, j) in enumerate(BLOCKS):
+
+    def block(i, j):
         part, i0, j0 = (top, i, j) if i < half else (corner, i - half, j - half)
-        block = part[i0 * TILE : (i0 + 1) * TILE, j0 * TILE : (j0 + 1) * TILE]
-        high = block.astype(bf16)
-        result[n * TILE : (n + 1) * TILE, :] = high
-        if i == j:
-            low = jnp.where(row == column, block - high.astype(f32), 0.0)
-            result[PACKED + i * TAIL : PACKED + (i + 1) * TAIL, :] = jnp.broadcast_to(
-                jnp.sum(low, axis=0, keepdims=True), (TAIL, TILE)
-            ).astype(bf16)
+        return part[i0 * TILE : (i0 + 1) * TILE, j0 * TILE : (j0 + 1) * TILE]
+
+    blocks, seconds = pack(block)
+    for n, part in enumerate(blocks):
+        result[n * TILE : (n + 1) * TILE, :] = part.astype(bf16)
+    lows = []
+    for i in range(SIDES):
+        diagonal = diagonal_of(block(i, i))
+        lows.append(diagonal - diagonal.astype(bf16).astype(f32))
+    rows = lows + seconds
+    rows.append(jnp.zeros((POLY_ROWS - DIAGONALS - len(rows), TILE), f32))
+    result[DIAGONALS:, :] = jnp.concatenate(rows, axis=0).astype(bf16)
 
 
 def polynomial(line, shared):
@@ -407,10 +511,10 @@
         functools.partial(polynomial_kernel, near, far, count),
         list(shared),
         [IN_VMEM] * near,
-        [jax.ShapeDtypeStruct((PACKED + RANK // TILE * TAIL, TILE), bf16)],
+        [jax.ShapeDtypeStruct((POLY_ROWS, TILE), bf16)],
         [IN_VMEM],
         name="polynomial",
-        scratch=[pltpu.VMEM((PACKED, TILE), f32)],
+        scratch=[pltpu.VMEM((near * far * count, TILE), f32)],
         vmem=20,
         work=(RANK**3, 2**16),
     )[0]
@@ -423,23 +527,29 @@
     updates, _, held, sems = refs[-4:]
     copies = []
     for n, d in enumerate(steps):
-        parts = {}
-        for k, (i, j) in enumerate(BLOCKS):
-            parts[i, j] = polys[n][k * TILE : (k + 1) * TILE, :]
-            if i != j:
-                parts[j, i] = parts[i, j].T
-        sides = range(RANK // TILE)
+        tail = polys[n][DIAGONALS:, :].astype(f32)
+        blocks = [polys[n][k * TILE : (k + 1) * TILE, :] for k in range(len(ABOVE) + len(TWOS))]
+        twos = [part.astype(f32) for part in blocks[len(ABOVE) :]]
+        seconds = [tail[SIDES + k : SIDES + k + 1] for k in range(len(TWOS))]
+        parts = unpack(blocks[: len(ABOVE)] + twos, seconds)
+        for i in range(SIDES):
+            parts[i, i] = parts[i, i].astype(bf16)
+        for i, j in ABOVE:
+            parts[j, i] = parts[i, j].T
+        sides = range(SIDES)
         poly = jnp.concatenate(
             [jnp.concatenate([parts[i, j] for j in sides], axis=1) for i in sides], axis=0
         )
-        low = jnp.concatenate(
-            [polys[n][PACKED + i * TAIL : PACKED + (i + 1) * TAIL, :][:1] for i in sides], axis=1
-        )
-        x = pieces[n][...] if picks[n] is None else pieces[n][picks[n]]
-        held[n] = (dot(x, poly) + x.astype(f32) * low.astype(f32)).astype(bf16)
+        low = jnp.concatenate([tail[i : i + 1] for i in sides], axis=1)
+        rows = held.shape[1]
+        tile = min(256, rows)
         target = updates.at[matrix_of(place, matrices, slots, slot, d)]
-        copies.append(pltpu.make_async_copy(held.at[n], target, sems.at[n]))
-        copies[-1].start()
+        for k in range(rows // tile):
+            part = pl.ds(k * tile, tile)
+            x = pieces[n][part] if picks[n] is None else pieces[n][picks[n], part]
+            held[n, part] = (dot(x, poly) + x.astype(f32) * low).astype(bf16)
+            copies.append(pltpu.make_async_copy(held.at[n, part], target.at[part], sems.at[len(copies)]))
+            copies[-1].start()
     for copy in copies:
         copy.wait()
 
@@ -460,7 +570,7 @@
         [IN_HBM, IN_VMEM],
         name="finish",
         token=1,
-        scratch=[pltpu.VMEM((len(steps), shape[1], RANK), bf16), pltpu.SemaphoreType.DMA((len(steps),))],
+        scratch=[pltpu.VMEM((len(steps), shape[1], RANK), bf16), pltpu.SemaphoreType.DMA((len(steps) * max(1, shape[1] // 256),))],
         aliases=aliases,
         vmem=12,
         work=(2 * len(steps) * shape[1] * RANK * RANK, 4 * len(steps) * shape[1] * RANK),
@@ -493,23 +603,32 @@
         for slot, d in pieces:
             arrived[slot, d] = lax.ppermute(picked[slot, d], "owner", partners(owners, d))
 
-    renewed, rows, returned, sums, lines, mine, gathered, polys = None, {}, {}, {}, {}, {}, {}, {}
+    fetched = {}
+    renewed, rows, returned, sums, lines, mine, whole_lines, gathered, polys = None, {}, {}, {}, {}, {}, {}, {}, {}
+
+    summed = packed_rows(group)
 
     def blend_piece(slot, d, then=()):
         nonlocal renewed
         line.waiting.update({piece: picked[piece] for piece in then})
-        renewed, rows[slot, d], sums[slot] = blend(
-            line,
-            arrived[slot, d] if d else gradients,
-            momentum,
-            slot,
-            d,
-            matrix_count,
-            renewed,
-            rows[slot, d - 1] if d > 1 and d % 2 else None,
-            sums.get(slot),
-            shares if d == owners - 1 else None,
-        )
+        gradient = arrived[slot, d] if d else gradients
+        if d == owners - 1:
+            renewed, rows[slot, d], sums[slot] = blend_last(
+                line, gradient, fetched[slot], slot, d, matrix_count, renewed, rows[slot, d - 1], sums[slot], shares
+            )
+        else:
+            renewed, rows[slot, d], sums[slot] = blend(
+                line,
+                gradient,
+                momentum,
+                slot,
+                d,
+                matrix_count,
+                renewed,
+                rows[slot, d - 1] if d > 1 and d % 2 else None,
+                sums.get(slot),
+                summed,
+            )
         picked.update({piece: line.passed[piece] for piece in then})
         send(then)
 
@@ -540,7 +659,10 @@
 
     def collect(slot):
         part = mine[slot]
-        whole_line = stack(line, [part] + [across_far(part, e2) for e2 in range(1, shares[1])])
+        whole_lines[slot] = stack(line, [part] + [across_far(part, e2) for e2 in range(1, shares[1])])
+
+    def send_line(slot):
+        whole_line = whole_lines[slot]
         gathered[slot] = [whole_line] + [across_near(whole_line, e1) for e1 in range(1, near)]
 
     def make_polynomial(slot):
@@ -586,15 +708,17 @@
             send_back(slot, d)
     for d in far_steps[:-1]:
         blend_piece(0, d)
+    fetched[0] = fetch(line, momentum, 0, owners - 1, matrix_count, gradients.shape[1])
     expect((0, 1))
     for d in far_steps[-1:]:
         blend_piece(0, d)
+    fetched[1] = fetch(line, momentum, 1, owners - 1, matrix_count, gradients.shape[1])
     expect((1, 1))
+    first_sum(0)
+    for d in far_steps[1::2]:
+        line.waiting[d] = rows[0, d]
     for d in far_steps[:-1]:
         blend_piece(1, d)
-    for d in far_steps[1::2]:
-        line.waiting[d] = rows[0, d]
-    first_sum(0)
     for d in far_steps[1::2]:
         rows[0, d] = line.passed[d]
         send_back(0, d - 1)
@@ -604,25 +728,29 @@
     second_sum(0)
     sums[1] = line.passed["sum"]
     first_sum(1)
-    collect(0)
-    expect(*[(0, d) for d in far_steps[::2]])
     for d in far_steps[1::2]:
         line.waiting[d] = rows[1, d]
-    second_sum(1)
+    collect(0)
     for d in far_steps[1::2]:
         rows[1, d] = line.passed[d]
         send_back(1, d - 1)
+    expect(*[(0, d) for d in far_steps[::2]])
+    line.waiting["line"] = whole_lines[0]
+    second_sum(1)
+    whole_lines[0] = line.passed["line"]
+    send_line(0)
     collect(1)
+    send_line(1)
     make_polynomial(0)
     expect(*[(1, d) for d in far_steps[::2]])
     make_polynomial(1)
     finish_steps(0, [0] + near_steps)
     pass_polynomials(0)
     finish_steps(1, [0] + near_steps)
+    pass_polynomials(1)
     finish_steps(0, far_steps)
-    pass_polynomials(1)
-    for d in far_steps:
-        finish_steps(1, [d])
+    for k in range(0, len(far_steps), 2):
+        finish_steps(1, far_steps[k : k + 2])
     return (updates, renewed)
 
 

time: 125 us -> 118 us (0.944)
  waiting for transfers between devices: 27.4 us -> 24.5 us
  Pallas kernels: 59.5 us -> 56.8 us
    ppermute x6, waiting for transfers between devices: 9.73 us -> 3.91 us  [send(): lax.ppermute(picked[slot, d], 'owner', partners(owners, d))]
    ppermute x4, waiting for transfers between devices: 3.84 us -> 7.28 us  [across_near(): return lax.ppermute(x, 'fsdp', partners(group, e1))]
    pallas_call x25 -> x26, Pallas kernels: 59.5 us -> 56.8 us  [run(): pl.pallas_call(body, grid_spec=pltpu.PrefetchScalarGridSpec(num_scalar_pr...]
    ppermute x4, waiting for transfers between devices: 0.01 us -> 1.7 us  [make_polynomial(): polys[slot, d] = lax.ppermute(polys[slot, 0], 'owner', partners(owners, d))]
    ppermute x6, starting transfers between devices: 5.33 us -> 6.91 us  [send(): lax.ppermute(picked[slot, d], 'owner', partners(owners, d))]
    ppermute x2, starting transfers between devices: 2.16 us -> 0.59 us  [send_back(): pair = lax.ppermute(rows[slot, d + 1], 'owner', partners(owners, d))]
    ppermute x12, waiting for transfers between devices: 12.3 us -> 11.1 us  [across_far(): return lax.ppermute(x, 'fsdp', partners(group, e2 * near))]
  transfers between devices with their start and end apart: 34 -> 34, of which waited for: 9 -> 10; matrix products, arithmetic and copies ran while one was open for 0% -> 0% of each run, Pallas kernels for 44% -> 45%
where the time goes in v5:
time: 118 us
  Pallas kernels  56.8 us (48%)
  starting transfers between devices  34.6 us (29%)
  waiting for transfers between devices  24.5 us (21%)
    pallas_call x26, Pallas kernels, run(): pl.pallas_call(body, grid_spec=pltpu.PrefetchScalarGridSpec(num_scalar_pr...  56.8 us
    ppermute x12, starting transfers between devices, across_far(): return lax.ppermute(x, 'fsdp', partners(group, e2 * near))  17.6 us
    ppermute x12, waiting for transfers between devices, across_far(): return lax.ppermute(x, 'fsdp', partners(group, e2 * near))  11.1 us
    ppermute x4, waiting for transfers between devices, across_near(): return lax.ppermute(x, 'fsdp', partners(group, e1))  7.28 us
    ppermute x6, starting transfers between devices, send(): lax.ppermute(picked[slot, d], 'owner', partners(owners, d))  6.91 us
    ppermute x4, starting transfers between devices, across_near(): return lax.ppermute(x, 'fsdp', partners(group, e1))  5.6 us
    ppermute x6, waiting for transfers between devices, send(): lax.ppermute(picked[slot, d], 'owner', partners(owners, d))  3.91 us
    ppermute x4, starting transfers between devices, make_polynomial(): polys[slot, d] = lax.ppermute(polys[slot, 0], 'owner', partners(owners, d))  2.42 us
  transfers between devices with their start and end apart: 34, of which 10 were waited for; matrix products, arithmetic and copies ran while one was open for 0% of the time, Pallas kernels for 45%

profile of v5, /device:TPU:0, one launch (start us, length us, event | category | flops | bytes accessed | tf_op | source)
XLA Modules:
  0.0 117.8 jit_solution(2639909814761412784)
XLA Ops:
  0.6 0.7 pad_add_fusion.place
  1.4 1.6 %pick.2.refs_0_ = bf16[512,512]{1,0:T(8,128)(2,1)S(1)} custom-call(s32[10]{0:T(128)S(1)} %pad_add_fusion.place, bf16[8,512,512]{2,1,0:T(8,128)(2,1)} %refs_1_.5), custom_call_target="tpu_custom_call" | custom-call | bytes 20971520 | tf_op jit(solution)/shard_map/pick/pallas_call | solution.py:229
  3.0 3.0 %collective-permute-start.2 = (bf16[512,512]{1,0:T(8,128)(2,1)S(1)}, bf16[512,512]{1,0:T(8,128)(2,1)S(1)}, u32[]{:S(2)}, u32[]{:S(2)}) collective-permute-start(bf16[512,512]{1,0:T(8,128)(2,1)S(1)} %pick.2.refs_0_), channel_id=1, source_target_pairs={{0,16},{8,24},{16,0},{24,8},{1,17},{9,25},{17,1},{25,9},{2,18},{10... | collective-permute-start | bytes 1572872 | tf_op jit(solution)/shard_map/ppermute | solution.py:604
  6.0 2.3 %pick.3 = (bf16[512,512]{1,0:T(8,128)(2,1)S(1)}, bf16[512,512]{1,0:T(8,128)(2,1)S(1)}, bf16[512,512]{1,0:T(8,128)(2,1)S(1)}, bf16[512,512]{1,0:T(8,128)(2,1)S(1)}, bf16[512,512]{1,0:T(8,128)(2,1)S(1)}) custom-call(s32[10]{0:T(128)S(1)} %pad_add_fusion.place, bf16[512,512]{1,0:T(8,128)(2,1)S(1)} %pick.2.refs_0_, bf16[8,512,512]{2,1,0:T(8,128)(2,1)} %refs_1_.5), custom_call_target="tpu_custom_call" | custom-call | bytes 104857600 | tf_op jit(solution)/shard_map/pick/pallas_call | solution.py:229
  8.3 0.1 collective-permute-start
  8.3 0.1 collective-permute-start.4
  8.5 3.3 %blend.6 = (f32[2,2048,512]{2,1,0:T(8,128)}, bf16[512,512]{1,0:T(8,128)(2,1)S(1)}, f32[1088,128]{1,0:T(8,128)S(1)}, bf16[512,512]{1,0:T(8,128)(2,1)S(1)}, bf16[5...) custom-call(s32[10]{0:T(128)S(1)} %pad_add_fusion.place, ...), custom_call_target="tpu_custom_call", output_to_operand_aliasing={{3}: (2, {}), {4}: (3, {}), {5}: (4, {})} | custom-call | flops 5368709120 | bytes 62914560 | tf_op jit(solution)/shard_map/blend/pallas_call | solution.py:229
  11.7 0.4 collective-permute-start.1
  12.1 1.7 %collective-permute-start.7 = (bf16[512,512]{1,0:T(8,128)(2,1)S(1)}, bf16[512,512]{1,0:T(8,128)(2,1)S(1)}, u32[]{:S(2)}, u32[]{:S(2)}) collective-permute-start(bf16[512,512]{1,0:T(8,128)(2,1)S(1)} %get-tuple-element.78), channel_id=1, source_target_pairs={{0,16},{8,24},{16,0},{24,8},{1,17},{9,25},{17,1},{25,9},{2,18},{10... | collective-permute-start | bytes 1572872 | tf_op jit(solution)/shard_map/ppermute | solution.py:604
  13.8 3.3 %blend.7 = (f32[2,2048,512]{2,1,0:T(8,128)}, bf16[512,512]{1,0:T(8,128)(2,1)S(1)}, f32[1088,128]{1,0:T(8,128)S(1)}) custom-call(s32[10]{0:T(128)S(1)} %pad_add_fusion.place, f32[1088,128]{1,0:T(8,128)S(1)} %get-tuple-element.60.refs_0_.refs_4_, bf16[8,512,512]{2,1,0:T(8,128)(2,1)} %refs_1_.5, ...), custom_call_target="tpu_custom_call", output_to_operand_aliasing={{0}: (4, {})} | custom-call | flops 5368709120 | bytes 62914560 | tf_op jit(solution)/shard_map/blend/pallas_call | solution.py:229
  17.1 3.2 %blend.8 = (f32[2,2048,512]{2,1,0:T(8,128)}, bf16[512,512]{1,0:T(8,128)(2,1)S(1)}, f32[1088,128]{1,0:T(8,128)S(1)}) custom-call(s32[10]{0:T(128)S(1)} %pad_add_fusion.place, f32[1088,128]{1,0:T(8,128)S(1)} %get-tuple-element.62.refs_0_.refs_4_, bf16[512,512]{1,0:T(8,128)(2,1)S(1)} %collective-permute-done.refs_1_, ...), custom_call_target="tpu_custom_call", output_to_operand_aliasing={{0}: (4, {})} | custom-call | flops 5368709120 | bytes 62914560 | tf_op jit(solution)/shard_map/blend/pallas_call | solution.py:229
  20.2 0.2 collective-permute-start.3
  20.4 3.2 %blend.9 = (f32[2,2048,512]{2,1,0:T(8,128)}, bf16[512,512]{1,0:T(8,128)(2,1)S(1)}, f32[1088,128]{1,0:T(8,128)S(1)}) custom-call(s32[10]{0:T(128)S(1)} %pad_add_fusion.place, f32[1088,128]{1,0:T(8,128)S(1)} %get-tuple-element.65.refs_0_.refs_4_, bf16[512,512]{1,0:T(8,128)(2,1)S(1)} %collective-permute-done.1.refs_1_, ...), custom_call_target="tpu_custom_call", output_to_operand_aliasing={{0}: (4, {})} | custom-call | flops 5368709120 | bytes 62914560 | tf_op jit(solution)/shard_map/blend/pallas_call | solution.py:229
  23.6 0.3 collective-permute-start.5
  23.9 3.2 %blend.10 = (f32[2,2048,512]{2,1,0:T(8,128)}, bf16[2,512,512]{2,1,0:T(8,128)(2,1)S(1)}, f32[1088,128]{1,0:T(8,128)S(1)}) custom-call(s32[10]{0:T(128)S(1)} %pad_add_fusion.place, f32[1088,128]{1,0:T(8,128)S(1)} %get-tuple-element.68.refs_0_.refs_5_, bf16[512,512]{1,0:T(8,128)(2,1)S(1)} %collective-permute-done.2.refs_1_, ...), custom_call_target="tpu_custom_call", output_to_operand_aliasing={{0}: (4, {})} | custom-call | flops 5368709120 | bytes 62914560 | tf_op jit(solution)/shard_map/blend/pallas_call | solution.py:229
  27.1 1.8 %fetch.2.refs_0_.refs_3_ = f32[512,512]{1,0:T(8,128)S(1)} custom-call(s32[10]{0:T(128)S(1)} %pad_add_fusion.place, f32[1088,128]{1,0:T(8,128)S(1)} %get-tuple-element.70.refs_0_.refs_6_, f32[2,2048,512]{2,1,0:T(8,128)} %refs_3_.1), custom_call_target="tpu_custom_call" | custom-call | bytes 41943040 | tf_op jit(solution)/shard_map/fetch/pallas_call | solution.py:229
  28.8 0.7 collective-permute-done.4.refs_2_
  29.5 1.8 %blend_last.2 = (f32[2,2048,512]{2,1,0:T(8,128)}, bf16[2,512,512]{2,1,0:T(8,128)(2,1)S(1)}, f32[2,4,136,128]{3,2,1,0:T(8,128)S(1)}) custom-call(s32[10]{0:T(128)S(1)} %pad_add_fusion.place, f32[512,512]{1,0:T(8,128)S(1)} %fetch.2.refs_0_.refs_3_, ...), custom_call_target="tpu_custom_call", output_to_operand_aliasing={{0}: (5, {}), {1}: (6, {})} | custom-call | flops 5368709120 | bytes 62914560 | tf_op jit(solution)/shard_map/blend_last/pallas_call | solution.py:229
  31.4 1.6 %collective-permute-start.6 = (f32[4,136,128]{2,1,0:T(8,128)S(1)}, f32[4,136,128]{2,1,0:T(8,128)S(1)}, u32[]{:S(2)}, u32[]{:S(2)}) collective-permute-start(f32[4,136,128]{2,1,0:T(8,128)S(1)} %slice_bitcast_fusion.1), channel_id=1, source_target_pairs={{0,1},{1,0},{2,3},{3,2},{4,5},{5,4},{6,7},{7,6},{8,9},{9,8},{10,11... | collective-permute-start | bytes 835592 | tf_op jit(solution)/shard_map/ppermute | solution.py:646
  33.0 1.6 %collective-permute-start.8 = (bf16[512,512]{1,0:T(8,128)(2,1)S(1)}, bf16[512,512]{1,0:T(8,128)(2,1)S(1)}, u32[]{:S(2)}, u32[]{:S(2)}) collective-permute-start(bf16[512,512]{1,0:T(8,128)(2,1)S(1)} %get-tuple-element.81), channel_id=1, source_target_pairs={{0,24},{8,16},{16,8},{24,0},{1,25},{9,17},{17,9},{25,1},{2,26},{10... | collective-permute-start | bytes 1572872 | tf_op jit(solution)/shard_map/ppermute | solution.py:604
  34.6 1.8 %fetch.3.refs_0_.refs_2_ = f32[512,512]{1,0:T(8,128)S(1)} custom-call(s32[10]{0:T(128)S(1)} %pad_add_fusion.place, f32[2,4,136,128]{3,2,1,0:T(8,128)S(1)} %get-tuple-element.74.refs_0_.refs_2_, f32[2,2048,512]{2,1,0:T(8,128)} %refs_3_.1), custom_call_target="tpu_custom_call" | custom-call | bytes 41943040 | tf_op jit(solution)/shard_map/fetch/pallas_call | solution.py:229
  36.4 4.2 %collective-permute-done.6.refs_3_ = f32[4,136,128]{2,1,0:T(8,128)S(1)} collective-permute-done((f32[4,136,128]{2,1,0:T(8,128)S(1)}, f32[4,136,128]{2,1,0:T(8,128)S(1)}, u32[]{:S(2)}, u32[]{:S(2)}) %collective-permute-start.6) | collective-permute-done | bytes 278560 | tf_op jit(solution)/shard_map/ppermute | solution.py:646
  40.6 0.6 add_near.2
  41.2 1.9 %collective-permute-start.9 = (f32[136,128]{1,0:T(8,128)S(1)}, f32[136,128]{1,0:T(8,128)S(1)}, u32[]{:S(2)}, u32[]{:S(2)}) collective-permute-start(f32[136,128]{1,0:T(8,128)S(1)} %get-tuple-element.85), channel_id=1, source_target_pairs={{0,2},{1,3},{2,0},{3,1},{4,6},{5,7},{6,4},{7,5},{8,10},{9,11},{10,... | collective-permute-start | bytes 208904 | tf_op jit(solution)/shard_map/ppermute | solution.py:649
  43.1 2.6 %collective-permute-start.10 = (f32[136,128]{1,0:T(8,128)S(1)}, f32[136,128]{1,0:T(8,128)S(1)}, u32[]{:S(2)}, u32[]{:S(2)}) collective-permute-start(f32[136,128]{1,0:T(8,128)S(1)} %get-tuple-element.86), channel_id=1, source_target_pairs={{0,4},{1,5},{2,6},{3,7},{4,0},{5,1},{6,2},{7,3},{8,12},{9,13},{10,... | collective-permute-start | bytes 208904 | tf_op jit(solution)/shard_map/ppermute | solution.py:649
  45.7 3.2 %blend.11 = (f32[2,2048,512]{2,1,0:T(8,128)}, bf16[2,512,512]{2,1,0:T(8,128)(2,1)S(1)}, f32[1088,128]{1,0:T(8,128)S(1)}, bf16[2,512,512]{2,1,0:T(8,128)(2,1)S(1)}) custom-call(s32[10]{0:T(128)S(1)} %pad_add_fusion.place, f32[136,128]{1,0:T(8,128)S(1)} %get-tuple-element.76.refs_0_.refs_2_, ...), custom_call_target="tpu_custom_call", output_to_operand_aliasing={{0}: (5, {}), {3}: (2, {})} | custom-call | flops 5368709120 | bytes 62914560 | tf_op jit(solution)/shard_map/blend/pallas_call | solution.py:229
  48.8 3.2 %collective-permute-done.8.refs_1_ = bf16[512,512]{1,0:T(8,128)(2,1)S(1)} collective-permute-done((bf16[512,512]{1,0:T(8,128)(2,1)S(1)}, bf16[512,512]{1,0:T(8,128)(2,1)S(1)}, u32[]{:S(2)}, u32[]{:S(2)}) %collective-permute-start.8) | collective-permute-done | bytes 524320 | tf_op jit(solution)/shard_map/ppermute | solution.py:604
  52.0 1.8 %blend_last.3 = (f32[2,2048,512]{2,1,0:T(8,128)}, bf16[2,512,512]{2,1,0:T(8,128)(2,1)S(1)}, f32[2,4,136,128]{3,2,1,0:T(8,128)S(1)}) custom-call(s32[10]{0:T(128)S(1)} %pad_add_fusion.place, f32[1088,128]{1,0:T(8,128)S(1)} %get-tuple-element.80.refs_0_.refs_5_, ...), custom_call_target="tpu_custom_call", output_to_operand_aliasing={{0}: (4, {}), {1}: (5, {})} | custom-call | flops 5368709120 | bytes 62914560 | tf_op jit(solution)/shard_map/blend_last/pallas_call | solution.py:229
  53.9 0.6 add_far.2
  54.5 1.6 %collective-permute-start.12 = (f32[4,136,128]{2,1,0:T(8,128)S(1)}, f32[4,136,128]{2,1,0:T(8,128)S(1)}, u32[]{:S(2)}, u32[]{:S(2)}) collective-permute-start(f32[4,136,128]{2,1,0:T(8,128)S(1)} %slice_bitcast_fusion), channel_id=1, source_target_pairs={{0,1},{1,0},{2,3},{3,2},{4,5},{5,4},{6,7},{7,6},{8,9},{9,8},{10,11... | collective-permute-start | bytes 835592 | tf_op jit(solution)/shard_map/ppermute | solution.py:646
  56.1 3.6 %collective-permute-start.15 = (f32[136,128]{1,0:T(8,128)S(1)}, f32[136,128]{1,0:T(8,128)S(1)}, u32[]{:S(2)}, u32[]{:S(2)}) collective-permute-start(f32[136,128]{1,0:T(8,128)S(1)} %get-tuple-element.88.refs_0_.refs_2_), channel_id=1, source_target_pairs={{0,6},{1,7},{2,4},{3,5},{4,2},{5,3},{6,0},{7,1},{8,14},{9,15},{10,... | collective-permute-start | bytes 208904 | tf_op jit(solution)/shard_map/ppermute | solution.py:649
  59.7 0.8 collective-permute-start.13
  60.5 3.1 %collective-permute-done.12.refs_2_ = f32[4,136,128]{2,1,0:T(8,128)S(1)} collective-permute-done((f32[4,136,128]{2,1,0:T(8,128)S(1)}, f32[4,136,128]{2,1,0:T(8,128)S(1)}, u32[]{:S(2)}, u32[]{:S(2)}) %collective-permute-start.12) | collective-permute-done | bytes 278560 | tf_op jit(solution)/shard_map/ppermute | solution.py:646
  63.6 0.6 add_near.3
  64.2 2.1 %collective-permute-done.14.refs_4_ = f32[136,128]{1,0:T(8,128)S(1)} collective-permute-done((f32[136,128]{1,0:T(8,128)S(1)}, f32[136,128]{1,0:T(8,128)S(1)}, u32[]{:S(2)}, u32[]{:S(2)}) %collective-permute-start.14) | collective-permute-done | bytes 69664 | tf_op jit(solution)/shard_map/ppermute | solution.py:649
  66.2 0.6 stack.10
  66.8 0.6 collective-permute-start.24
  67.4 0.9 collective-permute-start.17
  68.3 2.2 %collective-permute-start.18 = (f32[136,128]{1,0:T(8,128)S(1)}, f32[136,128]{1,0:T(8,128)S(1)}, u32[]{:S(2)}, u32[]{:S(2)}) collective-permute-start(f32[136,128]{1,0:T(8,128)S(1)} %get-tuple-element.95), channel_id=1, source_target_pairs={{0,4},{1,5},{2,6},{3,7},{4,0},{5,1},{6,2},{7,3},{8,12},{9,13},{10,... | collective-permute-start | bytes 208904 | tf_op jit(solution)/shard_map/ppermute | solution.py:649
  70.4 1.3 %collective-permute-start.19 = (f32[136,128]{1,0:T(8,128)S(1)}, f32[136,128]{1,0:T(8,128)S(1)}, u32[]{:S(2)}, u32[]{:S(2)}) collective-permute-start(f32[136,128]{1,0:T(8,128)S(1)} %get-tuple-element.96), channel_id=1, source_target_pairs={{0,6},{1,7},{2,4},{3,5},{4,2},{5,3},{6,0},{7,1},{8,14},{9,15},{10,... | collective-permute-start | bytes 208904 | tf_op jit(solution)/shard_map/ppermute | solution.py:649
  71.8 5.0 %collective-permute-done.18.refs_5_ = f32[136,128]{1,0:T(8,128)S(1)} collective-permute-done((f32[136,128]{1,0:T(8,128)S(1)}, f32[136,128]{1,0:T(8,128)S(1)}, u32[]{:S(2)}, u32[]{:S(2)}) %collective-permute-start.18) | collective-permute-done | bytes 69664 | tf_op jit(solution)/shard_map/ppermute | solution.py:649
  76.8 0.6 add_far.3
  77.4 0.8 collective-permute-start.23
  78.2 3.0 %collective-permute-start.22 = (f32[136,128]{1,0:T(8,128)S(1)}, f32[136,128]{1,0:T(8,128)S(1)}, u32[]{:S(2)}, u32[]{:S(2)}) collective-permute-start(f32[136,128]{1,0:T(8,128)S(1)} %get-tuple-element.97.refs_0_.refs_1_), channel_id=1, source_target_pairs={{0,6},{1,7},{2,4},{3,5},{4,2},{5,3},{6,0},{7,1},{8,14},{9,15},{10,... | collective-permute-start | bytes 208904 | tf_op jit(solution)/shard_map/ppermute | solution.py:649
  81.1 1.4 %collective-permute-start.20 = (f32[136,128]{1,0:T(8,128)S(1)}, f32[136,128]{1,0:T(8,128)S(1)}, u32[]{:S(2)}, u32[]{:S(2)}) collective-permute-start(f32[136,128]{1,0:T(8,128)S(1)} %get-tuple-element.97.refs_0_.refs_1_), channel_id=1, source_target_pairs={{0,2},{1,3},{2,0},{3,1},{4,6},{5,7},{6,4},{7,5},{8,10},{9,11},{10,... | collective-permute-start | bytes 208904 | tf_op jit(solution)/shard_map/ppermute | solution.py:649
  82.6 2.2 %collective-permute-done.22.refs_4_ = f32[136,128]{1,0:T(8,128)S(1)} collective-permute-done((f32[136,128]{1,0:T(8,128)S(1)}, f32[136,128]{1,0:T(8,128)S(1)}, u32[]{:S(2)}, u32[]{:S(2)}) %collective-permute-start.22) | collective-permute-done | bytes 69664 | tf_op jit(solution)/shard_map/ppermute | solution.py:649
  84.8 1.8 %collective-permute-done.21.refs_3_ = f32[136,128]{1,0:T(8,128)S(1)} collective-permute-done((f32[136,128]{1,0:T(8,128)S(1)}, f32[136,128]{1,0:T(8,128)S(1)}, u32[]{:S(2)}, u32[]{:S(2)}) %collective-permute-start.21) | collective-permute-done | bytes 69664 | tf_op jit(solution)/shard_map/ppermute | solution.py:649
  86.6 0.6 stack.11.refs_0_.refs_2_
  87.1 1.6 %collective-permute-start.25 = (f32[4,136,128]{2,1,0:T(8,128)S(1)}, f32[4,136,128]{2,1,0:T(8,128)S(1)}, u32[]{:S(2)}, u32[]{:S(2)}) collective-permute-start(f32[4,136,128]{2,1,0:T(8,128)S(1)} %stack.11.refs_0_.refs_2_), channel_id=1, source_target_pairs={{0,1},{1,0},{2,3},{3,2},{4,5},{5,4},{6,7},{7,6},{8,9},{9,8},{10,11... | collective-permute-start | bytes 835592 | tf_op jit(solution)/shard_map/ppermute | solution.py:646
  88.8 6.4 %polynomial.2.refs_0_.refs_3_ = bf16[1040,128]{1,0:T(8,128)(2,1)S(1)} custom-call(s32[10]{0:T(128)S(1)} %pad_add_fusion.place, f32[4,136,128]{2,1,0:T(8,128)S(1)} %stack.11.refs_0_.refs_2_, f32[4,136,128]{2,1,0:T(8,128)S(1)} %get-tuple-element.98.refs_1_, f32[4,136,128]{2,1,0:T(8,128)S(1)} %collective-permute-done.23.refs_2_), custom_call_target="tpu_custom_call" | custom-call | flops 2684354560 | bytes 1310720 | tf_op jit(solution)/shard_map/polynomial/pallas_call | solution.py:229
  95.3 0.5 collective-permute-start.30
  95.8 0.3 collective-permute-start.27
  96.1 0.5 collective-permute-done.24.refs_1_
  96.6 6.7 %polynomial.3.refs_0_.refs_3_ = bf16[1040,128]{1,0:T(8,128)(2,1)S(1)} custom-call(s32[10]{0:T(128)S(1)} %pad_add_fusion.place, bf16[1040,128]{1,0:T(8,128)(2,1)S(1)} %polynomial.2.refs_0_.refs_3_, bf16[2,512,512]{2,1,0:T(8,128)(2,1)S(1)} %collective-permute-done.24.refs_1_, f32[4,136,128]{2,1,0:T(8,128)S(1)} %stack.11.refs_0_.refs_2_, ...), custom_call_target="tpu_custom_call" | custom-call | flops 2684354560 | bytes 1310720 | tf_op jit(solution)/shard_map/polynomial/pallas_call | solution.py:229
  103.2 1.8 %collective-permute-start.29 = (bf16[1040,128]{1,0:T(8,128)(2,1)S(1)}, bf16[1040,128]{1,0:T(8,128)(2,1)S(1)}, u32[]{:S(2)}, u32[]{:S(2)}) collective-permute-start(bf16[1040,128]{1,0:T(8,128)(2,1)S(1)} %polynomial.3.refs_0_.refs_3_), channel_id=1, source_target_pairs={{0,16},{8,24},{16,0},{24,8},{1,17},{9,25},{17,1},{25,9},{2,18},{10... | collective-permute-start | bytes 798728 | tf_op jit(solution)/shard_map/ppermute | solution.py:671
  105.0 0.2 collective-permute-start.28
  105.3 2.1 %finish.4 = (bf16[8,512,512]{2,1,0:T(8,128)(2,1)}, f32[8,128]{1,0:T(8,128)S(1)}) custom-call(s32[10]{0:T(128)S(1)} %pad_add_fusion.place, bf16[1040,128]{1,0:T(8,128)(2,1)S(1)} %polynomial.3.refs_0_.refs_3_, bf16[512,512]{1,0:T(8,128)(2,1)S(1)} %get-tuple-element.100.refs_1_, bf16[512,512]{1,0:T(8,128)(2,1)S(1)} %collective-permute-done.3.refs_1_.refs_2_, ...), custom_call_target="tpu_custom_call" | custom-call | flops 10737418240 | bytes 41943040 | tf_op jit(solution)/shard_map/finish/pallas_call | solution.py:229
  107.4 0.5 step.2.refs_0_.refs_3_
  107.9 0.3 collective-permute-start.31
  108.3 2.1 %finish.5 = (bf16[8,512,512]{2,1,0:T(8,128)(2,1)}, f32[8,128]{1,0:T(8,128)S(1)}) custom-call(s32[10]{0:T(128)S(1)} %pad_add_fusion.place, bf16[1040,128]{1,0:T(8,128)(2,1)S(1)} %step.2.refs_0_.refs_3_, bf16[512,512]{1,0:T(8,128)(2,1)S(1)} %get-tuple-element.102.refs_1_, ...), custom_call_target="tpu_custom_call", output_to_operand_aliasing={{0}: (6, {})} | custom-call | flops 10737418240 | bytes 41943040 | tf_op jit(solution)/shard_map/finish/pallas_call | solution.py:229
  110.4 1.7 %collective-permute-done.29.refs_1_ = bf16[1040,128]{1,0:T(8,128)(2,1)S(1)} collective-permute-done((bf16[1040,128]{1,0:T(8,128)(2,1)S(1)}, bf16[1040,128]{1,0:T(8,128)(2,1)S(1)}, u32[]{:S(2)}, u32[]{:S(2)}) %collective-permute-start.29) | collective-permute-done | bytes 266272 | tf_op jit(solution)/shard_map/ppermute | solution.py:671
  112.1 0.5 step.3.refs_0_.refs_3_
  112.7 2.1 %finish.6 = (bf16[8,512,512]{2,1,0:T(8,128)(2,1)}, f32[8,128]{1,0:T(8,128)S(1)}) custom-call(s32[10]{0:T(128)S(1)} %pad_add_fusion.place, bf16[1040,128]{1,0:T(8,128)(2,1)S(1)} %step.3.refs_0_.refs_3_, bf16[2,512,512]{2,1,0:T(8,128)(2,1)S(1)} %collective-permute-done.16.refs_1_, ...), custom_call_target="tpu_custom_call", output_to_operand_aliasing={{0}: (6, {})} | custom-call | flops 10737418240 | bytes 41943040 | tf_op jit(solution)/shard_map/finish/pallas_call | solution.py:229
  114.9 2.7 %finish.7 = (bf16[8,512,512]{2,1,0:T(8,128)(2,1)}, f32[8,128]{1,0:T(8,128)}) custom-call(s32[10]{0:T(128)S(1)} %pad_add_fusion.place, f32[8,128]{1,0:T(8,128)S(1)} %get-tuple-element.106.refs_0_, bf16[2,512,512]{2,1,0:T(8,128)(2,1)S(1)} %collective-permute-done.24.refs_1_, ...), custom_call_target="tpu_custom_call", output_to_operand_aliasing={{0}: (6, {})} | custom-call | flops 10737418240 | bytes 41943040 | tf_op jit(solution)/shard_map/finish/pallas_call | solution.py:229
  (35 shorter events, 0.3 us)
Async XLA Ops:
  3.0 20.9 %collective-permute-start.2 = (bf16[512,512]{1,0:T(8,128)(2,1)S(1)}, bf16[512,512]{1,0:T(8,128)(2,1)S(1)}, u32[]{:S(2)}, u32[]{:S(2)}) collective-permute-start(bf16[512,512]{1,0:T(8,128)(2,1)S(1)} %pick.2.refs_0_), channel_id=1, source_target_pairs={{0,16},{8,24},{16,0},{24,8},{1,17},{9,25},{17,1},{25,9},{2,18},{10... | collective-permute-start | bytes 1572872 | tf_op jit(solution)/shard_map/ppermute | solution.py:604
  8.3 8.8 %collective-permute-start = (bf16[512,512]{1,0:T(8,128)(2,1)S(1)}, bf16[512,512]{1,0:T(8,128)(2,1)S(1)}, u32[]{:S(2)}, u32[]{:S(2)}) collective-permute-start(bf16[512,512]{1,0:T(8,128)(2,1)S(1)} %get-tuple-element.63), channel_id=1, source_target_pairs={{0,8},{8,0},{16,24},{24,16},{1,9},{9,1},{17,25},{25,17},{2,10},{10... | collective-permute-start | bytes 1572872 | tf_op jit(solution)/shard_map/ppermute | solution.py:604
  8.3 21.2 %collective-permute-start.4 = (bf16[512,512]{1,0:T(8,128)(2,1)S(1)}, bf16[512,512]{1,0:T(8,128)(2,1)S(1)}, u32[]{:S(2)}, u32[]{:S(2)}) collective-permute-start(bf16[512,512]{1,0:T(8,128)(2,1)S(1)} %get-tuple-element.56.refs_0_), channel_id=1, source_target_pairs={{0,24},{8,16},{16,8},{24,0},{1,25},{9,17},{17,9},{25,1},{2,26},{10... | collective-permute-start | bytes 1572872 | tf_op jit(solution)/shard_map/ppermute | solution.py:604
  11.7 8.7 %collective-permute-start.1 = (bf16[512,512]{1,0:T(8,128)(2,1)S(1)}, bf16[512,512]{1,0:T(8,128)(2,1)S(1)}, u32[]{:S(2)}, u32[]{:S(2)}) collective-permute-start(bf16[512,512]{1,0:T(8,128)(2,1)S(1)} %get-tuple-element.66), channel_id=1, source_target_pairs={{0,8},{8,0},{16,24},{24,16},{1,9},{9,1},{17,25},{25,17},{2,10},{10... | collective-permute-start | bytes 1572872 | tf_op jit(solution)/shard_map/ppermute | solution.py:604
  12.1 33.6 %collective-permute-start.7 = (bf16[512,512]{1,0:T(8,128)(2,1)S(1)}, bf16[512,512]{1,0:T(8,128)(2,1)S(1)}, u32[]{:S(2)}, u32[]{:S(2)}) collective-permute-start(bf16[512,512]{1,0:T(8,128)(2,1)S(1)} %get-tuple-element.78), channel_id=1, source_target_pairs={{0,16},{8,24},{16,0},{24,8},{1,17},{9,25},{17,1},{25,9},{2,18},{10... | collective-permute-start | bytes 1572872 | tf_op jit(solution)/shard_map/ppermute | solution.py:604
  20.2 9.3 %collective-permute-start.3 = (bf16[512,512]{1,0:T(8,128)(2,1)S(1)}, bf16[512,512]{1,0:T(8,128)(2,1)S(1)}, u32[]{:S(2)}, u32[]{:S(2)}) collective-permute-start(bf16[512,512]{1,0:T(8,128)(2,1)S(1)} %get-tuple-element.71), channel_id=1, source_target_pairs={{0,8},{8,0},{16,24},{24,16},{1,9},{9,1},{17,25},{25,17},{2,10},{10... | collective-permute-start | bytes 1572872 | tf_op jit(solution)/shard_map/ppermute | solution.py:639
  23.6 12.9 %collective-permute-start.5 = (bf16[512,512]{1,0:T(8,128)(2,1)S(1)}, bf16[512,512]{1,0:T(8,128)(2,1)S(1)}, u32[]{:S(2)}, u32[]{:S(2)}) collective-permute-start(bf16[512,512]{1,0:T(8,128)(2,1)S(1)} %get-tuple-element.75), channel_id=1, source_target_pairs={{0,8},{8,0},{16,24},{24,16},{1,9},{9,1},{17,25},{25,17},{2,10},{10... | collective-permute-start | bytes 1572872 | tf_op jit(solution)/shard_map/ppermute | solution.py:639
  31.4 9.2 %collective-permute-start.6 = (f32[4,136,128]{2,1,0:T(8,128)S(1)}, f32[4,136,128]{2,1,0:T(8,128)S(1)}, u32[]{:S(2)}, u32[]{:S(2)}) collective-permute-start(f32[4,136,128]{2,1,0:T(8,128)S(1)} %slice_bitcast_fusion.1), channel_id=1, source_target_pairs={{0,1},{1,0},{2,3},{3,2},{4,5},{5,4},{6,7},{7,6},{8,9},{9,8},{10,11... | collective-permute-start | bytes 835592 | tf_op jit(solution)/shard_map/ppermute | solution.py:646
  33.0 19.0 %collective-permute-start.8 = (bf16[512,512]{1,0:T(8,128)(2,1)S(1)}, bf16[512,512]{1,0:T(8,128)(2,1)S(1)}, u32[]{:S(2)}, u32[]{:S(2)}) collective-permute-start(bf16[512,512]{1,0:T(8,128)(2,1)S(1)} %get-tuple-element.81), channel_id=1, source_target_pairs={{0,24},{8,16},{16,8},{24,0},{1,25},{9,17},{17,9},{25,1},{2,26},{10... | collective-permute-start | bytes 1572872 | tf_op jit(solution)/shard_map/ppermute | solution.py:604
  41.2 12.7 %collective-permute-start.9 = (f32[136,128]{1,0:T(8,128)S(1)}, f32[136,128]{1,0:T(8,128)S(1)}, u32[]{:S(2)}, u32[]{:S(2)}) collective-permute-start(f32[136,128]{1,0:T(8,128)S(1)} %get-tuple-element.85), channel_id=1, source_target_pairs={{0,2},{1,3},{2,0},{3,1},{4,6},{5,7},{6,4},{7,5},{8,10},{9,11},{10,... | collective-permute-start | bytes 208904 | tf_op jit(solution)/shard_map/ppermute | solution.py:649
  43.1 10.8 %collective-permute-start.10 = (f32[136,128]{1,0:T(8,128)S(1)}, f32[136,128]{1,0:T(8,128)S(1)}, u32[]{:S(2)}, u32[]{:S(2)}) collective-permute-start(f32[136,128]{1,0:T(8,128)S(1)} %get-tuple-element.86), channel_id=1, source_target_pairs={{0,4},{1,5},{2,6},{3,7},{4,0},{5,1},{6,2},{7,3},{8,12},{9,13},{10,... | collective-permute-start | bytes 208904 | tf_op jit(solution)/shard_map/ppermute | solution.py:649
  45.7 8.3 %collective-permute-start.11 = (f32[136,128]{1,0:T(8,128)S(1)}, f32[136,128]{1,0:T(8,128)S(1)}, u32[]{:S(2)}, u32[]{:S(2)}) collective-permute-start(f32[136,128]{1,0:T(8,128)S(1)} %get-tuple-element.87), channel_id=1, source_target_pairs={{0,6},{1,7},{2,4},{3,5},{4,2},{5,3},{6,0},{7,1},{8,14},{9,15},{10,... | collective-permute-start | bytes 208904 | tf_op jit(solution)/shard_map/ppermute | solution.py:649
  48.8 28.0 %collective-permute-start.16 = (bf16[2,512,512]{2,1,0:T(8,128)(2,1)S(1)}, bf16[2,512,512]{2,1,0:T(8,128)(2,1)S(1)}, u32[]{:S(2)}, u32[]{:S(2)}) collective-permute-start(bf16[2,512,512]{2,1,0:T(8,128)(2,1)S(1)} %get-tuple-element.93), channel_id=1, source_target_pairs={{0,16},{8,24},{16,0},{24,8},{1,17},{9,25},{17,1},{25,9},{2,18},{10... | collective-permute-start | bytes 3145736 | tf_op jit(solution)/shard_map/ppermute | solution.py:641
  54.5 9.1 %collective-permute-start.12 = (f32[4,136,128]{2,1,0:T(8,128)S(1)}, f32[4,136,128]{2,1,0:T(8,128)S(1)}, u32[]{:S(2)}, u32[]{:S(2)}) collective-permute-start(f32[4,136,128]{2,1,0:T(8,128)S(1)} %slice_bitcast_fusion), channel_id=1, source_target_pairs={{0,1},{1,0},{2,3},{3,2},{4,5},{5,4},{6,7},{7,6},{8,9},{9,8},{10,11... | collective-permute-start | bytes 835592 | tf_op jit(solution)/shard_map/ppermute | solution.py:646
  56.1 8.0 %collective-permute-start.15 = (f32[136,128]{1,0:T(8,128)S(1)}, f32[136,128]{1,0:T(8,128)S(1)}, u32[]{:S(2)}, u32[]{:S(2)}) collective-permute-start(f32[136,128]{1,0:T(8,128)S(1)} %get-tuple-element.88.refs_0_.refs_2_), channel_id=1, source_target_pairs={{0,6},{1,7},{2,4},{3,5},{4,2},{5,3},{6,0},{7,1},{8,14},{9,15},{10,... | collective-permute-start | bytes 208904 | tf_op jit(solution)/shard_map/ppermute | solution.py:649
  59.7 6.5 %collective-permute-start.14 = (f32[136,128]{1,0:T(8,128)S(1)}, f32[136,128]{1,0:T(8,128)S(1)}, u32[]{:S(2)}, u32[]{:S(2)}) collective-permute-start(f32[136,128]{1,0:T(8,128)S(1)} %get-tuple-element.88.refs_0_.refs_2_), channel_id=1, source_target_pairs={{0,4},{1,5},{2,6},{3,7},{4,0},{5,1},{6,2},{7,3},{8,12},{9,13},{10,... | collective-permute-start | bytes 208904 | tf_op jit(solution)/shard_map/ppermute | solution.py:649
  59.7 6.5 %collective-permute-start.13 = (f32[136,128]{1,0:T(8,128)S(1)}, f32[136,128]{1,0:T(8,128)S(1)}, u32[]{:S(2)}, u32[]{:S(2)}) collective-permute-start(f32[136,128]{1,0:T(8,128)S(1)} %get-tuple-element.88.refs_0_.refs_2_), channel_id=1, source_target_pairs={{0,2},{1,3},{2,0},{3,1},{4,6},{5,7},{6,4},{7,5},{8,10},{9,11},{10,... | collective-permute-start | bytes 208904 | tf_op jit(solution)/shard_map/ppermute | solution.py:649
  66.8 29.8 %collective-permute-start.24 = (bf16[2,512,512]{2,1,0:T(8,128)(2,1)S(1)}, bf16[2,512,512]{2,1,0:T(8,128)(2,1)S(1)}, u32[]{:S(2)}, u32[]{:S(2)}) collective-permute-start(bf16[2,512,512]{2,1,0:T(8,128)(2,1)S(1)} %get-tuple-element.99), channel_id=1, source_target_pairs={{0,16},{8,24},{16,0},{24,8},{1,17},{9,25},{17,1},{25,9},{2,18},{10... | collective-permute-start | bytes 3145736 | tf_op jit(solution)/shard_map/ppermute | solution.py:641
  67.4 4.4 %collective-permute-start.17 = (f32[136,128]{1,0:T(8,128)S(1)}, f32[136,128]{1,0:T(8,128)S(1)}, u32[]{:S(2)}, u32[]{:S(2)}) collective-permute-start(f32[136,128]{1,0:T(8,128)S(1)} %get-tuple-element.94), channel_id=1, source_target_pairs={{0,2},{1,3},{2,0},{3,1},{4,6},{5,7},{6,4},{7,5},{8,10},{9,11},{10,... | collective-permute-start | bytes 208904 | tf_op jit(solution)/shard_map/ppermute | solution.py:649
  68.3 8.5 %collective-permute-start.18 = (f32[136,128]{1,0:T(8,128)S(1)}, f32[136,128]{1,0:T(8,128)S(1)}, u32[]{:S(2)}, u32[]{:S(2)}) collective-permute-start(f32[136,128]{1,0:T(8,128)S(1)} %get-tuple-element.95), channel_id=1, source_target_pairs={{0,4},{1,5},{2,6},{3,7},{4,0},{5,1},{6,2},{7,3},{8,12},{9,13},{10,... | collective-permute-start | bytes 208904 | tf_op jit(solution)/shard_map/ppermute | solution.py:649
  70.4 6.4 %collective-permute-start.19 = (f32[136,128]{1,0:T(8,128)S(1)}, f32[136,128]{1,0:T(8,128)S(1)}, u32[]{:S(2)}, u32[]{:S(2)}) collective-permute-start(f32[136,128]{1,0:T(8,128)S(1)} %get-tuple-element.96), channel_id=1, source_target_pairs={{0,6},{1,7},{2,4},{3,5},{4,2},{5,3},{6,0},{7,1},{8,14},{9,15},{10,... | collective-permute-start | bytes 208904 | tf_op jit(solution)/shard_map/ppermute | solution.py:649
  77.4 11.4 %collective-permute-start.23 = (f32[4,136,128]{2,1,0:T(8,128)S(1)}, f32[4,136,128]{2,1,0:T(8,128)S(1)}, u32[]{:S(2)}, u32[]{:S(2)}) collective-permute-start(f32[4,136,128]{2,1,0:T(8,128)S(1)} %get-tuple-element.98.refs_1_), channel_id=1, source_target_pairs={{0,1},{1,0},{2,3},{3,2},{4,5},{5,4},{6,7},{7,6},{8,9},{9,8},{10,11... | collective-permute-start | bytes 835592 | tf_op jit(solution)/shard_map/ppermute | solution.py:646
  78.2 6.6 %collective-permute-start.22 = (f32[136,128]{1,0:T(8,128)S(1)}, f32[136,128]{1,0:T(8,128)S(1)}, u32[]{:S(2)}, u32[]{:S(2)}) collective-permute-start(f32[136,128]{1,0:T(8,128)S(1)} %get-tuple-element.97.refs_0_.refs_1_), channel_id=1, source_target_pairs={{0,6},{1,7},{2,4},{3,5},{4,2},{5,3},{6,0},{7,1},{8,14},{9,15},{10,... | collective-permute-start | bytes 208904 | tf_op jit(solution)/shard_map/ppermute | solution.py:649
  81.1 5.4 %collective-permute-start.21 = (f32[136,128]{1,0:T(8,128)S(1)}, f32[136,128]{1,0:T(8,128)S(1)}, u32[]{:S(2)}, u32[]{:S(2)}) collective-permute-start(f32[136,128]{1,0:T(8,128)S(1)} %get-tuple-element.97.refs_0_.refs_1_), channel_id=1, source_target_pairs={{0,4},{1,5},{2,6},{3,7},{4,0},{5,1},{6,2},{7,3},{8,12},{9,13},{10,... | collective-permute-start | bytes 208904 | tf_op jit(solution)/shard_map/ppermute | solution.py:649
  81.1 5.4 %collective-permute-start.20 = (f32[136,128]{1,0:T(8,128)S(1)}, f32[136,128]{1,0:T(8,128)S(1)}, u32[]{:S(2)}, u32[]{:S(2)}) collective-permute-start(f32[136,128]{1,0:T(8,128)S(1)} %get-tuple-element.97.refs_0_.refs_1_), channel_id=1, source_target_pairs={{0,2},{1,3},{2,0},{3,1},{4,6},{5,7},{6,4},{7,5},{8,10},{9,11},{10,... | collective-permute-start | bytes 208904 | tf_op jit(solution)/shard_map/ppermute | solution.py:649
  87.1 9.4 %collective-permute-start.25 = (f32[4,136,128]{2,1,0:T(8,128)S(1)}, f32[4,136,128]{2,1,0:T(8,128)S(1)}, u32[]{:S(2)}, u32[]{:S(2)}) collective-permute-start(f32[4,136,128]{2,1,0:T(8,128)S(1)} %stack.11.refs_0_.refs_2_), channel_id=1, source_target_pairs={{0,1},{1,0},{2,3},{3,2},{4,5},{5,4},{6,7},{7,6},{8,9},{9,8},{10,11... | collective-permute-start | bytes 835592 | tf_op jit(solution)/shard_map/ppermute | solution.py:646
  95.2 9.8 %collective-permute-start.26 = (bf16[1040,128]{1,0:T(8,128)(2,1)S(1)}, bf16[1040,128]{1,0:T(8,128)(2,1)S(1)}, u32[]{:S(2)}, u32[]{:S(2)}) collective-permute-start(bf16[1040,128]{1,0:T(8,128)(2,1)S(1)} %polynomial.2.refs_0_.refs_3_), channel_id=1, source_target_pairs={{0,8},{8,0},{16,24},{24,16},{1,9},{9,1},{17,25},{25,17},{2,10},{10... | collective-permute-start | bytes 798728 | tf_op jit(solution)/shard_map/ppermute | solution.py:673
  95.3 17.5 %collective-permute-start.30 = (bf16[2,512,512]{2,1,0:T(8,128)(2,1)S(1)}, bf16[2,512,512]{2,1,0:T(8,128)(2,1)S(1)}, u32[]{:S(2)}, u32[]{:S(2)}) collective-permute-start(bf16[2,512,512]{2,1,0:T(8,128)(2,1)S(1)} %collective-permute-done.16.refs_1_), channel_id=1, source_target_pairs={{0,8},{8,0},{16,24},{24,16},{1,9},{9,1},{17,25},{25,17},{2,10},{10... | collective-permute-start | bytes 3145736 | tf_op jit(solution)/shard_map/ppermute | solution.py:643
  95.8 11.6 %collective-permute-start.27 = (bf16[1040,128]{1,0:T(8,128)(2,1)S(1)}, bf16[1040,128]{1,0:T(8,128)(2,1)S(1)}, u32[]{:S(2)}, u32[]{:S(2)}) collective-permute-start(bf16[1040,128]{1,0:T(8,128)(2,1)S(1)} %polynomial.2.refs_0_.refs_3_), channel_id=1, source_target_pairs={{0,16},{8,24},{16,0},{24,8},{1,17},{9,25},{17,1},{25,9},{2,18},{10... | collective-permute-start | bytes 798728 | tf_op jit(solution)/shard_map/ppermute | solution.py:671
  96.6 18.3 %collective-permute-start.32 = (bf16[2,512,512]{2,1,0:T(8,128)(2,1)S(1)}, bf16[2,512,512]{2,1,0:T(8,128)(2,1)S(1)}, u32[]{:S(2)}, u32[]{:S(2)}) collective-permute-start(bf16[2,512,512]{2,1,0:T(8,128)(2,1)S(1)} %collective-permute-done.24.refs_1_), channel_id=1, source_target_pairs={{0,8},{8,0},{16,24},{24,16},{1,9},{9,1},{17,25},{25,17},{2,10},{10... | collective-permute-start | bytes 3145736 | tf_op jit(solution)/shard_map/ppermute | solution.py:643
  103.2 8.9 %collective-permute-start.29 = (bf16[1040,128]{1,0:T(8,128)(2,1)S(1)}, bf16[1040,128]{1,0:T(8,128)(2,1)S(1)}, u32[]{:S(2)}, u32[]{:S(2)}) collective-permute-start(bf16[1040,128]{1,0:T(8,128)(2,1)S(1)} %polynomial.3.refs_0_.refs_3_), channel_id=1, source_target_pairs={{0,16},{8,24},{16,0},{24,8},{1,17},{9,25},{17,1},{25,9},{2,18},{10... | collective-permute-start | bytes 798728 | tf_op jit(solution)/shard_map/ppermute | solution.py:671
  105.0 3.3 %collective-permute-start.28 = (bf16[1040,128]{1,0:T(8,128)(2,1)S(1)}, bf16[1040,128]{1,0:T(8,128)(2,1)S(1)}, u32[]{:S(2)}, u32[]{:S(2)}) collective-permute-start(bf16[1040,128]{1,0:T(8,128)(2,1)S(1)} %polynomial.3.refs_0_.refs_3_), channel_id=1, source_target_pairs={{0,8},{8,0},{16,24},{24,16},{1,9},{9,1},{17,25},{25,17},{2,10},{10... | collective-permute-start | bytes 798728 | tf_op jit(solution)/shard_map/ppermute | solution.py:673
  107.9 4.8 %collective-permute-start.31 = (bf16[1040,128]{1,0:T(8,128)(2,1)S(1)}, bf16[1040,128]{1,0:T(8,128)(2,1)S(1)}, u32[]{:S(2)}, u32[]{:S(2)}) collective-permute-start(bf16[1040,128]{1,0:T(8,128)(2,1)S(1)} %step.2.refs_0_.refs_3_), channel_id=1, source_target_pairs={{0,8},{8,0},{16,24},{24,16},{1,9},{9,1},{17,25},{25,17},{2,10},{10... | collective-permute-start | bytes 798728 | tf_op jit(solution)/shard_map/ppermute | solution.py:678
  112.6 2.2 %collective-permute-start.33 = (bf16[1040,128]{1,0:T(8,128)(2,1)S(1)}, bf16[1040,128]{1,0:T(8,128)(2,1)S(1)}, u32[]{:S(2)}, u32[]{:S(2)}) collective-permute-start(bf16[1040,128]{1,0:T(8,128)(2,1)S(1)} %step.3.refs_0_.refs_3_), channel_id=1, source_target_pairs={{0,8},{8,0},{16,24},{24,16},{1,9},{9,1},{17,25},{25,17},{2,10},{10... | collective-permute-start | bytes 798728 | tf_op jit(solution)/shard_map/ppermute | solution.py:678

commit v6 on v5

--- a/solution.py
+++ b/solution.py
@@ -211,37 +211,48 @@
         scratch=(),
         aliases=None,
         vmem=8,
+        scalars=True,
     ):
         before = [] if self.last is None or (token is None and out_shape) else [self.last]
         before += self.due
         keys = list(self.waiting)
         before += [self.waiting[key] for key in keys]
         skip, given, results = len(before), len(before) + len(operands), len(out_shape)
-        aliases = {1 + skip + i: o for i, o in (aliases or {}).items()}
+        lead = 1 if scalars else 0
+        aliases = {lead + skip + i: o for i, o in (aliases or {}).items()}
         for k in range(len(keys)):
-            aliases[1 + skip - len(keys) + k] = results + k
-
-        def body(place, *refs):
-            kernel(place, *refs[skip : given + results], *refs[given + results + len(keys) :])
+            aliases[lead + skip - len(keys) + k] = results + k
+
+        def body(*refs):
+            refs, place = refs[lead:], refs[:lead]
+            kernel(*place, *refs[skip : given + results], *refs[given + results + len(keys) :])
 
         any_spec = pl.BlockSpec(memory_space=pl.ANY)
         flops, moved = work
+        in_specs = [any_spec] * skip + specs
+        out_specs = out_specs + [any_spec] * len(keys)
+        if scalars:
+            layout = {
+                "grid_spec": pltpu.PrefetchScalarGridSpec(
+                    num_scalar_prefetch=1,
+                    grid=grid,
+                    in_specs=in_specs,
+                    out_specs=out_specs,
+                    scratch_shapes=list(scratch),
+                )
+            }
+        else:
+            layout = {"in_specs": in_specs, "out_specs": out_specs, "scratch_shapes": list(scratch)}
         outs = pl.pallas_call(
             body,
-            grid_spec=pltpu.PrefetchScalarGridSpec(
-                num_scalar_prefetch=1,
-                grid=grid,
-                in_specs=[any_spec] * skip + specs,
-                out_specs=out_specs + [any_spec] * len(keys),
-                scratch_shapes=list(scratch),
-            ),
+            **layout,
             out_shape=out_shape
             + [jax.ShapeDtypeStruct(self.waiting[key].shape, self.waiting[key].dtype) for key in keys],
             input_output_aliases=aliases,
             compiler_params=pltpu.CompilerParams(vmem_limit_bytes=vmem * 2**20),
             cost_estimate=pl.CostEstimate(flops=20 * flops, bytes_accessed=20 * moved, transcendentals=0),
             name=name,
-        )(self.place, *before, *operands)
+        )(*([self.place] if scalars else []), *before, *operands)
         if token is not None:
             self.last = outs[token]
         elif not out_shape:
@@ -335,7 +346,7 @@
     )
 
 
-def add_near_kernel(place, share, *refs):
+def add_near_kernel(share, *refs):
     far = share.shape[1]
     received, targets = refs[: len(refs) - far], refs[len(refs) - far :]
     for e2, target in enumerate(targets):
@@ -354,11 +365,12 @@
         [jax.ShapeDtypeStruct((count, TILE), f32)] * far,
         [IN_VMEM] * far,
         name="add_near",
+        scalars=False,
         work=(0, 12 * far * count * TILE),
     )
 
 
-def add_far_kernel(place, *refs):
+def add_far_kernel(*refs):
     total = refs[0][...]
     for other in refs[1:-1]:
         total = total + other[...]
@@ -373,17 +385,19 @@
         [jax.ShapeDtypeStruct(parts[0].shape, f32)],
         [IN_VMEM],
         name="add_far",
+        scalars=False,
         work=(0, 4 * (len(parts) + 1) * parts[0].size),
     )[0]
 
 
-def step(line, array):
-    line.waiting["step"] = array
-    line.run(lambda place: None, [], [], [], [], name="step", token=None, work=(0, 0))
-    return line.passed["step"]
-
-
-def stack_kernel(place, *refs):
+def step(line, array=None):
+    if array is not None:
+        line.waiting["step"] = array
+    line.run(lambda: None, [], [], [], [], name="step", token=None, scalars=False, work=(0, 0))
+    return line.passed.get("step")
+
+
+def stack_kernel(*refs):
     for e, part in enumerate(refs[:-1]):
         refs[-1][e] = part[...]
 
@@ -396,6 +410,7 @@
         [jax.ShapeDtypeStruct((len(parts), *parts[0].shape), f32)],
         [IN_VMEM],
         name="stack",
+        scalars=False,
         work=(0, 8 * len(parts) * parts[0].size),
     )[0]
 
@@ -640,7 +655,6 @@
         else:
             pair = lax.ppermute(rows[slot, d + 1], "owner", partners(owners, d))
             returned[slot, d] = pair, 0
-            returned[slot, d + 1] = lax.ppermute(pair, "owner", partners(owners, 1)), 1
 
     def across_near(x, e1):
         return lax.ppermute(x, "fsdp", partners(group, e1))
@@ -742,8 +756,16 @@
     collect(1)
     send_line(1)
     make_polynomial(0)
-    expect(*[(1, d) for d in far_steps[::2]])
     make_polynomial(1)
+    for slot in all_slots:
+        for d in far_steps[::2]:
+            line.waiting[slot, d] = returned[slot, d][0]
+    step(line)
+    for slot in all_slots:
+        for d in far_steps[::2]:
+            pair = line.passed[slot, d]
+            returned[slot, d] = pair, 0
+            returned[slot, d + 1] = lax.ppermute(pair, "owner", partners(owners, 1)), 1
     finish_steps(0, [0] + near_steps)
     pass_polynomials(0)
     finish_steps(1, [0] + near_steps)

time: 118 us -> 115 us (0.975)
  Pallas kernels: 56.8 us -> 52.5 us
  waiting for transfers between devices: 24.5 us -> 26.5 us
    pallas_call x26 -> x27, Pallas kernels: 56.8 us -> 52.5 us  [run(): pl.pallas_call(body, **layout, out_shape=out_shape + [jax.ShapeDtypeStruc...]
  transfers between devices with their start and end apart: 34 -> 34, of which waited for: 10 -> 9; matrix products, arithmetic and copies ran while one was open for 0% -> 0% of each run, Pallas kernels for 45% -> 42%
where the time goes in v6:
time: 115 us
  Pallas kernels  52.5 us (46%)
  starting transfers between devices  33.9 us (29%)
  waiting for transfers between devices  26.5 us (23%)
    pallas_call x27, Pallas kernels, run(): pl.pallas_call(body, **layout, out_shape=out_shape + [jax.ShapeDtypeStruc...  52.5 us
    ppermute x12, starting transfers between devices, across_far(): return lax.ppermute(x, 'fsdp', partners(group, e2 * near))  17.6 us
    ppermute x12, waiting for transfers between devices, across_far(): return lax.ppermute(x, 'fsdp', partners(group, e2 * near))  12.1 us
    ppermute x4, waiting for transfers between devices, across_near(): return lax.ppermute(x, 'fsdp', partners(group, e1))  7.46 us
    ppermute x6, starting transfers between devices, send(): lax.ppermute(picked[slot, d], 'owner', partners(owners, d))  6.91 us
    ppermute x4, starting transfers between devices, across_near(): return lax.ppermute(x, 'fsdp', partners(group, e1))  4.98 us
    ppermute x6, waiting for transfers between devices, send(): lax.ppermute(picked[slot, d], 'owner', partners(owners, d))  4.49 us
    ppermute x4, waiting for transfers between devices, make_polynomial(): polys[slot, d] = lax.ppermute(polys[slot, 0], 'owner', partners(owners, d))  2.47 us
  transfers between devices with their start and end apart: 34, of which 9 were waited for; matrix products, arithmetic and copies ran while one was open for 0% of the time, Pallas kernels for 42%

profile of v6, /device:TPU:0, one launch (start us, length us, event | category | flops | bytes accessed | tf_op | source)
XLA Modules:
  0.0 114.8 jit_solution(6188950683728351498)
XLA Ops:
  0.6 0.7 pad_add_fusion.refs_0_
  1.4 1.6 %pick.2.refs_1_ = bf16[512,512]{1,0:T(8,128)(2,1)S(1)} custom-call(s32[10]{0:T(128)S(1)} %pad_add_fusion.refs_0_, bf16[8,512,512]{2,1,0:T(8,128)(2,1)} %refs_2_.5), custom_call_target="tpu_custom_call" | custom-call | bytes 20971520 | tf_op jit(solution)/shard_map/pick/pallas_call | solution.py:246
  3.0 3.0 %collective-permute-start.2 = (bf16[512,512]{1,0:T(8,128)(2,1)S(1)}, bf16[512,512]{1,0:T(8,128)(2,1)S(1)}, u32[]{:S(2)}, u32[]{:S(2)}) collective-permute-start(bf16[512,512]{1,0:T(8,128)(2,1)S(1)} %pick.2.refs_1_), channel_id=1, source_target_pairs={{0,16},{8,24},{16,0},{24,8},{1,17},{9,25},{17,1},{25,9},{2,18},{10... | collective-permute-start | bytes 1572872 | tf_op jit(solution)/shard_map/ppermute | solution.py:619
  6.0 2.3 %pick.3 = (bf16[512,512]{1,0:T(8,128)(2,1)S(1)}, bf16[512,512]{1,0:T(8,128)(2,1)S(1)}, bf16[512,512]{1,0:T(8,128)(2,1)S(1)}, bf16[512,512]{1,0:T(8,128)(2,1)S(1)}, bf16[512,512]{1,0:T(8,128)(2,1)S(1)}) custom-call(s32[10]{0:T(128)S(1)} %pad_add_fusion.refs_0_, bf16[512,512]{1,0:T(8,128)(2,1)S(1)} %pick.2.refs_1_, bf16[8,512,512]{2,1,0:T(8,128)(2,1)} %refs_2_.5), custom_call_target="tpu_custom_call" | custom-call | bytes 104857600 | tf_op jit(solution)/shard_map/pick/pallas_call | solution.py:246
  8.3 0.1 collective-permute-start
  8.3 0.1 collective-permute-start.4
  8.5 3.3 %blend.6 = (f32[2,2048,512]{2,1,0:T(8,128)}, bf16[512,512]{1,0:T(8,128)(2,1)S(1)}, f32[1088,128]{1,0:T(8,128)S(1)}, bf16[512,512]{1,0:T(8,128)(2,1)S(1)}, bf16[5...) custom-call(s32[10]{0:T(128)S(1)} %pad_add_fusion.refs_0_, ...), custom_call_target="tpu_custom_call", output_to_operand_aliasing={{3}: (2, {}), {4}: (3, {}), {5}: (4, {})} | custom-call | flops 5368709120 | bytes 62914560 | tf_op jit(solution)/shard_map/blend/pallas_call | solution.py:246
  11.7 0.4 collective-permute-start.1
  12.1 1.7 %collective-permute-start.7 = (bf16[512,512]{1,0:T(8,128)(2,1)S(1)}, bf16[512,512]{1,0:T(8,128)(2,1)S(1)}, u32[]{:S(2)}, u32[]{:S(2)}) collective-permute-start(bf16[512,512]{1,0:T(8,128)(2,1)S(1)} %get-tuple-element.80), channel_id=1, source_target_pairs={{0,16},{8,24},{16,0},{24,8},{1,17},{9,25},{17,1},{25,9},{2,18},{10... | collective-permute-start | bytes 1572872 | tf_op jit(solution)/shard_map/ppermute | solution.py:619
  13.8 3.3 %blend.7 = (f32[2,2048,512]{2,1,0:T(8,128)}, bf16[512,512]{1,0:T(8,128)(2,1)S(1)}, f32[1088,128]{1,0:T(8,128)S(1)}) custom-call(s32[10]{0:T(128)S(1)} %pad_add_fusion.refs_0_, f32[1088,128]{1,0:T(8,128)S(1)} %get-tuple-element.62.refs_1_.refs_5_, bf16[8,512,512]{2,1,0:T(8,128)(2,1)} %refs_2_.5, ...), custom_call_target="tpu_custom_call", output_to_operand_aliasing={{0}: (4, {})} | custom-call | flops 5368709120 | bytes 62914560 | tf_op jit(solution)/shard_map/blend/pallas_call | solution.py:246
  17.1 3.1 %blend.8 = (f32[2,2048,512]{2,1,0:T(8,128)}, bf16[512,512]{1,0:T(8,128)(2,1)S(1)}, f32[1088,128]{1,0:T(8,128)S(1)}) custom-call(s32[10]{0:T(128)S(1)} %pad_add_fusion.refs_0_, f32[1088,128]{1,0:T(8,128)S(1)} %get-tuple-element.64.refs_1_.refs_5_, bf16[512,512]{1,0:T(8,128)(2,1)S(1)} %collective-permute-done.refs_2_, ...), custom_call_target="tpu_custom_call", output_to_operand_aliasing={{0}: (4, {})} | custom-call | flops 5368709120 | bytes 62914560 | tf_op jit(solution)/shard_map/blend/pallas_call | solution.py:246
  20.2 0.2 collective-permute-start.3
  20.4 0.0 collective-permute-done.1.refs_2_
  20.4 3.2 %blend.9 = (f32[2,2048,512]{2,1,0:T(8,128)}, bf16[512,512]{1,0:T(8,128)(2,1)S(1)}, f32[1088,128]{1,0:T(8,128)S(1)}) custom-call(s32[10]{0:T(128)S(1)} %pad_add_fusion.refs_0_, f32[1088,128]{1,0:T(8,128)S(1)} %get-tuple-element.67.refs_1_.refs_5_, bf16[512,512]{1,0:T(8,128)(2,1)S(1)} %collective-permute-done.1.refs_2_, ...), custom_call_target="tpu_custom_call", output_to_operand_aliasing={{0}: (4, {})} | custom-call | flops 5368709120 | bytes 62914560 | tf_op jit(solution)/shard_map/blend/pallas_call | solution.py:246
  23.5 0.3 collective-permute-start.5
  23.9 0.0 collective-permute-done.2.refs_2_
  23.9 3.2 %blend.10 = (f32[2,2048,512]{2,1,0:T(8,128)}, bf16[2,512,512]{2,1,0:T(8,128)(2,1)S(1)}, f32[1088,128]{1,0:T(8,128)S(1)}) custom-call(s32[10]{0:T(128)S(1)} %pad_add_fusion.refs_0_, f32[1088,128]{1,0:T(8,128)S(1)} %get-tuple-element.70.refs_1_.refs_6_, bf16[512,512]{1,0:T(8,128)(2,1)S(1)} %collective-permute-done.2.refs_2_, ...), custom_call_target="tpu_custom_call", output_to_operand_aliasing={{0}: (4, {})} | custom-call | flops 5368709120 | bytes 62914560 | tf_op jit(solution)/shard_map/blend/pallas_call | solution.py:246
  27.0 1.8 %fetch.2.refs_1_.refs_4_ = f32[512,512]{1,0:T(8,128)S(1)} custom-call(s32[10]{0:T(128)S(1)} %pad_add_fusion.refs_0_, f32[1088,128]{1,0:T(8,128)S(1)} %get-tuple-element.72.refs_1_.refs_7_, f32[2,2048,512]{2,1,0:T(8,128)} %refs_4_.1), custom_call_target="tpu_custom_call" | custom-call | bytes 41943040 | tf_op jit(solution)/shard_map/fetch/pallas_call | solution.py:246
  28.8 0.7 collective-permute-done.4.refs_3_
  29.5 0.0 collective-permute-done.3.refs_2_.refs_3_
  29.5 1.8 %blend_last.2 = (f32[2,2048,512]{2,1,0:T(8,128)}, bf16[2,512,512]{2,1,0:T(8,128)(2,1)S(1)}, f32[2,4,136,128]{3,2,1,0:T(8,128)S(1)}) custom-call(s32[10]{0:T(128)S(1)} %pad_add_fusion.refs_0_, f32[512,512]{1,0:T(8,128)S(1)} %fetch.2.refs_1_.refs_4_, ...), custom_call_target="tpu_custom_call", output_to_operand_aliasing={{0}: (5, {}), {1}: (6, {})} | custom-call | flops 5368709120 | bytes 62914560 | tf_op jit(solution)/shard_map/blend_last/pallas_call | solution.py:246
  31.4 1.6 %collective-permute-start.6 = (f32[4,136,128]{2,1,0:T(8,128)S(1)}, f32[4,136,128]{2,1,0:T(8,128)S(1)}, u32[]{:S(2)}, u32[]{:S(2)}) collective-permute-start(f32[4,136,128]{2,1,0:T(8,128)S(1)} %slice_bitcast_fusion.1), channel_id=1, source_target_pairs={{0,1},{1,0},{2,3},{3,2},{4,5},{5,4},{6,7},{7,6},{8,9},{9,8},{10,11... | collective-permute-start | bytes 835592 | tf_op jit(solution)/shard_map/ppermute | solution.py:660
  33.0 1.6 %collective-permute-start.8 = (bf16[512,512]{1,0:T(8,128)(2,1)S(1)}, bf16[512,512]{1,0:T(8,128)(2,1)S(1)}, u32[]{:S(2)}, u32[]{:S(2)}) collective-permute-start(bf16[512,512]{1,0:T(8,128)(2,1)S(1)} %get-tuple-element.83), channel_id=1, source_target_pairs={{0,24},{8,16},{16,8},{24,0},{1,25},{9,17},{17,9},{25,1},{2,26},{10... | collective-permute-start | bytes 1572872 | tf_op jit(solution)/shard_map/ppermute | solution.py:619
  34.6 1.8 %fetch.3.refs_0_.refs_3_ = f32[512,512]{1,0:T(8,128)S(1)} custom-call(s32[10]{0:T(128)S(1)} %pad_add_fusion.refs_0_, f32[2,4,136,128]{3,2,1,0:T(8,128)S(1)} %get-tuple-element.76.refs_1_.refs_2_, f32[2,2048,512]{2,1,0:T(8,128)} %refs_4_.1), custom_call_target="tpu_custom_call" | custom-call | bytes 41943040 | tf_op jit(solution)/shard_map/fetch/pallas_call | solution.py:246
  36.4 0.0 collective-permute-done.5.refs_1_.refs_3_
  36.4 4.2 %collective-permute-done.6.refs_3_ = f32[4,136,128]{2,1,0:T(8,128)S(1)} collective-permute-done((f32[4,136,128]{2,1,0:T(8,128)S(1)}, f32[4,136,128]{2,1,0:T(8,128)S(1)}, u32[]{:S(2)}, u32[]{:S(2)}) %collective-permute-start.6) | collective-permute-done | bytes 278560 | tf_op jit(solution)/shard_map/ppermute | solution.py:660
  40.6 1.9 %collective-permute-start.9 = (f32[136,128]{1,0:T(8,128)S(1)}, f32[136,128]{1,0:T(8,128)S(1)}, u32[]{:S(2)}, u32[]{:S(2)}) collective-permute-start(f32[136,128]{1,0:T(8,128)S(1)} %get-tuple-element.87), channel_id=1, source_target_pairs={{0,2},{1,3},{2,0},{3,1},{4,6},{5,7},{6,4},{7,5},{8,10},{9,11},{10,... | collective-permute-start | bytes 208904 | tf_op jit(solution)/shard_map/ppermute | solution.py:663
  42.5 2.6 %collective-permute-start.10 = (f32[136,128]{1,0:T(8,128)S(1)}, f32[136,128]{1,0:T(8,128)S(1)}, u32[]{:S(2)}, u32[]{:S(2)}) collective-permute-start(f32[136,128]{1,0:T(8,128)S(1)} %get-tuple-element.88), channel_id=1, source_target_pairs={{0,4},{1,5},{2,6},{3,7},{4,0},{5,1},{6,2},{7,3},{8,12},{9,13},{10,... | collective-permute-start | bytes 208904 | tf_op jit(solution)/shard_map/ppermute | solution.py:663
  45.1 0.0 collective-permute-start.11
  45.1 3.2 %blend.11 = (f32[2,2048,512]{2,1,0:T(8,128)}, bf16[2,512,512]{2,1,0:T(8,128)(2,1)S(1)}, f32[1088,128]{1,0:T(8,128)S(1)}, bf16[2,512,512]{2,1,0:T(8,128)(2,1)S(1)}) custom-call(s32[10]{0:T(128)S(1)} %pad_add_fusion.refs_0_, f32[136,128]{1,0:T(8,128)S(1)} %get-tuple-element.78.refs_1_.refs_2_, ...), custom_call_target="tpu_custom_call", output_to_operand_aliasing={{0}: (5, {}), {3}: (2, {})} | custom-call | flops 5368709120 | bytes 62914560 | tf_op jit(solution)/shard_map/blend/pallas_call | solution.py:246
  48.3 3.7 %collective-permute-done.8.refs_2_ = bf16[512,512]{1,0:T(8,128)(2,1)S(1)} collective-permute-done((bf16[512,512]{1,0:T(8,128)(2,1)S(1)}, bf16[512,512]{1,0:T(8,128)(2,1)S(1)}, u32[]{:S(2)}, u32[]{:S(2)}) %collective-permute-start.8) | collective-permute-done | bytes 524320 | tf_op jit(solution)/shard_map/ppermute | solution.py:619
  52.0 1.8 %blend_last.3 = (f32[2,2048,512]{2,1,0:T(8,128)}, bf16[2,512,512]{2,1,0:T(8,128)(2,1)S(1)}, f32[2,4,136,128]{3,2,1,0:T(8,128)S(1)}) custom-call(s32[10]{0:T(128)S(1)} %pad_add_fusion.refs_0_, f32[1088,128]{1,0:T(8,128)S(1)} %get-tuple-element.82.refs_1_.refs_6_, ...), custom_call_target="tpu_custom_call", output_to_operand_aliasing={{0}: (4, {}), {1}: (5, {})} | custom-call | flops 5368709120 | bytes 62914560 | tf_op jit(solution)/shard_map/blend_last/pallas_call | solution.py:246
  53.9 0.0 collective-permute-done.11.refs_5_
  54.0 1.6 %collective-permute-start.12 = (f32[4,136,128]{2,1,0:T(8,128)S(1)}, f32[4,136,128]{2,1,0:T(8,128)S(1)}, u32[]{:S(2)}, u32[]{:S(2)}) collective-permute-start(f32[4,136,128]{2,1,0:T(8,128)S(1)} %slice_bitcast_fusion), channel_id=1, source_target_pairs={{0,1},{1,0},{2,3},{3,2},{4,5},{5,4},{6,7},{7,6},{8,9},{9,8},{10,11... | collective-permute-start | bytes 835592 | tf_op jit(solution)/shard_map/ppermute | solution.py:660
  55.6 3.6 %collective-permute-start.15 = (f32[136,128]{1,0:T(8,128)S(1)}, f32[136,128]{1,0:T(8,128)S(1)}, u32[]{:S(2)}, u32[]{:S(2)}) collective-permute-start(f32[136,128]{1,0:T(8,128)S(1)} %get-tuple-element.90.refs_0_.refs_2_), channel_id=1, source_target_pairs={{0,6},{1,7},{2,4},{3,5},{4,2},{5,3},{6,0},{7,1},{8,14},{9,15},{10,... | collective-permute-start | bytes 208904 | tf_op jit(solution)/shard_map/ppermute | solution.py:663
  59.2 0.8 collective-permute-start.13
  60.0 3.2 %collective-permute-done.12.refs_2_ = f32[4,136,128]{2,1,0:T(8,128)S(1)} collective-permute-done((f32[4,136,128]{2,1,0:T(8,128)S(1)}, f32[4,136,128]{2,1,0:T(8,128)S(1)}, u32[]{:S(2)}, u32[]{:S(2)}) %collective-permute-start.12) | collective-permute-done | bytes 278560 | tf_op jit(solution)/shard_map/ppermute | solution.py:660
  63.2 2.4 %collective-permute-done.14.refs_4_ = f32[136,128]{1,0:T(8,128)S(1)} collective-permute-done((f32[136,128]{1,0:T(8,128)S(1)}, f32[136,128]{1,0:T(8,128)S(1)}, u32[]{:S(2)}, u32[]{:S(2)}) %collective-permute-start.14) | collective-permute-done | bytes 69664 | tf_op jit(solution)/shard_map/ppermute | solution.py:663
  65.7 0.0 collective-permute-done.13.refs_3_
  65.7 0.6 collective-permute-start.25
  66.3 1.1 collective-permute-start.17
  67.4 2.0 %collective-permute-start.18 = (f32[136,128]{1,0:T(8,128)S(1)}, f32[136,128]{1,0:T(8,128)S(1)}, u32[]{:S(2)}, u32[]{:S(2)}) collective-permute-start(f32[136,128]{1,0:T(8,128)S(1)} %get-tuple-element.97), channel_id=1, source_target_pairs={{0,4},{1,5},{2,6},{3,7},{4,0},{5,1},{6,2},{7,3},{8,12},{9,13},{10,... | collective-permute-start | bytes 208904 | tf_op jit(solution)/shard_map/ppermute | solution.py:663
  69.5 1.2 %collective-permute-start.19 = (f32[136,128]{1,0:T(8,128)S(1)}, f32[136,128]{1,0:T(8,128)S(1)}, u32[]{:S(2)}, u32[]{:S(2)}) collective-permute-start(f32[136,128]{1,0:T(8,128)S(1)} %get-tuple-element.98), channel_id=1, source_target_pairs={{0,6},{1,7},{2,4},{3,5},{4,2},{5,3},{6,0},{7,1},{8,14},{9,15},{10,... | collective-permute-start | bytes 208904 | tf_op jit(solution)/shard_map/ppermute | solution.py:663
  70.7 5.2 %collective-permute-done.18.refs_5_ = f32[136,128]{1,0:T(8,128)S(1)} collective-permute-done((f32[136,128]{1,0:T(8,128)S(1)}, f32[136,128]{1,0:T(8,128)S(1)}, u32[]{:S(2)}, u32[]{:S(2)}) %collective-permute-start.18) | collective-permute-done | bytes 69664 | tf_op jit(solution)/shard_map/ppermute | solution.py:663
  75.9 0.0 collective-permute-done.19.refs_6_
  75.9 1.2 %collective-permute-start.23 = (f32[4,136,128]{2,1,0:T(8,128)S(1)}, f32[4,136,128]{2,1,0:T(8,128)S(1)}, u32[]{:S(2)}, u32[]{:S(2)}) collective-permute-start(f32[4,136,128]{2,1,0:T(8,128)S(1)} %get-tuple-element.100.refs_2_), channel_id=1, source_target_pairs={{0,1},{1,0},{2,3},{3,2},{4,5},{5,4},{6,7},{7,6},{8,9},{9,8},{10,11... | collective-permute-start | bytes 835592 | tf_op jit(solution)/shard_map/ppermute | solution.py:660
  77.1 3.6 %collective-permute-start.22 = (f32[136,128]{1,0:T(8,128)S(1)}, f32[136,128]{1,0:T(8,128)S(1)}, u32[]{:S(2)}, u32[]{:S(2)}) collective-permute-start(f32[136,128]{1,0:T(8,128)S(1)} %get-tuple-element.99.refs_0_.refs_1_), channel_id=1, source_target_pairs={{0,6},{1,7},{2,4},{3,5},{4,2},{5,3},{6,0},{7,1},{8,14},{9,15},{10,... | collective-permute-start | bytes 208904 | tf_op jit(solution)/shard_map/ppermute | solution.py:663
  80.7 0.8 collective-permute-start.20
  81.5 2.3 %collective-permute-done.22.refs_4_ = f32[136,128]{1,0:T(8,128)S(1)} collective-permute-done((f32[136,128]{1,0:T(8,128)S(1)}, f32[136,128]{1,0:T(8,128)S(1)}, u32[]{:S(2)}, u32[]{:S(2)}) %collective-permute-start.22) | collective-permute-done | bytes 69664 | tf_op jit(solution)/shard_map/ppermute | solution.py:663
  83.8 2.1 %collective-permute-done.21.refs_3_ = f32[136,128]{1,0:T(8,128)S(1)} collective-permute-done((f32[136,128]{1,0:T(8,128)S(1)}, f32[136,128]{1,0:T(8,128)S(1)}, u32[]{:S(2)}, u32[]{:S(2)}) %collective-permute-start.21) | collective-permute-done | bytes 69664 | tf_op jit(solution)/shard_map/ppermute | solution.py:663
  85.9 0.7 collective-permute-start.24
  86.6 6.4 %polynomial.2.refs_1_.refs_4_ = bf16[1040,128]{1,0:T(8,128)(2,1)S(1)} custom-call(s32[10]{0:T(128)S(1)} %pad_add_fusion.refs_0_, f32[4,136,128]{2,1,0:T(8,128)S(1)} %stack.11.refs_1_.refs_2_, f32[4,136,128]{2,1,0:T(8,128)S(1)} %get-tuple-element.100.refs_2_, f32[4,136,128]{2,1,0:T(8,128)S(1)} %collective-permute-done.23.refs_3_), custom_call_target="tpu_custom_call" | custom-call | flops 2684354560 | bytes 1310720 | tf_op jit(solution)/shard_map/polynomial/pallas_call | solution.py:246
  93.0 0.1 collective-permute-start.26
  93.1 1.5 %collective-permute-start.27 = (bf16[1040,128]{1,0:T(8,128)(2,1)S(1)}, bf16[1040,128]{1,0:T(8,128)(2,1)S(1)}, u32[]{:S(2)}, u32[]{:S(2)}) collective-permute-start(bf16[1040,128]{1,0:T(8,128)(2,1)S(1)} %polynomial.2.refs_1_.refs_4_), channel_id=1, source_target_pairs={{0,16},{8,24},{16,0},{24,8},{1,17},{9,25},{17,1},{25,9},{2,18},{10... | collective-permute-start | bytes 798728 | tf_op jit(solution)/shard_map/ppermute | solution.py:685
  94.6 6.6 %polynomial.3.refs_0_.refs_4_ = bf16[1040,128]{1,0:T(8,128)(2,1)S(1)} custom-call(s32[10]{0:T(128)S(1)} %pad_add_fusion.refs_0_, bf16[1040,128]{1,0:T(8,128)(2,1)S(1)} %polynomial.2.refs_1_.refs_4_, f32[4,136,128]{2,1,0:T(8,128)S(1)} %stack.11.refs_1_.refs_2_, f32[4,136,128]{2,1,0:T(8,128)S(1)} %collective-permute-done.24.refs_3_), custom_call_target="tpu_custom_call" | custom-call | flops 2684354560 | bytes 1310720 | tf_op jit(solution)/shard_map/polynomial/pallas_call | solution.py:246
  101.2 0.7 collective-permute-start.29
  101.9 0.5 collective-permute-start.32
  102.4 0.1 collective-permute-start.30
  102.5 2.1 %finish.4 = (bf16[8,512,512]{2,1,0:T(8,128)(2,1)}, f32[8,128]{1,0:T(8,128)S(1)}) custom-call(s32[10]{0:T(128)S(1)} %pad_add_fusion.refs_0_, bf16[2,512,512]{2,1,0:T(8,128)(2,1)S(1)} %get-tuple-element.102.refs_1_.refs_2_, bf16[512,512]{1,0:T(8,128)(2,1)S(1)} %get-tuple-element.103.refs_2_, bf16[512,512]{1,0:T(8,128)(2,1)S(1)} %collective-permute-done.3.refs_2_.refs_3_, ...), custom_call_target="tpu_custom_call" | custom-call | flops 10737418240 | bytes 41943040 | tf_op jit(solution)/shard_map/finish/pallas_call | solution.py:246
  104.6 0.5 collective-permute-start.31
  105.2 2.1 %finish.5 = (bf16[8,512,512]{2,1,0:T(8,128)(2,1)}, f32[8,128]{1,0:T(8,128)S(1)}) custom-call(s32[10]{0:T(128)S(1)} %pad_add_fusion.refs_0_, bf16[1040,128]{1,0:T(8,128)(2,1)S(1)} %step.4.refs_1_.refs_4_, bf16[512,512]{1,0:T(8,128)(2,1)S(1)} %get-tuple-element.105.refs_2_, ...), custom_call_target="tpu_custom_call", output_to_operand_aliasing={{0}: (6, {})} | custom-call | flops 10737418240 | bytes 41943040 | tf_op jit(solution)/shard_map/finish/pallas_call | solution.py:246
  107.3 2.5 %collective-permute-done.29.refs_1_ = bf16[1040,128]{1,0:T(8,128)(2,1)S(1)} collective-permute-done((bf16[1040,128]{1,0:T(8,128)(2,1)S(1)}, bf16[1040,128]{1,0:T(8,128)(2,1)S(1)}, u32[]{:S(2)}, u32[]{:S(2)}) %collective-permute-start.29) | collective-permute-done | bytes 266272 | tf_op jit(solution)/shard_map/ppermute | solution.py:685
  109.8 2.1 %finish.6 = (bf16[8,512,512]{2,1,0:T(8,128)(2,1)}, f32[8,128]{1,0:T(8,128)S(1)}) custom-call(s32[10]{0:T(128)S(1)} %pad_add_fusion.refs_0_, bf16[1040,128]{1,0:T(8,128)(2,1)S(1)} %step.5.refs_1_.refs_4_, bf16[2,512,512]{2,1,0:T(8,128)(2,1)S(1)} %get-tuple-element.102.refs_1_.refs_2_, ...), custom_call_target="tpu_custom_call", output_to_operand_aliasing={{0}: (6, {})} | custom-call | flops 10737418240 | bytes 41943040 | tf_op jit(solution)/shard_map/finish/pallas_call | solution.py:246
  111.9 2.7 %finish.7 = (bf16[8,512,512]{2,1,0:T(8,128)(2,1)}, f32[8,128]{1,0:T(8,128)}) custom-call(s32[10]{0:T(128)S(1)} %pad_add_fusion.refs_0_, f32[8,128]{1,0:T(8,128)S(1)} %get-tuple-element.109.refs_1_, bf16[2,512,512]{2,1,0:T(8,128)(2,1)S(1)} %get-tuple-element.110.refs_2_, ...), custom_call_target="tpu_custom_call", output_to_operand_aliasing={{0}: (6, {})} | custom-call | flops 10737418240 | bytes 41943040 | tf_op jit(solution)/shard_map/finish/pallas_call | solution.py:246
  (36 shorter events, 0.3 us)
Async XLA Ops:
  3.0 20.9 %collective-permute-start.2 = (bf16[512,512]{1,0:T(8,128)(2,1)S(1)}, bf16[512,512]{1,0:T(8,128)(2,1)S(1)}, u32[]{:S(2)}, u32[]{:S(2)}) collective-permute-start(bf16[512,512]{1,0:T(8,128)(2,1)S(1)} %pick.2.refs_1_), channel_id=1, source_target_pairs={{0,16},{8,24},{16,0},{24,8},{1,17},{9,25},{17,1},{25,9},{2,18},{10... | collective-permute-start | bytes 1572872 | tf_op jit(solution)/shard_map/ppermute | solution.py:619
  8.3 8.8 %collective-permute-start = (bf16[512,512]{1,0:T(8,128)(2,1)S(1)}, bf16[512,512]{1,0:T(8,128)(2,1)S(1)}, u32[]{:S(2)}, u32[]{:S(2)}) collective-permute-start(bf16[512,512]{1,0:T(8,128)(2,1)S(1)} %get-tuple-element.65), channel_id=1, source_target_pairs={{0,8},{8,0},{16,24},{24,16},{1,9},{9,1},{17,25},{25,17},{2,10},{10... | collective-permute-start | bytes 1572872 | tf_op jit(solution)/shard_map/ppermute | solution.py:619
  8.3 21.2 %collective-permute-start.4 = (bf16[512,512]{1,0:T(8,128)(2,1)S(1)}, bf16[512,512]{1,0:T(8,128)(2,1)S(1)}, u32[]{:S(2)}, u32[]{:S(2)}) collective-permute-start(bf16[512,512]{1,0:T(8,128)(2,1)S(1)} %get-tuple-element.58.refs_1_), channel_id=1, source_target_pairs={{0,24},{8,16},{16,8},{24,0},{1,25},{9,17},{17,9},{25,1},{2,26},{10... | collective-permute-start | bytes 1572872 | tf_op jit(solution)/shard_map/ppermute | solution.py:619
  11.7 8.6 %collective-permute-start.1 = (bf16[512,512]{1,0:T(8,128)(2,1)S(1)}, bf16[512,512]{1,0:T(8,128)(2,1)S(1)}, u32[]{:S(2)}, u32[]{:S(2)}) collective-permute-start(bf16[512,512]{1,0:T(8,128)(2,1)S(1)} %get-tuple-element.68), channel_id=1, source_target_pairs={{0,8},{8,0},{16,24},{24,16},{1,9},{9,1},{17,25},{25,17},{2,10},{10... | collective-permute-start | bytes 1572872 | tf_op jit(solution)/shard_map/ppermute | solution.py:619
  12.1 33.0 %collective-permute-start.7 = (bf16[512,512]{1,0:T(8,128)(2,1)S(1)}, bf16[512,512]{1,0:T(8,128)(2,1)S(1)}, u32[]{:S(2)}, u32[]{:S(2)}) collective-permute-start(bf16[512,512]{1,0:T(8,128)(2,1)S(1)} %get-tuple-element.80), channel_id=1, source_target_pairs={{0,16},{8,24},{16,0},{24,8},{1,17},{9,25},{17,1},{25,9},{2,18},{10... | collective-permute-start | bytes 1572872 | tf_op jit(solution)/shard_map/ppermute | solution.py:619
  20.2 9.3 %collective-permute-start.3 = (bf16[512,512]{1,0:T(8,128)(2,1)S(1)}, bf16[512,512]{1,0:T(8,128)(2,1)S(1)}, u32[]{:S(2)}, u32[]{:S(2)}) collective-permute-start(bf16[512,512]{1,0:T(8,128)(2,1)S(1)} %get-tuple-element.73), channel_id=1, source_target_pairs={{0,8},{8,0},{16,24},{24,16},{1,9},{9,1},{17,25},{25,17},{2,10},{10... | collective-permute-start | bytes 1572872 | tf_op jit(solution)/shard_map/ppermute | solution.py:654
  23.5 12.9 %collective-permute-start.5 = (bf16[512,512]{1,0:T(8,128)(2,1)S(1)}, bf16[512,512]{1,0:T(8,128)(2,1)S(1)}, u32[]{:S(2)}, u32[]{:S(2)}) collective-permute-start(bf16[512,512]{1,0:T(8,128)(2,1)S(1)} %get-tuple-element.77), channel_id=1, source_target_pairs={{0,8},{8,0},{16,24},{24,16},{1,9},{9,1},{17,25},{25,17},{2,10},{10... | collective-permute-start | bytes 1572872 | tf_op jit(solution)/shard_map/ppermute | solution.py:654
  31.4 9.2 %collective-permute-start.6 = (f32[4,136,128]{2,1,0:T(8,128)S(1)}, f32[4,136,128]{2,1,0:T(8,128)S(1)}, u32[]{:S(2)}, u32[]{:S(2)}) collective-permute-start(f32[4,136,128]{2,1,0:T(8,128)S(1)} %slice_bitcast_fusion.1), channel_id=1, source_target_pairs={{0,1},{1,0},{2,3},{3,2},{4,5},{5,4},{6,7},{7,6},{8,9},{9,8},{10,11... | collective-permute-start | bytes 835592 | tf_op jit(solution)/shard_map/ppermute | solution.py:660
  33.0 19.0 %collective-permute-start.8 = (bf16[512,512]{1,0:T(8,128)(2,1)S(1)}, bf16[512,512]{1,0:T(8,128)(2,1)S(1)}, u32[]{:S(2)}, u32[]{:S(2)}) collective-permute-start(bf16[512,512]{1,0:T(8,128)(2,1)S(1)} %get-tuple-element.83), channel_id=1, source_target_pairs={{0,24},{8,16},{16,8},{24,0},{1,25},{9,17},{17,9},{25,1},{2,26},{10... | collective-permute-start | bytes 1572872 | tf_op jit(solution)/shard_map/ppermute | solution.py:619
  40.6 13.2 %collective-permute-start.9 = (f32[136,128]{1,0:T(8,128)S(1)}, f32[136,128]{1,0:T(8,128)S(1)}, u32[]{:S(2)}, u32[]{:S(2)}) collective-permute-start(f32[136,128]{1,0:T(8,128)S(1)} %get-tuple-element.87), channel_id=1, source_target_pairs={{0,2},{1,3},{2,0},{3,1},{4,6},{5,7},{6,4},{7,5},{8,10},{9,11},{10,... | collective-permute-start | bytes 208904 | tf_op jit(solution)/shard_map/ppermute | solution.py:663
  42.5 11.4 %collective-permute-start.10 = (f32[136,128]{1,0:T(8,128)S(1)}, f32[136,128]{1,0:T(8,128)S(1)}, u32[]{:S(2)}, u32[]{:S(2)}) collective-permute-start(f32[136,128]{1,0:T(8,128)S(1)} %get-tuple-element.88), channel_id=1, source_target_pairs={{0,4},{1,5},{2,6},{3,7},{4,0},{5,1},{6,2},{7,3},{8,12},{9,13},{10,... | collective-permute-start | bytes 208904 | tf_op jit(solution)/shard_map/ppermute | solution.py:663
  45.1 8.8 %collective-permute-start.11 = (f32[136,128]{1,0:T(8,128)S(1)}, f32[136,128]{1,0:T(8,128)S(1)}, u32[]{:S(2)}, u32[]{:S(2)}) collective-permute-start(f32[136,128]{1,0:T(8,128)S(1)} %get-tuple-element.89), channel_id=1, source_target_pairs={{0,6},{1,7},{2,4},{3,5},{4,2},{5,3},{6,0},{7,1},{8,14},{9,15},{10,... | collective-permute-start | bytes 208904 | tf_op jit(solution)/shard_map/ppermute | solution.py:663
  48.3 27.6 %collective-permute-start.16 = (bf16[2,512,512]{2,1,0:T(8,128)(2,1)S(1)}, bf16[2,512,512]{2,1,0:T(8,128)(2,1)S(1)}, u32[]{:S(2)}, u32[]{:S(2)}) collective-permute-start(bf16[2,512,512]{2,1,0:T(8,128)(2,1)S(1)} %get-tuple-element.95), channel_id=1, source_target_pairs={{0,16},{8,24},{16,0},{24,8},{1,17},{9,25},{17,1},{25,9},{2,18},{10... | collective-permute-start | bytes 3145736 | tf_op jit(solution)/shard_map/ppermute | solution.py:656
  54.0 9.2 %collective-permute-start.12 = (f32[4,136,128]{2,1,0:T(8,128)S(1)}, f32[4,136,128]{2,1,0:T(8,128)S(1)}, u32[]{:S(2)}, u32[]{:S(2)}) collective-permute-start(f32[4,136,128]{2,1,0:T(8,128)S(1)} %slice_bitcast_fusion), channel_id=1, source_target_pairs={{0,1},{1,0},{2,3},{3,2},{4,5},{5,4},{6,7},{7,6},{8,9},{9,8},{10,11... | collective-permute-start | bytes 835592 | tf_op jit(solution)/shard_map/ppermute | solution.py:660
  55.6 7.7 %collective-permute-start.15 = (f32[136,128]{1,0:T(8,128)S(1)}, f32[136,128]{1,0:T(8,128)S(1)}, u32[]{:S(2)}, u32[]{:S(2)}) collective-permute-start(f32[136,128]{1,0:T(8,128)S(1)} %get-tuple-element.90.refs_0_.refs_2_), channel_id=1, source_target_pairs={{0,6},{1,7},{2,4},{3,5},{4,2},{5,3},{6,0},{7,1},{8,14},{9,15},{10,... | collective-permute-start | bytes 208904 | tf_op jit(solution)/shard_map/ppermute | solution.py:663
  59.2 6.5 %collective-permute-start.14 = (f32[136,128]{1,0:T(8,128)S(1)}, f32[136,128]{1,0:T(8,128)S(1)}, u32[]{:S(2)}, u32[]{:S(2)}) collective-permute-start(f32[136,128]{1,0:T(8,128)S(1)} %get-tuple-element.90.refs_0_.refs_2_), channel_id=1, source_target_pairs={{0,4},{1,5},{2,6},{3,7},{4,0},{5,1},{6,2},{7,3},{8,12},{9,13},{10,... | collective-permute-start | bytes 208904 | tf_op jit(solution)/shard_map/ppermute | solution.py:663
  59.2 6.5 %collective-permute-start.13 = (f32[136,128]{1,0:T(8,128)S(1)}, f32[136,128]{1,0:T(8,128)S(1)}, u32[]{:S(2)}, u32[]{:S(2)}) collective-permute-start(f32[136,128]{1,0:T(8,128)S(1)} %get-tuple-element.90.refs_0_.refs_2_), channel_id=1, source_target_pairs={{0,2},{1,3},{2,0},{3,1},{4,6},{5,7},{6,4},{7,5},{8,10},{9,11},{10,... | collective-permute-start | bytes 208904 | tf_op jit(solution)/shard_map/ppermute | solution.py:663
  65.7 36.2 %collective-permute-start.25 = (bf16[2,512,512]{2,1,0:T(8,128)(2,1)S(1)}, bf16[2,512,512]{2,1,0:T(8,128)(2,1)S(1)}, u32[]{:S(2)}, u32[]{:S(2)}) collective-permute-start(bf16[2,512,512]{2,1,0:T(8,128)(2,1)S(1)} %get-tuple-element.101), channel_id=1, source_target_pairs={{0,16},{8,24},{16,0},{24,8},{1,17},{9,25},{17,1},{25,9},{2,18},{10... | collective-permute-start | bytes 3145736 | tf_op jit(solution)/shard_map/ppermute | solution.py:656
  66.3 4.4 %collective-permute-start.17 = (f32[136,128]{1,0:T(8,128)S(1)}, f32[136,128]{1,0:T(8,128)S(1)}, u32[]{:S(2)}, u32[]{:S(2)}) collective-permute-start(f32[136,128]{1,0:T(8,128)S(1)} %get-tuple-element.96), channel_id=1, source_target_pairs={{0,2},{1,3},{2,0},{3,1},{4,6},{5,7},{6,4},{7,5},{8,10},{9,11},{10,... | collective-permute-start | bytes 208904 | tf_op jit(solution)/shard_map/ppermute | solution.py:663
  67.4 8.5 %collective-permute-start.18 = (f32[136,128]{1,0:T(8,128)S(1)}, f32[136,128]{1,0:T(8,128)S(1)}, u32[]{:S(2)}, u32[]{:S(2)}) collective-permute-start(f32[136,128]{1,0:T(8,128)S(1)} %get-tuple-element.97), channel_id=1, source_target_pairs={{0,4},{1,5},{2,6},{3,7},{4,0},{5,1},{6,2},{7,3},{8,12},{9,13},{10,... | collective-permute-start | bytes 208904 | tf_op jit(solution)/shard_map/ppermute | solution.py:663
  69.5 6.4 %collective-permute-start.19 = (f32[136,128]{1,0:T(8,128)S(1)}, f32[136,128]{1,0:T(8,128)S(1)}, u32[]{:S(2)}, u32[]{:S(2)}) collective-permute-start(f32[136,128]{1,0:T(8,128)S(1)} %get-tuple-element.98), channel_id=1, source_target_pairs={{0,6},{1,7},{2,4},{3,5},{4,2},{5,3},{6,0},{7,1},{8,14},{9,15},{10,... | collective-permute-start | bytes 208904 | tf_op jit(solution)/shard_map/ppermute | solution.py:663
  75.9 10.7 %collective-permute-start.23 = (f32[4,136,128]{2,1,0:T(8,128)S(1)}, f32[4,136,128]{2,1,0:T(8,128)S(1)}, u32[]{:S(2)}, u32[]{:S(2)}) collective-permute-start(f32[4,136,128]{2,1,0:T(8,128)S(1)} %get-tuple-element.100.refs_2_), channel_id=1, source_target_pairs={{0,1},{1,0},{2,3},{3,2},{4,5},{5,4},{6,7},{7,6},{8,9},{9,8},{10,11... | collective-permute-start | bytes 835592 | tf_op jit(solution)/shard_map/ppermute | solution.py:660
  77.1 6.7 %collective-permute-start.22 = (f32[136,128]{1,0:T(8,128)S(1)}, f32[136,128]{1,0:T(8,128)S(1)}, u32[]{:S(2)}, u32[]{:S(2)}) collective-permute-start(f32[136,128]{1,0:T(8,128)S(1)} %get-tuple-element.99.refs_0_.refs_1_), channel_id=1, source_target_pairs={{0,6},{1,7},{2,4},{3,5},{4,2},{5,3},{6,0},{7,1},{8,14},{9,15},{10,... | collective-permute-start | bytes 208904 | tf_op jit(solution)/shard_map/ppermute | solution.py:663
  80.7 5.2 %collective-permute-start.21 = (f32[136,128]{1,0:T(8,128)S(1)}, f32[136,128]{1,0:T(8,128)S(1)}, u32[]{:S(2)}, u32[]{:S(2)}) collective-permute-start(f32[136,128]{1,0:T(8,128)S(1)} %get-tuple-element.99.refs_0_.refs_1_), channel_id=1, source_target_pairs={{0,4},{1,5},{2,6},{3,7},{4,0},{5,1},{6,2},{7,3},{8,12},{9,13},{10,... | collective-permute-start | bytes 208904 | tf_op jit(solution)/shard_map/ppermute | solution.py:663
  80.7 5.2 %collective-permute-start.20 = (f32[136,128]{1,0:T(8,128)S(1)}, f32[136,128]{1,0:T(8,128)S(1)}, u32[]{:S(2)}, u32[]{:S(2)}) collective-permute-start(f32[136,128]{1,0:T(8,128)S(1)} %get-tuple-element.99.refs_0_.refs_1_), channel_id=1, source_target_pairs={{0,2},{1,3},{2,0},{3,1},{4,6},{5,7},{6,4},{7,5},{8,10},{9,11},{10,... | collective-permute-start | bytes 208904 | tf_op jit(solution)/shard_map/ppermute | solution.py:663
  85.9 8.6 %collective-permute-start.24 = (f32[4,136,128]{2,1,0:T(8,128)S(1)}, f32[4,136,128]{2,1,0:T(8,128)S(1)}, u32[]{:S(2)}, u32[]{:S(2)}) collective-permute-start(f32[4,136,128]{2,1,0:T(8,128)S(1)} %stack.11.refs_1_.refs_2_), channel_id=1, source_target_pairs={{0,1},{1,0},{2,3},{3,2},{4,5},{5,4},{6,7},{7,6},{8,9},{9,8},{10,11... | collective-permute-start | bytes 835592 | tf_op jit(solution)/shard_map/ppermute | solution.py:660
  93.0 9.4 %collective-permute-start.26 = (bf16[1040,128]{1,0:T(8,128)(2,1)S(1)}, bf16[1040,128]{1,0:T(8,128)(2,1)S(1)}, u32[]{:S(2)}, u32[]{:S(2)}) collective-permute-start(bf16[1040,128]{1,0:T(8,128)(2,1)S(1)} %polynomial.2.refs_1_.refs_4_), channel_id=1, source_target_pairs={{0,8},{8,0},{16,24},{24,16},{1,9},{9,1},{17,25},{25,17},{2,10},{10... | collective-permute-start | bytes 798728 | tf_op jit(solution)/shard_map/ppermute | solution.py:687
  93.1 11.5 %collective-permute-start.27 = (bf16[1040,128]{1,0:T(8,128)(2,1)S(1)}, bf16[1040,128]{1,0:T(8,128)(2,1)S(1)}, u32[]{:S(2)}, u32[]{:S(2)}) collective-permute-start(bf16[1040,128]{1,0:T(8,128)(2,1)S(1)} %polynomial.2.refs_1_.refs_4_), channel_id=1, source_target_pairs={{0,16},{8,24},{16,0},{24,8},{1,17},{9,25},{17,1},{25,9},{2,18},{10... | collective-permute-start | bytes 798728 | tf_op jit(solution)/shard_map/ppermute | solution.py:685
  101.2 8.5 %collective-permute-start.29 = (bf16[1040,128]{1,0:T(8,128)(2,1)S(1)}, bf16[1040,128]{1,0:T(8,128)(2,1)S(1)}, u32[]{:S(2)}, u32[]{:S(2)}) collective-permute-start(bf16[1040,128]{1,0:T(8,128)(2,1)S(1)} %polynomial.3.refs_0_.refs_4_), channel_id=1, source_target_pairs={{0,16},{8,24},{16,0},{24,8},{1,17},{9,25},{17,1},{25,9},{2,18},{10... | collective-permute-start | bytes 798728 | tf_op jit(solution)/shard_map/ppermute | solution.py:685
  101.9 3.3 %collective-permute-start.28 = (bf16[1040,128]{1,0:T(8,128)(2,1)S(1)}, bf16[1040,128]{1,0:T(8,128)(2,1)S(1)}, u32[]{:S(2)}, u32[]{:S(2)}) collective-permute-start(bf16[1040,128]{1,0:T(8,128)(2,1)S(1)} %polynomial.3.refs_0_.refs_4_), channel_id=1, source_target_pairs={{0,8},{8,0},{16,24},{24,16},{1,9},{9,1},{17,25},{25,17},{2,10},{10... | collective-permute-start | bytes 798728 | tf_op jit(solution)/shard_map/ppermute | solution.py:687
  101.9 10.0 %collective-permute-start.32 = (bf16[2,512,512]{2,1,0:T(8,128)(2,1)S(1)}, bf16[2,512,512]{2,1,0:T(8,128)(2,1)S(1)}, u32[]{:S(2)}, u32[]{:S(2)}) collective-permute-start(bf16[2,512,512]{2,1,0:T(8,128)(2,1)S(1)} %get-tuple-element.110.refs_2_), channel_id=1, source_target_pairs={{0,8},{8,0},{16,24},{24,16},{1,9},{9,1},{17,25},{25,17},{2,10},{10... | collective-permute-start | bytes 3145736 | tf_op jit(solution)/shard_map/ppermute | solution.py:768
  102.4 7.3 %collective-permute-start.30 = (bf16[2,512,512]{2,1,0:T(8,128)(2,1)S(1)}, bf16[2,512,512]{2,1,0:T(8,128)(2,1)S(1)}, u32[]{:S(2)}, u32[]{:S(2)}) collective-permute-start(bf16[2,512,512]{2,1,0:T(8,128)(2,1)S(1)} %get-tuple-element.102.refs_1_.refs_2_), channel_id=1, source_target_pairs={{0,8},{8,0},{16,24},{24,16},{1,9},{9,1},{17,25},{25,17},{2,10},{10... | collective-permute-start | bytes 3145736 | tf_op jit(solution)/shard_map/ppermute | solution.py:768
  104.6 5.1 %collective-permute-start.31 = (bf16[1040,128]{1,0:T(8,128)(2,1)S(1)}, bf16[1040,128]{1,0:T(8,128)(2,1)S(1)}, u32[]{:S(2)}, u32[]{:S(2)}) collective-permute-start(bf16[1040,128]{1,0:T(8,128)(2,1)S(1)} %step.4.refs_1_.refs_4_), channel_id=1, source_target_pairs={{0,8},{8,0},{16,24},{24,16},{1,9},{9,1},{17,25},{25,17},{2,10},{10... | collective-permute-start | bytes 798728 | tf_op jit(solution)/shard_map/ppermute | solution.py:692
  109.7 2.1 %collective-permute-start.33 = (bf16[1040,128]{1,0:T(8,128)(2,1)S(1)}, bf16[1040,128]{1,0:T(8,128)(2,1)S(1)}, u32[]{:S(2)}, u32[]{:S(2)}) collective-permute-start(bf16[1040,128]{1,0:T(8,128)(2,1)S(1)} %step.5.refs_1_.refs_4_), channel_id=1, source_target_pairs={{0,8},{8,0},{16,24},{24,16},{1,9},{9,1},{17,25},{25,17},{2,10},{10... | collective-permute-start | bytes 798728 | tf_op jit(solution)/shard_map/ppermute | solution.py:692

commit v7 on v6

--- a/solution.py
+++ b/solution.py
@@ -144,7 +144,7 @@
 def blend_last_kernel(slot, d, count, place, gradient, momentum, _buffer, _pair, before, renewed, pair, total, held, new, sems):
     rows = gradient.shape[0]
     tile = min(256, rows)
-    first = jnp.bitwise_xor(place[count], d) * rows
+    first = jnp.bitwise_xor(place.owner(), d) * rows
     copies = []
     for n in range(rows // tile):
         part = pl.ds(n * tile, tile)
@@ -160,7 +160,7 @@
     near, far, size, _ = total.shape
     for e1 in range(near):
         for e2 in range(far):
-            who = jnp.bitwise_xor(group_index(place), e2 * near + e1)
+            who = jnp.bitwise_xor(place.group(), e2 * near + e1)
             total[e1, e2] = held[pl.ds(pl.multiple_of(who * size, 8), size), :]
     for copy in copies:
         copy.wait()
@@ -180,6 +180,7 @@
         ],
         [IN_HBM, IN_VMEM, IN_VMEM],
         name="blend_last",
+        scalars=SPOTS,
         token=2,
         scratch=[
             pltpu.VMEM(before.shape, f32),
@@ -187,14 +188,41 @@
             pltpu.SemaphoreType.DMA((piece_rows // min(256, piece_rows),)),
         ],
         aliases={2: 0, 3: 1},
-        vmem=12,
+        vmem=8,
         work=(2 * piece_rows * RANK * RANK, piece_rows * RANK * 12),
     )
+
+
+SPOTS = "spots"
+
+
+class Spots:
+    def __init__(self, ref, owners):
+        self.ref, self.owners = ref, owners
+
+    def matrix(self, slot, d):
+        return self.ref[slot * self.owners + d, 0]
+
+    def owner(self):
+        return self.ref[self.ref.shape[0] - 2, 0]
+
+    def group(self):
+        return self.ref[self.ref.shape[0] - 1, 0]
+
+
+def make_spots(place, count, slots, owners):
+    targets = slots * jnp.bitwise_xor(place[count], jnp.arange(owners))[None, :] + jnp.arange(slots)[:, None]
+    found = place[None, :count] == targets.reshape(-1, 1)
+    matrices = jnp.sum(jnp.where(found, jnp.arange(count)[None, :], 0), axis=1).astype(jnp.int32)
+    free = -(matrices.shape[0] + 2) % 8
+    column = jnp.concatenate([matrices, jnp.zeros((free,), jnp.int32), place[count:]])
+    return jnp.broadcast_to(column[:, None], (column.shape[0], TILE))
 
 
 class Line:
     def __init__(self, place):
         self.place, self.last, self.due, self.waiting, self.passed = place, None, [], {}, {}
+        self.spots, self.owners = None, 0
 
     def run(
         self,
@@ -219,19 +247,23 @@
         before += [self.waiting[key] for key in keys]
         skip, given, results = len(before), len(before) + len(operands), len(out_shape)
         lead = 1 if scalars else 0
+        prefetched = scalars is True
+        spots = None if scalars is not SPOTS else self.spots
         aliases = {lead + skip + i: o for i, o in (aliases or {}).items()}
         for k in range(len(keys)):
             aliases[lead + skip - len(keys) + k] = results + k
 
         def body(*refs):
             refs, place = refs[lead:], refs[:lead]
+            if spots is not None:
+                place = (Spots(place[0], self.owners),)
             kernel(*place, *refs[skip : given + results], *refs[given + results + len(keys) :])
 
         any_spec = pl.BlockSpec(memory_space=pl.ANY)
         flops, moved = work
         in_specs = [any_spec] * skip + specs
         out_specs = out_specs + [any_spec] * len(keys)
-        if scalars:
+        if prefetched:
             layout = {
                 "grid_spec": pltpu.PrefetchScalarGridSpec(
                     num_scalar_prefetch=1,
@@ -242,6 +274,7 @@
                 )
             }
         else:
+            in_specs = [IN_VMEM] * lead + in_specs
             layout = {"in_specs": in_specs, "out_specs": out_specs, "scratch_shapes": list(scratch)}
         outs = pl.pallas_call(
             body,
@@ -252,7 +285,7 @@
             compiler_params=pltpu.CompilerParams(vmem_limit_bytes=vmem * 2**20),
             cost_estimate=pl.CostEstimate(flops=20 * flops, bytes_accessed=20 * moved, transcendentals=0),
             name=name,
-        )(*([self.place] if scalars else []), *before, *operands)
+        )(*([self.place] if prefetched else [spots] * lead), *before, *operands)
         if token is not None:
             self.last = outs[token]
         elif not out_shape:
@@ -341,7 +374,7 @@
         grid=(steps,),
         scratch=[pltpu.VMEM(total, f32)],
         aliases=aliases,
-        vmem=12,
+        vmem=8,
         work=(2 * piece_rows * RANK * RANK, piece_rows * RANK * 12),
     )
 
@@ -463,7 +496,7 @@
     *shared, result, packed = refs
     for e1, other in enumerate(shared):
         for e2 in range(far):
-            who = jnp.bitwise_xor(group_index(place), e2 * near + e1)
+            who = jnp.bitwise_xor(place.group(), e2 * near + e1)
             packed[pl.ds(pl.multiple_of(who * count, 8), count), :] = other[e2]
     blocks = [packed[n * TILE : (n + 1) * TILE, :] for n in range(len(ABOVE) + len(TWOS))]
     diagonals = [packed[DIAGONALS + n : DIAGONALS + n + 1, :] for n in range(len(TWOS))]
@@ -529,8 +562,9 @@
         [jax.ShapeDtypeStruct((POLY_ROWS, TILE), bf16)],
         [IN_VMEM],
         name="polynomial",
+        scalars=SPOTS,
         scratch=[pltpu.VMEM((near * far * count, TILE), f32)],
-        vmem=20,
+        vmem=12,
         work=(RANK**3, 2**16),
     )[0]
 
@@ -558,7 +592,7 @@
         low = jnp.concatenate([tail[i : i + 1] for i in sides], axis=1)
         rows = held.shape[1]
         tile = min(256, rows)
-        target = updates.at[matrix_of(place, matrices, slots, slot, d)]
+        target = updates.at[place.matrix(slot, d)]
         for k in range(rows // tile):
             part = pl.ds(k * tile, tile)
             x = pieces[n][part] if picks[n] is None else pieces[n][picks[n], part]
@@ -584,10 +618,11 @@
         [pltpu.HBM(shape, bf16), jax.ShapeDtypeStruct((8, TILE), f32)],
         [IN_HBM, IN_VMEM],
         name="finish",
+        scalars=SPOTS,
         token=1,
         scratch=[pltpu.VMEM((len(steps), shape[1], RANK), bf16), pltpu.SemaphoreType.DMA((len(steps) * max(1, shape[1] // 256),))],
         aliases=aliases,
-        vmem=12,
+        vmem=8,
         work=(2 * len(steps) * shape[1] * RANK * RANK, 4 * len(steps) * shape[1] * RANK),
     )[0]
 
@@ -605,6 +640,8 @@
     )
 
     line = Line(place)
+    line.owners = owners
+    line.spots = make_spots(place, matrix_count, held_slots, owners)
     all_slots = range(held_slots)
     far_steps, near_steps = list(range(2, owners)), list(range(1, min(2, owners)))
     arrived = {}
@@ -769,10 +806,10 @@
     finish_steps(0, [0] + near_steps)
     pass_polynomials(0)
     finish_steps(1, [0] + near_steps)
+    finish_steps(0, far_steps)
     pass_polynomials(1)
-    finish_steps(0, far_steps)
-    for k in range(0, len(far_steps), 2):
-        finish_steps(1, far_steps[k : k + 2])
+    for d in far_steps:
+        finish_steps(1, [d])
     return (updates, renewed)
 
 

time: 115 us -> 113 us (0.983)
  Pallas kernels: 52.5 us -> 50.6 us
  waiting for transfers between devices: 26.5 us -> 24.7 us
  local copies, waits for them, and re-layouts: 0.1 us -> 1.86 us
    ppermute x6, waiting for transfers between devices: 4.49 us -> 1.65 us  [send(): lax.ppermute(picked[slot, d], 'owner', partners(owners, d))]
    pallas_call x27 -> x28, Pallas kernels: 52.5 us -> 50.6 us  [run(): pl.pallas_call(body, **layout, out_shape=out_shape + [jax.ShapeDtypeStruc...]
    ppermute x4, waiting for transfers between devices: 2.47 us -> 0.76 us  [make_polynomial(): polys[slot, d] = lax.ppermute(polys[slot, 0], 'owner', partners(owners, d))]
    unnamed x2 -> x12, local copies, waits for them, and re-layouts: 0.06 us -> 1.66 us
    ppermute x6, starting transfers between devices: 6.91 us -> 5.31 us  [send(): lax.ppermute(picked[slot, d], 'owner', partners(owners, d))]
  transfers between devices with their start and end apart: 34 -> 34, of which waited for: 9 -> 12; matrix products, arithmetic and copies ran while one was open for 0% -> 0% of each run, Pallas kernels for 42% -> 42%
where the time goes in v7:
time: 113 us; the launch traced here: 112 us
  Pallas kernels  50.6 us (45%)
  starting transfers between devices  33 us (29%)
  waiting for transfers between devices  24.7 us (22%)
  local copies, waits for them, and re-layouts  1.86 us (2%)
    pallas_call x28, Pallas kernels, run(): pl.pallas_call(body, **layout, out_shape=out_shape + [jax.ShapeDtypeStruc...  50.6 us
    ppermute x12, starting transfers between devices, across_far(): return lax.ppermute(x, 'fsdp', partners(group, e2 * near))  17.6 us
    ppermute x12, waiting for transfers between devices, across_far(): return lax.ppermute(x, 'fsdp', partners(group, e2 * near))  12 us
    ppermute x4, waiting for transfers between devices, across_near(): return lax.ppermute(x, 'fsdp', partners(group, e1))  8.36 us
    ppermute x4, starting transfers between devices, across_near(): return lax.ppermute(x, 'fsdp', partners(group, e1))  5.32 us
    ppermute x6, starting transfers between devices, send(): lax.ppermute(picked[slot, d], 'owner', partners(owners, d))  5.31 us
  transfers between devices with their start and end apart: 34, of which 12 were waited for; matrix products, arithmetic and copies ran while one was open for 0% of the time, Pallas kernels for 42%

profile of v7, /device:TPU:0, one launch (start us, length us, event | category | flops | bytes accessed | tf_op | source)
XLA Modules:
  0.0 112.3 jit_solution(13873639260762771555)
XLA Ops:
  0.6 0.7 pad_add_fusion.1.refs_0_
  1.4 1.6 %pick.2.refs_1_ = bf16[512,512]{1,0:T(8,128)(2,1)S(1)} custom-call(s32[10]{0:T(128)S(1)} %pad_add_fusion.1.refs_0_, bf16[8,512,512]{2,1,0:T(8,128)(2,1)} %refs_2_.5), custom_call_target="tpu_custom_call" | custom-call | bytes 20971520 | tf_op jit(solution)/shard_map/pick/pallas_call | solution.py:279
  3.0 3.0 %collective-permute-start.2 = (bf16[512,512]{1,0:T(8,128)(2,1)S(1)}, bf16[512,512]{1,0:T(8,128)(2,1)S(1)}, u32[]{:S(2)}, u32[]{:S(2)}) collective-permute-start(bf16[512,512]{1,0:T(8,128)(2,1)S(1)} %pick.2.refs_1_), channel_id=1, source_target_pairs={{0,16},{8,24},{16,0},{24,8},{1,17},{9,25},{17,1},{25,9},{2,18},{10... | collective-permute-start | bytes 1572872 | tf_op jit(solution)/shard_map/ppermute | solution.py:656
  6.0 3.4 %pick.3 = (bf16[512,512]{1,0:T(8,128)(2,1)S(1)}, bf16[512,512]{1,0:T(8,128)(2,1)}, bf16[512,512]{1,0:T(8,128)(2,1)}, bf16[512,512]{1,0:T(8,128)(2,1)}, bf16[512,512]{1,0:T(8,128)(2,1)S(1)}) custom-call(s32[10]{0:T(128)S(1)} %pad_add_fusion.1.refs_0_, bf16[512,512]{1,0:T(8,128)(2,1)S(1)} %pick.2.refs_1_, bf16[8,512,512]{2,1,0:T(8,128)(2,1)} %refs_2_.5), custom_call_target="tpu_custom_call" | custom-call | bytes 104857600 | tf_op jit(solution)/shard_map/pick/pallas_call | solution.py:279
  9.4 0.1 collective-permute-start
  9.5 0.1 collective-permute-start.4
  9.6 3.3 %blend.6 = (f32[2,2048,512]{2,1,0:T(8,128)}, bf16[512,512]{1,0:T(8,128)(2,1)S(1)}, f32[1088,128]{1,0:T(8,128)S(1)}, bf16[512,512]{1,0:T(8,128)(2,1)}, bf16[512,5...) custom-call(s32[10]{0:T(128)S(1)} %pad_add_fusion.1.refs_0_, ...), custom_call_target="tpu_custom_call", output_to_operand_aliasing={{3}: (2, {}), {4}: (3, {}), {5}: (4, {})} | custom-call | flops 5368709120 | bytes 62914560 | tf_op jit(solution)/shard_map/blend/pallas_call | solution.py:279
  12.9 0.8 copy-done
  13.7 0.8 copy-done.2
  14.5 0.4 collective-permute-start.1
  14.8 1.7 %collective-permute-start.7 = (bf16[512,512]{1,0:T(8,128)(2,1)}, bf16[512,512]{1,0:T(8,128)(2,1)S(1)}, u32[]{:S(2)}, u32[]{:S(2)}) collective-permute-start(bf16[512,512]{1,0:T(8,128)(2,1)} %get-tuple-element.82), channel_id=1, source_target_pairs={{0,16},{8,24},{16,0},{24,8},{1,17},{9,25},{17,1},{25,9},{2,18},{10... | collective-permute-start | bytes 1572872 | tf_op jit(solution)/shard_map/ppermute | solution.py:656
  16.6 0.1 add.23
  16.7 0.2 select_reduce_fusion
  16.8 3.3 %blend.7 = (f32[2,2048,512]{2,1,0:T(8,128)}, bf16[512,512]{1,0:T(8,128)(2,1)S(1)}, f32[1088,128]{1,0:T(8,128)S(1)}) custom-call(s32[10]{0:T(128)S(1)} %pad_add_fusion.1.refs_0_, f32[1088,128]{1,0:T(8,128)S(1)} %get-tuple-element.64.refs_1_.refs_5_, bf16[8,512,512]{2,1,0:T(8,128)(2,1)} %refs_2_.5, ...), custom_call_target="tpu_custom_call", output_to_operand_aliasing={{0}: (4, {})} | custom-call | flops 5368709120 | bytes 62914560 | tf_op jit(solution)/shard_map/blend/pallas_call | solution.py:279
  20.1 0.1 pad_add_fusion
  20.2 3.2 %blend.8 = (f32[2,2048,512]{2,1,0:T(8,128)}, bf16[512,512]{1,0:T(8,128)(2,1)S(1)}, f32[1088,128]{1,0:T(8,128)S(1)}) custom-call(s32[10]{0:T(128)S(1)} %pad_add_fusion.1.refs_0_, f32[1088,128]{1,0:T(8,128)S(1)} %get-tuple-element.66.refs_1_.refs_5_, bf16[512,512]{1,0:T(8,128)(2,1)} %collective-permute-done.refs_2_, ...), custom_call_target="tpu_custom_call", output_to_operand_aliasing={{0}: (4, {})} | custom-call | flops 5368709120 | bytes 62914560 | tf_op jit(solution)/shard_map/blend/pallas_call | solution.py:279
  23.4 0.2 collective-permute-start.3
  23.6 3.2 %blend.9 = (f32[2,2048,512]{2,1,0:T(8,128)}, bf16[512,512]{1,0:T(8,128)(2,1)S(1)}, f32[1088,128]{1,0:T(8,128)S(1)}) custom-call(s32[10]{0:T(128)S(1)} %pad_add_fusion.1.refs_0_, f32[1088,128]{1,0:T(8,128)S(1)} %get-tuple-element.69.refs_1_.refs_5_, bf16[512,512]{1,0:T(8,128)(2,1)} %collective-permute-done.1.refs_2_, ...), custom_call_target="tpu_custom_call", output_to_operand_aliasing={{0}: (4, {})} | custom-call | flops 5368709120 | bytes 62914560 | tf_op jit(solution)/shard_map/blend/pallas_call | solution.py:279
  26.8 0.3 collective-permute-start.5
  27.2 3.2 %blend.10 = (f32[2,2048,512]{2,1,0:T(8,128)}, bf16[2,512,512]{2,1,0:T(8,128)(2,1)S(1)}, f32[1088,128]{1,0:T(8,128)S(1)}) custom-call(s32[10]{0:T(128)S(1)} %pad_add_fusion.1.refs_0_, f32[1088,128]{1,0:T(8,128)S(1)} %get-tuple-element.72.refs_1_.refs_6_, bf16[512,512]{1,0:T(8,128)(2,1)S(1)} %collective-permute-done.2.refs_2_, ...), custom_call_target="tpu_custom_call", output_to_operand_aliasing={{0}: (4, {})} | custom-call | flops 5368709120 | bytes 62914560 | tf_op jit(solution)/shard_map/blend/pallas_call | solution.py:279
  30.3 1.8 %fetch.2.refs_1_.refs_4_ = f32[512,512]{1,0:T(8,128)S(1)} custom-call(s32[10]{0:T(128)S(1)} %pad_add_fusion.1.refs_0_, f32[1088,128]{1,0:T(8,128)S(1)} %get-tuple-element.74.refs_1_.refs_7_, f32[2,2048,512]{2,1,0:T(8,128)} %refs_4_.1), custom_call_target="tpu_custom_call" | custom-call | bytes 41943040 | tf_op jit(solution)/shard_map/fetch/pallas_call | solution.py:279
  32.2 1.4 %blend_last.2 = (f32[2,2048,512]{2,1,0:T(8,128)}, bf16[2,512,512]{2,1,0:T(8,128)(2,1)S(1)}, f32[2,4,136,128]{3,2,1,0:T(8,128)S(1)}) custom-call(s32[16,128]{1,0:T(8,128)S(1)} %broadcast_in_dim.24.refs_0_, f32[512,512]{1,0:T(8,128)S(1)} %fetch.2.refs_1_.refs_4_, ...), custom_call_target="tpu_custom_call", output_to_operand_aliasing={{0}: (5, {}), {1}: (6, {})} | custom-call | flops 5368709120 | bytes 62914560 | tf_op jit(solution)/shard_map/blend_last/pallas_call | solution.py:279
  33.6 1.6 %collective-permute-start.6 = (f32[4,136,128]{2,1,0:T(8,128)S(1)}, f32[4,136,128]{2,1,0:T(8,128)S(1)}, u32[]{:S(2)}, u32[]{:S(2)}) collective-permute-start(f32[4,136,128]{2,1,0:T(8,128)S(1)} %slice_bitcast_fusion.1), channel_id=1, source_target_pairs={{0,1},{1,0},{2,3},{3,2},{4,5},{5,4},{6,7},{7,6},{8,9},{9,8},{10,11... | collective-permute-start | bytes 835592 | tf_op jit(solution)/shard_map/ppermute | solution.py:697
  35.2 1.8 %fetch.3.refs_0_.refs_3_ = f32[512,512]{1,0:T(8,128)S(1)} custom-call(s32[10]{0:T(128)S(1)} %pad_add_fusion.1.refs_0_, f32[2,4,136,128]{3,2,1,0:T(8,128)S(1)} %get-tuple-element.78.refs_1_.refs_2_, f32[2,2048,512]{2,1,0:T(8,128)} %refs_4_.1), custom_call_target="tpu_custom_call" | custom-call | bytes 41943040 | tf_op jit(solution)/shard_map/fetch/pallas_call | solution.py:279
  37.0 5.4 %collective-permute-done.6.refs_3_ = f32[4,136,128]{2,1,0:T(8,128)S(1)} collective-permute-done((f32[4,136,128]{2,1,0:T(8,128)S(1)}, f32[4,136,128]{2,1,0:T(8,128)S(1)}, u32[]{:S(2)}, u32[]{:S(2)}) %collective-permute-start.6) | collective-permute-done | bytes 278560 | tf_op jit(solution)/shard_map/ppermute | solution.py:697
  42.4 1.6 %collective-permute-start.9 = (f32[136,128]{1,0:T(8,128)S(1)}, f32[136,128]{1,0:T(8,128)S(1)}, u32[]{:S(2)}, u32[]{:S(2)}) collective-permute-start(f32[136,128]{1,0:T(8,128)S(1)} %get-tuple-element.89), channel_id=1, source_target_pairs={{0,2},{1,3},{2,0},{3,1},{4,6},{5,7},{6,4},{7,5},{8,10},{9,11},{10,... | collective-permute-start | bytes 208904 | tf_op jit(solution)/shard_map/ppermute | solution.py:700
  44.1 2.6 %collective-permute-start.10 = (f32[136,128]{1,0:T(8,128)S(1)}, f32[136,128]{1,0:T(8,128)S(1)}, u32[]{:S(2)}, u32[]{:S(2)}) collective-permute-start(f32[136,128]{1,0:T(8,128)S(1)} %get-tuple-element.90), channel_id=1, source_target_pairs={{0,4},{1,5},{2,6},{3,7},{4,0},{5,1},{6,2},{7,3},{8,12},{9,13},{10,... | collective-permute-start | bytes 208904 | tf_op jit(solution)/shard_map/ppermute | solution.py:700
  46.7 0.2 collective-permute-start.11
  46.9 3.2 %blend.11 = (f32[2,2048,512]{2,1,0:T(8,128)}, bf16[2,512,512]{2,1,0:T(8,128)(2,1)S(1)}, f32[1088,128]{1,0:T(8,128)S(1)}, bf16[2,512,512]{2,1,0:T(8,128)(2,1)S(1)}) custom-call(s32[10]{0:T(128)S(1)} %pad_add_fusion.1.refs_0_, f32[136,128]{1,0:T(8,128)S(1)} %get-tuple-element.80.refs_1_.refs_2_, ...), custom_call_target="tpu_custom_call", output_to_operand_aliasing={{0}: (5, {}), {3}: (2, {})} | custom-call | flops 5368709120 | bytes 62914560 | tf_op jit(solution)/shard_map/blend/pallas_call | solution.py:279
  50.1 0.3 collective-permute-start.16
  50.4 1.6 %collective-permute-done.8.refs_2_ = bf16[512,512]{1,0:T(8,128)(2,1)S(1)} collective-permute-done((bf16[512,512]{1,0:T(8,128)(2,1)S(1)}, bf16[512,512]{1,0:T(8,128)(2,1)S(1)}, u32[]{:S(2)}, u32[]{:S(2)}) %collective-permute-start.8) | collective-permute-done | bytes 524320 | tf_op jit(solution)/shard_map/ppermute | solution.py:656
  52.0 1.4 %blend_last.3 = (f32[2,2048,512]{2,1,0:T(8,128)}, bf16[2,512,512]{2,1,0:T(8,128)(2,1)S(1)}, f32[2,4,136,128]{3,2,1,0:T(8,128)S(1)}) custom-call(s32[16,128]{1,0:T(8,128)S(1)} %broadcast_in_dim.24.refs_0_, f32[1088,128]{1,0:T(8,128)S(1)} %get-tuple-element.84.refs_1_.refs_6_, ...), custom_call_target="tpu_custom_call", output_to_operand_aliasing={{0}: (4, {}), {1}: (5, {})} | custom-call | flops 5368709120 | bytes 62914560 | tf_op jit(solution)/shard_map/blend_last/pallas_call | solution.py:279
  53.5 1.6 %collective-permute-start.12 = (f32[4,136,128]{2,1,0:T(8,128)S(1)}, f32[4,136,128]{2,1,0:T(8,128)S(1)}, u32[]{:S(2)}, u32[]{:S(2)}) collective-permute-start(f32[4,136,128]{2,1,0:T(8,128)S(1)} %slice_bitcast_fusion), channel_id=1, source_target_pairs={{0,1},{1,0},{2,3},{3,2},{4,5},{5,4},{6,7},{7,6},{8,9},{9,8},{10,11... | collective-permute-start | bytes 835592 | tf_op jit(solution)/shard_map/ppermute | solution.py:697
  55.1 3.6 %collective-permute-start.15 = (f32[136,128]{1,0:T(8,128)S(1)}, f32[136,128]{1,0:T(8,128)S(1)}, u32[]{:S(2)}, u32[]{:S(2)}) collective-permute-start(f32[136,128]{1,0:T(8,128)S(1)} %get-tuple-element.92.refs_0_.refs_2_), channel_id=1, source_target_pairs={{0,6},{1,7},{2,4},{3,5},{4,2},{5,3},{6,0},{7,1},{8,14},{9,15},{10,... | collective-permute-start | bytes 208904 | tf_op jit(solution)/shard_map/ppermute | solution.py:700
  58.7 0.8 collective-permute-start.13
  59.5 3.0 %collective-permute-done.12.refs_2_ = f32[4,136,128]{2,1,0:T(8,128)S(1)} collective-permute-done((f32[4,136,128]{2,1,0:T(8,128)S(1)}, f32[4,136,128]{2,1,0:T(8,128)S(1)}, u32[]{:S(2)}, u32[]{:S(2)}) %collective-permute-start.12) | collective-permute-done | bytes 278560 | tf_op jit(solution)/shard_map/ppermute | solution.py:697
  62.5 2.7 %collective-permute-done.14.refs_4_ = f32[136,128]{1,0:T(8,128)S(1)} collective-permute-done((f32[136,128]{1,0:T(8,128)S(1)}, f32[136,128]{1,0:T(8,128)S(1)}, u32[]{:S(2)}, u32[]{:S(2)}) %collective-permute-start.14) | collective-permute-done | bytes 69664 | tf_op jit(solution)/shard_map/ppermute | solution.py:700
  65.3 0.6 collective-permute-start.25
  65.8 0.4 collective-permute-start.17
  66.2 2.7 %collective-permute-start.18 = (f32[136,128]{1,0:T(8,128)S(1)}, f32[136,128]{1,0:T(8,128)S(1)}, u32[]{:S(2)}, u32[]{:S(2)}) collective-permute-start(f32[136,128]{1,0:T(8,128)S(1)} %get-tuple-element.99), channel_id=1, source_target_pairs={{0,4},{1,5},{2,6},{3,7},{4,0},{5,1},{6,2},{7,3},{8,12},{9,13},{10,... | collective-permute-start | bytes 208904 | tf_op jit(solution)/shard_map/ppermute | solution.py:700
  68.9 1.4 %collective-permute-start.19 = (f32[136,128]{1,0:T(8,128)S(1)}, f32[136,128]{1,0:T(8,128)S(1)}, u32[]{:S(2)}, u32[]{:S(2)}) collective-permute-start(f32[136,128]{1,0:T(8,128)S(1)} %get-tuple-element.100), channel_id=1, source_target_pairs={{0,6},{1,7},{2,4},{3,5},{4,2},{5,3},{6,0},{7,1},{8,14},{9,15},{10,... | collective-permute-start | bytes 208904 | tf_op jit(solution)/shard_map/ppermute | solution.py:700
  70.3 4.0 %collective-permute-done.18.refs_5_ = f32[136,128]{1,0:T(8,128)S(1)} collective-permute-done((f32[136,128]{1,0:T(8,128)S(1)}, f32[136,128]{1,0:T(8,128)S(1)}, u32[]{:S(2)}, u32[]{:S(2)}) %collective-permute-start.18) | collective-permute-done | bytes 69664 | tf_op jit(solution)/shard_map/ppermute | solution.py:700
  74.3 0.8 collective-permute-done.19.refs_6_
  75.1 1.1 collective-permute-done.16.refs_1_
  76.2 1.6 %collective-permute-start.23 = (f32[4,136,128]{2,1,0:T(8,128)S(1)}, f32[4,136,128]{2,1,0:T(8,128)S(1)}, u32[]{:S(2)}, u32[]{:S(2)}) collective-permute-start(f32[4,136,128]{2,1,0:T(8,128)S(1)} %get-tuple-element.102.refs_2_), channel_id=1, source_target_pairs={{0,1},{1,0},{2,3},{3,2},{4,5},{5,4},{6,7},{7,6},{8,9},{9,8},{10,11... | collective-permute-start | bytes 835592 | tf_op jit(solution)/shard_map/ppermute | solution.py:697
  77.8 3.6 %collective-permute-start.22 = (f32[136,128]{1,0:T(8,128)S(1)}, f32[136,128]{1,0:T(8,128)S(1)}, u32[]{:S(2)}, u32[]{:S(2)}) collective-permute-start(f32[136,128]{1,0:T(8,128)S(1)} %get-tuple-element.101.refs_0_.refs_1_), channel_id=1, source_target_pairs={{0,6},{1,7},{2,4},{3,5},{4,2},{5,3},{6,0},{7,1},{8,14},{9,15},{10,... | collective-permute-start | bytes 208904 | tf_op jit(solution)/shard_map/ppermute | solution.py:700
  81.4 0.8 collective-permute-start.20
  82.1 1.7 %collective-permute-done.22.refs_4_ = f32[136,128]{1,0:T(8,128)S(1)} collective-permute-done((f32[136,128]{1,0:T(8,128)S(1)}, f32[136,128]{1,0:T(8,128)S(1)}, u32[]{:S(2)}, u32[]{:S(2)}) %collective-permute-start.22) | collective-permute-done | bytes 69664 | tf_op jit(solution)/shard_map/ppermute | solution.py:700
  83.9 2.7 %collective-permute-done.21.refs_3_ = f32[136,128]{1,0:T(8,128)S(1)} collective-permute-done((f32[136,128]{1,0:T(8,128)S(1)}, f32[136,128]{1,0:T(8,128)S(1)}, u32[]{:S(2)}, u32[]{:S(2)}) %collective-permute-start.21) | collective-permute-done | bytes 69664 | tf_op jit(solution)/shard_map/ppermute | solution.py:700
  86.6 0.6 collective-permute-start.24
  87.2 5.9 %polynomial.2.refs_1_.refs_4_ = bf16[1040,128]{1,0:T(8,128)(2,1)S(1)} custom-call(s32[16,128]{1,0:T(8,128)S(1)} %broadcast_in_dim.24.refs_0_, f32[4,136,128]{2,1,0:T(8,128)S(1)} %stack.12.refs_1_.refs_2_, f32[4,136,128]{2,1,0:T(8,128)S(1)} %get-tuple-element.102.refs_2_, f32[4,136,128]{2,1,0:T(8,128)S(1)} %collective-permute-done.23.refs_3_), custom_call_target="tpu_custom_call" | custom-call | flops 2684354560 | bytes 1310720 | tf_op jit(solution)/shard_map/polynomial/pallas_call | solution.py:279
  93.2 0.9 collective-permute-start.27
  94.1 6.1 %polynomial.3.refs_0_.refs_4_ = bf16[1040,128]{1,0:T(8,128)(2,1)S(1)} custom-call(s32[16,128]{1,0:T(8,128)S(1)} %broadcast_in_dim.24.refs_0_, bf16[1040,128]{1,0:T(8,128)(2,1)S(1)} %polynomial.2.refs_1_.refs_4_, f32[4,136,128]{2,1,0:T(8,128)S(1)} %stack.12.refs_1_.refs_2_, f32[4,136,128]{2,1,0:T(8,128)S(1)} %collective-permute-done.24.refs_3_), custom_call_target="tpu_custom_call" | custom-call | flops 2684354560 | bytes 1310720 | tf_op jit(solution)/shard_map/polynomial/pallas_call | solution.py:279
  100.2 1.3 %collective-permute-start.31 = (bf16[1040,128]{1,0:T(8,128)(2,1)S(1)}, bf16[1040,128]{1,0:T(8,128)(2,1)S(1)}, u32[]{:S(2)}, u32[]{:S(2)}) collective-permute-start(bf16[1040,128]{1,0:T(8,128)(2,1)S(1)} %polynomial.3.refs_0_.refs_4_), channel_id=1, source_target_pairs={{0,16},{8,24},{16,0},{24,8},{1,17},{9,25},{17,1},{25,9},{2,18},{10... | collective-permute-start | bytes 798728 | tf_op jit(solution)/shard_map/ppermute | solution.py:722
  101.5 0.5 collective-permute-start.32
  102.0 1.6 %finish.5 = (bf16[8,512,512]{2,1,0:T(8,128)(2,1)}, f32[8,128]{1,0:T(8,128)S(1)}) custom-call(s32[16,128]{1,0:T(8,128)S(1)} %broadcast_in_dim.24.refs_0_, bf16[2,512,512]{2,1,0:T(8,128)(2,1)S(1)} %get-tuple-element.104.refs_1_.refs_2_, bf16[512,512]{1,0:T(8,128)(2,1)S(1)} %copy-done.3, bf16[512,512]{1,0:T(8,128)(2,1)S(1)} %collective-permute-done.3.refs_2_.refs_3_, ...), custom_call_target="tpu_custom_call" | custom-call | flops 10737418240 | bytes 41943040 | tf_op jit(solution)/shard_map/finish/pallas_call | solution.py:279
  103.6 0.5 collective-permute-start.30
  104.1 1.6 %finish.6 = (bf16[8,512,512]{2,1,0:T(8,128)(2,1)}, f32[8,128]{1,0:T(8,128)S(1)}) custom-call(s32[16,128]{1,0:T(8,128)S(1)} %broadcast_in_dim.24.refs_0_, bf16[1040,128]{1,0:T(8,128)(2,1)S(1)} %step.4.refs_1_.refs_4_, bf16[512,512]{1,0:T(8,128)(2,1)S(1)} %get-tuple-element.107.refs_2_, ...), custom_call_target="tpu_custom_call", output_to_operand_aliasing={{0}: (6, {})} | custom-call | flops 10737418240 | bytes 41943040 | tf_op jit(solution)/shard_map/finish/pallas_call | solution.py:279
  105.7 0.6 collective-permute-done.30.refs_5_
  106.4 1.6 %finish.7 = (bf16[8,512,512]{2,1,0:T(8,128)(2,1)}, f32[8,128]{1,0:T(8,128)S(1)}) custom-call(s32[16,128]{1,0:T(8,128)S(1)} %broadcast_in_dim.24.refs_0_, f32[8,128]{1,0:T(8,128)S(1)} %get-tuple-element.109.refs_1_, bf16[2,512,512]{2,1,0:T(8,128)(2,1)S(1)} %get-tuple-element.104.refs_1_.refs_2_, ...), custom_call_target="tpu_custom_call", output_to_operand_aliasing={{0}: (6, {})} | custom-call | flops 10737418240 | bytes 41943040 | tf_op jit(solution)/shard_map/finish/pallas_call | solution.py:279
  108.0 0.7 collective-permute-done.31.refs_1_
  108.7 1.2 %finish.8 = (bf16[8,512,512]{2,1,0:T(8,128)(2,1)}, f32[8,128]{1,0:T(8,128)S(1)}) custom-call(s32[16,128]{1,0:T(8,128)S(1)} %broadcast_in_dim.24.refs_0_, bf16[1040,128]{1,0:T(8,128)(2,1)S(1)} %step.5.refs_1_.refs_3_, bf16[2,512,512]{2,1,0:T(8,128)(2,1)S(1)} %get-tuple-element.112.refs_2_, ...), custom_call_target="tpu_custom_call", output_to_operand_aliasing={{0}: (4, {})} | custom-call | flops 5368709120 | bytes 20971520 | tf_op jit(solution)/shard_map/finish/pallas_call | solution.py:279
  110.0 0.3 collective-permute-done.33.refs_3_
  110.2 1.8 %finish.9 = (bf16[8,512,512]{2,1,0:T(8,128)(2,1)}, f32[8,128]{1,0:T(8,128)}) custom-call(s32[16,128]{1,0:T(8,128)S(1)} %broadcast_in_dim.24.refs_0_, f32[8,128]{1,0:T(8,128)S(1)} %get-tuple-element.114.refs_1_, bf16[2,512,512]{2,1,0:T(8,128)(2,1)S(1)} %collective-permute-done.32.refs_2_, ...), custom_call_target="tpu_custom_call", output_to_operand_aliasing={{0}: (4, {})} | custom-call | flops 5368709120 | bytes 20971520 | tf_op jit(solution)/shard_map/finish/pallas_call | solution.py:279
  (54 shorter events, 0.6 us)
Async XLA Ops:
  3.0 24.2 %collective-permute-start.2 = (bf16[512,512]{1,0:T(8,128)(2,1)S(1)}, bf16[512,512]{1,0:T(8,128)(2,1)S(1)}, u32[]{:S(2)}, u32[]{:S(2)}) collective-permute-start(bf16[512,512]{1,0:T(8,128)(2,1)S(1)} %pick.2.refs_1_), channel_id=1, source_target_pairs={{0,16},{8,24},{16,0},{24,8},{1,17},{9,25},{17,1},{25,9},{2,18},{10... | collective-permute-start | bytes 1572872 | tf_op jit(solution)/shard_map/ppermute | solution.py:656
  9.4 10.8 %collective-permute-start = (bf16[512,512]{1,0:T(8,128)(2,1)}, bf16[512,512]{1,0:T(8,128)(2,1)}, u32[]{:S(2)}, u32[]{:S(2)}) collective-permute-start(bf16[512,512]{1,0:T(8,128)(2,1)} %get-tuple-element.67), channel_id=1, source_target_pairs={{0,8},{8,0},{16,24},{24,16},{1,9},{9,1},{17,25},{25,17},{2,10},{10... | collective-permute-start | bytes 1572872 | tf_op jit(solution)/shard_map/ppermute | solution.py:656
  9.5 22.6 %collective-permute-start.4 = (bf16[512,512]{1,0:T(8,128)(2,1)S(1)}, bf16[512,512]{1,0:T(8,128)(2,1)S(1)}, u32[]{:S(2)}, u32[]{:S(2)}) collective-permute-start(bf16[512,512]{1,0:T(8,128)(2,1)S(1)} %get-tuple-element.60.refs_1_), channel_id=1, source_target_pairs={{0,24},{8,16},{16,8},{24,0},{1,25},{9,17},{17,9},{25,1},{2,26},{10... | collective-permute-start | bytes 1572872 | tf_op jit(solution)/shard_map/ppermute | solution.py:656
  9.6 7.0 %copy-start.4 = (s32[8]{0:T(128)S(1)}, s32[8]{0:T(128)}, u32[]{:S(2)}) copy-start(s32[8]{0:T(128)} %param.5) | copy-start | bytes 100
  12.9 0.8 copy-start
  13.7 0.8 copy-start.2
  14.5 9.1 %collective-permute-start.1 = (bf16[512,512]{1,0:T(8,128)(2,1)}, bf16[512,512]{1,0:T(8,128)(2,1)}, u32[]{:S(2)}, u32[]{:S(2)}) collective-permute-start(bf16[512,512]{1,0:T(8,128)(2,1)} %get-tuple-element.70), channel_id=1, source_target_pairs={{0,8},{8,0},{16,24},{24,16},{1,9},{9,1},{17,25},{25,17},{2,10},{10... | collective-permute-start | bytes 1572872 | tf_op jit(solution)/shard_map/ppermute | solution.py:656
  14.8 32.1 %collective-permute-start.7 = (bf16[512,512]{1,0:T(8,128)(2,1)}, bf16[512,512]{1,0:T(8,128)(2,1)S(1)}, u32[]{:S(2)}, u32[]{:S(2)}) collective-permute-start(bf16[512,512]{1,0:T(8,128)(2,1)} %get-tuple-element.82), channel_id=1, source_target_pairs={{0,16},{8,24},{16,0},{24,8},{1,17},{9,25},{17,1},{25,9},{2,18},{10... | collective-permute-start | bytes 1572872 | tf_op jit(solution)/shard_map/ppermute | solution.py:656
  23.4 8.7 %collective-permute-start.3 = (bf16[512,512]{1,0:T(8,128)(2,1)S(1)}, bf16[512,512]{1,0:T(8,128)(2,1)S(1)}, u32[]{:S(2)}, u32[]{:S(2)}) collective-permute-start(bf16[512,512]{1,0:T(8,128)(2,1)S(1)} %get-tuple-element.75), channel_id=1, source_target_pairs={{0,8},{8,0},{16,24},{24,16},{1,9},{9,1},{17,25},{25,17},{2,10},{10... | collective-permute-start | bytes 1572872 | tf_op jit(solution)/shard_map/ppermute | solution.py:691
  26.8 10.2 %collective-permute-start.5 = (bf16[512,512]{1,0:T(8,128)(2,1)S(1)}, bf16[512,512]{1,0:T(8,128)(2,1)S(1)}, u32[]{:S(2)}, u32[]{:S(2)}) collective-permute-start(bf16[512,512]{1,0:T(8,128)(2,1)S(1)} %get-tuple-element.79), channel_id=1, source_target_pairs={{0,8},{8,0},{16,24},{24,16},{1,9},{9,1},{17,25},{25,17},{2,10},{10... | collective-permute-start | bytes 1572872 | tf_op jit(solution)/shard_map/ppermute | solution.py:691
  32.2 3.0 %copy-start.1 = (bf16[512,512]{1,0:T(8,128)(2,1)S(1)}, bf16[512,512]{1,0:T(8,128)(2,1)}, u32[]{:S(2)}) copy-start(bf16[512,512]{1,0:T(8,128)(2,1)} %copy-done) | copy-start | bytes 1572868
  33.6 8.8 %collective-permute-start.6 = (f32[4,136,128]{2,1,0:T(8,128)S(1)}, f32[4,136,128]{2,1,0:T(8,128)S(1)}, u32[]{:S(2)}, u32[]{:S(2)}) collective-permute-start(f32[4,136,128]{2,1,0:T(8,128)S(1)} %slice_bitcast_fusion.1), channel_id=1, source_target_pairs={{0,1},{1,0},{2,3},{3,2},{4,5},{5,4},{6,7},{7,6},{8,9},{9,8},{10,11... | collective-permute-start | bytes 835592 | tf_op jit(solution)/shard_map/ppermute | solution.py:697
  35.2 16.8 %collective-permute-start.8 = (bf16[512,512]{1,0:T(8,128)(2,1)S(1)}, bf16[512,512]{1,0:T(8,128)(2,1)S(1)}, u32[]{:S(2)}, u32[]{:S(2)}) collective-permute-start(bf16[512,512]{1,0:T(8,128)(2,1)S(1)} %copy-done.1), channel_id=1, source_target_pairs={{0,24},{8,16},{16,8},{24,0},{1,25},{9,17},{17,9},{25,1},{2,26},{10... | collective-permute-start | bytes 1572872 | tf_op jit(solution)/shard_map/ppermute | solution.py:656
  42.4 11.0 %collective-permute-start.9 = (f32[136,128]{1,0:T(8,128)S(1)}, f32[136,128]{1,0:T(8,128)S(1)}, u32[]{:S(2)}, u32[]{:S(2)}) collective-permute-start(f32[136,128]{1,0:T(8,128)S(1)} %get-tuple-element.89), channel_id=1, source_target_pairs={{0,2},{1,3},{2,0},{3,1},{4,6},{5,7},{6,4},{7,5},{8,10},{9,11},{10,... | collective-permute-start | bytes 208904 | tf_op jit(solution)/shard_map/ppermute | solution.py:700
  44.1 9.4 %collective-permute-start.10 = (f32[136,128]{1,0:T(8,128)S(1)}, f32[136,128]{1,0:T(8,128)S(1)}, u32[]{:S(2)}, u32[]{:S(2)}) collective-permute-start(f32[136,128]{1,0:T(8,128)S(1)} %get-tuple-element.90), channel_id=1, source_target_pairs={{0,4},{1,5},{2,6},{3,7},{4,0},{5,1},{6,2},{7,3},{8,12},{9,13},{10,... | collective-permute-start | bytes 208904 | tf_op jit(solution)/shard_map/ppermute | solution.py:700
  46.7 6.8 %collective-permute-start.11 = (f32[136,128]{1,0:T(8,128)S(1)}, f32[136,128]{1,0:T(8,128)S(1)}, u32[]{:S(2)}, u32[]{:S(2)}) collective-permute-start(f32[136,128]{1,0:T(8,128)S(1)} %get-tuple-element.91), channel_id=1, source_target_pairs={{0,6},{1,7},{2,4},{3,5},{4,2},{5,3},{6,0},{7,1},{8,14},{9,15},{10,... | collective-permute-start | bytes 208904 | tf_op jit(solution)/shard_map/ppermute | solution.py:700
  50.1 26.1 %collective-permute-start.16 = (bf16[2,512,512]{2,1,0:T(8,128)(2,1)S(1)}, bf16[2,512,512]{2,1,0:T(8,128)(2,1)S(1)}, u32[]{:S(2)}, u32[]{:S(2)}) collective-permute-start(bf16[2,512,512]{2,1,0:T(8,128)(2,1)S(1)} %get-tuple-element.97), channel_id=1, source_target_pairs={{0,16},{8,24},{16,0},{24,8},{1,17},{9,25},{17,1},{25,9},{2,18},{10... | collective-permute-start | bytes 3145736 | tf_op jit(solution)/shard_map/ppermute | solution.py:693
  53.5 8.9 %collective-permute-start.12 = (f32[4,136,128]{2,1,0:T(8,128)S(1)}, f32[4,136,128]{2,1,0:T(8,128)S(1)}, u32[]{:S(2)}, u32[]{:S(2)}) collective-permute-start(f32[4,136,128]{2,1,0:T(8,128)S(1)} %slice_bitcast_fusion), channel_id=1, source_target_pairs={{0,1},{1,0},{2,3},{3,2},{4,5},{5,4},{6,7},{7,6},{8,9},{9,8},{10,11... | collective-permute-start | bytes 835592 | tf_op jit(solution)/shard_map/ppermute | solution.py:697
  55.1 7.4 %collective-permute-start.15 = (f32[136,128]{1,0:T(8,128)S(1)}, f32[136,128]{1,0:T(8,128)S(1)}, u32[]{:S(2)}, u32[]{:S(2)}) collective-permute-start(f32[136,128]{1,0:T(8,128)S(1)} %get-tuple-element.92.refs_0_.refs_2_), channel_id=1, source_target_pairs={{0,6},{1,7},{2,4},{3,5},{4,2},{5,3},{6,0},{7,1},{8,14},{9,15},{10,... | collective-permute-start | bytes 208904 | tf_op jit(solution)/shard_map/ppermute | solution.py:700
  58.7 6.5 %collective-permute-start.14 = (f32[136,128]{1,0:T(8,128)S(1)}, f32[136,128]{1,0:T(8,128)S(1)}, u32[]{:S(2)}, u32[]{:S(2)}) collective-permute-start(f32[136,128]{1,0:T(8,128)S(1)} %get-tuple-element.92.refs_0_.refs_2_), channel_id=1, source_target_pairs={{0,4},{1,5},{2,6},{3,7},{4,0},{5,1},{6,2},{7,3},{8,12},{9,13},{10,... | collective-permute-start | bytes 208904 | tf_op jit(solution)/shard_map/ppermute | solution.py:700
  58.7 6.5 %collective-permute-start.13 = (f32[136,128]{1,0:T(8,128)S(1)}, f32[136,128]{1,0:T(8,128)S(1)}, u32[]{:S(2)}, u32[]{:S(2)}) collective-permute-start(f32[136,128]{1,0:T(8,128)S(1)} %get-tuple-element.92.refs_0_.refs_2_), channel_id=1, source_target_pairs={{0,2},{1,3},{2,0},{3,1},{4,6},{5,7},{6,4},{7,5},{8,10},{9,11},{10,... | collective-permute-start | bytes 208904 | tf_op jit(solution)/shard_map/ppermute | solution.py:700
  65.3 36.2 %collective-permute-start.25 = (bf16[2,512,512]{2,1,0:T(8,128)(2,1)S(1)}, bf16[2,512,512]{2,1,0:T(8,128)(2,1)S(1)}, u32[]{:S(2)}, u32[]{:S(2)}) collective-permute-start(bf16[2,512,512]{2,1,0:T(8,128)(2,1)S(1)} %get-tuple-element.103), channel_id=1, source_target_pairs={{0,16},{8,24},{16,0},{24,8},{1,17},{9,25},{17,1},{25,9},{2,18},{10... | collective-permute-start | bytes 3145736 | tf_op jit(solution)/shard_map/ppermute | solution.py:693
  65.8 4.4 %collective-permute-start.17 = (f32[136,128]{1,0:T(8,128)S(1)}, f32[136,128]{1,0:T(8,128)S(1)}, u32[]{:S(2)}, u32[]{:S(2)}) collective-permute-start(f32[136,128]{1,0:T(8,128)S(1)} %get-tuple-element.98), channel_id=1, source_target_pairs={{0,2},{1,3},{2,0},{3,1},{4,6},{5,7},{6,4},{7,5},{8,10},{9,11},{10,... | collective-permute-start | bytes 208904 | tf_op jit(solution)/shard_map/ppermute | solution.py:700
  66.2 8.0 %collective-permute-start.18 = (f32[136,128]{1,0:T(8,128)S(1)}, f32[136,128]{1,0:T(8,128)S(1)}, u32[]{:S(2)}, u32[]{:S(2)}) collective-permute-start(f32[136,128]{1,0:T(8,128)S(1)} %get-tuple-element.99), channel_id=1, source_target_pairs={{0,4},{1,5},{2,6},{3,7},{4,0},{5,1},{6,2},{7,3},{8,12},{9,13},{10,... | collective-permute-start | bytes 208904 | tf_op jit(solution)/shard_map/ppermute | solution.py:700
  68.9 6.2 %collective-permute-start.19 = (f32[136,128]{1,0:T(8,128)S(1)}, f32[136,128]{1,0:T(8,128)S(1)}, u32[]{:S(2)}, u32[]{:S(2)}) collective-permute-start(f32[136,128]{1,0:T(8,128)S(1)} %get-tuple-element.100), channel_id=1, source_target_pairs={{0,6},{1,7},{2,4},{3,5},{4,2},{5,3},{6,0},{7,1},{8,14},{9,15},{10,... | collective-permute-start | bytes 208904 | tf_op jit(solution)/shard_map/ppermute | solution.py:700
  76.2 11.0 %collective-permute-start.23 = (f32[4,136,128]{2,1,0:T(8,128)S(1)}, f32[4,136,128]{2,1,0:T(8,128)S(1)}, u32[]{:S(2)}, u32[]{:S(2)}) collective-permute-start(f32[4,136,128]{2,1,0:T(8,128)S(1)} %get-tuple-element.102.refs_2_), channel_id=1, source_target_pairs={{0,1},{1,0},{2,3},{3,2},{4,5},{5,4},{6,7},{7,6},{8,9},{9,8},{10,11... | collective-permute-start | bytes 835592 | tf_op jit(solution)/shard_map/ppermute | solution.py:697
  77.8 6.1 %collective-permute-start.22 = (f32[136,128]{1,0:T(8,128)S(1)}, f32[136,128]{1,0:T(8,128)S(1)}, u32[]{:S(2)}, u32[]{:S(2)}) collective-permute-start(f32[136,128]{1,0:T(8,128)S(1)} %get-tuple-element.101.refs_0_.refs_1_), channel_id=1, source_target_pairs={{0,6},{1,7},{2,4},{3,5},{4,2},{5,3},{6,0},{7,1},{8,14},{9,15},{10,... | collective-permute-start | bytes 208904 | tf_op jit(solution)/shard_map/ppermute | solution.py:700
  81.4 5.2 %collective-permute-start.21 = (f32[136,128]{1,0:T(8,128)S(1)}, f32[136,128]{1,0:T(8,128)S(1)}, u32[]{:S(2)}, u32[]{:S(2)}) collective-permute-start(f32[136,128]{1,0:T(8,128)S(1)} %get-tuple-element.101.refs_0_.refs_1_), channel_id=1, source_target_pairs={{0,4},{1,5},{2,6},{3,7},{4,0},{5,1},{6,2},{7,3},{8,12},{9,13},{10,... | collective-permute-start | bytes 208904 | tf_op jit(solution)/shard_map/ppermute | solution.py:700
  81.4 5.2 %collective-permute-start.20 = (f32[136,128]{1,0:T(8,128)S(1)}, f32[136,128]{1,0:T(8,128)S(1)}, u32[]{:S(2)}, u32[]{:S(2)}) collective-permute-start(f32[136,128]{1,0:T(8,128)S(1)} %get-tuple-element.101.refs_0_.refs_1_), channel_id=1, source_target_pairs={{0,2},{1,3},{2,0},{3,1},{4,6},{5,7},{6,4},{7,5},{8,10},{9,11},{10,... | collective-permute-start | bytes 208904 | tf_op jit(solution)/shard_map/ppermute | solution.py:700
  86.6 7.4 %collective-permute-start.24 = (f32[4,136,128]{2,1,0:T(8,128)S(1)}, f32[4,136,128]{2,1,0:T(8,128)S(1)}, u32[]{:S(2)}, u32[]{:S(2)}) collective-permute-start(f32[4,136,128]{2,1,0:T(8,128)S(1)} %stack.12.refs_1_.refs_2_), channel_id=1, source_target_pairs={{0,1},{1,0},{2,3},{3,2},{4,5},{5,4},{6,7},{7,6},{8,9},{9,8},{10,11... | collective-permute-start | bytes 835592 | tf_op jit(solution)/shard_map/ppermute | solution.py:697
  93.1 9.0 %copy-start.3 = (bf16[512,512]{1,0:T(8,128)(2,1)S(1)}, bf16[512,512]{1,0:T(8,128)(2,1)}, u32[]{:S(2)}) copy-start(bf16[512,512]{1,0:T(8,128)(2,1)} %copy-done.2) | copy-start | bytes 1572868
  93.1 8.9 %collective-permute-start.26 = (bf16[1040,128]{1,0:T(8,128)(2,1)S(1)}, bf16[1040,128]{1,0:T(8,128)(2,1)S(1)}, u32[]{:S(2)}, u32[]{:S(2)}) collective-permute-start(bf16[1040,128]{1,0:T(8,128)(2,1)S(1)} %polynomial.2.refs_1_.refs_4_), channel_id=1, source_target_pairs={{0,8},{8,0},{16,24},{24,16},{1,9},{9,1},{17,25},{25,17},{2,10},{10... | collective-permute-start | bytes 798728 | tf_op jit(solution)/shard_map/ppermute | solution.py:724
  93.2 10.4 %collective-permute-start.27 = (bf16[1040,128]{1,0:T(8,128)(2,1)S(1)}, bf16[1040,128]{1,0:T(8,128)(2,1)S(1)}, u32[]{:S(2)}, u32[]{:S(2)}) collective-permute-start(bf16[1040,128]{1,0:T(8,128)(2,1)S(1)} %polynomial.2.refs_1_.refs_4_), channel_id=1, source_target_pairs={{0,16},{8,24},{16,0},{24,8},{1,17},{9,25},{17,1},{25,9},{2,18},{10... | collective-permute-start | bytes 798728 | tf_op jit(solution)/shard_map/ppermute | solution.py:722
  100.2 8.5 %collective-permute-start.31 = (bf16[1040,128]{1,0:T(8,128)(2,1)S(1)}, bf16[1040,128]{1,0:T(8,128)(2,1)S(1)}, u32[]{:S(2)}, u32[]{:S(2)}) collective-permute-start(bf16[1040,128]{1,0:T(8,128)(2,1)S(1)} %polynomial.3.refs_0_.refs_4_), channel_id=1, source_target_pairs={{0,16},{8,24},{16,0},{24,8},{1,17},{9,25},{17,1},{25,9},{2,18},{10... | collective-permute-start | bytes 798728 | tf_op jit(solution)/shard_map/ppermute | solution.py:722
  101.5 2.7 %collective-permute-start.28 = (bf16[1040,128]{1,0:T(8,128)(2,1)S(1)}, bf16[1040,128]{1,0:T(8,128)(2,1)S(1)}, u32[]{:S(2)}, u32[]{:S(2)}) collective-permute-start(bf16[1040,128]{1,0:T(8,128)(2,1)S(1)} %polynomial.3.refs_0_.refs_4_), channel_id=1, source_target_pairs={{0,8},{8,0},{16,24},{24,16},{1,9},{9,1},{17,25},{25,17},{2,10},{10... | collective-permute-start | bytes 798728 | tf_op jit(solution)/shard_map/ppermute | solution.py:724
  101.5 8.5 %collective-permute-start.32 = (bf16[2,512,512]{2,1,0:T(8,128)(2,1)S(1)}, bf16[2,512,512]{2,1,0:T(8,128)(2,1)S(1)}, u32[]{:S(2)}, u32[]{:S(2)}) collective-permute-start(bf16[2,512,512]{2,1,0:T(8,128)(2,1)S(1)} %get-tuple-element.112.refs_2_), channel_id=1, source_target_pairs={{0,8},{8,0},{16,24},{24,16},{1,9},{9,1},{17,25},{25,17},{2,10},{10... | collective-permute-start | bytes 3145736 | tf_op jit(solution)/shard_map/ppermute | solution.py:805
  102.0 4.4 %collective-permute-start.29 = (bf16[2,512,512]{2,1,0:T(8,128)(2,1)S(1)}, bf16[2,512,512]{2,1,0:T(8,128)(2,1)S(1)}, u32[]{:S(2)}, u32[]{:S(2)}) collective-permute-start(bf16[2,512,512]{2,1,0:T(8,128)(2,1)S(1)} %get-tuple-element.104.refs_1_.refs_2_), channel_id=1, source_target_pairs={{0,8},{8,0},{16,24},{24,16},{1,9},{9,1},{17,25},{25,17},{2,10},{10... | collective-permute-start | bytes 3145736 | tf_op jit(solution)/shard_map/ppermute | solution.py:805
  103.6 2.7 %collective-permute-start.30 = (bf16[1040,128]{1,0:T(8,128)(2,1)S(1)}, bf16[1040,128]{1,0:T(8,128)(2,1)S(1)}, u32[]{:S(2)}, u32[]{:S(2)}) collective-permute-start(bf16[1040,128]{1,0:T(8,128)(2,1)S(1)} %step.4.refs_1_.refs_4_), channel_id=1, source_target_pairs={{0,8},{8,0},{16,24},{24,16},{1,9},{9,1},{17,25},{25,17},{2,10},{10... | collective-permute-start | bytes 798728 | tf_op jit(solution)/shard_map/ppermute | solution.py:729
  108.7 1.5 %collective-permute-start.33 = (bf16[1040,128]{1,0:T(8,128)(2,1)S(1)}, bf16[1040,128]{1,0:T(8,128)(2,1)S(1)}, u32[]{:S(2)}, u32[]{:S(2)}) collective-permute-start(bf16[1040,128]{1,0:T(8,128)(2,1)S(1)} %step.5.refs_1_.refs_3_), channel_id=1, source_target_pairs={{0,8},{8,0},{16,24},{24,16},{1,9},{9,1},{17,25},{25,17},{2,10},{10... | collective-permute-start | bytes 798728 | tf_op jit(solution)/shard_map/ppermute | solution.py:729

commit v8 on v7

--- a/solution.py
+++ b/solution.py
@@ -118,6 +118,74 @@
         held[n * TILE : (n + 1) * TILE, :] += part
     for n, part in enumerate(diagonals):
         held[DIAGONALS + n : DIAGONALS + n + 1, :] += part
+
+
+def blend_whole_kernel(slot, d, has_pair, place, gradient, momentum, _buffer, before, *refs):
+    renewed, rows, total, loaded, new, sems = refs[1:] if has_pair else refs
+    size = gradient.shape[0]
+    tile = min(256, size)
+    count = size // tile
+    first = jnp.bitwise_xor(place.owner(), d) * size
+    parts = [pl.ds(n * tile, tile) for n in range(count)]
+    spans = [pl.ds(pl.multiple_of(first + n * tile, 8), tile) for n in range(count)]
+    loads = [
+        pltpu.make_async_copy(momentum.at[slot, spans[n]], loaded.at[parts[n]], sems.at[n])
+        for n in range(count)
+    ]
+    stores = [
+        pltpu.make_async_copy(new.at[parts[n]], renewed.at[slot, spans[n]], sems.at[count + n])
+        for n in range(count)
+    ]
+    for load in loads:
+        load.start()
+    total[...] = before[...]
+    for n, part in enumerate(parts):
+        loads[n].wait()
+        g = gradient[part].astype(f32)
+        m = momentum_decay * loaded[part] + g
+        new[part] = m
+        stores[n].start()
+        x = (g + momentum_decay * m).astype(bf16)
+        if d < 2:
+            rows[part] = x
+        else:
+            rows[d % 2, part] = x
+    add_gram(total, rows[...] if d < 2 else rows[d % 2])
+    for store in stores:
+        store.wait()
+
+
+def blend_whole(line, gradient, momentum, slot, d, buffer, pair, before):
+    size = gradient.shape[0]
+    count = size // min(256, size)
+    aliases = {2: 0}
+    operands, specs = [gradient, in_hbm(momentum), in_hbm(buffer), before], [IN_VMEM, IN_HBM, IN_HBM, IN_VMEM]
+    if pair is not None:
+        aliases[4] = 1
+        operands.append(pair)
+        specs.append(IN_VMEM)
+    return line.run(
+        functools.partial(blend_whole_kernel, slot, d, pair is not None),
+        operands,
+        specs,
+        [
+            pltpu.HBM(buffer.shape, f32),
+            jax.ShapeDtypeStruct((size, RANK) if d < 2 else (2, size, RANK), bf16),
+            jax.ShapeDtypeStruct(before.shape, f32),
+        ],
+        [IN_HBM, IN_VMEM, IN_VMEM],
+        name="blend_whole",
+        scalars=SPOTS,
+        token=2,
+        scratch=[
+            pltpu.VMEM((size, RANK), f32),
+            pltpu.VMEM((size, RANK), f32),
+            pltpu.SemaphoreType.DMA((2 * count,)),
+        ],
+        aliases=aliases,
+        vmem=8,
+        work=(2 * size * RANK * RANK, size * RANK * 12),
+    )
 
 
 def fetch_kernel(slot, d, count, place, momentum, target, sem):
@@ -193,7 +261,15 @@
     )
 
 
-SPOTS = "spots"
+SPOTS, RAW = "spots", "raw"
+
+
+class Column:
+    def __init__(self, ref):
+        self.ref = ref
+
+    def __getitem__(self, k):
+        return self.ref[k, 0]
 
 
 class Spots:
@@ -222,7 +298,7 @@
 class Line:
     def __init__(self, place):
         self.place, self.last, self.due, self.waiting, self.passed = place, None, [], {}, {}
-        self.spots, self.owners = None, 0
+        self.spots, self.raw, self.owners = None, None, 0
 
     def run(
         self,
@@ -248,7 +324,7 @@
         skip, given, results = len(before), len(before) + len(operands), len(out_shape)
         lead = 1 if scalars else 0
         prefetched = scalars is True
-        spots = None if scalars is not SPOTS else self.spots
+        spots = {SPOTS: self.spots, RAW: self.raw}.get(scalars) if lead else None
         aliases = {lead + skip + i: o for i, o in (aliases or {}).items()}
         for k in range(len(keys)):
             aliases[lead + skip - len(keys) + k] = results + k
@@ -256,7 +332,7 @@
         def body(*refs):
             refs, place = refs[lead:], refs[:lead]
             if spots is not None:
-                place = (Spots(place[0], self.owners),)
+                place = (Spots(place[0], self.owners) if scalars is SPOTS else Column(place[0]),)
             kernel(*place, *refs[skip : given + results], *refs[given + results + len(keys) :])
 
         any_spec = pl.BlockSpec(memory_space=pl.ANY)
@@ -319,6 +395,7 @@
         [jax.ShapeDtypeStruct((rows, RANK), bf16) for _ in wanted],
         [IN_VMEM for _ in wanted],
         name="pick",
+        scalars=RAW,
         scratch=[pltpu.SemaphoreType.DMA((len(wanted),))],
         work=(0, 4 * len(wanted) * rows * RANK),
     )
@@ -641,6 +718,7 @@
 
     line = Line(place)
     line.owners = owners
+    line.raw = jnp.broadcast_to(jnp.pad(place, (0, -place.shape[0] % 8))[:, None], (-(-place.shape[0] // 8) * 8, TILE))
     line.spots = make_spots(place, matrix_count, held_slots, owners)
     all_slots = range(held_slots)
     far_steps, near_steps = list(range(2, owners)), list(range(1, min(2, owners)))
@@ -667,6 +745,17 @@
         if d == owners - 1:
             renewed, rows[slot, d], sums[slot] = blend_last(
                 line, gradient, fetched[slot], slot, d, matrix_count, renewed, rows[slot, d - 1], sums[slot], shares
+            )
+        elif d:
+            renewed, rows[slot, d], sums[slot] = blend_whole(
+                line,
+                gradient,
+                momentum,
+                slot,
+                d,
+                renewed,
+                rows[slot, d - 1] if d > 1 and d % 2 else None,
+                sums[slot],
             )
         else:
             renewed, rows[slot, d], sums[slot] = blend(
@@ -765,15 +854,13 @@
         blend_piece(0, d)
     fetched[1] = fetch(line, momentum, 1, owners - 1, matrix_count, gradients.shape[1])
     expect((1, 1))
-    first_sum(0)
     for d in far_steps[1::2]:
         line.waiting[d] = rows[0, d]
-    for d in far_steps[:-1]:
-        blend_piece(1, d)
+    first_sum(0)
     for d in far_steps[1::2]:
         rows[0, d] = line.passed[d]
         send_back(0, d - 1)
-    for d in far_steps[-1:]:
+    for d in far_steps:
         blend_piece(1, d)
     line.waiting["sum"] = sums[1]
     second_sum(0)

time: 113 us -> 112 us (level)
  Pallas kernels: 50.6 us -> 47.9 us
  waiting for transfers between devices: 24.7 us -> 26.4 us
    pallas_call x28, Pallas kernels: 50.6 us -> 47.9 us  [run(): pl.pallas_call(body, **layout, out_shape=out_shape + [jax.ShapeDtypeStruc...]
    ppermute x6, waiting for transfers between devices: 1.65 us -> 3.38 us  [send(): lax.ppermute(picked[slot, d], 'owner', partners(owners, d))]
  transfers between devices with their start and end apart: 34 -> 34, of which waited for: 12 -> 10; matrix products, arithmetic and copies ran while one was open for 0% -> 0% of each run, Pallas kernels for 42% -> 40%
where the time goes in v8:
time: 112 us
  Pallas kernels  47.9 us (43%)
  starting transfers between devices  33.4 us (30%)
  waiting for transfers between devices  26.4 us (24%)
  local copies, waits for them, and re-layouts  1.94 us (2%)
  between operations  1.12 us (1%)
    pallas_call x28, Pallas kernels, run(): pl.pallas_call(body, **layout, out_shape=out_shape + [jax.ShapeDtypeStruc...  47.9 us
    ppermute x12, starting transfers between devices, across_far(): return lax.ppermute(x, 'fsdp', partners(group, e2 * near))  17.6 us
    ppermute x12, waiting for transfers between devices, across_far(): return lax.ppermute(x, 'fsdp', partners(group, e2 * near))  12 us
    ppermute x4, waiting for transfers between devices, across_near(): return lax.ppermute(x, 'fsdp', partners(group, e1))  8.62 us
    ppermute x4, starting transfers between devices, across_near(): return lax.ppermute(x, 'fsdp', partners(group, e1))  5.35 us
    ppermute x6, starting transfers between devices, send(): lax.ppermute(picked[slot, d], 'owner', partners(owners, d))  5.32 us
    ppermute x6, waiting for transfers between devices, send(): lax.ppermute(picked[slot, d], 'owner', partners(owners, d))  3.38 us
  transfers between devices with their start and end apart: 34, of which 10 were waited for; matrix products, arithmetic and copies ran while one was open for 0% of the time, Pallas kernels for 40%

profile of v8, /device:TPU:0, one launch (start us, length us, event | category | flops | bytes accessed | tf_op | source)
XLA Modules:
  0.0 111.8 jit_solution(8136890313078663986)
XLA Ops:
  0.6 0.7 pad_add_fusion.1.refs_0_
  1.4 0.1 broadcast_in_dim.19.refs_0_
  1.4 1.1 pick.2.refs_1_
  2.6 3.0 %collective-permute-start.2 = (bf16[512,512]{1,0:T(8,128)(2,1)S(1)}, bf16[512,512]{1,0:T(8,128)(2,1)S(1)}, u32[]{:S(2)}, u32[]{:S(2)}) collective-permute-start(bf16[512,512]{1,0:T(8,128)(2,1)S(1)} %pick.2.refs_1_), channel_id=1, source_target_pairs={{0,16},{8,24},{16,0},{24,8},{1,17},{9,25},{17,1},{25,9},{2,18},{10... | collective-permute-start | bytes 1572872 | tf_op jit(solution)/shard_map/ppermute | solution.py:734
  5.6 2.9 %pick.3 = (bf16[512,512]{1,0:T(8,128)(2,1)S(1)}, bf16[512,512]{1,0:T(8,128)(2,1)}, bf16[512,512]{1,0:T(8,128)(2,1)}, bf16[512,512]{1,0:T(8,128)(2,1)}, bf16[512,512]{1,0:T(8,128)(2,1)S(1)}) custom-call(s32[16,128]{1,0:T(8,128)S(1)} %broadcast_in_dim.19.refs_0_, bf16[512,512]{1,0:T(8,128)(2,1)S(1)} %pick.2.refs_1_, bf16[8,512,512]{2,1,0:T(8,128)(2,1)} %refs_2_.5), custom_call_target="tpu_custom_call" | custom-call | bytes 104857600 | tf_op jit(solution)/shard_map/pick/pallas_call | solution.py:355
  8.5 0.1 collective-permute-start
  8.6 0.1 collective-permute-start.4
  8.7 3.3 %blend.2 = (f32[2,2048,512]{2,1,0:T(8,128)}, bf16[512,512]{1,0:T(8,128)(2,1)S(1)}, f32[1088,128]{1,0:T(8,128)S(1)}, bf16[512,512]{1,0:T(8,128)(2,1)}, bf16[512,5...) custom-call(s32[10]{0:T(128)S(1)} %pad_add_fusion.1.refs_0_, ...), custom_call_target="tpu_custom_call", output_to_operand_aliasing={{3}: (2, {}), {4}: (3, {}), {5}: (4, {})} | custom-call | flops 5368709120 | bytes 62914560 | tf_op jit(solution)/shard_map/blend/pallas_call | solution.py:355
  12.0 0.8 copy-done
  12.8 0.8 copy-done.2
  13.6 0.4 collective-permute-start.1
  13.9 1.7 %collective-permute-start.7 = (bf16[512,512]{1,0:T(8,128)(2,1)}, bf16[512,512]{1,0:T(8,128)(2,1)S(1)}, u32[]{:S(2)}, u32[]{:S(2)}) collective-permute-start(bf16[512,512]{1,0:T(8,128)(2,1)} %get-tuple-element.82), channel_id=1, source_target_pairs={{0,16},{8,24},{16,0},{24,8},{1,17},{9,25},{17,1},{25,9},{2,18},{10... | collective-permute-start | bytes 1572872 | tf_op jit(solution)/shard_map/ppermute | solution.py:734
  15.7 0.1 add.25
  15.7 0.2 select_reduce_fusion
  15.9 3.3 %blend.3 = (f32[2,2048,512]{2,1,0:T(8,128)}, bf16[512,512]{1,0:T(8,128)(2,1)S(1)}, f32[1088,128]{1,0:T(8,128)S(1)}) custom-call(s32[10]{0:T(128)S(1)} %pad_add_fusion.1.refs_0_, f32[1088,128]{1,0:T(8,128)S(1)} %get-tuple-element.64.refs_1_.refs_5_, bf16[8,512,512]{2,1,0:T(8,128)(2,1)} %refs_2_.5, ...), custom_call_target="tpu_custom_call", output_to_operand_aliasing={{0}: (4, {})} | custom-call | flops 5368709120 | bytes 62914560 | tf_op jit(solution)/shard_map/blend/pallas_call | solution.py:355
  19.2 0.1 pad_add_fusion
  19.3 3.3 %blend_whole.4 = (f32[2,2048,512]{2,1,0:T(8,128)}, bf16[512,512]{1,0:T(8,128)(2,1)S(1)}, f32[1088,128]{1,0:T(8,128)S(1)}) custom-call(s32[16,128]{1,0:T(8,128)S(1)} %broadcast_in_dim.18.refs_0_, f32[1088,128]{1,0:T(8,128)S(1)} %get-tuple-element.66.refs_1_.refs_5_, bf16[512,512]{1,0:T(8,128)(2,1)} %collective-permute-done.refs_2_, ...), custom_call_target="tpu_custom_call", output_to_operand_aliasing={{0}: (4, {})} | custom-call | flops 5368709120 | bytes 62914560 | tf_op jit(solution)/shard_map/blend_whole/pallas_call | solution.py:355
  22.7 0.2 collective-permute-start.3
  22.9 3.3 %blend_whole.5 = (f32[2,2048,512]{2,1,0:T(8,128)}, bf16[512,512]{1,0:T(8,128)(2,1)S(1)}, f32[1088,128]{1,0:T(8,128)S(1)}) custom-call(s32[16,128]{1,0:T(8,128)S(1)} %broadcast_in_dim.18.refs_0_, f32[1088,128]{1,0:T(8,128)S(1)} %get-tuple-element.69.refs_1_.refs_5_, bf16[512,512]{1,0:T(8,128)(2,1)} %collective-permute-done.1.refs_2_, ...), custom_call_target="tpu_custom_call", output_to_operand_aliasing={{0}: (4, {})} | custom-call | flops 5368709120 | bytes 62914560 | tf_op jit(solution)/shard_map/blend_whole/pallas_call | solution.py:355
  26.2 0.4 collective-permute-start.5
  26.6 2.3 %blend_whole.6 = (f32[2,2048,512]{2,1,0:T(8,128)}, bf16[2,512,512]{2,1,0:T(8,128)(2,1)S(1)}, f32[1088,128]{1,0:T(8,128)S(1)}) custom-call(s32[16,128]{1,0:T(8,128)S(1)} %broadcast_in_dim.18.refs_0_, f32[1088,128]{1,0:T(8,128)S(1)} %get-tuple-element.72.refs_1_.refs_5_, ...), custom_call_target="tpu_custom_call", output_to_operand_aliasing={{0}: (4, {})} | custom-call | flops 5368709120 | bytes 62914560 | tf_op jit(solution)/shard_map/blend_whole/pallas_call | solution.py:355
  28.9 1.8 %fetch.2.refs_1_.refs_4_ = f32[512,512]{1,0:T(8,128)S(1)} custom-call(s32[10]{0:T(128)S(1)} %pad_add_fusion.1.refs_0_, f32[1088,128]{1,0:T(8,128)S(1)} %get-tuple-element.74.refs_1_.refs_7_, f32[2,2048,512]{2,1,0:T(8,128)} %refs_3_.9), custom_call_target="tpu_custom_call" | custom-call | bytes 41943040 | tf_op jit(solution)/shard_map/fetch/pallas_call | solution.py:355
  30.7 1.4 %blend_last.2 = (f32[2,2048,512]{2,1,0:T(8,128)}, bf16[2,512,512]{2,1,0:T(8,128)(2,1)S(1)}, f32[2,4,136,128]{3,2,1,0:T(8,128)S(1)}) custom-call(s32[16,128]{1,0:T(8,128)S(1)} %broadcast_in_dim.18.refs_0_, f32[512,512]{1,0:T(8,128)S(1)} %fetch.2.refs_1_.refs_4_, ...), custom_call_target="tpu_custom_call", output_to_operand_aliasing={{0}: (5, {}), {1}: (6, {})} | custom-call | flops 5368709120 | bytes 62914560 | tf_op jit(solution)/shard_map/blend_last/pallas_call | solution.py:355
  32.1 1.6 %collective-permute-start.6 = (f32[4,136,128]{2,1,0:T(8,128)S(1)}, f32[4,136,128]{2,1,0:T(8,128)S(1)}, u32[]{:S(2)}, u32[]{:S(2)}) collective-permute-start(f32[4,136,128]{2,1,0:T(8,128)S(1)} %slice_bitcast_fusion.1), channel_id=1, source_target_pairs={{0,1},{1,0},{2,3},{3,2},{4,5},{5,4},{6,7},{7,6},{8,9},{9,8},{10,11... | collective-permute-start | bytes 835592 | tf_op jit(solution)/shard_map/ppermute | solution.py:786
  33.8 1.8 %fetch.3.refs_0_.refs_3_ = f32[512,512]{1,0:T(8,128)S(1)} custom-call(s32[10]{0:T(128)S(1)} %pad_add_fusion.1.refs_0_, f32[2,4,136,128]{3,2,1,0:T(8,128)S(1)} %get-tuple-element.78.refs_1_.refs_3_, f32[2,2048,512]{2,1,0:T(8,128)} %refs_3_.9), custom_call_target="tpu_custom_call" | custom-call | bytes 41943040 | tf_op jit(solution)/shard_map/fetch/pallas_call | solution.py:355
  35.6 5.4 %collective-permute-done.6.refs_4_ = f32[4,136,128]{2,1,0:T(8,128)S(1)} collective-permute-done((f32[4,136,128]{2,1,0:T(8,128)S(1)}, f32[4,136,128]{2,1,0:T(8,128)S(1)}, u32[]{:S(2)}, u32[]{:S(2)}) %collective-permute-start.6) | collective-permute-done | bytes 278560 | tf_op jit(solution)/shard_map/ppermute | solution.py:786
  41.0 1.6 %collective-permute-start.9 = (f32[136,128]{1,0:T(8,128)S(1)}, f32[136,128]{1,0:T(8,128)S(1)}, u32[]{:S(2)}, u32[]{:S(2)}) collective-permute-start(f32[136,128]{1,0:T(8,128)S(1)} %get-tuple-element.89), channel_id=1, source_target_pairs={{0,2},{1,3},{2,0},{3,1},{4,6},{5,7},{6,4},{7,5},{8,10},{9,11},{10,... | collective-permute-start | bytes 208904 | tf_op jit(solution)/shard_map/ppermute | solution.py:789
  42.6 2.6 %collective-permute-start.10 = (f32[136,128]{1,0:T(8,128)S(1)}, f32[136,128]{1,0:T(8,128)S(1)}, u32[]{:S(2)}, u32[]{:S(2)}) collective-permute-start(f32[136,128]{1,0:T(8,128)S(1)} %get-tuple-element.90), channel_id=1, source_target_pairs={{0,4},{1,5},{2,6},{3,7},{4,0},{5,1},{6,2},{7,3},{8,12},{9,13},{10,... | collective-permute-start | bytes 208904 | tf_op jit(solution)/shard_map/ppermute | solution.py:789
  45.2 0.2 collective-permute-start.11
  45.4 0.5 collective-permute-start.16
  46.0 2.2 %blend_whole.7 = (f32[2,2048,512]{2,1,0:T(8,128)}, bf16[2,512,512]{2,1,0:T(8,128)(2,1)S(1)}, f32[1088,128]{1,0:T(8,128)S(1)}) custom-call(s32[16,128]{1,0:T(8,128)S(1)} %broadcast_in_dim.18.refs_0_, f32[136,128]{1,0:T(8,128)S(1)} %get-tuple-element.81.refs_1_.refs_2_, ...), custom_call_target="tpu_custom_call", output_to_operand_aliasing={{0}: (4, {})} | custom-call | flops 5368709120 | bytes 62914560 | tf_op jit(solution)/shard_map/blend_whole/pallas_call | solution.py:355
  48.2 3.4 %collective-permute-done.8.refs_2_ = bf16[512,512]{1,0:T(8,128)(2,1)S(1)} collective-permute-done((bf16[512,512]{1,0:T(8,128)(2,1)S(1)}, bf16[512,512]{1,0:T(8,128)(2,1)S(1)}, u32[]{:S(2)}, u32[]{:S(2)}) %collective-permute-start.8) | collective-permute-done | bytes 524320 | tf_op jit(solution)/shard_map/ppermute | solution.py:734
  51.6 1.4 %blend_last.3 = (f32[2,2048,512]{2,1,0:T(8,128)}, bf16[2,512,512]{2,1,0:T(8,128)(2,1)S(1)}, f32[2,4,136,128]{3,2,1,0:T(8,128)S(1)}) custom-call(s32[16,128]{1,0:T(8,128)S(1)} %broadcast_in_dim.18.refs_0_, f32[1088,128]{1,0:T(8,128)S(1)} %get-tuple-element.84.refs_1_.refs_6_, ...), custom_call_target="tpu_custom_call", output_to_operand_aliasing={{0}: (4, {}), {1}: (5, {})} | custom-call | flops 5368709120 | bytes 62914560 | tf_op jit(solution)/shard_map/blend_last/pallas_call | solution.py:355
  53.1 1.6 %collective-permute-start.12 = (f32[4,136,128]{2,1,0:T(8,128)S(1)}, f32[4,136,128]{2,1,0:T(8,128)S(1)}, u32[]{:S(2)}, u32[]{:S(2)}) collective-permute-start(f32[4,136,128]{2,1,0:T(8,128)S(1)} %slice_bitcast_fusion), channel_id=1, source_target_pairs={{0,1},{1,0},{2,3},{3,2},{4,5},{5,4},{6,7},{7,6},{8,9},{9,8},{10,11... | collective-permute-start | bytes 835592 | tf_op jit(solution)/shard_map/ppermute | solution.py:786
  54.7 3.6 %collective-permute-start.15 = (f32[136,128]{1,0:T(8,128)S(1)}, f32[136,128]{1,0:T(8,128)S(1)}, u32[]{:S(2)}, u32[]{:S(2)}) collective-permute-start(f32[136,128]{1,0:T(8,128)S(1)} %get-tuple-element.92.refs_0_.refs_2_), channel_id=1, source_target_pairs={{0,6},{1,7},{2,4},{3,5},{4,2},{5,3},{6,0},{7,1},{8,14},{9,15},{10,... | collective-permute-start | bytes 208904 | tf_op jit(solution)/shard_map/ppermute | solution.py:789
  58.3 0.8 collective-permute-start.13
  59.1 3.2 %collective-permute-done.12.refs_2_ = f32[4,136,128]{2,1,0:T(8,128)S(1)} collective-permute-done((f32[4,136,128]{2,1,0:T(8,128)S(1)}, f32[4,136,128]{2,1,0:T(8,128)S(1)}, u32[]{:S(2)}, u32[]{:S(2)}) %collective-permute-start.12) | collective-permute-done | bytes 278560 | tf_op jit(solution)/shard_map/ppermute | solution.py:786
  62.4 2.4 %collective-permute-done.14.refs_4_ = f32[136,128]{1,0:T(8,128)S(1)} collective-permute-done((f32[136,128]{1,0:T(8,128)S(1)}, f32[136,128]{1,0:T(8,128)S(1)}, u32[]{:S(2)}, u32[]{:S(2)}) %collective-permute-start.14) | collective-permute-done | bytes 69664 | tf_op jit(solution)/shard_map/ppermute | solution.py:789
  64.8 0.6 collective-permute-start.25
  65.4 1.1 %collective-permute-start.17 = (f32[136,128]{1,0:T(8,128)S(1)}, f32[136,128]{1,0:T(8,128)S(1)}, u32[]{:S(2)}, u32[]{:S(2)}) collective-permute-start(f32[136,128]{1,0:T(8,128)S(1)} %get-tuple-element.98), channel_id=1, source_target_pairs={{0,2},{1,3},{2,0},{3,1},{4,6},{5,7},{6,4},{7,5},{8,10},{9,11},{10,... | collective-permute-start | bytes 208904 | tf_op jit(solution)/shard_map/ppermute | solution.py:789
  66.6 2.0 %collective-permute-start.18 = (f32[136,128]{1,0:T(8,128)S(1)}, f32[136,128]{1,0:T(8,128)S(1)}, u32[]{:S(2)}, u32[]{:S(2)}) collective-permute-start(f32[136,128]{1,0:T(8,128)S(1)} %get-tuple-element.99), channel_id=1, source_target_pairs={{0,4},{1,5},{2,6},{3,7},{4,0},{5,1},{6,2},{7,3},{8,12},{9,13},{10,... | collective-permute-start | bytes 208904 | tf_op jit(solution)/shard_map/ppermute | solution.py:789
  68.6 1.2 %collective-permute-start.19 = (f32[136,128]{1,0:T(8,128)S(1)}, f32[136,128]{1,0:T(8,128)S(1)}, u32[]{:S(2)}, u32[]{:S(2)}) collective-permute-start(f32[136,128]{1,0:T(8,128)S(1)} %get-tuple-element.100), channel_id=1, source_target_pairs={{0,6},{1,7},{2,4},{3,5},{4,2},{5,3},{6,0},{7,1},{8,14},{9,15},{10,... | collective-permute-start | bytes 208904 | tf_op jit(solution)/shard_map/ppermute | solution.py:789
  69.8 5.2 %collective-permute-done.18.refs_5_ = f32[136,128]{1,0:T(8,128)S(1)} collective-permute-done((f32[136,128]{1,0:T(8,128)S(1)}, f32[136,128]{1,0:T(8,128)S(1)}, u32[]{:S(2)}, u32[]{:S(2)}) %collective-permute-start.18) | collective-permute-done | bytes 69664 | tf_op jit(solution)/shard_map/ppermute | solution.py:789
  75.1 1.6 %collective-permute-start.23 = (f32[4,136,128]{2,1,0:T(8,128)S(1)}, f32[4,136,128]{2,1,0:T(8,128)S(1)}, u32[]{:S(2)}, u32[]{:S(2)}) collective-permute-start(f32[4,136,128]{2,1,0:T(8,128)S(1)} %get-tuple-element.102.refs_2_), channel_id=1, source_target_pairs={{0,1},{1,0},{2,3},{3,2},{4,5},{5,4},{6,7},{7,6},{8,9},{9,8},{10,11... | collective-permute-start | bytes 835592 | tf_op jit(solution)/shard_map/ppermute | solution.py:786
  76.7 3.6 %collective-permute-start.22 = (f32[136,128]{1,0:T(8,128)S(1)}, f32[136,128]{1,0:T(8,128)S(1)}, u32[]{:S(2)}, u32[]{:S(2)}) collective-permute-start(f32[136,128]{1,0:T(8,128)S(1)} %get-tuple-element.101.refs_0_.refs_1_), channel_id=1, source_target_pairs={{0,6},{1,7},{2,4},{3,5},{4,2},{5,3},{6,0},{7,1},{8,14},{9,15},{10,... | collective-permute-start | bytes 208904 | tf_op jit(solution)/shard_map/ppermute | solution.py:789
  80.3 0.8 collective-permute-start.20
  81.1 2.3 %collective-permute-done.22.refs_4_ = f32[136,128]{1,0:T(8,128)S(1)} collective-permute-done((f32[136,128]{1,0:T(8,128)S(1)}, f32[136,128]{1,0:T(8,128)S(1)}, u32[]{:S(2)}, u32[]{:S(2)}) %collective-permute-start.22) | collective-permute-done | bytes 69664 | tf_op jit(solution)/shard_map/ppermute | solution.py:789
  83.3 2.1 %collective-permute-done.21.refs_3_ = f32[136,128]{1,0:T(8,128)S(1)} collective-permute-done((f32[136,128]{1,0:T(8,128)S(1)}, f32[136,128]{1,0:T(8,128)S(1)}, u32[]{:S(2)}, u32[]{:S(2)}) %collective-permute-start.21) | collective-permute-done | bytes 69664 | tf_op jit(solution)/shard_map/ppermute | solution.py:789
  85.5 0.6 collective-permute-start.24
  86.1 5.9 %polynomial.2.refs_1_.refs_4_ = bf16[1040,128]{1,0:T(8,128)(2,1)S(1)} custom-call(s32[16,128]{1,0:T(8,128)S(1)} %broadcast_in_dim.18.refs_0_, f32[4,136,128]{2,1,0:T(8,128)S(1)} %stack.12.refs_1_.refs_2_, f32[4,136,128]{2,1,0:T(8,128)S(1)} %get-tuple-element.102.refs_2_, f32[4,136,128]{2,1,0:T(8,128)S(1)} %collective-permute-done.23.refs_3_), custom_call_target="tpu_custom_call" | custom-call | flops 2684354560 | bytes 1310720 | tf_op jit(solution)/shard_map/polynomial/pallas_call | solution.py:355
  92.0 0.1 collective-permute-start.26
  92.1 1.6 %collective-permute-start.27 = (bf16[1040,128]{1,0:T(8,128)(2,1)S(1)}, bf16[1040,128]{1,0:T(8,128)(2,1)S(1)}, u32[]{:S(2)}, u32[]{:S(2)}) collective-permute-start(bf16[1040,128]{1,0:T(8,128)(2,1)S(1)} %polynomial.2.refs_1_.refs_4_), channel_id=1, source_target_pairs={{0,16},{8,24},{16,0},{24,8},{1,17},{9,25},{17,1},{25,9},{2,18},{10... | collective-permute-start | bytes 798728 | tf_op jit(solution)/shard_map/ppermute | solution.py:811
  93.6 6.1 %polynomial.3.refs_0_.refs_4_ = bf16[1040,128]{1,0:T(8,128)(2,1)S(1)} custom-call(s32[16,128]{1,0:T(8,128)S(1)} %broadcast_in_dim.18.refs_0_, bf16[1040,128]{1,0:T(8,128)(2,1)S(1)} %polynomial.2.refs_1_.refs_4_, f32[4,136,128]{2,1,0:T(8,128)S(1)} %stack.12.refs_1_.refs_2_, f32[4,136,128]{2,1,0:T(8,128)S(1)} %collective-permute-done.24.refs_3_), custom_call_target="tpu_custom_call" | custom-call | flops 2684354560 | bytes 1310720 | tf_op jit(solution)/shard_map/polynomial/pallas_call | solution.py:355
  99.7 0.6 collective-permute-start.31
  100.3 0.5 collective-permute-start.32
  100.9 1.6 %finish.5 = (bf16[8,512,512]{2,1,0:T(8,128)(2,1)}, f32[8,128]{1,0:T(8,128)S(1)}) custom-call(s32[16,128]{1,0:T(8,128)S(1)} %broadcast_in_dim.18.refs_0_, bf16[2,512,512]{2,1,0:T(8,128)(2,1)S(1)} %get-tuple-element.104.refs_1_.refs_2_, bf16[512,512]{1,0:T(8,128)(2,1)S(1)} %copy-done.3, bf16[512,512]{1,0:T(8,128)(2,1)S(1)} %collective-permute-done.3.refs_2_.refs_3_, ...), custom_call_target="tpu_custom_call" | custom-call | flops 10737418240 | bytes 41943040 | tf_op jit(solution)/shard_map/finish/pallas_call | solution.py:355
  102.5 0.5 collective-permute-start.30
  103.0 1.6 %finish.6 = (bf16[8,512,512]{2,1,0:T(8,128)(2,1)}, f32[8,128]{1,0:T(8,128)S(1)}) custom-call(s32[16,128]{1,0:T(8,128)S(1)} %broadcast_in_dim.18.refs_0_, bf16[1040,128]{1,0:T(8,128)(2,1)S(1)} %step.4.refs_1_.refs_4_, bf16[512,512]{1,0:T(8,128)(2,1)S(1)} %get-tuple-element.107.refs_2_, ...), custom_call_target="tpu_custom_call", output_to_operand_aliasing={{0}: (6, {})} | custom-call | flops 10737418240 | bytes 41943040 | tf_op jit(solution)/shard_map/finish/pallas_call | solution.py:355
  104.6 0.6 collective-permute-done.30.refs_5_
  105.2 1.6 %finish.7 = (bf16[8,512,512]{2,1,0:T(8,128)(2,1)}, f32[8,128]{1,0:T(8,128)S(1)}) custom-call(s32[16,128]{1,0:T(8,128)S(1)} %broadcast_in_dim.18.refs_0_, f32[8,128]{1,0:T(8,128)S(1)} %get-tuple-element.109.refs_1_, bf16[2,512,512]{2,1,0:T(8,128)(2,1)S(1)} %get-tuple-element.104.refs_1_.refs_2_, ...), custom_call_target="tpu_custom_call", output_to_operand_aliasing={{0}: (6, {})} | custom-call | flops 10737418240 | bytes 41943040 | tf_op jit(solution)/shard_map/finish/pallas_call | solution.py:355
  106.8 1.4 %collective-permute-done.31.refs_1_ = bf16[1040,128]{1,0:T(8,128)(2,1)S(1)} collective-permute-done((bf16[1040,128]{1,0:T(8,128)(2,1)S(1)}, bf16[1040,128]{1,0:T(8,128)(2,1)S(1)}, u32[]{:S(2)}, u32[]{:S(2)}) %collective-permute-start.31) | collective-permute-done | bytes 266272 | tf_op jit(solution)/shard_map/ppermute | solution.py:811
  108.2 1.2 %finish.8 = (bf16[8,512,512]{2,1,0:T(8,128)(2,1)}, f32[8,128]{1,0:T(8,128)S(1)}) custom-call(s32[16,128]{1,0:T(8,128)S(1)} %broadcast_in_dim.18.refs_0_, bf16[1040,128]{1,0:T(8,128)(2,1)S(1)} %step.5.refs_1_.refs_3_, bf16[2,512,512]{2,1,0:T(8,128)(2,1)S(1)} %get-tuple-element.112.refs_2_, ...), custom_call_target="tpu_custom_call", output_to_operand_aliasing={{0}: (4, {})} | custom-call | flops 5368709120 | bytes 20971520 | tf_op jit(solution)/shard_map/finish/pallas_call | solution.py:355
  109.5 0.3 collective-permute-done.33.refs_3_
  109.8 1.8 %finish.9 = (bf16[8,512,512]{2,1,0:T(8,128)(2,1)}, f32[8,128]{1,0:T(8,128)}) custom-call(s32[16,128]{1,0:T(8,128)S(1)} %broadcast_in_dim.18.refs_0_, f32[8,128]{1,0:T(8,128)S(1)} %get-tuple-element.114.refs_1_, bf16[2,512,512]{2,1,0:T(8,128)(2,1)S(1)} %collective-permute-done.32.refs_2_, ...), custom_call_target="tpu_custom_call", output_to_operand_aliasing={{0}: (4, {})} | custom-call | flops 5368709120 | bytes 20971520 | tf_op jit(solution)/shard_map/finish/pallas_call | solution.py:355
  (56 shorter events, 0.5 us)
Async XLA Ops:
  2.6 24.1 %collective-permute-start.2 = (bf16[512,512]{1,0:T(8,128)(2,1)S(1)}, bf16[512,512]{1,0:T(8,128)(2,1)S(1)}, u32[]{:S(2)}, u32[]{:S(2)}) collective-permute-start(bf16[512,512]{1,0:T(8,128)(2,1)S(1)} %pick.2.refs_1_), channel_id=1, source_target_pairs={{0,16},{8,24},{16,0},{24,8},{1,17},{9,25},{17,1},{25,9},{2,18},{10... | collective-permute-start | bytes 1572872 | tf_op jit(solution)/shard_map/ppermute | solution.py:734
  8.5 10.8 %collective-permute-start = (bf16[512,512]{1,0:T(8,128)(2,1)}, bf16[512,512]{1,0:T(8,128)(2,1)}, u32[]{:S(2)}, u32[]{:S(2)}) collective-permute-start(bf16[512,512]{1,0:T(8,128)(2,1)} %get-tuple-element.67), channel_id=1, source_target_pairs={{0,8},{8,0},{16,24},{24,16},{1,9},{9,1},{17,25},{25,17},{2,10},{10... | collective-permute-start | bytes 1572872 | tf_op jit(solution)/shard_map/ppermute | solution.py:734
  8.6 22.1 %collective-permute-start.4 = (bf16[512,512]{1,0:T(8,128)(2,1)S(1)}, bf16[512,512]{1,0:T(8,128)(2,1)S(1)}, u32[]{:S(2)}, u32[]{:S(2)}) collective-permute-start(bf16[512,512]{1,0:T(8,128)(2,1)S(1)} %get-tuple-element.60.refs_1_), channel_id=1, source_target_pairs={{0,24},{8,16},{16,8},{24,0},{1,25},{9,17},{17,9},{25,1},{2,26},{10... | collective-permute-start | bytes 1572872 | tf_op jit(solution)/shard_map/ppermute | solution.py:734
  8.7 7.0 %copy-start.4 = (s32[8]{0:T(128)S(1)}, s32[8]{0:T(128)}, u32[]{:S(2)}) copy-start(s32[8]{0:T(128)} %param.5) | copy-start | bytes 100
  12.0 0.8 copy-start
  12.8 0.8 copy-start.2
  13.6 9.3 %collective-permute-start.1 = (bf16[512,512]{1,0:T(8,128)(2,1)}, bf16[512,512]{1,0:T(8,128)(2,1)}, u32[]{:S(2)}, u32[]{:S(2)}) collective-permute-start(bf16[512,512]{1,0:T(8,128)(2,1)} %get-tuple-element.70), channel_id=1, source_target_pairs={{0,8},{8,0},{16,24},{24,16},{1,9},{9,1},{17,25},{25,17},{2,10},{10... | collective-permute-start | bytes 1572872 | tf_op jit(solution)/shard_map/ppermute | solution.py:734
  13.9 31.5 %collective-permute-start.7 = (bf16[512,512]{1,0:T(8,128)(2,1)}, bf16[512,512]{1,0:T(8,128)(2,1)S(1)}, u32[]{:S(2)}, u32[]{:S(2)}) collective-permute-start(bf16[512,512]{1,0:T(8,128)(2,1)} %get-tuple-element.82), channel_id=1, source_target_pairs={{0,16},{8,24},{16,0},{24,8},{1,17},{9,25},{17,1},{25,9},{2,18},{10... | collective-permute-start | bytes 1572872 | tf_op jit(solution)/shard_map/ppermute | solution.py:734
  22.7 8.0 %collective-permute-start.3 = (bf16[512,512]{1,0:T(8,128)(2,1)S(1)}, bf16[512,512]{1,0:T(8,128)(2,1)S(1)}, u32[]{:S(2)}, u32[]{:S(2)}) collective-permute-start(bf16[512,512]{1,0:T(8,128)(2,1)S(1)} %get-tuple-element.75), channel_id=1, source_target_pairs={{0,8},{8,0},{16,24},{24,16},{1,9},{9,1},{17,25},{25,17},{2,10},{10... | collective-permute-start | bytes 1572872 | tf_op jit(solution)/shard_map/ppermute | solution.py:780
  26.2 9.3 %collective-permute-start.5 = (bf16[512,512]{1,0:T(8,128)(2,1)S(1)}, bf16[512,512]{1,0:T(8,128)(2,1)S(1)}, u32[]{:S(2)}, u32[]{:S(2)}) collective-permute-start(bf16[512,512]{1,0:T(8,128)(2,1)S(1)} %get-tuple-element.79), channel_id=1, source_target_pairs={{0,8},{8,0},{16,24},{24,16},{1,9},{9,1},{17,25},{25,17},{2,10},{10... | collective-permute-start | bytes 1572872 | tf_op jit(solution)/shard_map/ppermute | solution.py:780
  30.7 3.0 %copy-start.1 = (bf16[512,512]{1,0:T(8,128)(2,1)S(1)}, bf16[512,512]{1,0:T(8,128)(2,1)}, u32[]{:S(2)}) copy-start(bf16[512,512]{1,0:T(8,128)(2,1)} %copy-done) | copy-start | bytes 1572868
  32.1 8.8 %collective-permute-start.6 = (f32[4,136,128]{2,1,0:T(8,128)S(1)}, f32[4,136,128]{2,1,0:T(8,128)S(1)}, u32[]{:S(2)}, u32[]{:S(2)}) collective-permute-start(f32[4,136,128]{2,1,0:T(8,128)S(1)} %slice_bitcast_fusion.1), channel_id=1, source_target_pairs={{0,1},{1,0},{2,3},{3,2},{4,5},{5,4},{6,7},{7,6},{8,9},{9,8},{10,11... | collective-permute-start | bytes 835592 | tf_op jit(solution)/shard_map/ppermute | solution.py:786
  33.7 17.9 %collective-permute-start.8 = (bf16[512,512]{1,0:T(8,128)(2,1)S(1)}, bf16[512,512]{1,0:T(8,128)(2,1)S(1)}, u32[]{:S(2)}, u32[]{:S(2)}) collective-permute-start(bf16[512,512]{1,0:T(8,128)(2,1)S(1)} %copy-done.1), channel_id=1, source_target_pairs={{0,24},{8,16},{16,8},{24,0},{1,25},{9,17},{17,9},{25,1},{2,26},{10... | collective-permute-start | bytes 1572872 | tf_op jit(solution)/shard_map/ppermute | solution.py:734
  41.0 12.1 %collective-permute-start.9 = (f32[136,128]{1,0:T(8,128)S(1)}, f32[136,128]{1,0:T(8,128)S(1)}, u32[]{:S(2)}, u32[]{:S(2)}) collective-permute-start(f32[136,128]{1,0:T(8,128)S(1)} %get-tuple-element.89), channel_id=1, source_target_pairs={{0,2},{1,3},{2,0},{3,1},{4,6},{5,7},{6,4},{7,5},{8,10},{9,11},{10,... | collective-permute-start | bytes 208904 | tf_op jit(solution)/shard_map/ppermute | solution.py:789
  42.6 10.4 %collective-permute-start.10 = (f32[136,128]{1,0:T(8,128)S(1)}, f32[136,128]{1,0:T(8,128)S(1)}, u32[]{:S(2)}, u32[]{:S(2)}) collective-permute-start(f32[136,128]{1,0:T(8,128)S(1)} %get-tuple-element.90), channel_id=1, source_target_pairs={{0,4},{1,5},{2,6},{3,7},{4,0},{5,1},{6,2},{7,3},{8,12},{9,13},{10,... | collective-permute-start | bytes 208904 | tf_op jit(solution)/shard_map/ppermute | solution.py:789
  45.2 7.8 %collective-permute-start.11 = (f32[136,128]{1,0:T(8,128)S(1)}, f32[136,128]{1,0:T(8,128)S(1)}, u32[]{:S(2)}, u32[]{:S(2)}) collective-permute-start(f32[136,128]{1,0:T(8,128)S(1)} %get-tuple-element.91), channel_id=1, source_target_pairs={{0,6},{1,7},{2,4},{3,5},{4,2},{5,3},{6,0},{7,1},{8,14},{9,15},{10,... | collective-permute-start | bytes 208904 | tf_op jit(solution)/shard_map/ppermute | solution.py:789
  45.4 29.6 %collective-permute-start.16 = (bf16[2,512,512]{2,1,0:T(8,128)(2,1)S(1)}, bf16[2,512,512]{2,1,0:T(8,128)(2,1)S(1)}, u32[]{:S(2)}, u32[]{:S(2)}) collective-permute-start(bf16[2,512,512]{2,1,0:T(8,128)(2,1)S(1)} %get-tuple-element.97), channel_id=1, source_target_pairs={{0,16},{8,24},{16,0},{24,8},{1,17},{9,25},{17,1},{25,9},{2,18},{10... | collective-permute-start | bytes 3145736 | tf_op jit(solution)/shard_map/ppermute | solution.py:782
  53.1 9.2 %collective-permute-start.12 = (f32[4,136,128]{2,1,0:T(8,128)S(1)}, f32[4,136,128]{2,1,0:T(8,128)S(1)}, u32[]{:S(2)}, u32[]{:S(2)}) collective-permute-start(f32[4,136,128]{2,1,0:T(8,128)S(1)} %slice_bitcast_fusion), channel_id=1, source_target_pairs={{0,1},{1,0},{2,3},{3,2},{4,5},{5,4},{6,7},{7,6},{8,9},{9,8},{10,11... | collective-permute-start | bytes 835592 | tf_op jit(solution)/shard_map/ppermute | solution.py:786
  54.7 7.7 %collective-permute-start.15 = (f32[136,128]{1,0:T(8,128)S(1)}, f32[136,128]{1,0:T(8,128)S(1)}, u32[]{:S(2)}, u32[]{:S(2)}) collective-permute-start(f32[136,128]{1,0:T(8,128)S(1)} %get-tuple-element.92.refs_0_.refs_2_), channel_id=1, source_target_pairs={{0,6},{1,7},{2,4},{3,5},{4,2},{5,3},{6,0},{7,1},{8,14},{9,15},{10,... | collective-permute-start | bytes 208904 | tf_op jit(solution)/shard_map/ppermute | solution.py:789
  58.3 6.5 %collective-permute-start.14 = (f32[136,128]{1,0:T(8,128)S(1)}, f32[136,128]{1,0:T(8,128)S(1)}, u32[]{:S(2)}, u32[]{:S(2)}) collective-permute-start(f32[136,128]{1,0:T(8,128)S(1)} %get-tuple-element.92.refs_0_.refs_2_), channel_id=1, source_target_pairs={{0,4},{1,5},{2,6},{3,7},{4,0},{5,1},{6,2},{7,3},{8,12},{9,13},{10,... | collective-permute-start | bytes 208904 | tf_op jit(solution)/shard_map/ppermute | solution.py:789
  58.3 6.5 %collective-permute-start.13 = (f32[136,128]{1,0:T(8,128)S(1)}, f32[136,128]{1,0:T(8,128)S(1)}, u32[]{:S(2)}, u32[]{:S(2)}) collective-permute-start(f32[136,128]{1,0:T(8,128)S(1)} %get-tuple-element.92.refs_0_.refs_2_), channel_id=1, source_target_pairs={{0,2},{1,3},{2,0},{3,1},{4,6},{5,7},{6,4},{7,5},{8,10},{9,11},{10,... | collective-permute-start | bytes 208904 | tf_op jit(solution)/shard_map/ppermute | solution.py:789
  64.8 35.5 %collective-permute-start.25 = (bf16[2,512,512]{2,1,0:T(8,128)(2,1)S(1)}, bf16[2,512,512]{2,1,0:T(8,128)(2,1)S(1)}, u32[]{:S(2)}, u32[]{:S(2)}) collective-permute-start(bf16[2,512,512]{2,1,0:T(8,128)(2,1)S(1)} %get-tuple-element.103), channel_id=1, source_target_pairs={{0,16},{8,24},{16,0},{24,8},{1,17},{9,25},{17,1},{25,9},{2,18},{10... | collective-permute-start | bytes 3145736 | tf_op jit(solution)/shard_map/ppermute | solution.py:782
  65.4 4.4 %collective-permute-start.17 = (f32[136,128]{1,0:T(8,128)S(1)}, f32[136,128]{1,0:T(8,128)S(1)}, u32[]{:S(2)}, u32[]{:S(2)}) collective-permute-start(f32[136,128]{1,0:T(8,128)S(1)} %get-tuple-element.98), channel_id=1, source_target_pairs={{0,2},{1,3},{2,0},{3,1},{4,6},{5,7},{6,4},{7,5},{8,10},{9,11},{10,... | collective-permute-start | bytes 208904 | tf_op jit(solution)/shard_map/ppermute | solution.py:789
  66.6 8.5 %collective-permute-start.18 = (f32[136,128]{1,0:T(8,128)S(1)}, f32[136,128]{1,0:T(8,128)S(1)}, u32[]{:S(2)}, u32[]{:S(2)}) collective-permute-start(f32[136,128]{1,0:T(8,128)S(1)} %get-tuple-element.99), channel_id=1, source_target_pairs={{0,4},{1,5},{2,6},{3,7},{4,0},{5,1},{6,2},{7,3},{8,12},{9,13},{10,... | collective-permute-start | bytes 208904 | tf_op jit(solution)/shard_map/ppermute | solution.py:789
  68.6 6.4 %collective-permute-start.19 = (f32[136,128]{1,0:T(8,128)S(1)}, f32[136,128]{1,0:T(8,128)S(1)}, u32[]{:S(2)}, u32[]{:S(2)}) collective-permute-start(f32[136,128]{1,0:T(8,128)S(1)} %get-tuple-element.100), channel_id=1, source_target_pairs={{0,6},{1,7},{2,4},{3,5},{4,2},{5,3},{6,0},{7,1},{8,14},{9,15},{10,... | collective-permute-start | bytes 208904 | tf_op jit(solution)/shard_map/ppermute | solution.py:789
  75.1 11.0 %collective-permute-start.23 = (f32[4,136,128]{2,1,0:T(8,128)S(1)}, f32[4,136,128]{2,1,0:T(8,128)S(1)}, u32[]{:S(2)}, u32[]{:S(2)}) collective-permute-start(f32[4,136,128]{2,1,0:T(8,128)S(1)} %get-tuple-element.102.refs_2_), channel_id=1, source_target_pairs={{0,1},{1,0},{2,3},{3,2},{4,5},{5,4},{6,7},{7,6},{8,9},{9,8},{10,11... | collective-permute-start | bytes 835592 | tf_op jit(solution)/shard_map/ppermute | solution.py:786
  76.7 6.7 %collective-permute-start.22 = (f32[136,128]{1,0:T(8,128)S(1)}, f32[136,128]{1,0:T(8,128)S(1)}, u32[]{:S(2)}, u32[]{:S(2)}) collective-permute-start(f32[136,128]{1,0:T(8,128)S(1)} %get-tuple-element.101.refs_0_.refs_1_), channel_id=1, source_target_pairs={{0,6},{1,7},{2,4},{3,5},{4,2},{5,3},{6,0},{7,1},{8,14},{9,15},{10,... | collective-permute-start | bytes 208904 | tf_op jit(solution)/shard_map/ppermute | solution.py:789
  80.3 5.2 %collective-permute-start.21 = (f32[136,128]{1,0:T(8,128)S(1)}, f32[136,128]{1,0:T(8,128)S(1)}, u32[]{:S(2)}, u32[]{:S(2)}) collective-permute-start(f32[136,128]{1,0:T(8,128)S(1)} %get-tuple-element.101.refs_0_.refs_1_), channel_id=1, source_target_pairs={{0,4},{1,5},{2,6},{3,7},{4,0},{5,1},{6,2},{7,3},{8,12},{9,13},{10,... | collective-permute-start | bytes 208904 | tf_op jit(solution)/shard_map/ppermute | solution.py:789
  80.3 5.2 %collective-permute-start.20 = (f32[136,128]{1,0:T(8,128)S(1)}, f32[136,128]{1,0:T(8,128)S(1)}, u32[]{:S(2)}, u32[]{:S(2)}) collective-permute-start(f32[136,128]{1,0:T(8,128)S(1)} %get-tuple-element.101.refs_0_.refs_1_), channel_id=1, source_target_pairs={{0,2},{1,3},{2,0},{3,1},{4,6},{5,7},{6,4},{7,5},{8,10},{9,11},{10,... | collective-permute-start | bytes 208904 | tf_op jit(solution)/shard_map/ppermute | solution.py:789
  85.5 8.1 %collective-permute-start.24 = (f32[4,136,128]{2,1,0:T(8,128)S(1)}, f32[4,136,128]{2,1,0:T(8,128)S(1)}, u32[]{:S(2)}, u32[]{:S(2)}) collective-permute-start(f32[4,136,128]{2,1,0:T(8,128)S(1)} %stack.12.refs_1_.refs_2_), channel_id=1, source_target_pairs={{0,1},{1,0},{2,3},{3,2},{4,5},{5,4},{6,7},{7,6},{8,9},{9,8},{10,11... | collective-permute-start | bytes 835592 | tf_op jit(solution)/shard_map/ppermute | solution.py:786
  92.0 8.9 %copy-start.3 = (bf16[512,512]{1,0:T(8,128)(2,1)S(1)}, bf16[512,512]{1,0:T(8,128)(2,1)}, u32[]{:S(2)}) copy-start(bf16[512,512]{1,0:T(8,128)(2,1)} %copy-done.2) | copy-start | bytes 1572868
  92.0 8.8 %collective-permute-start.26 = (bf16[1040,128]{1,0:T(8,128)(2,1)S(1)}, bf16[1040,128]{1,0:T(8,128)(2,1)S(1)}, u32[]{:S(2)}, u32[]{:S(2)}) collective-permute-start(bf16[1040,128]{1,0:T(8,128)(2,1)S(1)} %polynomial.2.refs_1_.refs_4_), channel_id=1, source_target_pairs={{0,8},{8,0},{16,24},{24,16},{1,9},{9,1},{17,25},{25,17},{2,10},{10... | collective-permute-start | bytes 798728 | tf_op jit(solution)/shard_map/ppermute | solution.py:813
  92.1 10.4 %collective-permute-start.27 = (bf16[1040,128]{1,0:T(8,128)(2,1)S(1)}, bf16[1040,128]{1,0:T(8,128)(2,1)S(1)}, u32[]{:S(2)}, u32[]{:S(2)}) collective-permute-start(bf16[1040,128]{1,0:T(8,128)(2,1)S(1)} %polynomial.2.refs_1_.refs_4_), channel_id=1, source_target_pairs={{0,16},{8,24},{16,0},{24,8},{1,17},{9,25},{17,1},{25,9},{2,18},{10... | collective-permute-start | bytes 798728 | tf_op jit(solution)/shard_map/ppermute | solution.py:811
  99.7 8.5 %collective-permute-start.31 = (bf16[1040,128]{1,0:T(8,128)(2,1)S(1)}, bf16[1040,128]{1,0:T(8,128)(2,1)S(1)}, u32[]{:S(2)}, u32[]{:S(2)}) collective-permute-start(bf16[1040,128]{1,0:T(8,128)(2,1)S(1)} %polynomial.3.refs_0_.refs_4_), channel_id=1, source_target_pairs={{0,16},{8,24},{16,0},{24,8},{1,17},{9,25},{17,1},{25,9},{2,18},{10... | collective-permute-start | bytes 798728 | tf_op jit(solution)/shard_map/ppermute | solution.py:811
  100.3 2.7 %collective-permute-start.28 = (bf16[1040,128]{1,0:T(8,128)(2,1)S(1)}, bf16[1040,128]{1,0:T(8,128)(2,1)S(1)}, u32[]{:S(2)}, u32[]{:S(2)}) collective-permute-start(bf16[1040,128]{1,0:T(8,128)(2,1)S(1)} %polynomial.3.refs_0_.refs_4_), channel_id=1, source_target_pairs={{0,8},{8,0},{16,24},{24,16},{1,9},{9,1},{17,25},{25,17},{2,10},{10... | collective-permute-start | bytes 798728 | tf_op jit(solution)/shard_map/ppermute | solution.py:813
  100.3 9.2 %collective-permute-start.32 = (bf16[2,512,512]{2,1,0:T(8,128)(2,1)S(1)}, bf16[2,512,512]{2,1,0:T(8,128)(2,1)S(1)}, u32[]{:S(2)}, u32[]{:S(2)}) collective-permute-start(bf16[2,512,512]{2,1,0:T(8,128)(2,1)S(1)} %get-tuple-element.112.refs_2_), channel_id=1, source_target_pairs={{0,8},{8,0},{16,24},{24,16},{1,9},{9,1},{17,25},{25,17},{2,10},{10... | collective-permute-start | bytes 3145736 | tf_op jit(solution)/shard_map/ppermute | solution.py:892
  100.8 4.4 %collective-permute-start.29 = (bf16[2,512,512]{2,1,0:T(8,128)(2,1)S(1)}, bf16[2,512,512]{2,1,0:T(8,128)(2,1)S(1)}, u32[]{:S(2)}, u32[]{:S(2)}) collective-permute-start(bf16[2,512,512]{2,1,0:T(8,128)(2,1)S(1)} %get-tuple-element.104.refs_1_.refs_2_), channel_id=1, source_target_pairs={{0,8},{8,0},{16,24},{24,16},{1,9},{9,1},{17,25},{25,17},{2,10},{10... | collective-permute-start | bytes 3145736 | tf_op jit(solution)/shard_map/ppermute | solution.py:892
  102.5 2.7 %collective-permute-start.30 = (bf16[1040,128]{1,0:T(8,128)(2,1)S(1)}, bf16[1040,128]{1,0:T(8,128)(2,1)S(1)}, u32[]{:S(2)}, u32[]{:S(2)}) collective-permute-start(bf16[1040,128]{1,0:T(8,128)(2,1)S(1)} %step.4.refs_1_.refs_4_), channel_id=1, source_target_pairs={{0,8},{8,0},{16,24},{24,16},{1,9},{9,1},{17,25},{25,17},{2,10},{10... | collective-permute-start | bytes 798728 | tf_op jit(solution)/shard_map/ppermute | solution.py:818
  108.2 1.5 %collective-permute-start.33 = (bf16[1040,128]{1,0:T(8,128)(2,1)S(1)}, bf16[1040,128]{1,0:T(8,128)(2,1)S(1)}, u32[]{:S(2)}, u32[]{:S(2)}) collective-permute-start(bf16[1040,128]{1,0:T(8,128)(2,1)S(1)} %step.5.refs_1_.refs_3_), channel_id=1, source_target_pairs={{0,8},{8,0},{16,24},{24,16},{1,9},{9,1},{17,25},{25,17},{2,10},{10... | collective-permute-start | bytes 798728 | tf_op jit(solution)/shard_map/ppermute | solution.py:818

commit v9 on v8

--- a/solution.py
+++ b/solution.py
@@ -646,11 +646,11 @@
     )[0]
 
 
-def finish_kernel(slots, slot, steps, matrices, picks, place, *refs):
+def finish_kernel(slots, slot, steps, matrices, picks, last, place, *refs):
     refs = list(refs)
     count = len(steps)
     pieces, polys = refs[:count], refs[count : 2 * count]
-    updates, _, held, sems = refs[-4:]
+    updates, held, sems = refs[len(refs) - (3 if last else 4)], *refs[-2:]
     copies = []
     for n, d in enumerate(steps):
         tail = polys[n][DIAGONALS:, :].astype(f32)
@@ -680,7 +680,7 @@
         copy.wait()
 
 
-def finish(line, slots, slot, steps, pieces, polys, shape, buffer):
+def finish(line, slots, slot, steps, pieces, polys, shape, buffer, last):
     operands = [piece for piece, _ in pieces] + list(polys)
     specs = [IN_VMEM] * len(operands)
     aliases = {}
@@ -689,14 +689,14 @@
         operands.append(in_hbm(buffer))
         specs.append(IN_HBM)
     return line.run(
-        functools.partial(finish_kernel, slots, slot, steps, shape[0], [index for _, index in pieces]),
+        functools.partial(finish_kernel, slots, slot, steps, shape[0], [index for _, index in pieces], last),
         operands,
         specs,
-        [pltpu.HBM(shape, bf16), jax.ShapeDtypeStruct((8, TILE), f32)],
-        [IN_HBM, IN_VMEM],
+        [pltpu.HBM(shape, bf16)] + [jax.ShapeDtypeStruct((8, TILE), f32)] * (not last),
+        [IN_HBM] + [IN_VMEM] * (not last),
         name="finish",
         scalars=SPOTS,
-        token=1,
+        token=0 if last else 1,
         scratch=[pltpu.VMEM((len(steps), shape[1], RANK), bf16), pltpu.SemaphoreType.DMA((len(steps) * max(1, shape[1] // 256),))],
         aliases=aliases,
         vmem=8,
@@ -830,6 +830,7 @@
             [polys[slot, d] for d in steps],
             gradients.shape,
             updates,
+            slot == held_slots - 1 and steps[-1] == owners - 1,
         )
 
     def expect(*wanted):

time: 112 us -> 112 us (level)
  no operation moved by 1% of the time
where the time goes in v9:
time: 112 us; the launch traced here: 111 us
  Pallas kernels  47.3 us (42%)
  starting transfers between devices  33.4 us (30%)
  waiting for transfers between devices  26.4 us (24%)
  local copies, waits for them, and re-layouts  1.95 us (2%)
  between operations  1.12 us (1%)
    pallas_call x28, Pallas kernels, run(): pl.pallas_call(body, **layout, out_shape=out_shape + [jax.ShapeDtypeStruc...  47.3 us
    ppermute x12, starting transfers between devices, across_far(): return lax.ppermute(x, 'fsdp', partners(group, e2 * near))  17.6 us
    ppermute x12, waiting for transfers between devices, across_far(): return lax.ppermute(x, 'fsdp', partners(group, e2 * near))  12 us
    ppermute x4, waiting for transfers between devices, across_near(): return lax.ppermute(x, 'fsdp', partners(group, e1))  8.63 us
    ppermute x4, starting transfers between devices, across_near(): return lax.ppermute(x, 'fsdp', partners(group, e1))  5.35 us
    ppermute x6, starting transfers between devices, send(): lax.ppermute(picked[slot, d], 'owner', partners(owners, d))  5.31 us
    ppermute x6, waiting for transfers between devices, send(): lax.ppermute(picked[slot, d], 'owner', partners(owners, d))  3.38 us
  transfers between devices with their start and end apart: 34, of which 10 were waited for; matrix products, arithmetic and copies ran while one was open for 0% of the time, Pallas kernels for 40%

profile of v9, /device:TPU:0, one launch (start us, length us, event | category | flops | bytes accessed | tf_op | source)
XLA Modules:
  0.0 111.2 jit_solution(13061714551148233048)
XLA Ops:
  0.6 0.7 pad_add_fusion.1.refs_0_
  1.4 0.1 broadcast_in_dim.19.refs_0_
  1.4 1.1 pick.2.refs_1_
  2.6 3.0 %collective-permute-start.2 = (bf16[512,512]{1,0:T(8,128)(2,1)S(1)}, bf16[512,512]{1,0:T(8,128)(2,1)S(1)}, u32[]{:S(2)}, u32[]{:S(2)}) collective-permute-start(bf16[512,512]{1,0:T(8,128)(2,1)S(1)} %pick.2.refs_1_), channel_id=1, source_target_pairs={{0,16},{8,24},{16,0},{24,8},{1,17},{9,25},{17,1},{25,9},{2,18},{10... | collective-permute-start | bytes 1572872 | tf_op jit(solution)/shard_map/ppermute | solution.py:734
  5.6 2.9 %pick.3 = (bf16[512,512]{1,0:T(8,128)(2,1)S(1)}, bf16[512,512]{1,0:T(8,128)(2,1)}, bf16[512,512]{1,0:T(8,128)(2,1)}, bf16[512,512]{1,0:T(8,128)(2,1)}, bf16[512,512]{1,0:T(8,128)(2,1)S(1)}) custom-call(s32[16,128]{1,0:T(8,128)S(1)} %broadcast_in_dim.19.refs_0_, bf16[512,512]{1,0:T(8,128)(2,1)S(1)} %pick.2.refs_1_, bf16[8,512,512]{2,1,0:T(8,128)(2,1)} %refs_2_.5), custom_call_target="tpu_custom_call" | custom-call | bytes 104857600 | tf_op jit(solution)/shard_map/pick/pallas_call | solution.py:355
  8.5 0.1 collective-permute-start
  8.6 0.1 collective-permute-start.4
  8.7 3.3 %blend.2 = (f32[2,2048,512]{2,1,0:T(8,128)}, bf16[512,512]{1,0:T(8,128)(2,1)S(1)}, f32[1088,128]{1,0:T(8,128)S(1)}, bf16[512,512]{1,0:T(8,128)(2,1)}, bf16[512,5...) custom-call(s32[10]{0:T(128)S(1)} %pad_add_fusion.1.refs_0_, ...), custom_call_target="tpu_custom_call", output_to_operand_aliasing={{3}: (2, {}), {4}: (3, {}), {5}: (4, {})} | custom-call | flops 5368709120 | bytes 62914560 | tf_op jit(solution)/shard_map/blend/pallas_call | solution.py:355
  12.0 0.8 copy-done
  12.8 0.8 copy-done.2
  13.6 0.4 collective-permute-start.1
  13.9 1.7 %collective-permute-start.7 = (bf16[512,512]{1,0:T(8,128)(2,1)}, bf16[512,512]{1,0:T(8,128)(2,1)S(1)}, u32[]{:S(2)}, u32[]{:S(2)}) collective-permute-start(bf16[512,512]{1,0:T(8,128)(2,1)} %get-tuple-element.81), channel_id=1, source_target_pairs={{0,16},{8,24},{16,0},{24,8},{1,17},{9,25},{17,1},{25,9},{2,18},{10... | collective-permute-start | bytes 1572872 | tf_op jit(solution)/shard_map/ppermute | solution.py:734
  15.7 0.1 add.25
  15.8 0.2 select_reduce_fusion
  15.9 3.3 %blend.3 = (f32[2,2048,512]{2,1,0:T(8,128)}, bf16[512,512]{1,0:T(8,128)(2,1)S(1)}, f32[1088,128]{1,0:T(8,128)S(1)}) custom-call(s32[10]{0:T(128)S(1)} %pad_add_fusion.1.refs_0_, f32[1088,128]{1,0:T(8,128)S(1)} %get-tuple-element.63.refs_1_.refs_5_, bf16[8,512,512]{2,1,0:T(8,128)(2,1)} %refs_2_.5, ...), custom_call_target="tpu_custom_call", output_to_operand_aliasing={{0}: (4, {})} | custom-call | flops 5368709120 | bytes 62914560 | tf_op jit(solution)/shard_map/blend/pallas_call | solution.py:355
  19.2 0.1 pad_add_fusion
  19.4 3.3 %blend_whole.4 = (f32[2,2048,512]{2,1,0:T(8,128)}, bf16[512,512]{1,0:T(8,128)(2,1)S(1)}, f32[1088,128]{1,0:T(8,128)S(1)}) custom-call(s32[16,128]{1,0:T(8,128)S(1)} %broadcast_in_dim.18.refs_0_, f32[1088,128]{1,0:T(8,128)S(1)} %get-tuple-element.65.refs_1_.refs_5_, bf16[512,512]{1,0:T(8,128)(2,1)} %collective-permute-done.refs_2_, ...), custom_call_target="tpu_custom_call", output_to_operand_aliasing={{0}: (4, {})} | custom-call | flops 5368709120 | bytes 62914560 | tf_op jit(solution)/shard_map/blend_whole/pallas_call | solution.py:355
  22.7 0.2 collective-permute-start.3
  22.9 3.3 %blend_whole.5 = (f32[2,2048,512]{2,1,0:T(8,128)}, bf16[512,512]{1,0:T(8,128)(2,1)S(1)}, f32[1088,128]{1,0:T(8,128)S(1)}) custom-call(s32[16,128]{1,0:T(8,128)S(1)} %broadcast_in_dim.18.refs_0_, f32[1088,128]{1,0:T(8,128)S(1)} %get-tuple-element.68.refs_1_.refs_5_, bf16[512,512]{1,0:T(8,128)(2,1)} %collective-permute-done.1.refs_2_, ...), custom_call_target="tpu_custom_call", output_to_operand_aliasing={{0}: (4, {})} | custom-call | flops 5368709120 | bytes 62914560 | tf_op jit(solution)/shard_map/blend_whole/pallas_call | solution.py:355
  26.2 0.4 collective-permute-start.5
  26.6 2.3 %blend_whole.6 = (f32[2,2048,512]{2,1,0:T(8,128)}, bf16[2,512,512]{2,1,0:T(8,128)(2,1)S(1)}, f32[1088,128]{1,0:T(8,128)S(1)}) custom-call(s32[16,128]{1,0:T(8,128)S(1)} %broadcast_in_dim.18.refs_0_, f32[1088,128]{1,0:T(8,128)S(1)} %get-tuple-element.71.refs_1_.refs_5_, ...), custom_call_target="tpu_custom_call", output_to_operand_aliasing={{0}: (4, {})} | custom-call | flops 5368709120 | bytes 62914560 | tf_op jit(solution)/shard_map/blend_whole/pallas_call | solution.py:355
  28.9 1.8 %fetch.2.refs_1_.refs_4_ = f32[512,512]{1,0:T(8,128)S(1)} custom-call(s32[10]{0:T(128)S(1)} %pad_add_fusion.1.refs_0_, f32[1088,128]{1,0:T(8,128)S(1)} %get-tuple-element.73.refs_1_.refs_7_, f32[2,2048,512]{2,1,0:T(8,128)} %refs_3_.9), custom_call_target="tpu_custom_call" | custom-call | bytes 41943040 | tf_op jit(solution)/shard_map/fetch/pallas_call | solution.py:355
  30.7 1.4 %blend_last.2 = (f32[2,2048,512]{2,1,0:T(8,128)}, bf16[2,512,512]{2,1,0:T(8,128)(2,1)S(1)}, f32[2,4,136,128]{3,2,1,0:T(8,128)S(1)}) custom-call(s32[16,128]{1,0:T(8,128)S(1)} %broadcast_in_dim.18.refs_0_, f32[512,512]{1,0:T(8,128)S(1)} %fetch.2.refs_1_.refs_4_, ...), custom_call_target="tpu_custom_call", output_to_operand_aliasing={{0}: (5, {}), {1}: (6, {})} | custom-call | flops 5368709120 | bytes 62914560 | tf_op jit(solution)/shard_map/blend_last/pallas_call | solution.py:355
  32.1 1.6 %collective-permute-start.6 = (f32[4,136,128]{2,1,0:T(8,128)S(1)}, f32[4,136,128]{2,1,0:T(8,128)S(1)}, u32[]{:S(2)}, u32[]{:S(2)}) collective-permute-start(f32[4,136,128]{2,1,0:T(8,128)S(1)} %slice_bitcast_fusion.1), channel_id=1, source_target_pairs={{0,1},{1,0},{2,3},{3,2},{4,5},{5,4},{6,7},{7,6},{8,9},{9,8},{10,11... | collective-permute-start | bytes 835592 | tf_op jit(solution)/shard_map/ppermute | solution.py:786
  33.8 1.8 %fetch.3.refs_0_.refs_3_ = f32[512,512]{1,0:T(8,128)S(1)} custom-call(s32[10]{0:T(128)S(1)} %pad_add_fusion.1.refs_0_, f32[2,4,136,128]{3,2,1,0:T(8,128)S(1)} %get-tuple-element.77.refs_1_.refs_3_, f32[2,2048,512]{2,1,0:T(8,128)} %refs_3_.9), custom_call_target="tpu_custom_call" | custom-call | bytes 41943040 | tf_op jit(solution)/shard_map/fetch/pallas_call | solution.py:355
  35.6 5.4 %collective-permute-done.6.refs_4_ = f32[4,136,128]{2,1,0:T(8,128)S(1)} collective-permute-done((f32[4,136,128]{2,1,0:T(8,128)S(1)}, f32[4,136,128]{2,1,0:T(8,128)S(1)}, u32[]{:S(2)}, u32[]{:S(2)}) %collective-permute-start.6) | collective-permute-done | bytes 278560 | tf_op jit(solution)/shard_map/ppermute | solution.py:786
  41.0 1.6 %collective-permute-start.9 = (f32[136,128]{1,0:T(8,128)S(1)}, f32[136,128]{1,0:T(8,128)S(1)}, u32[]{:S(2)}, u32[]{:S(2)}) collective-permute-start(f32[136,128]{1,0:T(8,128)S(1)} %get-tuple-element.88), channel_id=1, source_target_pairs={{0,2},{1,3},{2,0},{3,1},{4,6},{5,7},{6,4},{7,5},{8,10},{9,11},{10,... | collective-permute-start | bytes 208904 | tf_op jit(solution)/shard_map/ppermute | solution.py:789
  42.6 2.6 %collective-permute-start.10 = (f32[136,128]{1,0:T(8,128)S(1)}, f32[136,128]{1,0:T(8,128)S(1)}, u32[]{:S(2)}, u32[]{:S(2)}) collective-permute-start(f32[136,128]{1,0:T(8,128)S(1)} %get-tuple-element.89), channel_id=1, source_target_pairs={{0,4},{1,5},{2,6},{3,7},{4,0},{5,1},{6,2},{7,3},{8,12},{9,13},{10,... | collective-permute-start | bytes 208904 | tf_op jit(solution)/shard_map/ppermute | solution.py:789
  45.2 0.2 collective-permute-start.11
  45.4 0.5 collective-permute-start.16
  46.0 2.2 %blend_whole.7 = (f32[2,2048,512]{2,1,0:T(8,128)}, bf16[2,512,512]{2,1,0:T(8,128)(2,1)S(1)}, f32[1088,128]{1,0:T(8,128)S(1)}) custom-call(s32[16,128]{1,0:T(8,128)S(1)} %broadcast_in_dim.18.refs_0_, f32[136,128]{1,0:T(8,128)S(1)} %get-tuple-element.80.refs_1_.refs_2_, ...), custom_call_target="tpu_custom_call", output_to_operand_aliasing={{0}: (4, {})} | custom-call | flops 5368709120 | bytes 62914560 | tf_op jit(solution)/shard_map/blend_whole/pallas_call | solution.py:355
  48.2 3.4 %collective-permute-done.8.refs_2_ = bf16[512,512]{1,0:T(8,128)(2,1)S(1)} collective-permute-done((bf16[512,512]{1,0:T(8,128)(2,1)S(1)}, bf16[512,512]{1,0:T(8,128)(2,1)S(1)}, u32[]{:S(2)}, u32[]{:S(2)}) %collective-permute-start.8) | collective-permute-done | bytes 524320 | tf_op jit(solution)/shard_map/ppermute | solution.py:734
  51.6 1.4 %blend_last.3 = (f32[2,2048,512]{2,1,0:T(8,128)}, bf16[2,512,512]{2,1,0:T(8,128)(2,1)S(1)}, f32[2,4,136,128]{3,2,1,0:T(8,128)S(1)}) custom-call(s32[16,128]{1,0:T(8,128)S(1)} %broadcast_in_dim.18.refs_0_, f32[1088,128]{1,0:T(8,128)S(1)} %get-tuple-element.83.refs_1_.refs_6_, ...), custom_call_target="tpu_custom_call", output_to_operand_aliasing={{0}: (4, {}), {1}: (5, {})} | custom-call | flops 5368709120 | bytes 62914560 | tf_op jit(solution)/shard_map/blend_last/pallas_call | solution.py:355
  53.1 1.6 %collective-permute-start.12 = (f32[4,136,128]{2,1,0:T(8,128)S(1)}, f32[4,136,128]{2,1,0:T(8,128)S(1)}, u32[]{:S(2)}, u32[]{:S(2)}) collective-permute-start(f32[4,136,128]{2,1,0:T(8,128)S(1)} %slice_bitcast_fusion), channel_id=1, source_target_pairs={{0,1},{1,0},{2,3},{3,2},{4,5},{5,4},{6,7},{7,6},{8,9},{9,8},{10,11... | collective-permute-start | bytes 835592 | tf_op jit(solution)/shard_map/ppermute | solution.py:786
  54.7 3.6 %collective-permute-start.15 = (f32[136,128]{1,0:T(8,128)S(1)}, f32[136,128]{1,0:T(8,128)S(1)}, u32[]{:S(2)}, u32[]{:S(2)}) collective-permute-start(f32[136,128]{1,0:T(8,128)S(1)} %get-tuple-element.91.refs_0_.refs_2_), channel_id=1, source_target_pairs={{0,6},{1,7},{2,4},{3,5},{4,2},{5,3},{6,0},{7,1},{8,14},{9,15},{10,... | collective-permute-start | bytes 208904 | tf_op jit(solution)/shard_map/ppermute | solution.py:789
  58.3 0.8 collective-permute-start.13
  59.1 3.2 %collective-permute-done.12.refs_2_ = f32[4,136,128]{2,1,0:T(8,128)S(1)} collective-permute-done((f32[4,136,128]{2,1,0:T(8,128)S(1)}, f32[4,136,128]{2,1,0:T(8,128)S(1)}, u32[]{:S(2)}, u32[]{:S(2)}) %collective-permute-start.12) | collective-permute-done | bytes 278560 | tf_op jit(solution)/shard_map/ppermute | solution.py:786
  62.4 2.4 %collective-permute-done.14.refs_4_ = f32[136,128]{1,0:T(8,128)S(1)} collective-permute-done((f32[136,128]{1,0:T(8,128)S(1)}, f32[136,128]{1,0:T(8,128)S(1)}, u32[]{:S(2)}, u32[]{:S(2)}) %collective-permute-start.14) | collective-permute-done | bytes 69664 | tf_op jit(solution)/shard_map/ppermute | solution.py:789
  64.8 0.6 collective-permute-start.25
  65.4 1.1 %collective-permute-start.17 = (f32[136,128]{1,0:T(8,128)S(1)}, f32[136,128]{1,0:T(8,128)S(1)}, u32[]{:S(2)}, u32[]{:S(2)}) collective-permute-start(f32[136,128]{1,0:T(8,128)S(1)} %get-tuple-element.97), channel_id=1, source_target_pairs={{0,2},{1,3},{2,0},{3,1},{4,6},{5,7},{6,4},{7,5},{8,10},{9,11},{10,... | collective-permute-start | bytes 208904 | tf_op jit(solution)/shard_map/ppermute | solution.py:789
  66.6 2.0 %collective-permute-start.18 = (f32[136,128]{1,0:T(8,128)S(1)}, f32[136,128]{1,0:T(8,128)S(1)}, u32[]{:S(2)}, u32[]{:S(2)}) collective-permute-start(f32[136,128]{1,0:T(8,128)S(1)} %get-tuple-element.98), channel_id=1, source_target_pairs={{0,4},{1,5},{2,6},{3,7},{4,0},{5,1},{6,2},{7,3},{8,12},{9,13},{10,... | collective-permute-start | bytes 208904 | tf_op jit(solution)/shard_map/ppermute | solution.py:789
  68.6 1.2 %collective-permute-start.19 = (f32[136,128]{1,0:T(8,128)S(1)}, f32[136,128]{1,0:T(8,128)S(1)}, u32[]{:S(2)}, u32[]{:S(2)}) collective-permute-start(f32[136,128]{1,0:T(8,128)S(1)} %get-tuple-element.99), channel_id=1, source_target_pairs={{0,6},{1,7},{2,4},{3,5},{4,2},{5,3},{6,0},{7,1},{8,14},{9,15},{10,... | collective-permute-start | bytes 208904 | tf_op jit(solution)/shard_map/ppermute | solution.py:789
  69.8 5.2 %collective-permute-done.18.refs_5_ = f32[136,128]{1,0:T(8,128)S(1)} collective-permute-done((f32[136,128]{1,0:T(8,128)S(1)}, f32[136,128]{1,0:T(8,128)S(1)}, u32[]{:S(2)}, u32[]{:S(2)}) %collective-permute-start.18) | collective-permute-done | bytes 69664 | tf_op jit(solution)/shard_map/ppermute | solution.py:789
  75.1 1.6 %collective-permute-start.23 = (f32[4,136,128]{2,1,0:T(8,128)S(1)}, f32[4,136,128]{2,1,0:T(8,128)S(1)}, u32[]{:S(2)}, u32[]{:S(2)}) collective-permute-start(f32[4,136,128]{2,1,0:T(8,128)S(1)} %get-tuple-element.101.refs_2_), channel_id=1, source_target_pairs={{0,1},{1,0},{2,3},{3,2},{4,5},{5,4},{6,7},{7,6},{8,9},{9,8},{10,11... | collective-permute-start | bytes 835592 | tf_op jit(solution)/shard_map/ppermute | solution.py:786
  76.7 3.6 %collective-permute-start.22 = (f32[136,128]{1,0:T(8,128)S(1)}, f32[136,128]{1,0:T(8,128)S(1)}, u32[]{:S(2)}, u32[]{:S(2)}) collective-permute-start(f32[136,128]{1,0:T(8,128)S(1)} %get-tuple-element.100.refs_0_.refs_1_), channel_id=1, source_target_pairs={{0,6},{1,7},{2,4},{3,5},{4,2},{5,3},{6,0},{7,1},{8,14},{9,15},{10,... | collective-permute-start | bytes 208904 | tf_op jit(solution)/shard_map/ppermute | solution.py:789
  80.3 0.8 collective-permute-start.20
  81.1 2.3 %collective-permute-done.22.refs_4_ = f32[136,128]{1,0:T(8,128)S(1)} collective-permute-done((f32[136,128]{1,0:T(8,128)S(1)}, f32[136,128]{1,0:T(8,128)S(1)}, u32[]{:S(2)}, u32[]{:S(2)}) %collective-permute-start.22) | collective-permute-done | bytes 69664 | tf_op jit(solution)/shard_map/ppermute | solution.py:789
  83.3 2.1 %collective-permute-done.21.refs_3_ = f32[136,128]{1,0:T(8,128)S(1)} collective-permute-done((f32[136,128]{1,0:T(8,128)S(1)}, f32[136,128]{1,0:T(8,128)S(1)}, u32[]{:S(2)}, u32[]{:S(2)}) %collective-permute-start.21) | collective-permute-done | bytes 69664 | tf_op jit(solution)/shard_map/ppermute | solution.py:789
  85.5 0.6 collective-permute-start.24
  86.1 5.9 %polynomial.2.refs_1_.refs_4_ = bf16[1040,128]{1,0:T(8,128)(2,1)S(1)} custom-call(s32[16,128]{1,0:T(8,128)S(1)} %broadcast_in_dim.18.refs_0_, f32[4,136,128]{2,1,0:T(8,128)S(1)} %stack.12.refs_1_.refs_2_, f32[4,136,128]{2,1,0:T(8,128)S(1)} %get-tuple-element.101.refs_2_, f32[4,136,128]{2,1,0:T(8,128)S(1)} %collective-permute-done.23.refs_3_), custom_call_target="tpu_custom_call" | custom-call | flops 2684354560 | bytes 1310720 | tf_op jit(solution)/shard_map/polynomial/pallas_call | solution.py:355
  92.0 0.1 collective-permute-start.26
  92.1 1.6 %collective-permute-start.27 = (bf16[1040,128]{1,0:T(8,128)(2,1)S(1)}, bf16[1040,128]{1,0:T(8,128)(2,1)S(1)}, u32[]{:S(2)}, u32[]{:S(2)}) collective-permute-start(bf16[1040,128]{1,0:T(8,128)(2,1)S(1)} %polynomial.2.refs_1_.refs_4_), channel_id=1, source_target_pairs={{0,16},{8,24},{16,0},{24,8},{1,17},{9,25},{17,1},{25,9},{2,18},{10... | collective-permute-start | bytes 798728 | tf_op jit(solution)/shard_map/ppermute | solution.py:811
  93.6 6.1 %polynomial.3.refs_0_.refs_4_ = bf16[1040,128]{1,0:T(8,128)(2,1)S(1)} custom-call(s32[16,128]{1,0:T(8,128)S(1)} %broadcast_in_dim.18.refs_0_, bf16[1040,128]{1,0:T(8,128)(2,1)S(1)} %polynomial.2.refs_1_.refs_4_, f32[4,136,128]{2,1,0:T(8,128)S(1)} %stack.12.refs_1_.refs_2_, f32[4,136,128]{2,1,0:T(8,128)S(1)} %collective-permute-done.24.refs_3_), custom_call_target="tpu_custom_call" | custom-call | flops 2684354560 | bytes 1310720 | tf_op jit(solution)/shard_map/polynomial/pallas_call | solution.py:355
  99.7 0.6 collective-permute-start.31
  100.3 0.5 collective-permute-start.32
  100.9 1.6 %finish.5 = (bf16[8,512,512]{2,1,0:T(8,128)(2,1)}, f32[8,128]{1,0:T(8,128)S(1)}) custom-call(s32[16,128]{1,0:T(8,128)S(1)} %broadcast_in_dim.18.refs_0_, bf16[2,512,512]{2,1,0:T(8,128)(2,1)S(1)} %get-tuple-element.103.refs_1_.refs_2_, bf16[512,512]{1,0:T(8,128)(2,1)S(1)} %copy-done.3, bf16[512,512]{1,0:T(8,128)(2,1)S(1)} %collective-permute-done.3.refs_2_.refs_3_, ...), custom_call_target="tpu_custom_call" | custom-call | flops 10737418240 | bytes 41943040 | tf_op jit(solution)/shard_map/finish/pallas_call | solution.py:355
  102.5 0.5 collective-permute-start.30
  103.0 1.6 %finish.6 = (bf16[8,512,512]{2,1,0:T(8,128)(2,1)}, f32[8,128]{1,0:T(8,128)S(1)}) custom-call(s32[16,128]{1,0:T(8,128)S(1)} %broadcast_in_dim.18.refs_0_, bf16[1040,128]{1,0:T(8,128)(2,1)S(1)} %step.4.refs_1_.refs_4_, bf16[512,512]{1,0:T(8,128)(2,1)S(1)} %get-tuple-element.106.refs_2_, ...), custom_call_target="tpu_custom_call", output_to_operand_aliasing={{0}: (6, {})} | custom-call | flops 10737418240 | bytes 41943040 | tf_op jit(solution)/shard_map/finish/pallas_call | solution.py:355
  104.6 0.6 collective-permute-done.30.refs_5_
  105.2 1.6 %finish.7 = (bf16[8,512,512]{2,1,0:T(8,128)(2,1)}, f32[8,128]{1,0:T(8,128)S(1)}) custom-call(s32[16,128]{1,0:T(8,128)S(1)} %broadcast_in_dim.18.refs_0_, f32[8,128]{1,0:T(8,128)S(1)} %get-tuple-element.108.refs_1_, bf16[2,512,512]{2,1,0:T(8,128)(2,1)S(1)} %get-tuple-element.103.refs_1_.refs_2_, ...), custom_call_target="tpu_custom_call", output_to_operand_aliasing={{0}: (6, {})} | custom-call | flops 10737418240 | bytes 41943040 | tf_op jit(solution)/shard_map/finish/pallas_call | solution.py:355
  106.8 1.4 %collective-permute-done.31.refs_1_ = bf16[1040,128]{1,0:T(8,128)(2,1)S(1)} collective-permute-done((bf16[1040,128]{1,0:T(8,128)(2,1)S(1)}, bf16[1040,128]{1,0:T(8,128)(2,1)S(1)}, u32[]{:S(2)}, u32[]{:S(2)}) %collective-permute-start.31) | collective-permute-done | bytes 266272 | tf_op jit(solution)/shard_map/ppermute | solution.py:811
  108.2 1.2 %finish.8 = (bf16[8,512,512]{2,1,0:T(8,128)(2,1)}, f32[8,128]{1,0:T(8,128)S(1)}) custom-call(s32[16,128]{1,0:T(8,128)S(1)} %broadcast_in_dim.18.refs_0_, bf16[1040,128]{1,0:T(8,128)(2,1)S(1)} %step.5.refs_1_.refs_3_, bf16[2,512,512]{2,1,0:T(8,128)(2,1)S(1)} %get-tuple-element.111.refs_2_, ...), custom_call_target="tpu_custom_call", output_to_operand_aliasing={{0}: (4, {})} | custom-call | flops 5368709120 | bytes 20971520 | tf_op jit(solution)/shard_map/finish/pallas_call | solution.py:355
  109.5 0.3 collective-permute-done.33.refs_3_
  109.8 1.2 %finish.9 = bf16[8,512,512]{2,1,0:T(8,128)(2,1)} custom-call(s32[16,128]{1,0:T(8,128)S(1)} %broadcast_in_dim.18.refs_0_, f32[8,128]{1,0:T(8,128)S(1)} %get-tuple-element.113.refs_1_, bf16[2,512,512]{2,1,0:T(8,128)(2,1)S(1)} %collective-permute-done.32.refs_2_, bf16[1040,128]{1,0:T(8,128)(2,1)S(1)} %collective-permute-done.33.refs_3_, ...), custom_call_target="tpu_custom_call", output_to_operand_aliasing={{}: (4, {})} | custom-call | flops 5368709120 | bytes 20971520 | tf_op jit(solution)/shard_map/finish/pallas_call | solution.py:355
  (56 shorter events, 0.5 us)
Async XLA Ops:
  2.6 24.1 %collective-permute-start.2 = (bf16[512,512]{1,0:T(8,128)(2,1)S(1)}, bf16[512,512]{1,0:T(8,128)(2,1)S(1)}, u32[]{:S(2)}, u32[]{:S(2)}) collective-permute-start(bf16[512,512]{1,0:T(8,128)(2,1)S(1)} %pick.2.refs_1_), channel_id=1, source_target_pairs={{0,16},{8,24},{16,0},{24,8},{1,17},{9,25},{17,1},{25,9},{2,18},{10... | collective-permute-start | bytes 1572872 | tf_op jit(solution)/shard_map/ppermute | solution.py:734
  8.5 10.8 %collective-permute-start = (bf16[512,512]{1,0:T(8,128)(2,1)}, bf16[512,512]{1,0:T(8,128)(2,1)}, u32[]{:S(2)}, u32[]{:S(2)}) collective-permute-start(bf16[512,512]{1,0:T(8,128)(2,1)} %get-tuple-element.66), channel_id=1, source_target_pairs={{0,8},{8,0},{16,24},{24,16},{1,9},{9,1},{17,25},{25,17},{2,10},{10... | collective-permute-start | bytes 1572872 | tf_op jit(solution)/shard_map/ppermute | solution.py:734
  8.6 22.1 %collective-permute-start.4 = (bf16[512,512]{1,0:T(8,128)(2,1)S(1)}, bf16[512,512]{1,0:T(8,128)(2,1)S(1)}, u32[]{:S(2)}, u32[]{:S(2)}) collective-permute-start(bf16[512,512]{1,0:T(8,128)(2,1)S(1)} %get-tuple-element.59.refs_1_), channel_id=1, source_target_pairs={{0,24},{8,16},{16,8},{24,0},{1,25},{9,17},{17,9},{25,1},{2,26},{10... | collective-permute-start | bytes 1572872 | tf_op jit(solution)/shard_map/ppermute | solution.py:734
  8.7 7.0 %copy-start.4 = (s32[8]{0:T(128)S(1)}, s32[8]{0:T(128)}, u32[]{:S(2)}) copy-start(s32[8]{0:T(128)} %param.5) | copy-start | bytes 100
  12.0 0.8 copy-start
  12.8 0.8 copy-start.2
  13.6 9.3 %collective-permute-start.1 = (bf16[512,512]{1,0:T(8,128)(2,1)}, bf16[512,512]{1,0:T(8,128)(2,1)}, u32[]{:S(2)}, u32[]{:S(2)}) collective-permute-start(bf16[512,512]{1,0:T(8,128)(2,1)} %get-tuple-element.69), channel_id=1, source_target_pairs={{0,8},{8,0},{16,24},{24,16},{1,9},{9,1},{17,25},{25,17},{2,10},{10... | collective-permute-start | bytes 1572872 | tf_op jit(solution)/shard_map/ppermute | solution.py:734
  13.9 31.5 %collective-permute-start.7 = (bf16[512,512]{1,0:T(8,128)(2,1)}, bf16[512,512]{1,0:T(8,128)(2,1)S(1)}, u32[]{:S(2)}, u32[]{:S(2)}) collective-permute-start(bf16[512,512]{1,0:T(8,128)(2,1)} %get-tuple-element.81), channel_id=1, source_target_pairs={{0,16},{8,24},{16,0},{24,8},{1,17},{9,25},{17,1},{25,9},{2,18},{10... | collective-permute-start | bytes 1572872 | tf_op jit(solution)/shard_map/ppermute | solution.py:734
  22.7 8.0 %collective-permute-start.3 = (bf16[512,512]{1,0:T(8,128)(2,1)S(1)}, bf16[512,512]{1,0:T(8,128)(2,1)S(1)}, u32[]{:S(2)}, u32[]{:S(2)}) collective-permute-start(bf16[512,512]{1,0:T(8,128)(2,1)S(1)} %get-tuple-element.74), channel_id=1, source_target_pairs={{0,8},{8,0},{16,24},{24,16},{1,9},{9,1},{17,25},{25,17},{2,10},{10... | collective-permute-start | bytes 1572872 | tf_op jit(solution)/shard_map/ppermute | solution.py:780
  26.2 9.3 %collective-permute-start.5 = (bf16[512,512]{1,0:T(8,128)(2,1)S(1)}, bf16[512,512]{1,0:T(8,128)(2,1)S(1)}, u32[]{:S(2)}, u32[]{:S(2)}) collective-permute-start(bf16[512,512]{1,0:T(8,128)(2,1)S(1)} %get-tuple-element.78), channel_id=1, source_target_pairs={{0,8},{8,0},{16,24},{24,16},{1,9},{9,1},{17,25},{25,17},{2,10},{10... | collective-permute-start | bytes 1572872 | tf_op jit(solution)/shard_map/ppermute | solution.py:780
  30.7 3.0 %copy-start.1 = (bf16[512,512]{1,0:T(8,128)(2,1)S(1)}, bf16[512,512]{1,0:T(8,128)(2,1)}, u32[]{:S(2)}) copy-start(bf16[512,512]{1,0:T(8,128)(2,1)} %copy-done) | copy-start | bytes 1572868
  32.1 8.8 %collective-permute-start.6 = (f32[4,136,128]{2,1,0:T(8,128)S(1)}, f32[4,136,128]{2,1,0:T(8,128)S(1)}, u32[]{:S(2)}, u32[]{:S(2)}) collective-permute-start(f32[4,136,128]{2,1,0:T(8,128)S(1)} %slice_bitcast_fusion.1), channel_id=1, source_target_pairs={{0,1},{1,0},{2,3},{3,2},{4,5},{5,4},{6,7},{7,6},{8,9},{9,8},{10,11... | collective-permute-start | bytes 835592 | tf_op jit(solution)/shard_map/ppermute | solution.py:786
  33.7 17.9 %collective-permute-start.8 = (bf16[512,512]{1,0:T(8,128)(2,1)S(1)}, bf16[512,512]{1,0:T(8,128)(2,1)S(1)}, u32[]{:S(2)}, u32[]{:S(2)}) collective-permute-start(bf16[512,512]{1,0:T(8,128)(2,1)S(1)} %copy-done.1), channel_id=1, source_target_pairs={{0,24},{8,16},{16,8},{24,0},{1,25},{9,17},{17,9},{25,1},{2,26},{10... | collective-permute-start | bytes 1572872 | tf_op jit(solution)/shard_map/ppermute | solution.py:734
  41.0 12.1 %collective-permute-start.9 = (f32[136,128]{1,0:T(8,128)S(1)}, f32[136,128]{1,0:T(8,128)S(1)}, u32[]{:S(2)}, u32[]{:S(2)}) collective-permute-start(f32[136,128]{1,0:T(8,128)S(1)} %get-tuple-element.88), channel_id=1, source_target_pairs={{0,2},{1,3},{2,0},{3,1},{4,6},{5,7},{6,4},{7,5},{8,10},{9,11},{10,... | collective-permute-start | bytes 208904 | tf_op jit(solution)/shard_map/ppermute | solution.py:789
  42.6 10.4 %collective-permute-start.10 = (f32[136,128]{1,0:T(8,128)S(1)}, f32[136,128]{1,0:T(8,128)S(1)}, u32[]{:S(2)}, u32[]{:S(2)}) collective-permute-start(f32[136,128]{1,0:T(8,128)S(1)} %get-tuple-element.89), channel_id=1, source_target_pairs={{0,4},{1,5},{2,6},{3,7},{4,0},{5,1},{6,2},{7,3},{8,12},{9,13},{10,... | collective-permute-start | bytes 208904 | tf_op jit(solution)/shard_map/ppermute | solution.py:789
  45.2 7.8 %collective-permute-start.11 = (f32[136,128]{1,0:T(8,128)S(1)}, f32[136,128]{1,0:T(8,128)S(1)}, u32[]{:S(2)}, u32[]{:S(2)}) collective-permute-start(f32[136,128]{1,0:T(8,128)S(1)} %get-tuple-element.90), channel_id=1, source_target_pairs={{0,6},{1,7},{2,4},{3,5},{4,2},{5,3},{6,0},{7,1},{8,14},{9,15},{10,... | collective-permute-start | bytes 208904 | tf_op jit(solution)/shard_map/ppermute | solution.py:789
  45.4 29.6 %collective-permute-start.16 = (bf16[2,512,512]{2,1,0:T(8,128)(2,1)S(1)}, bf16[2,512,512]{2,1,0:T(8,128)(2,1)S(1)}, u32[]{:S(2)}, u32[]{:S(2)}) collective-permute-start(bf16[2,512,512]{2,1,0:T(8,128)(2,1)S(1)} %get-tuple-element.96), channel_id=1, source_target_pairs={{0,16},{8,24},{16,0},{24,8},{1,17},{9,25},{17,1},{25,9},{2,18},{10... | collective-permute-start | bytes 3145736 | tf_op jit(solution)/shard_map/ppermute | solution.py:782
  53.1 9.2 %collective-permute-start.12 = (f32[4,136,128]{2,1,0:T(8,128)S(1)}, f32[4,136,128]{2,1,0:T(8,128)S(1)}, u32[]{:S(2)}, u32[]{:S(2)}) collective-permute-start(f32[4,136,128]{2,1,0:T(8,128)S(1)} %slice_bitcast_fusion), channel_id=1, source_target_pairs={{0,1},{1,0},{2,3},{3,2},{4,5},{5,4},{6,7},{7,6},{8,9},{9,8},{10,11... | collective-permute-start | bytes 835592 | tf_op jit(solution)/shard_map/ppermute | solution.py:786
  54.7 7.7 %collective-permute-start.15 = (f32[136,128]{1,0:T(8,128)S(1)}, f32[136,128]{1,0:T(8,128)S(1)}, u32[]{:S(2)}, u32[]{:S(2)}) collective-permute-start(f32[136,128]{1,0:T(8,128)S(1)} %get-tuple-element.91.refs_0_.refs_2_), channel_id=1, source_target_pairs={{0,6},{1,7},{2,4},{3,5},{4,2},{5,3},{6,0},{7,1},{8,14},{9,15},{10,... | collective-permute-start | bytes 208904 | tf_op jit(solution)/shard_map/ppermute | solution.py:789
  58.3 6.5 %collective-permute-start.14 = (f32[136,128]{1,0:T(8,128)S(1)}, f32[136,128]{1,0:T(8,128)S(1)}, u32[]{:S(2)}, u32[]{:S(2)}) collective-permute-start(f32[136,128]{1,0:T(8,128)S(1)} %get-tuple-element.91.refs_0_.refs_2_), channel_id=1, source_target_pairs={{0,4},{1,5},{2,6},{3,7},{4,0},{5,1},{6,2},{7,3},{8,12},{9,13},{10,... | collective-permute-start | bytes 208904 | tf_op jit(solution)/shard_map/ppermute | solution.py:789
  58.3 6.5 %collective-permute-start.13 = (f32[136,128]{1,0:T(8,128)S(1)}, f32[136,128]{1,0:T(8,128)S(1)}, u32[]{:S(2)}, u32[]{:S(2)}) collective-permute-start(f32[136,128]{1,0:T(8,128)S(1)} %get-tuple-element.91.refs_0_.refs_2_), channel_id=1, source_target_pairs={{0,2},{1,3},{2,0},{3,1},{4,6},{5,7},{6,4},{7,5},{8,10},{9,11},{10,... | collective-permute-start | bytes 208904 | tf_op jit(solution)/shard_map/ppermute | solution.py:789
  64.8 35.5 %collective-permute-start.25 = (bf16[2,512,512]{2,1,0:T(8,128)(2,1)S(1)}, bf16[2,512,512]{2,1,0:T(8,128)(2,1)S(1)}, u32[]{:S(2)}, u32[]{:S(2)}) collective-permute-start(bf16[2,512,512]{2,1,0:T(8,128)(2,1)S(1)} %get-tuple-element.102), channel_id=1, source_target_pairs={{0,16},{8,24},{16,0},{24,8},{1,17},{9,25},{17,1},{25,9},{2,18},{10... | collective-permute-start | bytes 3145736 | tf_op jit(solution)/shard_map/ppermute | solution.py:782
  65.4 4.4 %collective-permute-start.17 = (f32[136,128]{1,0:T(8,128)S(1)}, f32[136,128]{1,0:T(8,128)S(1)}, u32[]{:S(2)}, u32[]{:S(2)}) collective-permute-start(f32[136,128]{1,0:T(8,128)S(1)} %get-tuple-element.97), channel_id=1, source_target_pairs={{0,2},{1,3},{2,0},{3,1},{4,6},{5,7},{6,4},{7,5},{8,10},{9,11},{10,... | collective-permute-start | bytes 208904 | tf_op jit(solution)/shard_map/ppermute | solution.py:789
  66.6 8.5 %collective-permute-start.18 = (f32[136,128]{1,0:T(8,128)S(1)}, f32[136,128]{1,0:T(8,128)S(1)}, u32[]{:S(2)}, u32[]{:S(2)}) collective-permute-start(f32[136,128]{1,0:T(8,128)S(1)} %get-tuple-element.98), channel_id=1, source_target_pairs={{0,4},{1,5},{2,6},{3,7},{4,0},{5,1},{6,2},{7,3},{8,12},{9,13},{10,... | collective-permute-start | bytes 208904 | tf_op jit(solution)/shard_map/ppermute | solution.py:789
  68.6 6.4 %collective-permute-start.19 = (f32[136,128]{1,0:T(8,128)S(1)}, f32[136,128]{1,0:T(8,128)S(1)}, u32[]{:S(2)}, u32[]{:S(2)}) collective-permute-start(f32[136,128]{1,0:T(8,128)S(1)} %get-tuple-element.99), channel_id=1, source_target_pairs={{0,6},{1,7},{2,4},{3,5},{4,2},{5,3},{6,0},{7,1},{8,14},{9,15},{10,... | collective-permute-start | bytes 208904 | tf_op jit(solution)/shard_map/ppermute | solution.py:789
  75.1 11.0 %collective-permute-start.23 = (f32[4,136,128]{2,1,0:T(8,128)S(1)}, f32[4,136,128]{2,1,0:T(8,128)S(1)}, u32[]{:S(2)}, u32[]{:S(2)}) collective-permute-start(f32[4,136,128]{2,1,0:T(8,128)S(1)} %get-tuple-element.101.refs_2_), channel_id=1, source_target_pairs={{0,1},{1,0},{2,3},{3,2},{4,5},{5,4},{6,7},{7,6},{8,9},{9,8},{10,11... | collective-permute-start | bytes 835592 | tf_op jit(solution)/shard_map/ppermute | solution.py:786
  76.7 6.7 %collective-permute-start.22 = (f32[136,128]{1,0:T(8,128)S(1)}, f32[136,128]{1,0:T(8,128)S(1)}, u32[]{:S(2)}, u32[]{:S(2)}) collective-permute-start(f32[136,128]{1,0:T(8,128)S(1)} %get-tuple-element.100.refs_0_.refs_1_), channel_id=1, source_target_pairs={{0,6},{1,7},{2,4},{3,5},{4,2},{5,3},{6,0},{7,1},{8,14},{9,15},{10,... | collective-permute-start | bytes 208904 | tf_op jit(solution)/shard_map/ppermute | solution.py:789
  80.3 5.2 %collective-permute-start.21 = (f32[136,128]{1,0:T(8,128)S(1)}, f32[136,128]{1,0:T(8,128)S(1)}, u32[]{:S(2)}, u32[]{:S(2)}) collective-permute-start(f32[136,128]{1,0:T(8,128)S(1)} %get-tuple-element.100.refs_0_.refs_1_), channel_id=1, source_target_pairs={{0,4},{1,5},{2,6},{3,7},{4,0},{5,1},{6,2},{7,3},{8,12},{9,13},{10,... | collective-permute-start | bytes 208904 | tf_op jit(solution)/shard_map/ppermute | solution.py:789
  80.3 5.2 %collective-permute-start.20 = (f32[136,128]{1,0:T(8,128)S(1)}, f32[136,128]{1,0:T(8,128)S(1)}, u32[]{:S(2)}, u32[]{:S(2)}) collective-permute-start(f32[136,128]{1,0:T(8,128)S(1)} %get-tuple-element.100.refs_0_.refs_1_), channel_id=1, source_target_pairs={{0,2},{1,3},{2,0},{3,1},{4,6},{5,7},{6,4},{7,5},{8,10},{9,11},{10,... | collective-permute-start | bytes 208904 | tf_op jit(solution)/shard_map/ppermute | solution.py:789
  85.5 8.1 %collective-permute-start.24 = (f32[4,136,128]{2,1,0:T(8,128)S(1)}, f32[4,136,128]{2,1,0:T(8,128)S(1)}, u32[]{:S(2)}, u32[]{:S(2)}) collective-permute-start(f32[4,136,128]{2,1,0:T(8,128)S(1)} %stack.12.refs_1_.refs_2_), channel_id=1, source_target_pairs={{0,1},{1,0},{2,3},{3,2},{4,5},{5,4},{6,7},{7,6},{8,9},{9,8},{10,11... | collective-permute-start | bytes 835592 | tf_op jit(solution)/shard_map/ppermute | solution.py:786
  92.0 8.9 %copy-start.3 = (bf16[512,512]{1,0:T(8,128)(2,1)S(1)}, bf16[512,512]{1,0:T(8,128)(2,1)}, u32[]{:S(2)}) copy-start(bf16[512,512]{1,0:T(8,128)(2,1)} %copy-done.2) | copy-start | bytes 1572868
  92.0 8.8 %collective-permute-start.26 = (bf16[1040,128]{1,0:T(8,128)(2,1)S(1)}, bf16[1040,128]{1,0:T(8,128)(2,1)S(1)}, u32[]{:S(2)}, u32[]{:S(2)}) collective-permute-start(bf16[1040,128]{1,0:T(8,128)(2,1)S(1)} %polynomial.2.refs_1_.refs_4_), channel_id=1, source_target_pairs={{0,8},{8,0},{16,24},{24,16},{1,9},{9,1},{17,25},{25,17},{2,10},{10... | collective-permute-start | bytes 798728 | tf_op jit(solution)/shard_map/ppermute | solution.py:813
  92.1 10.4 %collective-permute-start.27 = (bf16[1040,128]{1,0:T(8,128)(2,1)S(1)}, bf16[1040,128]{1,0:T(8,128)(2,1)S(1)}, u32[]{:S(2)}, u32[]{:S(2)}) collective-permute-start(bf16[1040,128]{1,0:T(8,128)(2,1)S(1)} %polynomial.2.refs_1_.refs_4_), channel_id=1, source_target_pairs={{0,16},{8,24},{16,0},{24,8},{1,17},{9,25},{17,1},{25,9},{2,18},{10... | collective-permute-start | bytes 798728 | tf_op jit(solution)/shard_map/ppermute | solution.py:811
  99.7 8.5 %collective-permute-start.31 = (bf16[1040,128]{1,0:T(8,128)(2,1)S(1)}, bf16[1040,128]{1,0:T(8,128)(2,1)S(1)}, u32[]{:S(2)}, u32[]{:S(2)}) collective-permute-start(bf16[1040,128]{1,0:T(8,128)(2,1)S(1)} %polynomial.3.refs_0_.refs_4_), channel_id=1, source_target_pairs={{0,16},{8,24},{16,0},{24,8},{1,17},{9,25},{17,1},{25,9},{2,18},{10... | collective-permute-start | bytes 798728 | tf_op jit(solution)/shard_map/ppermute | solution.py:811
  100.3 2.7 %collective-permute-start.28 = (bf16[1040,128]{1,0:T(8,128)(2,1)S(1)}, bf16[1040,128]{1,0:T(8,128)(2,1)S(1)}, u32[]{:S(2)}, u32[]{:S(2)}) collective-permute-start(bf16[1040,128]{1,0:T(8,128)(2,1)S(1)} %polynomial.3.refs_0_.refs_4_), channel_id=1, source_target_pairs={{0,8},{8,0},{16,24},{24,16},{1,9},{9,1},{17,25},{25,17},{2,10},{10... | collective-permute-start | bytes 798728 | tf_op jit(solution)/shard_map/ppermute | solution.py:813
  100.3 9.2 %collective-permute-start.32 = (bf16[2,512,512]{2,1,0:T(8,128)(2,1)S(1)}, bf16[2,512,512]{2,1,0:T(8,128)(2,1)S(1)}, u32[]{:S(2)}, u32[]{:S(2)}) collective-permute-start(bf16[2,512,512]{2,1,0:T(8,128)(2,1)S(1)} %get-tuple-element.111.refs_2_), channel_id=1, source_target_pairs={{0,8},{8,0},{16,24},{24,16},{1,9},{9,1},{17,25},{25,17},{2,10},{10... | collective-permute-start | bytes 3145736 | tf_op jit(solution)/shard_map/ppermute | solution.py:893
  100.8 4.4 %collective-permute-start.29 = (bf16[2,512,512]{2,1,0:T(8,128)(2,1)S(1)}, bf16[2,512,512]{2,1,0:T(8,128)(2,1)S(1)}, u32[]{:S(2)}, u32[]{:S(2)}) collective-permute-start(bf16[2,512,512]{2,1,0:T(8,128)(2,1)S(1)} %get-tuple-element.103.refs_1_.refs_2_), channel_id=1, source_target_pairs={{0,8},{8,0},{16,24},{24,16},{1,9},{9,1},{17,25},{25,17},{2,10},{10... | collective-permute-start | bytes 3145736 | tf_op jit(solution)/shard_map/ppermute | solution.py:893
  102.5 2.7 %collective-permute-start.30 = (bf16[1040,128]{1,0:T(8,128)(2,1)S(1)}, bf16[1040,128]{1,0:T(8,128)(2,1)S(1)}, u32[]{:S(2)}, u32[]{:S(2)}) collective-permute-start(bf16[1040,128]{1,0:T(8,128)(2,1)S(1)} %step.4.refs_1_.refs_4_), channel_id=1, source_target_pairs={{0,8},{8,0},{16,24},{24,16},{1,9},{9,1},{17,25},{25,17},{2,10},{10... | collective-permute-start | bytes 798728 | tf_op jit(solution)/shard_map/ppermute | solution.py:818
  108.2 1.5 %collective-permute-start.33 = (bf16[1040,128]{1,0:T(8,128)(2,1)S(1)}, bf16[1040,128]{1,0:T(8,128)(2,1)S(1)}, u32[]{:S(2)}, u32[]{:S(2)}) collective-permute-start(bf16[1040,128]{1,0:T(8,128)(2,1)S(1)} %step.5.refs_1_.refs_3_), channel_id=1, source_target_pairs={{0,8},{8,0},{16,24},{24,16},{1,9},{9,1},{17,25},{25,17},{2,10},{10... | collective-permute-start | bytes 798728 | tf_op jit(solution)/shard_map/ppermute | solution.py:818
